TPU v7x, 32 devices: a whole 2x2x4 slice. The times are simulated.
32 devices in a mesh: rcv: 8 (over z, core), tm: 4 (over y, x).
Axes of the slice: x: 2, y: 2, z: 4, core: 2. Of those that a mesh axis runs over, the one named last changes fastest.
Arguments:
- spectra: bfloat16 [1024, 4, 3072], P('rcv', 'tm'), may hold values from -6 to 6
- valid: int32 [1024, 4], P('rcv', 'tm'), may hold values 0 or 1
- sources: int32 [2, 8], replicated, may hold values from 0 to 1023
Outputs:
- stack: float32 [2, 8, 1024, 301], P(None, None, ('rcv', 'tm'))
All inputs are finite; a program needn't handle non-finite values. No bound on the sum of `valid` on one device may be relied on, other than what follows from the above.
Results may differ from a plain program's by a relative error of at most 0.004.
Values may be sent and summed in bfloat16 or wider, within the bound.
No kernel may reach another device: no remote copies, remote signals or barrier semaphores. Data moves between devices by JAX's collectives and lax.ppermute only.
A program may use at most 64 MiB of HBM per device.

v0:
```python
import functools
import math

import jax
import jax.numpy as jnp
import numpy as np
from jax import lax
from jax.experimental import pallas as pl
from jax.experimental.pallas import tpu as pltpu
from jax.sharding import PartitionSpec as P

NT = 4096
LAG = 150
HALF_WIN = 64
EPSILON = 1e-06

UNUSABLE = 64.0
USABLE_BELOW = 32.0

LANES = 128
BLOCK = 256
MEBI = 1 << 20


def band_matrix():
    row = np.arange(BLOCK + 2 * LANES)[:, None] - LANES
    col = np.arange(BLOCK)[None, :]
    return (np.abs(row - col) <= HALF_WIN).astype(jnp.bfloat16)


def lag_table(nbins):
    winding = np.mod(
        np.arange(1, nbins + 1, dtype=np.int64)[:, None]
        * np.arange(-LAG, LAG + 1, dtype=np.int64)[None, :],
        NT,
    )
    theta = winding * (2.0 * math.pi / NT)
    table = np.concatenate([np.cos(theta), -np.sin(theta)], axis=0)
    columns = table.shape[1]
    padded = -(-columns // LANES) * LANES
    return np.pad(table, ((0, 0), (0, padded - columns))).astype(jnp.bfloat16)


def whiten_rows(rows, nbins, band_ref, high, low, store):
    count = rows.shape[0]
    real = rows[:, :nbins].astype(jnp.float32)
    imag = rows[:, nbins:].astype(jnp.float32)
    amplitude = jnp.sqrt(real * real + imag * imag)
    rounded = amplitude.astype(jnp.bfloat16)
    edge = jnp.zeros((count, LANES), jnp.bfloat16)
    for part, value in (
        (high, rounded),
        (low, (amplitude - rounded.astype(jnp.float32)).astype(jnp.bfloat16)),
    ):
        part[:count, :LANES] = edge
        part[:count, LANES : LANES + nbins] = value
        part[:count, LANES + nbins :] = edge
    band = band_ref[...]
    for first in range(0, nbins, BLOCK):
        span = slice(first, first + BLOCK + 2 * LANES)
        window = jnp.dot(high[:count, span], band, preferred_element_type=jnp.float32)
        window += jnp.dot(low[:count, span], band, preferred_element_type=jnp.float32)
        index = first + lax.broadcasted_iota(jnp.int32, (1, BLOCK), 1)
        counted = jnp.minimum(index, HALF_WIN) + jnp.minimum(nbins - 1 - index, HALF_WIN) + 1
        smooth = window / counted.astype(jnp.float32)
        factor = 1.0 / (smooth + EPSILON)
        re = real[:, first : first + BLOCK]
        im = imag[:, first : first + BLOCK]
        usable = re < USABLE_BELOW
        store(
            first,
            jnp.where(usable, re * factor, 0.0).astype(jnp.bfloat16),
            jnp.where(usable, im * factor, 0.0).astype(jnp.bfloat16),
        )


def whiten_kernel(segments, *refs):
    blocks, (band_ref, out_ref, valid_ref, high, low) = refs[:segments], refs[segments:]
    rows = jnp.concatenate([ref[...] for ref in blocks], axis=0)
    nbins = rows.shape[1] // 2

    def store(first, re, im):
        out_ref[:, first : first + BLOCK] = re
        out_ref[:, nbins + first : nbins + first + BLOCK] = im

    whiten_rows(rows, nbins, band_ref, high, low, store)
    valid_ref[...] = jnp.where(rows[:, :LANES].astype(jnp.float32) < USABLE_BELOW, 1.0, 0.0)


def stack_kernel(segments, keep, *refs):
    blocks = refs[:segments]
    rcv_ref, rcv_valid, band_ref, table_ref, out_ref, src, src_valid, high, low, cross = refs[
        segments:
    ]
    nsrc = blocks[0].shape[0]
    nbins = rcv_ref.shape[1] // 2
    rows = jnp.concatenate([ref[...] for ref in blocks], axis=0)

    def store(first, re, im):
        src[:, first : first + BLOCK] = re.astype(jnp.float32)
        src[:, nbins + first : nbins + first + BLOCK] = im.astype(jnp.float32)

    whiten_rows(rows, nbins, band_ref, high, low, store)
    src_valid[...] = jnp.where(rows[:, :LANES].astype(jnp.float32) < USABLE_BELOW, 1.0, 0.0)

    def one_block(block, carry):
        re_at = pl.ds(pl.multiple_of(block * LANES, LANES), LANES)
        im_at = pl.ds(pl.multiple_of(nbins + block * LANES, LANES), LANES)
        rcv_re = rcv_ref[:, re_at].astype(jnp.float32)
        rcv_im = rcv_ref[:, im_at].astype(jnp.float32)
        for source in range(nsrc):
            real, imag = 0.0, 0.0
            for segment in range(segments):
                row = segment * nsrc + source
                s_re, s_im = src[row : row + 1, re_at], src[row : row + 1, im_at]
                r_re = rcv_re[segment * keep : (segment + 1) * keep]
                r_im = rcv_im[segment * keep : (segment + 1) * keep]
                real = real + (s_re * r_re + s_im * r_im)
                imag = imag + (s_im * r_re - s_re * r_im)
            at = slice(source * keep, (source + 1) * keep)
            cross[at, re_at] = real.astype(cross.dtype)
            cross[at, im_at] = imag.astype(cross.dtype)
        return carry

    lax.fori_loop(0, nbins // LANES, one_block, 0)

    lags = out_ref.shape[1]
    scale = 2.0 / math.sqrt(nbins)
    lagged = jnp.dot(
        cross[...].astype(jnp.bfloat16), table_ref[...], preferred_element_type=jnp.float32
    )
    for source in range(nsrc):
        pairs = 0.0
        for segment in range(segments):
            row = segment * nsrc + source
            pairs = pairs + src_valid[row : row + 1, :] * rcv_valid[
                segment * keep : (segment + 1) * keep, :
            ]
        weight = scale / jnp.maximum(pairs, 1.0)
        for first in range(0, lags, LANES):
            last = min(first + LANES, lags)
            value = lagged[source * keep : (source + 1) * keep, first : first + LANES] * weight
            out_ref[source * keep : (source + 1) * keep, first:last] = value[:, : last - first]


def whiten_blocks(blocks, band):
    segments, (keep, width) = len(blocks), blocks[0].shape
    count, nbins = segments * keep, width // 2
    padded = pltpu.VMEM((count, nbins + 2 * LANES), jnp.bfloat16)
    vmem = pl.BlockSpec(memory_space=pltpu.VMEM)
    return pl.pallas_call(
        functools.partial(whiten_kernel, segments),
        out_shape=(
            jax.ShapeDtypeStruct((count, width), jnp.bfloat16),
            jax.ShapeDtypeStruct((count, LANES), jnp.float32),
        ),
        in_specs=[vmem] * (segments + 1),
        out_specs=(vmem, vmem),
        scratch_shapes=[padded, padded],
        compiler_params=pltpu.CompilerParams(vmem_limit_bytes=32 * MEBI),
        cost_estimate=pl.CostEstimate(
            flops=count * width * 1024, bytes_accessed=count * width * 4, transcendentals=0
        ),
        name="whiten_receivers",
    )(*blocks, band)


def stack_blocks(sources, receivers, receivers_valid, band, table):
    segments, (nsrc, width) = len(sources), sources[0].shape
    keep = receivers.shape[0] // segments
    nbins, count = width // 2, segments * nsrc
    padded = pltpu.VMEM((count, nbins + 2 * LANES), jnp.bfloat16)
    cross_type = jnp.bfloat16 if keep % 16 == 0 else jnp.float32
    vmem = pl.BlockSpec(memory_space=pltpu.VMEM)
    return pl.pallas_call(
        functools.partial(stack_kernel, segments, keep),
        out_shape=jax.ShapeDtypeStruct((nsrc * keep, 2 * LAG + 1), jnp.float32),
        in_specs=[vmem] * (segments + 4),
        out_specs=vmem,
        scratch_shapes=[
            pltpu.VMEM((count, width), jnp.float32),
            pltpu.VMEM((count, LANES), jnp.float32),
            padded,
            padded,
            pltpu.VMEM((nsrc * keep, width), cross_type),
        ],
        compiler_params=pltpu.CompilerParams(vmem_limit_bytes=40 * MEBI),
        cost_estimate=pl.CostEstimate(
            flops=2 * nsrc * keep * width * 2 * LAG,
            bytes_accessed=width * 1024,
            transcendentals=0,
        ),
        name="stack_sources",
    )(*sources, receivers, receivers_valid, band, table)


def swapped(value, axis, size, step):
    return lax.ppermute(value, axis, [(i, i ^ step) for i in range(size)])


def shards(rcv_size, tm_size, spectra, valid, sources):
    channels, _, width = spectra.shape
    keep = channels // tm_size
    rounds, per_round = sources.shape
    mine = lax.axis_index("tm")
    encoded = jnp.where(valid != 0, spectra[:, 0, :], jnp.bfloat16(UNUSABLE))

    onehot = (
        sources.reshape(-1)[:, None] - lax.axis_index("rcv") * channels
        == jnp.arange(channels, dtype=jnp.int32)[None, :]
    )
    picked = jnp.dot(
        onehot.astype(jnp.bfloat16), encoded, preferred_element_type=jnp.float32
    ).astype(jnp.bfloat16)

    def block_for(step):
        return lax.dynamic_slice_in_dim(encoded, (mine ^ step) * keep, keep, 0)

    receivers = [block_for(0)] + [
        swapped(block_for(step), "tm", tm_size, step) for step in range(1, tm_size)
    ]
    step = 1
    while step < rcv_size:
        picked = picked + swapped(picked, "rcv", rcv_size, step)
        step *= 2
    chosen = [picked] + [swapped(picked, "tm", tm_size, step) for step in range(1, tm_size)]

    band = jnp.asarray(band_matrix())
    whitened, usable = whiten_blocks(receivers, band)
    stack = stack_blocks(chosen, whitened, usable, band, jnp.asarray(lag_table(width // 2)))
    return stack.reshape(rounds, per_round, keep, 2 * LAG + 1)


def solution(mesh):
    body = functools.partial(shards, mesh.shape["rcv"], mesh.shape["tm"])
    in_specs = (P("rcv", "tm", None), P("rcv", "tm"), P())
    out_specs = P(None, None, ("rcv", "tm"), None)
    return jax.shard_map(body, mesh=mesh, in_specs=in_specs, out_specs=out_specs, check_vma=False)
```

profile of v0, /device:TPU:0, one launch (start us, length us, event | category | flops | bytes accessed | tf_op | source)
XLA Modules:
  0.0 33.5 jit_solution(6776291444900168045)
XLA Ops:
  0.0 0.7 %compare_bitcast_fusion = pred[128]{0:T(512)(128)(4,1)S(1)} fusion(s32[128,1]{0,1:T(1,128)} %param.6), kind=kLoop, calls=%fused_computation.4 | loop fusion | flops 128 | bytes 640 | tf_op jit(solution)/shard_map/jit(_where)/broadcast_in_dim | solution.py:206
  0.7 0.7 %broadcast_subtract_fusion = s32[2,8]{1,0:T(2,128)S(1)} fusion(s32[2,8]{1,0:T(2,128)} %param.7, s32[]{:T(128)S(6)} %mul.15), kind=kLoop, calls=%fused_computation.9 | loop fusion | flops 16 | bytes 132 | tf_op jit(solution)/shard_map/sub | solution.py:209
  1.3 0.1 sub.16
  1.4 0.0 copy-start.1
  1.4 1.3 %bitcast_select_fusion = bf16[128,3072]{1,0:T(8,128)(2,1)S(1)} fusion(bf16[128,1,3072]{2,0,1:T(8,128)(2,1)} %param.5, pred[128]{0:T(512)(128)(4,1)S(1)} %compare_bitcast_fusion), kind=kLoop, calls=%fused_computation.1 | loop fusion | flops 393216 | bytes 1572992 | tf_op jit(solution)/shard_map/jit(_where)/select_n | solution.py:206
  2.7 0.0 copy-start
  2.8 0.3 convolution_convert_fusion
  3.0 0.5 %collective-permute-start = (bf16[16,3072]{1,0:T(8,128)(2,1)S(1)}, bf16[16,3072]{1,0:T(8,128)(2,1)}, u32[]{:S(2)}, u32[]{:S(2)}) collective-permute-start(bf16[16,3072]{1,0:T(8,128)(2,1)S(1)} %convolution_convert_fusion), channel_id=1, source_target_pairs={{0,4},{4,0},{8,12},{12,8},{16,20},{20,16},{24,28},{28,24},{1,5},{5... | collective-permute-start | bytes 294920 | tf_op jit(solution)/shard_map/ppermute | solution.py:198
  3.5 1.1 %collective-permute-done = bf16[16,3072]{1,0:T(8,128)(2,1)} collective-permute-done((bf16[16,3072]{1,0:T(8,128)(2,1)S(1)}, bf16[16,3072]{1,0:T(8,128)(2,1)}, u32[]{:S(2)}, u32[]{:S(2)}) %collective-permute-start) | collective-permute-done | bytes 98336 | tf_op jit(solution)/shard_map/ppermute | solution.py:198
  4.6 0.9 %add.21 = bf16[16,3072]{1,0:T(8,128)(2,1)S(1)} add(bf16[16,3072]{1,0:T(8,128)(2,1)S(1)} %convolution_convert_fusion, bf16[16,3072]{1,0:T(8,128)(2,1)} %collective-permute-done) | non-fusion elementwise | flops 49152 | bytes 294912 | tf_op jit(solution)/shard_map/add | solution.py:224
  5.5 3.0 %collective-permute-start.1 = (bf16[16,3072]{1,0:T(8,128)(2,1)S(1)}, bf16[16,3072]{1,0:T(8,128)(2,1)S(1)}, u32[]{:S(2)}, u32[]{:S(2)}) collective-permute-start(bf16[16,3072]{1,0:T(8,128)(2,1)S(1)} %add.21), channel_id=1, source_target_pairs={{0,8},{4,12},{8,0},{12,4},{16,24},{20,28},{24,16},{28,20},{1,9},{5... | collective-permute-start | bytes 294920 | tf_op jit(solution)/shard_map/ppermute | solution.py:198
  8.5 0.1 constant_dynamic-slice_fusion
  8.6 2.5 %collective-permute-start.8 = (bf16[32,3072]{1,0:T(8,128)(2,1)S(1)}, bf16[32,3072]{1,0:T(8,128)(2,1)S(1)}, u32[]{:S(2)}, u32[]{:S(2)}) collective-permute-start(bf16[32,3072]{1,0:T(8,128)(2,1)S(1)} %get-tuple-element.9), channel_id=1, source_target_pairs={{0,3},{1,2},{2,1},{3,0},{4,7},{5,6},{6,5},{7,4},{8,11},{9,10},{10,... | collective-permute-start | bytes 589832 | tf_op jit(solution)/shard_map/ppermute | solution.py:198
  11.1 0.5 %collective-permute-start.7 = (bf16[32,3072]{1,0:T(8,128)(2,1)S(1)}, bf16[32,3072]{1,0:T(8,128)(2,1)S(1)}, u32[]{:S(2)}, u32[]{:S(2)}) collective-permute-start(bf16[32,3072]{1,0:T(8,128)(2,1)S(1)} %get-tuple-element.10), channel_id=1, source_target_pairs={{0,2},{1,3},{2,0},{3,1},{4,6},{5,7},{6,4},{7,5},{8,10},{9,11},{10,... | collective-permute-start | bytes 589832 | tf_op jit(solution)/shard_map/ppermute | solution.py:198
  11.6 0.5 %collective-permute-start.6 = (bf16[32,3072]{1,0:T(8,128)(2,1)S(1)}, bf16[32,3072]{1,0:T(8,128)(2,1)S(1)}, u32[]{:S(2)}, u32[]{:S(2)}) collective-permute-start(bf16[32,3072]{1,0:T(8,128)(2,1)S(1)} %get-tuple-element.11), channel_id=1, source_target_pairs={{0,1},{1,0},{2,3},{3,2},{4,5},{5,4},{6,7},{7,6},{8,9},{9,8},{10,11... | collective-permute-start | bytes 589832 | tf_op jit(solution)/shard_map/ppermute | solution.py:198
  12.1 0.0 collective-permute-done.1
  12.2 2.7 %collective-permute-start.2 = (bf16[16,3072]{1,0:T(8,128)(2,1)S(1)}, bf16[16,3072]{1,0:T(8,128)(2,1)S(1)}, u32[]{:S(2)}, u32[]{:S(2)}) collective-permute-start(bf16[16,3072]{1,0:T(8,128)(2,1)S(1)} %add.22), channel_id=1, source_target_pairs={{0,16},{4,20},{8,24},{12,28},{16,0},{20,4},{24,8},{28,12},{1,17},{... | collective-permute-start | bytes 294920 | tf_op jit(solution)/shard_map/ppermute | solution.py:198
  14.8 4.3 %collective-permute-done.2 = bf16[16,3072]{1,0:T(8,128)(2,1)S(1)} collective-permute-done((bf16[16,3072]{1,0:T(8,128)(2,1)S(1)}, bf16[16,3072]{1,0:T(8,128)(2,1)S(1)}, u32[]{:S(2)}, u32[]{:S(2)}) %collective-permute-start.2) | collective-permute-done | bytes 98336 | tf_op jit(solution)/shard_map/ppermute | solution.py:198
  19.1 2.4 %collective-permute-start.5 = (bf16[16,3072]{1,0:T(8,128)(2,1)S(1)}, bf16[16,3072]{1,0:T(8,128)(2,1)S(1)}, u32[]{:S(2)}, u32[]{:S(2)}) collective-permute-start(bf16[16,3072]{1,0:T(8,128)(2,1)S(1)} %add.23.refs_0_), channel_id=1, source_target_pairs={{0,3},{1,2},{2,1},{3,0},{4,7},{5,6},{6,5},{7,4},{8,11},{9,10},{10,... | collective-permute-start | bytes 294920 | tf_op jit(solution)/shard_map/ppermute | solution.py:198
  21.5 0.5 %collective-permute-start.4 = (bf16[16,3072]{1,0:T(8,128)(2,1)S(1)}, bf16[16,3072]{1,0:T(8,128)(2,1)S(1)}, u32[]{:S(2)}, u32[]{:S(2)}) collective-permute-start(bf16[16,3072]{1,0:T(8,128)(2,1)S(1)} %add.23.refs_0_), channel_id=1, source_target_pairs={{0,2},{1,3},{2,0},{3,1},{4,6},{5,7},{6,4},{7,5},{8,10},{9,11},{10,... | collective-permute-start | bytes 294920 | tf_op jit(solution)/shard_map/ppermute | solution.py:198
  22.0 0.0 collective-permute-done.8.refs_3_
  22.0 0.6 %collective-permute-start.3 = (bf16[16,3072]{1,0:T(8,128)(2,1)S(1)}, bf16[16,3072]{1,0:T(8,128)(2,1)S(1)}, u32[]{:S(2)}, u32[]{:S(2)}) collective-permute-start(bf16[16,3072]{1,0:T(8,128)(2,1)S(1)} %add.23.refs_0_), channel_id=1, source_target_pairs={{0,1},{1,0},{2,3},{3,2},{4,5},{5,4},{6,7},{7,6},{8,9},{9,8},{10,11... | collective-permute-start | bytes 294920 | tf_op jit(solution)/shard_map/ppermute | solution.py:198
  22.7 0.0 collective-permute-done.7.refs_2_
  22.7 0.0 collective-permute-done.6.refs_1_
  22.7 0.0 copy-done.1
  22.7 0.9 %whiten_receivers.1 = (bf16[128,3072]{1,0:T(8,128)(2,1)S(1)}, f32[128,128]{1,0:T(8,128)S(1)}) custom-call(bf16[32,3072]{1,0:T(8,128)(2,1)S(1)} %get-tuple-element.12.refs_0_, bf16[32,3072]{1,0:T(8,128)(2,1)S(1)} %collective-permute-done.6.refs_1_, bf16[32,3072]{1,0:T(8,128)(2,1)S(1)} %collective-permute-done.7.refs_2_, ...), custom_call_target="tpu_custom_call" | custom-call | flops 402653184 | bytes 1572864 | tf_op jit(solution)/shard_map/whiten_receivers/pallas_call | solution.py:151
  23.5 1.1 %collective-permute-done.5.refs_3_ = bf16[16,3072]{1,0:T(8,128)(2,1)S(1)} collective-permute-done((bf16[16,3072]{1,0:T(8,128)(2,1)S(1)}, bf16[16,3072]{1,0:T(8,128)(2,1)S(1)}, u32[]{:S(2)}, u32[]{:S(2)}) %collective-permute-start.5) | collective-permute-done | bytes 98336 | tf_op jit(solution)/shard_map/ppermute | solution.py:198
  24.7 1.4 %collective-permute-done.4.refs_2_ = bf16[16,3072]{1,0:T(8,128)(2,1)S(1)} collective-permute-done((bf16[16,3072]{1,0:T(8,128)(2,1)S(1)}, bf16[16,3072]{1,0:T(8,128)(2,1)S(1)}, u32[]{:S(2)}, u32[]{:S(2)}) %collective-permute-start.4) | collective-permute-done | bytes 98336 | tf_op jit(solution)/shard_map/ppermute | solution.py:198
  26.1 0.5 %collective-permute-done.3.refs_1_ = bf16[16,3072]{1,0:T(8,128)(2,1)S(1)} collective-permute-done((bf16[16,3072]{1,0:T(8,128)(2,1)S(1)}, bf16[16,3072]{1,0:T(8,128)(2,1)S(1)}, u32[]{:S(2)}, u32[]{:S(2)}) %collective-permute-start.3) | collective-permute-done | bytes 98336 | tf_op jit(solution)/shard_map/ppermute | solution.py:198
  26.6 0.0 copy-done
  26.6 6.8 %stack_sources.1 = f32[512,301]{1,0:T(8,128)} custom-call(bf16[16,3072]{1,0:T(8,128)(2,1)S(1)} %add.23.refs_0_, bf16[16,3072]{1,0:T(8,128)(2,1)S(1)} %collective-permute-done.3.refs_1_, bf16[16,3072]{1,0:T(8,128)(2,1)S(1)} %collective-permute-done.4.refs_2_, bf16[16,3072]{1,0:T(8,128)(2,1)S(1)} %collective-permute-done.5.refs_3_, ...), custom_call_target="tpu_custom_call" | custom-call | flops 943718400 | bytes 3145728 | tf_op jit(solution)/shard_map/stack_sources/pallas_call | solution.py:175
  (2 shorter events, 0.1 us)
Async XLA Ops:
  1.4 21.2 %copy-start.1 = (bf16[512,256]{1,0:T(8,128)(2,1)S(1)}, bf16[512,256]{1,0:T(8,128)(2,1)}, u32[]{:S(2)}) copy-start(bf16[512,256]{1,0:T(8,128)(2,1)} %constant.28.clone.refs_4_.refs_6_) | copy-start | bytes 786436
  2.7 23.9 %copy-start = (bf16[3072,384]{1,0:T(8,128)(2,1)S(1)}, bf16[3072,384]{1,0:T(8,128)(2,1)}, u32[]{:S(2)}) copy-start(bf16[3072,384]{1,0:T(8,128)(2,1)} %constant.29.clone.refs_7_) | copy-start | bytes 7077892
  3.0 1.6 %collective-permute-start = (bf16[16,3072]{1,0:T(8,128)(2,1)S(1)}, bf16[16,3072]{1,0:T(8,128)(2,1)}, u32[]{:S(2)}, u32[]{:S(2)}) collective-permute-start(bf16[16,3072]{1,0:T(8,128)(2,1)S(1)} %convolution_convert_fusion), channel_id=1, source_target_pairs={{0,4},{4,0},{8,12},{12,8},{16,20},{20,16},{24,28},{28,24},{1,5},{5... | collective-permute-start | bytes 294920 | tf_op jit(solution)/shard_map/ppermute | solution.py:198
  5.5 6.6 %collective-permute-start.1 = (bf16[16,3072]{1,0:T(8,128)(2,1)S(1)}, bf16[16,3072]{1,0:T(8,128)(2,1)S(1)}, u32[]{:S(2)}, u32[]{:S(2)}) collective-permute-start(bf16[16,3072]{1,0:T(8,128)(2,1)S(1)} %add.21), channel_id=1, source_target_pairs={{0,8},{4,12},{8,0},{12,4},{16,24},{20,28},{24,16},{28,20},{1,9},{5... | collective-permute-start | bytes 294920 | tf_op jit(solution)/shard_map/ppermute | solution.py:198
  8.6 13.4 %collective-permute-start.8 = (bf16[32,3072]{1,0:T(8,128)(2,1)S(1)}, bf16[32,3072]{1,0:T(8,128)(2,1)S(1)}, u32[]{:S(2)}, u32[]{:S(2)}) collective-permute-start(bf16[32,3072]{1,0:T(8,128)(2,1)S(1)} %get-tuple-element.9), channel_id=1, source_target_pairs={{0,3},{1,2},{2,1},{3,0},{4,7},{5,6},{6,5},{7,4},{8,11},{9,10},{10,... | collective-permute-start | bytes 589832 | tf_op jit(solution)/shard_map/ppermute | solution.py:198
  11.1 11.6 %collective-permute-start.7 = (bf16[32,3072]{1,0:T(8,128)(2,1)S(1)}, bf16[32,3072]{1,0:T(8,128)(2,1)S(1)}, u32[]{:S(2)}, u32[]{:S(2)}) collective-permute-start(bf16[32,3072]{1,0:T(8,128)(2,1)S(1)} %get-tuple-element.10), channel_id=1, source_target_pairs={{0,2},{1,3},{2,0},{3,1},{4,6},{5,7},{6,4},{7,5},{8,10},{9,11},{10,... | collective-permute-start | bytes 589832 | tf_op jit(solution)/shard_map/ppermute | solution.py:198
  11.6 11.1 %collective-permute-start.6 = (bf16[32,3072]{1,0:T(8,128)(2,1)S(1)}, bf16[32,3072]{1,0:T(8,128)(2,1)S(1)}, u32[]{:S(2)}, u32[]{:S(2)}) collective-permute-start(bf16[32,3072]{1,0:T(8,128)(2,1)S(1)} %get-tuple-element.11), channel_id=1, source_target_pairs={{0,1},{1,0},{2,3},{3,2},{4,5},{5,4},{6,7},{7,6},{8,9},{9,8},{10,11... | collective-permute-start | bytes 589832 | tf_op jit(solution)/shard_map/ppermute | solution.py:198
  12.2 6.9 %collective-permute-start.2 = (bf16[16,3072]{1,0:T(8,128)(2,1)S(1)}, bf16[16,3072]{1,0:T(8,128)(2,1)S(1)}, u32[]{:S(2)}, u32[]{:S(2)}) collective-permute-start(bf16[16,3072]{1,0:T(8,128)(2,1)S(1)} %add.22), channel_id=1, source_target_pairs={{0,16},{4,20},{8,24},{12,28},{16,0},{20,4},{24,8},{28,12},{1,17},{... | collective-permute-start | bytes 294920 | tf_op jit(solution)/shard_map/ppermute | solution.py:198
  19.1 5.6 %collective-permute-start.5 = (bf16[16,3072]{1,0:T(8,128)(2,1)S(1)}, bf16[16,3072]{1,0:T(8,128)(2,1)S(1)}, u32[]{:S(2)}, u32[]{:S(2)}) collective-permute-start(bf16[16,3072]{1,0:T(8,128)(2,1)S(1)} %add.23.refs_0_), channel_id=1, source_target_pairs={{0,3},{1,2},{2,1},{3,0},{4,7},{5,6},{6,5},{7,4},{8,11},{9,10},{10,... | collective-permute-start | bytes 294920 | tf_op jit(solution)/shard_map/ppermute | solution.py:198
  21.5 4.6 %collective-permute-start.4 = (bf16[16,3072]{1,0:T(8,128)(2,1)S(1)}, bf16[16,3072]{1,0:T(8,128)(2,1)S(1)}, u32[]{:S(2)}, u32[]{:S(2)}) collective-permute-start(bf16[16,3072]{1,0:T(8,128)(2,1)S(1)} %add.23.refs_0_), channel_id=1, source_target_pairs={{0,2},{1,3},{2,0},{3,1},{4,6},{5,7},{6,4},{7,5},{8,10},{9,11},{10,... | collective-permute-start | bytes 294920 | tf_op jit(solution)/shard_map/ppermute | solution.py:198
  22.0 4.6 %collective-permute-start.3 = (bf16[16,3072]{1,0:T(8,128)(2,1)S(1)}, bf16[16,3072]{1,0:T(8,128)(2,1)S(1)}, u32[]{:S(2)}, u32[]{:S(2)}) collective-permute-start(bf16[16,3072]{1,0:T(8,128)(2,1)S(1)} %add.23.refs_0_), channel_id=1, source_target_pairs={{0,1},{1,0},{2,3},{3,2},{4,5},{5,4},{6,7},{7,6},{8,9},{9,8},{10,11... | collective-permute-start | bytes 294920 | tf_op jit(solution)/shard_map/ppermute | solution.py:198
where the time goes:
time: 33.6 us; the launch traced here: 33.5 us
  starting transfers between devices  13.3 us (40%)
  waiting for transfers between devices  8.43 us (25%)
  Pallas kernels  7.68 us (23%)
  other arithmetic  3.62 us (11%)
    ppermute x9, starting transfers between devices, swapped(): return lax.ppermute(value, axis, [(i, i ^ step) for i in range(size)])  13.3 us
    ppermute x9, waiting for transfers between devices, swapped(): return lax.ppermute(value, axis, [(i, i ^ step) for i in range(size)])  8.43 us
    pallas_call x1, Pallas kernels, stack_blocks(): pl.pallas_call(functools.partial(stack_kernel, segments, keep), out_shape...  6.81 us
    select_n x1, other arithmetic, shards(): encoded = jnp.where(valid != 0, spectra[:, 0, :], jnp.bfloat16(UNUSABLE))  1.31 us
    add x3, other arithmetic, shards(): picked = picked + swapped(picked, 'rcv', rcv_size, step)  0.97 us
    pallas_call x1, Pallas kernels, whiten_blocks(): pl.pallas_call(functools.partial(whiten_kernel, segments), out_shape=(jax...  0.87 us
    sub x1, other arithmetic, shards(): sources.reshape(-1)[:, None] - lax.axis_index('rcv') * channels  0.68 us
  transfers between devices with their start and end apart: 9, of which 5 were waited for; matrix products, arithmetic and copies ran while one was open for 0% of the time, Pallas kernels for 3%

commit v1 on v0

v1 whole, which is shorter than its diff:
```python
import functools
import math

import jax
import jax.numpy as jnp
import numpy as np
from jax import lax
from jax.experimental import pallas as pl
from jax.experimental.pallas import tpu as pltpu
from jax.sharding import PartitionSpec as P

NT = 4096
LAG = 150
HALF_WIN = 64
EPSILON = 1e-06

UNUSABLE = 64.0
USABLE_BELOW = 32.0

LANES = 128
BLOCK = 256
MEBI = 1 << 20
VMEM = pl.BlockSpec(memory_space=pltpu.VMEM)
HBM = pl.BlockSpec(memory_space=pltpu.HBM)
ANY = pl.BlockSpec(memory_space=pl.ANY)


def lag_table(nbins):
    winding = np.mod(
        np.arange(1, nbins + 1, dtype=np.int64)[:, None]
        * np.arange(-LAG, LAG + 1, dtype=np.int64)[None, :],
        NT,
    )
    theta = winding * (2.0 * math.pi / NT)
    table = np.concatenate([np.cos(theta), -np.sin(theta)], axis=0)
    columns = table.shape[1]
    padded = -(-columns // LANES) * LANES
    return np.pad(table, ((0, 0), (0, padded - columns))).astype(jnp.bfloat16)


def iota(shape, dim):
    return lax.broadcasted_iota(jnp.int32, shape, dim)


def whitening(real, imag, high, low):
    count, nbins = real.shape
    blocks = nbins // BLOCK
    span = BLOCK + 2 * LANES
    amplitude = jnp.sqrt(real * real + imag * imag)
    rounded = amplitude.astype(jnp.bfloat16)
    edge = jnp.zeros((count, LANES), jnp.bfloat16)
    for part, value in (
        (high, rounded),
        (low, (amplitude - rounded.astype(jnp.float32)).astype(jnp.bfloat16)),
    ):
        part[:, :LANES] = edge
        part[:, LANES : LANES + nbins] = value
        part[:, LANES + nbins :] = edge
    near = jnp.abs(iota((span, BLOCK), 0) - LANES - iota((span, BLOCK), 1)) <= HALF_WIN
    band = jnp.where(near, 1.0, 0.0).astype(jnp.bfloat16)
    pieces = [
        part[:, block * BLOCK : block * BLOCK + span] for block in range(blocks) for part in (high, low)
    ]
    windows = jnp.dot(
        jnp.concatenate(pieces, axis=0), band, preferred_element_type=jnp.float32
    )
    for block in range(blocks):
        first = block * BLOCK
        at = 2 * block * count
        window = windows[at : at + count] + windows[at + count : at + 2 * count]
        index = first + iota((1, BLOCK), 1)
        counted = jnp.minimum(index, HALF_WIN) + jnp.minimum(nbins - 1 - index, HALF_WIN) + 1
        factor = 1.0 / (window / counted.astype(jnp.float32) + EPSILON)
        re = real[:, first : first + BLOCK]
        im = imag[:, first : first + BLOCK]
        usable = re < USABLE_BELOW
        re = jnp.where(usable, re * factor, 0.0).astype(jnp.bfloat16).astype(jnp.float32)
        im = jnp.where(usable, im * factor, 0.0).astype(jnp.bfloat16).astype(jnp.float32)
        yield slice(first, first + BLOCK), re, im


def usable_rows(real):
    return jnp.where(real[:, :LANES] < USABLE_BELOW, 1.0, 0.0)


def encode_kernel(
    spectra_ref, valid_ref, sources_ref, encoded_ref, own_ref, other_ref,
    spectra, valid, sources, arrived
):
    copies = [
        pltpu.make_async_copy(sources_ref, sources, arrived.at[0]),
        pltpu.make_async_copy(valid_ref, valid, arrived.at[1]),
        pltpu.make_async_copy(spectra_ref, spectra, arrived.at[2]),
    ]
    for copy in copies:
        copy.start()
    channels, width = spectra_ref.shape
    nbins = width // 2
    per_round = sources.shape[1]
    half = sources.shape[0] * per_round // 2
    index = lax.axis_index("rcv")
    copies[0].wait()
    copies[1].wait()
    diagonal = iota((channels, channels), 0) == iota((channels, channels), 1)
    usable = jnp.sum(jnp.where(diagonal, valid[...], 0), axis=1, keepdims=True) != 0
    onehots = []
    for part in (index % 2, 1 - index % 2):
        onehot = jnp.zeros((half, channels), jnp.float32)
        for source in range(half):
            number = part * half + source
            local = sources[number // per_round, number % per_round] - index * channels
            hit = (iota((half, channels), 0) == source) & (iota((half, channels), 1) == local)
            onehot = jnp.where(hit, 1.0, onehot)
        onehots.append(onehot)
    onehot = jnp.concatenate(onehots, axis=0).astype(jnp.bfloat16)
    copies[2].wait()
    encoded = jnp.where(usable, spectra[...].astype(jnp.float32), UNUSABLE).astype(jnp.bfloat16)
    encoded_ref[...] = encoded
    picked = jnp.dot(onehot, encoded, preferred_element_type=jnp.float32)
    for part, ref in enumerate((own_ref, other_ref)):
        rows = picked[part * half : (part + 1) * half]
        ref[...] = jnp.concatenate([rows[:, :nbins], rows[:, nbins:]], axis=0).astype(ref.dtype)


def whiten_kernel(segments, *refs):
    blocks, (real_ref, imag_ref, both_ref, valid_ref, high, low) = refs[:segments], refs[segments:]
    rows = jnp.concatenate([ref[...].astype(jnp.float32) for ref in blocks], axis=0)
    nbins = rows.shape[1] // 2
    real, imag = rows[:, :nbins], rows[:, nbins:]
    for at, re, im in whitening(real, imag, high, low):
        real_ref[:, at] = re
        imag_ref[:, at] = im
        both_ref[:, at] = re + im
    valid_ref[...] = usable_rows(real)


def stack_kernel(segments, swap, *refs):
    (
        slabs_ref, rcv_re, rcv_im, rcv_both, rcv_valid, table_ref, *_, out_ref,
        src_re, src_diff, src_sum, high, low, cross_a, cross_b, total, result, written
    ) = refs
    half = slabs_ref.shape[0] // (2 * segments)
    nbins = slabs_ref.shape[1]
    keep = rcv_re.shape[0] // segments
    chunk = min(keep, 16)
    slabs = slabs_ref[...].astype(jnp.float32)
    real = jnp.concatenate(
        [slabs[2 * half * t : 2 * half * t + half] for t in range(segments)], axis=0
    )
    imag = jnp.concatenate(
        [slabs[2 * half * t + half : 2 * half * (t + 1)] for t in range(segments)], axis=0
    )
    for at, re, im in whitening(real, imag, high, low):
        src_re[:, at] = re
        src_diff[:, at] = im - re
        src_sum[:, at] = im + re
    src_valid = usable_rows(real)
    total[...] = jnp.zeros_like(total)
    cross_b[...] = jnp.zeros_like(cross_b)

    def multiply(block, cross):
        for sub in range(BLOCK // LANES):
            at = pl.ds(pl.multiple_of(block * BLOCK + sub * LANES, LANES), LANES)
            for first in range(0, keep, chunk):
                rows = [slice(t * keep + first, t * keep + first + chunk) for t in range(segments)]
                r_re = [rcv_re[row, at] for row in rows]
                r_im = [rcv_im[row, at] for row in rows]
                r_both = [rcv_both[row, at] for row in rows]
                for source in range(half):
                    p, q, w = 0.0, 0.0, 0.0
                    for t in range(segments):
                        row = slice(t * half + source, t * half + source + 1)
                        p = p + src_re[row, at] * r_both[t]
                        q = q + src_diff[row, at] * r_im[t]
                        w = w + src_sum[row, at] * r_re[t]
                    to = slice(source * keep + first, source * keep + first + chunk)
                    cross[to, sub * LANES : (sub + 1) * LANES] = (p + q).astype(cross.dtype)
                    cross[to, BLOCK + sub * LANES : BLOCK + (sub + 1) * LANES] = (w - p).astype(
                        cross.dtype
                    )

    def project(block, cross):
        value = cross[...].astype(jnp.bfloat16)
        re_at = pl.ds(pl.multiple_of(block * BLOCK, BLOCK), BLOCK)
        im_at = pl.ds(pl.multiple_of(nbins + block * BLOCK, BLOCK), BLOCK)
        total[...] += jnp.dot(
            value[:, :BLOCK], table_ref[re_at, :], preferred_element_type=jnp.float32
        ) + jnp.dot(value[:, BLOCK:], table_ref[im_at, :], preferred_element_type=jnp.float32)

    def two_blocks(pair, carry):
        multiply(2 * pair, cross_a)
        project(jnp.maximum(2 * pair - 1, 0), cross_b)
        multiply(2 * pair + 1, cross_b)
        project(2 * pair, cross_a)
        return carry

    pairs = nbins // (2 * BLOCK)
    lax.fori_loop(0, pairs, two_blocks, 0)
    project(2 * pairs - 1, cross_b)

    lags = result.shape[1]
    scale = 2.0 / math.sqrt(nbins)
    for source in range(half):
        common = 0.0
        for t in range(segments):
            row = t * half + source
            common = common + src_valid[row : row + 1] * rcv_valid[t * keep : (t + 1) * keep, :]
        weight = scale / jnp.maximum(common, 1.0)
        to = slice(source * keep, (source + 1) * keep)
        for first in range(0, lags, LANES):
            last = min(first + LANES, lags)
            value = total[to, first : first + LANES] * weight
            result[to, first:last] = value[:, : last - first]
    part = (lax.axis_index("rcv") + swap) % 2
    count = half * keep
    copy = pltpu.make_async_copy(
        result, out_ref.at[pl.ds(pl.multiple_of(part * count, count), count)], written
    )
    copy.start()
    copy.wait()


def encode(spectra, valid, sources):
    channels, width = spectra.shape
    count = sources.size
    slab = jax.ShapeDtypeStruct((count, width // 2), jnp.bfloat16)
    return pl.pallas_call(
        encode_kernel,
        out_shape=(jax.ShapeDtypeStruct((channels, width), jnp.bfloat16), slab, slab),
        in_specs=[HBM] * 3,
        out_specs=(VMEM,) * 3,
        scratch_shapes=[
            pltpu.VMEM((channels, width), jnp.bfloat16),
            pltpu.VMEM((1, channels), jnp.int32),
            pltpu.SMEM(sources.shape, jnp.int32),
            pltpu.SemaphoreType.DMA((3,)),
        ],
        compiler_params=pltpu.CompilerParams(vmem_limit_bytes=60 * MEBI),
        name="encode_and_pick",
    )(spectra, valid, sources)


def whiten_blocks(blocks):
    segments, (keep, width) = len(blocks), blocks[0].shape
    count, nbins = segments * keep, width // 2
    padded = pltpu.VMEM((count, nbins + 2 * LANES), jnp.bfloat16)
    part = jax.ShapeDtypeStruct((count, nbins), jnp.float32)
    return pl.pallas_call(
        functools.partial(whiten_kernel, segments),
        out_shape=(part, part, part, jax.ShapeDtypeStruct((count, LANES), jnp.float32)),
        in_specs=[VMEM] * segments,
        out_specs=(VMEM,) * 4,
        scratch_shapes=[padded, padded],
        compiler_params=pltpu.CompilerParams(vmem_limit_bytes=24 * MEBI),
        cost_estimate=pl.CostEstimate(
            flops=count * width * 1024, bytes_accessed=count * width * 4, transcendentals=0
        ),
        name="whiten_receivers",
    )(*blocks)


def stack_half(segments, swap, slabs, receivers, table, rest=()):
    half, nbins = slabs.shape[0] // (2 * segments), slabs.shape[1]
    keep = receivers[0].shape[0] // segments
    count, rows = segments * half, half * keep
    padded = pltpu.VMEM((count, nbins + 2 * LANES), jnp.bfloat16)
    part = pltpu.VMEM((count, nbins), jnp.float32)
    cross = pltpu.VMEM((rows, 2 * BLOCK), jnp.bfloat16 if keep % 16 == 0 else jnp.float32)
    return pl.pallas_call(
        functools.partial(stack_kernel, segments, swap),
        out_shape=jax.ShapeDtypeStruct((2 * rows, 2 * LAG + 1), jnp.float32),
        in_specs=[VMEM] * 6 + [ANY] * len(rest),
        out_specs=ANY,
        input_output_aliases={6: 0} if rest else {},
        scratch_shapes=[
            part,
            part,
            part,
            padded,
            padded,
            cross,
            cross,
            pltpu.VMEM((rows, table.shape[1]), jnp.float32),
            pltpu.VMEM((rows, 2 * LAG + 1), jnp.float32),
            pltpu.SemaphoreType.DMA,
        ],
        compiler_params=pltpu.CompilerParams(vmem_limit_bytes=32 * MEBI),
        cost_estimate=pl.CostEstimate(
            flops=4 * rows * nbins * 2 * LAG, bytes_accessed=nbins * 2048, transcendentals=0
        ),
        name="stack_other_half" if swap else "stack_own_half",
    )(slabs, *receivers, table, *rest)


def swapped(value, axis, size, step):
    return lax.ppermute(value, axis, [(i, i ^ step) for i in range(size)])


def shards(rcv_size, tm_size, spectra, valid, sources):
    channels, _, width = spectra.shape
    keep = channels // tm_size
    rounds, per_round = sources.shape
    mine = lax.axis_index("tm")
    encoded, own, other = encode(spectra[:, 0, :], valid.reshape(1, channels), sources)

    def block_for(step, block):
        return lax.dynamic_slice_in_dim(block, (mine ^ step) * keep, keep, 0)

    own = own + swapped(other, "rcv", rcv_size, 1)
    receivers = [block_for(0, encoded)]
    step, later = 2, tm_size - 1
    while step < rcv_size:
        now, later = later - later // 2, later // 2
        own, encoded = lax.optimization_barrier((own, encoded))
        for swap in range(len(receivers), len(receivers) + now):
            receivers.append(swapped(block_for(swap, encoded), "tm", tm_size, swap))
        own = own + swapped(own, "rcv", rcv_size, step)
        step *= 2
    for swap in range(len(receivers), tm_size):
        receivers.append(swapped(block_for(swap, encoded), "tm", tm_size, swap))
    own, receivers = lax.optimization_barrier((own, receivers))
    own = [own] + [swapped(own, "tm", tm_size, step) for step in range(1, tm_size)]
    whitened = whiten_blocks(receivers)
    own, whitened = lax.optimization_barrier((own, whitened))
    own = jnp.concatenate(own, axis=0)
    other = swapped(own, "rcv", rcv_size, 1)

    table = jnp.asarray(lag_table(width // 2))
    stack = stack_half(tm_size, 0, own, whitened, table)
    stack = stack_half(tm_size, 1, other, whitened, table, (stack,))
    return stack.reshape(rounds, per_round, keep, 2 * LAG + 1)


def solution(mesh):
    body = functools.partial(shards, mesh.shape["rcv"], mesh.shape["tm"])
    in_specs = (P("rcv", "tm", None), P("rcv", "tm"), P())
    out_specs = P(None, None, ("rcv", "tm"), None)
    return jax.shard_map(body, mesh=mesh, in_specs=in_specs, out_specs=out_specs, check_vma=False)
```

time: 33.6 us -> 37.2 us (1.11)
  Pallas kernels: 7.68 us -> 11.7 us
  local copies, waits for them, and re-layouts: 0.15 us -> 2.95 us
  other arithmetic: 3.62 us -> 0.84 us
  waiting for transfers between devices: 8.43 us -> 7.64 us
  starting transfers between devices: 13.3 us -> 13.7 us
    pallas_call x2 -> x4, Pallas kernels: 7.68 us -> 11.7 us  [the longest x2 8.36 us: stack_half(): pl.pallas_call(functools.partial(stack_kernel, segments, swap), out_shape...]
    dynamic_slice x1 -> x3, local copies, waits for them, and re-layouts: 0.05 us -> 2.93 us  [block_for(): return lax.dynamic_slice_in_dim(block, (mine ^ step) * keep, keep, 0)]
    select_n x1 -> x0, other arithmetic: 1.31 us -> none  [shards(): encoded = jnp.where(valid != 0, spectra[:, 0, :], jnp.bfloat16(UNUSABLE))]
    ppermute x9 -> x10, waiting for transfers between devices: 8.43 us -> 7.64 us  [swapped(): return lax.ppermute(value, axis, [(i, i ^ step) for i in range(size)])]
    sub x1 -> x0, other arithmetic: 0.68 us -> none  [shards(): sources.reshape(-1)[:, None] - lax.axis_index('rcv') * channels]
    broadcast_in_dim x1 -> x0, other arithmetic: 0.66 us -> none  [shards(): encoded = jnp.where(valid != 0, spectra[:, 0, :], jnp.bfloat16(UNUSABLE))]
    ppermute x9 -> x10, starting transfers between devices: 13.3 us -> 13.7 us  [swapped(): return lax.ppermute(value, axis, [(i, i ^ step) for i in range(size)])]
  transfers between devices with their start and end apart: 9 -> 10, of which waited for: 5 -> 5; matrix products, arithmetic and copies ran while one was open for 0% -> 8% of each run, Pallas kernels for 3% -> 14%
where the time goes in v1:
time: 37.2 us; the launch traced here: 36.9 us
  starting transfers between devices  13.7 us (37%)
  Pallas kernels  11.7 us (31%)
  waiting for transfers between devices  7.64 us (21%)
  local copies, waits for them, and re-layouts  2.95 us (8%)
  other arithmetic  0.84 us (2%)
    ppermute x10, starting transfers between devices, swapped(): return lax.ppermute(value, axis, [(i, i ^ step) for i in range(size)])  13.7 us
    pallas_call x2, Pallas kernels, stack_half(): pl.pallas_call(functools.partial(stack_kernel, segments, swap), out_shape...  8.36 us
    ppermute x10, waiting for transfers between devices, swapped(): return lax.ppermute(value, axis, [(i, i ^ step) for i in range(size)])  7.64 us
    dynamic_slice x3, local copies, waits for them, and re-layouts, block_for(): return lax.dynamic_slice_in_dim(block, (mine ^ step) * keep, keep, 0)  2.93 us
    pallas_call x1, Pallas kernels, encode(): pl.pallas_call(encode_kernel, out_shape=(jax.ShapeDtypeStruct((channels,...  2.37 us
    pallas_call x1, Pallas kernels, whiten_blocks(): pl.pallas_call(functools.partial(whiten_kernel, segments), out_shape=(par...  0.98 us
    add x1, other arithmetic, shards(): own = own + swapped(other, 'rcv', rcv_size, 1)  0.81 us
  transfers between devices with their start and end apart: 10, of which 5 were waited for; matrix products, arithmetic and copies ran while one was open for 8% of the time, Pallas kernels for 14%

profile of v1, /device:TPU:0, one launch (start us, length us, event | category | flops | bytes accessed | tf_op | source)
XLA Modules:
  0.0 36.9 jit_solution(11080529225881213483)
XLA Ops:
  0.0 0.0 copy-start
  0.0 2.4 %encode_and_pick.1 = (bf16[128,3072]{1,0:T(8,128)(2,1)}, bf16[16,1536]{1,0:T(8,128)(2,1)}, bf16[16,1536]{1,0:T(8,128)(2,1)}) custom-call(bf16[128,3072]{1,0:T(8,128)(2,1)} %bitcast.3, s32[1,128]{1,0:T(1,128)} %bitcast.4, s32[2,8]{1,0:T(2,128)} %sources_ref.1), custom_call_target="tpu_custom_call" | custom-call | tf_op jit(solution)/shard_map/encode_and_pick/pallas_call | solution.py:227
  2.4 0.5 %collective-permute-start = (bf16[16,1536]{1,0:T(8,128)(2,1)}, bf16[16,1536]{1,0:T(8,128)(2,1)S(1)}, u32[]{:S(2)}, u32[]{:S(2)}) collective-permute-start(bf16[16,1536]{1,0:T(8,128)(2,1)} %get-tuple-element.30), channel_id=1, source_target_pairs={{0,4},{4,0},{8,12},{12,8},{16,20},{20,16},{24,28},{28,24},{1,5},{5... | collective-permute-start | bytes 147464 | tf_op jit(solution)/shard_map/ppermute | solution.py:296
  2.9 1.1 %collective-permute-done = bf16[16,1536]{1,0:T(8,128)(2,1)S(1)} collective-permute-done((bf16[16,1536]{1,0:T(8,128)(2,1)}, bf16[16,1536]{1,0:T(8,128)(2,1)S(1)}, u32[]{:S(2)}, u32[]{:S(2)}) %collective-permute-start) | collective-permute-done | bytes 49184 | tf_op jit(solution)/shard_map/ppermute | solution.py:296
  4.0 0.8 %add.21 = bf16[16,1536]{1,0:T(8,128)(2,1)S(1)} add(bf16[16,1536]{1,0:T(8,128)(2,1)} %get-tuple-element.29, bf16[16,1536]{1,0:T(8,128)(2,1)S(1)} %collective-permute-done) | non-fusion elementwise | flops 24576 | bytes 147456 | tf_op jit(solution)/shard_map/add | solution.py:309
  4.8 3.0 %collective-permute-start.1 = (bf16[16,1536]{1,0:T(8,128)(2,1)S(1)}, bf16[16,1536]{1,0:T(8,128)(2,1)S(1)}, u32[]{:S(2)}, u32[]{:S(2)}) collective-permute-start(bf16[16,1536]{1,0:T(8,128)(2,1)S(1)} %add.21), channel_id=1, source_target_pairs={{0,8},{4,12},{8,0},{12,4},{16,24},{20,28},{24,16},{28,20},{1,9},{5... | collective-permute-start | bytes 147464 | tf_op jit(solution)/shard_map/ppermute | solution.py:296
  7.8 1.0 %constant_dynamic-slice_fusion.1 = (bf16[32,3072]{1,0:T(8,128)(2,1)S(1)}, bf16[32,3072]{1,0:T(8,128)(2,1)S(1)}) fusion(bf16[128,3072]{1,0:T(8,128)(2,1)} %get-tuple-element.35, s32[]{:T(128)S(6)} %select_n.14, s32[]{:T(128)S(6)} %select_n.13), kind=kLoop, calls=%fused_computation.5 | loop fusion | bytes 786440 | tf_op jit(solution)/shard_map/dynamic_slice | solution.py:307
  8.8 1.6 %collective-permute-start.4 = (bf16[32,3072]{1,0:T(8,128)(2,1)S(1)}, bf16[32,3072]{1,0:T(8,128)(2,1)S(1)}, u32[]{:S(2)}, u32[]{:S(2)}) collective-permute-start(bf16[32,3072]{1,0:T(8,128)(2,1)S(1)} %get-tuple-element.53), channel_id=1, source_target_pairs={{0,2},{1,3},{2,0},{3,1},{4,6},{5,7},{6,4},{7,5},{8,10},{9,11},{10,... | collective-permute-start | bytes 589832 | tf_op jit(solution)/shard_map/ppermute | solution.py:296
  10.4 1.5 %collective-permute-start.3 = (bf16[32,3072]{1,0:T(8,128)(2,1)S(1)}, bf16[32,3072]{1,0:T(8,128)(2,1)S(1)}, u32[]{:S(2)}, u32[]{:S(2)}) collective-permute-start(bf16[32,3072]{1,0:T(8,128)(2,1)S(1)} %get-tuple-element.54), channel_id=1, source_target_pairs={{0,1},{1,0},{2,3},{3,2},{4,5},{5,4},{6,7},{7,6},{8,9},{9,8},{10,11... | collective-permute-start | bytes 589832 | tf_op jit(solution)/shard_map/ppermute | solution.py:296
  11.9 0.0 collective-permute-done.1
  11.9 2.7 %collective-permute-start.2 = (bf16[16,1536]{1,0:T(8,128)(2,1)S(1)}, bf16[16,1536]{1,0:T(8,128)(2,1)S(1)}, u32[]{:S(2)}, u32[]{:S(2)}) collective-permute-start(bf16[16,1536]{1,0:T(8,128)(2,1)S(1)} %add.22), channel_id=1, source_target_pairs={{0,16},{4,20},{8,24},{12,28},{16,0},{20,4},{24,8},{28,12},{1,17},{... | collective-permute-start | bytes 147464 | tf_op jit(solution)/shard_map/ppermute | solution.py:296
  14.6 0.9 %constant_dynamic-slice_fusion = bf16[32,3072]{1,0:T(8,128)(2,1)S(1)} fusion(bf16[128,3072]{1,0:T(8,128)(2,1)} %get-tuple-element.35, s32[]{:T(128)S(6)} %select_n.15), kind=kLoop, calls=%fused_computation.4 | loop fusion | bytes 393220 | tf_op jit(solution)/shard_map/dynamic_slice | solution.py:307
  15.5 0.9 %collective-permute-start.5 = (bf16[32,3072]{1,0:T(8,128)(2,1)S(1)}, bf16[32,3072]{1,0:T(8,128)(2,1)S(1)}, u32[]{:S(2)}, u32[]{:S(2)}) collective-permute-start(bf16[32,3072]{1,0:T(8,128)(2,1)S(1)} %constant_dynamic-slice_fusion), channel_id=1, source_target_pairs={{0,3},{1,2},{2,1},{3,0},{4,7},{5,6},{6,5},{7,4},{8,11},{9,10},{10,... | collective-permute-start | bytes 589832 | tf_op jit(solution)/shard_map/ppermute | solution.py:296
  16.4 0.9 %constant_dynamic-slice_fusion.3.refs_0_ = bf16[32,3072]{1,0:T(8,128)(2,1)S(1)} fusion(bf16[128,3072]{1,0:T(8,128)(2,1)} %get-tuple-element.35, s32[]{:T(128)S(6)} %select_n.12), kind=kLoop, calls=%fused_computation.7 | loop fusion | bytes 393220 | tf_op jit(solution)/shard_map/dynamic_slice | solution.py:307
  17.4 0.0 collective-permute-done.2
  17.4 0.0 collective-permute-done.4.refs_2_
  17.4 0.0 collective-permute-done.3.refs_1_
  17.4 4.9 %collective-permute-done.5.refs_3_ = bf16[32,3072]{1,0:T(8,128)(2,1)S(1)} collective-permute-done((bf16[32,3072]{1,0:T(8,128)(2,1)S(1)}, bf16[32,3072]{1,0:T(8,128)(2,1)S(1)}, u32[]{:S(2)}, u32[]{:S(2)}) %collective-permute-start.5) | collective-permute-done | bytes 196640 | tf_op jit(solution)/shard_map/ppermute | solution.py:296
  22.3 1.1 %collective-permute-start.8 = (bf16[16,1536]{1,0:T(8,128)(2,1)S(1)}, bf16[16,1536]{1,0:T(8,128)(2,1)S(1)}, u32[]{:S(2)}, u32[]{:S(2)}) collective-permute-start(bf16[16,1536]{1,0:T(8,128)(2,1)S(1)} %add.23), channel_id=1, source_target_pairs={{0,3},{1,2},{2,1},{3,0},{4,7},{5,6},{6,5},{7,4},{8,11},{9,10},{10,... | collective-permute-start | bytes 147464 | tf_op jit(solution)/shard_map/ppermute | solution.py:296
  23.4 0.9 %collective-permute-start.7 = (bf16[16,1536]{1,0:T(8,128)(2,1)S(1)}, bf16[16,1536]{1,0:T(8,128)(2,1)S(1)}, u32[]{:S(2)}, u32[]{:S(2)}) collective-permute-start(bf16[16,1536]{1,0:T(8,128)(2,1)S(1)} %add.23), channel_id=1, source_target_pairs={{0,2},{1,3},{2,0},{3,1},{4,6},{5,7},{6,4},{7,5},{8,10},{9,11},{10,... | collective-permute-start | bytes 147464 | tf_op jit(solution)/shard_map/ppermute | solution.py:296
  24.3 1.5 %collective-permute-start.6 = (bf16[16,1536]{1,0:T(8,128)(2,1)S(1)}, bf16[16,1536]{1,0:T(8,128)(2,1)S(1)}, u32[]{:S(2)}, u32[]{:S(2)}) collective-permute-start(bf16[16,1536]{1,0:T(8,128)(2,1)S(1)} %add.23), channel_id=1, source_target_pairs={{0,1},{1,0},{2,3},{3,2},{4,5},{5,4},{6,7},{7,6},{8,9},{9,8},{10,11... | collective-permute-start | bytes 147464 | tf_op jit(solution)/shard_map/ppermute | solution.py:296
  25.8 1.0 %whiten_receivers.1 = (f32[128,1536]{1,0:T(8,128)S(1)}, f32[128,1536]{1,0:T(8,128)S(1)}, f32[128,1536]{1,0:T(8,128)S(1)}, f32[128,128]{1,0:T(8,128)S(1)}) custom-call(bf16[32,3072]{1,0:T(8,128)(2,1)S(1)} %constant_dynamic-slice_fusion.3.refs_0_, bf16[32,3072]{1,0:T(8,128)(2,1)S(1)} %collective-permute-done.3.refs_1_, ...), custom_call_target="tpu_custom_call" | custom-call | flops 402653184 | bytes 1572864 | tf_op jit(solution)/shard_map/whiten_receivers/pallas_call | solution.py:248
  26.8 0.5 %collective-permute-done.8 = bf16[16,1536]{1,0:T(8,128)(2,1)S(1)} collective-permute-done((bf16[16,1536]{1,0:T(8,128)(2,1)S(1)}, bf16[16,1536]{1,0:T(8,128)(2,1)S(1)}, u32[]{:S(2)}, u32[]{:S(2)}) %collective-permute-start.8) | collective-permute-done | bytes 49184 | tf_op jit(solution)/shard_map/ppermute | solution.py:296
  27.4 0.5 %collective-permute-done.7 = bf16[16,1536]{1,0:T(8,128)(2,1)S(1)} collective-permute-done((bf16[16,1536]{1,0:T(8,128)(2,1)S(1)}, bf16[16,1536]{1,0:T(8,128)(2,1)S(1)}, u32[]{:S(2)}, u32[]{:S(2)}) %collective-permute-start.7) | collective-permute-done | bytes 49184 | tf_op jit(solution)/shard_map/ppermute | solution.py:296
  27.9 0.6 %collective-permute-done.6 = bf16[16,1536]{1,0:T(8,128)(2,1)S(1)} collective-permute-done((bf16[16,1536]{1,0:T(8,128)(2,1)S(1)}, bf16[16,1536]{1,0:T(8,128)(2,1)S(1)}, u32[]{:S(2)}, u32[]{:S(2)}) %collective-permute-start.6) | collective-permute-done | bytes 49184 | tf_op jit(solution)/shard_map/ppermute | solution.py:296
  28.5 0.1 collective-permute-start.9
  28.6 0.0 copy-done
  28.6 4.2 %stack_own_half.1.refs_6_ = f32[512,301]{1,0:T(8,128)} custom-call(bf16[64,1536]{1,0:T(8,128)(2,1)S(1)} %constant_dynamic-update-slice_fusion.refs_0_, f32[128,1536]{1,0:T(8,128)S(1)} %get-tuple-element.49.refs_1_, f32[128,1536]{1,0:T(8,128)S(1)} %get-tuple-element.50.refs_2_, f32[128,1536]{1,0:T(8,128)S(1)} %get-tuple-element.51.refs_3_, ...), custom_call_target="tpu_custom_call" | custom-call | flops 471859200 | bytes 3145728 | tf_op jit(solution)/shard_map/stack_own_half/pallas_call | solution.py:269
  32.8 0.0 collective-permute-done.9.refs_0_
  32.8 4.2 %stack_other_half.1 = f32[512,301]{1,0:T(8,128)} custom-call(bf16[64,1536]{1,0:T(8,128)(2,1)S(1)} %collective-permute-done.9.refs_0_, f32[128,1536]{1,0:T(8,128)S(1)} %get-tuple-element.49.refs_1_, f32[128,1536]{1,0:T(8,128)S(1)} %get-tuple-element.50.refs_2_, f32[128,1536]{1,0:T(8,128)S(1)} %get-tuple-element.51.refs_3_, ...), custom_call_target="tpu_custom_call", output_to_operand_aliasing={{}: (6, {})} | custom-call | flops 471859200 | bytes 3145728 | tf_op jit(solution)/shard_map/stack_other_half/pallas_call | solution.py:269
  (6 shorter events, 0.0 us)
Async XLA Ops:
  0.0 28.6 %copy-start = (bf16[3072,384]{1,0:T(8,128)(2,1)S(1)}, bf16[3072,384]{1,0:T(8,128)(2,1)}, u32[]{:S(2)}) copy-start(bf16[3072,384]{1,0:T(8,128)(2,1)} %constant.18.clone.refs_5_) | copy-start | bytes 7077892
  2.4 1.6 %collective-permute-start = (bf16[16,1536]{1,0:T(8,128)(2,1)}, bf16[16,1536]{1,0:T(8,128)(2,1)S(1)}, u32[]{:S(2)}, u32[]{:S(2)}) collective-permute-start(bf16[16,1536]{1,0:T(8,128)(2,1)} %get-tuple-element.30), channel_id=1, source_target_pairs={{0,4},{4,0},{8,12},{12,8},{16,20},{20,16},{24,28},{28,24},{1,5},{5... | collective-permute-start | bytes 147464 | tf_op jit(solution)/shard_map/ppermute | solution.py:296
  4.8 7.1 %collective-permute-start.1 = (bf16[16,1536]{1,0:T(8,128)(2,1)S(1)}, bf16[16,1536]{1,0:T(8,128)(2,1)S(1)}, u32[]{:S(2)}, u32[]{:S(2)}) collective-permute-start(bf16[16,1536]{1,0:T(8,128)(2,1)S(1)} %add.21), channel_id=1, source_target_pairs={{0,8},{4,12},{8,0},{12,4},{16,24},{20,28},{24,16},{28,20},{1,9},{5... | collective-permute-start | bytes 147464 | tf_op jit(solution)/shard_map/ppermute | solution.py:296
  8.8 8.6 %collective-permute-start.4 = (bf16[32,3072]{1,0:T(8,128)(2,1)S(1)}, bf16[32,3072]{1,0:T(8,128)(2,1)S(1)}, u32[]{:S(2)}, u32[]{:S(2)}) collective-permute-start(bf16[32,3072]{1,0:T(8,128)(2,1)S(1)} %get-tuple-element.53), channel_id=1, source_target_pairs={{0,2},{1,3},{2,0},{3,1},{4,6},{5,7},{6,4},{7,5},{8,10},{9,11},{10,... | collective-permute-start | bytes 589832 | tf_op jit(solution)/shard_map/ppermute | solution.py:296
  10.4 7.0 %collective-permute-start.3 = (bf16[32,3072]{1,0:T(8,128)(2,1)S(1)}, bf16[32,3072]{1,0:T(8,128)(2,1)S(1)}, u32[]{:S(2)}, u32[]{:S(2)}) collective-permute-start(bf16[32,3072]{1,0:T(8,128)(2,1)S(1)} %get-tuple-element.54), channel_id=1, source_target_pairs={{0,1},{1,0},{2,3},{3,2},{4,5},{5,4},{6,7},{7,6},{8,9},{9,8},{10,11... | collective-permute-start | bytes 589832 | tf_op jit(solution)/shard_map/ppermute | solution.py:296
  11.9 5.5 %collective-permute-start.2 = (bf16[16,1536]{1,0:T(8,128)(2,1)S(1)}, bf16[16,1536]{1,0:T(8,128)(2,1)S(1)}, u32[]{:S(2)}, u32[]{:S(2)}) collective-permute-start(bf16[16,1536]{1,0:T(8,128)(2,1)S(1)} %add.22), channel_id=1, source_target_pairs={{0,16},{4,20},{8,24},{12,28},{16,0},{20,4},{24,8},{28,12},{1,17},{... | collective-permute-start | bytes 147464 | tf_op jit(solution)/shard_map/ppermute | solution.py:296
  15.5 6.8 %collective-permute-start.5 = (bf16[32,3072]{1,0:T(8,128)(2,1)S(1)}, bf16[32,3072]{1,0:T(8,128)(2,1)S(1)}, u32[]{:S(2)}, u32[]{:S(2)}) collective-permute-start(bf16[32,3072]{1,0:T(8,128)(2,1)S(1)} %constant_dynamic-slice_fusion), channel_id=1, source_target_pairs={{0,3},{1,2},{2,1},{3,0},{4,7},{5,6},{6,5},{7,4},{8,11},{9,10},{10,... | collective-permute-start | bytes 589832 | tf_op jit(solution)/shard_map/ppermute | solution.py:296
  22.3 5.0 %collective-permute-start.8 = (bf16[16,1536]{1,0:T(8,128)(2,1)S(1)}, bf16[16,1536]{1,0:T(8,128)(2,1)S(1)}, u32[]{:S(2)}, u32[]{:S(2)}) collective-permute-start(bf16[16,1536]{1,0:T(8,128)(2,1)S(1)} %add.23), channel_id=1, source_target_pairs={{0,3},{1,2},{2,1},{3,0},{4,7},{5,6},{6,5},{7,4},{8,11},{9,10},{10,... | collective-permute-start | bytes 147464 | tf_op jit(solution)/shard_map/ppermute | solution.py:296
  23.4 4.4 %collective-permute-start.7 = (bf16[16,1536]{1,0:T(8,128)(2,1)S(1)}, bf16[16,1536]{1,0:T(8,128)(2,1)S(1)}, u32[]{:S(2)}, u32[]{:S(2)}) collective-permute-start(bf16[16,1536]{1,0:T(8,128)(2,1)S(1)} %add.23), channel_id=1, source_target_pairs={{0,2},{1,3},{2,0},{3,1},{4,6},{5,7},{6,4},{7,5},{8,10},{9,11},{10,... | collective-permute-start | bytes 147464 | tf_op jit(solution)/shard_map/ppermute | solution.py:296
  24.3 4.1 %collective-permute-start.6 = (bf16[16,1536]{1,0:T(8,128)(2,1)S(1)}, bf16[16,1536]{1,0:T(8,128)(2,1)S(1)}, u32[]{:S(2)}, u32[]{:S(2)}) collective-permute-start(bf16[16,1536]{1,0:T(8,128)(2,1)S(1)} %add.23), channel_id=1, source_target_pairs={{0,1},{1,0},{2,3},{3,2},{4,5},{5,4},{6,7},{7,6},{8,9},{9,8},{10,11... | collective-permute-start | bytes 147464 | tf_op jit(solution)/shard_map/ppermute | solution.py:296
  28.5 4.3 %collective-permute-start.9 = (bf16[64,1536]{1,0:T(8,128)(2,1)S(1)}, bf16[64,1536]{1,0:T(8,128)(2,1)S(1)}, u32[]{:S(2)}, u32[]{:S(2)}) collective-permute-start(bf16[64,1536]{1,0:T(8,128)(2,1)S(1)} %constant_dynamic-update-slice_fusion.refs_0_), channel_id=1, source_target_pairs={{0,4},{4,0},{8,12},{12,8},{16,20},{20,16},{24,28},{28,24},{1,5},{5... | collective-permute-start | bytes 589832 | tf_op jit(solution)/shard_map/ppermute | solution.py:296

commit v2 on v1

v2 whole, which is shorter than its diff:
```python
import functools
import math

import jax
import jax.numpy as jnp
import numpy as np
from jax import lax
from jax.experimental import pallas as pl
from jax.experimental.pallas import tpu as pltpu
from jax.sharding import PartitionSpec as P

NT = 4096
LAG = 150
HALF_WIN = 64
EPSILON = 1e-06

UNUSABLE = 64.0
USABLE_BELOW = 32.0

LANES = 128
BLOCK = 256
MEBI = 1 << 20
FIRST_LAG = LANES - LAG
VMEM = pl.BlockSpec(memory_space=pltpu.VMEM)
HBM = pl.BlockSpec(memory_space=pltpu.HBM)


def lag_table(nbins):
    winding = np.mod(
        np.arange(1, nbins + 1, dtype=np.int64)[:, None]
        * np.arange(FIRST_LAG, FIRST_LAG + BLOCK, dtype=np.int64)[None, :],
        NT,
    )
    theta = winding * (2.0 * math.pi / NT)
    return np.concatenate([np.cos(theta), -np.sin(theta)], axis=0).astype(jnp.bfloat16)


def iota(shape, dim):
    return lax.broadcasted_iota(jnp.int32, shape, dim)


def whitening(real, imag, high, low):
    count, nbins = real.shape
    blocks = nbins // BLOCK
    span = BLOCK + 2 * LANES
    amplitude = jnp.sqrt(real * real + imag * imag)
    rounded = amplitude.astype(jnp.bfloat16)
    edge = jnp.zeros((count, LANES), jnp.bfloat16)
    for part, value in (
        (high, rounded),
        (low, (amplitude - rounded.astype(jnp.float32)).astype(jnp.bfloat16)),
    ):
        part[:, :LANES] = edge
        part[:, LANES : LANES + nbins] = value
        part[:, LANES + nbins :] = edge
    near = jnp.abs(iota((span, BLOCK), 0) - LANES - iota((span, BLOCK), 1)) <= HALF_WIN
    band = jnp.where(near, 1.0, 0.0).astype(jnp.bfloat16)
    pieces = [
        part[:, block * BLOCK : block * BLOCK + span] for block in range(blocks) for part in (high, low)
    ]
    windows = jnp.dot(
        jnp.concatenate(pieces, axis=0), band, preferred_element_type=jnp.float32
    )
    for block in range(blocks):
        first = block * BLOCK
        at = 2 * block * count
        window = windows[at : at + count] + windows[at + count : at + 2 * count]
        index = first + iota((1, BLOCK), 1)
        counted = jnp.minimum(index, HALF_WIN) + jnp.minimum(nbins - 1 - index, HALF_WIN) + 1
        factor = 1.0 / (window / counted.astype(jnp.float32) + EPSILON)
        re = real[:, first : first + BLOCK]
        im = imag[:, first : first + BLOCK]
        usable = re < USABLE_BELOW
        re = jnp.where(usable, re * factor, 0.0).astype(jnp.bfloat16).astype(jnp.float32)
        im = jnp.where(usable, im * factor, 0.0).astype(jnp.bfloat16).astype(jnp.float32)
        yield slice(first, first + BLOCK), re, im


def usable_rows(real):
    return jnp.where(real[:, :LANES] < USABLE_BELOW, 1.0, 0.0)


def encode_kernel(
    segments, spectra_ref, valid_ref, sources_ref, picked_ref, *refs
):
    blocks, (encoded_ref, spectra, valid, sources, arrived) = refs[:segments], refs[segments:]
    copies = [
        pltpu.make_async_copy(sources_ref, sources, arrived.at[0]),
        pltpu.make_async_copy(valid_ref, valid, arrived.at[1]),
        pltpu.make_async_copy(spectra_ref, spectra, arrived.at[2]),
    ]
    for copy in copies:
        copy.start()
    channels, width = spectra_ref.shape
    rounds, per_round = sources.shape
    count = rounds * per_round
    first_channel = lax.axis_index("rcv") * channels
    copies[0].wait()
    copies[1].wait()
    diagonal = iota((channels, channels), 0) == iota((channels, channels), 1)
    usable = jnp.sum(jnp.where(diagonal, valid[...], 0), axis=1, keepdims=True) != 0
    local = jnp.zeros((count, channels), jnp.int32)
    for source in range(count):
        here = sources[source // per_round, source % per_round] - first_channel
        local = jnp.where(iota((count, channels), 0) == source, here, local)
    onehot = jnp.where(local == iota((count, channels), 1), 1.0, 0.0).astype(jnp.bfloat16)
    copies[2].wait()
    encoded = jnp.where(usable, spectra[...].astype(jnp.float32), UNUSABLE)
    encoded_ref[...] = encoded
    picked = jnp.dot(onehot, encoded.astype(jnp.bfloat16), preferred_element_type=jnp.float32)
    parts = picked_ref.shape[0]
    for part in range(parts):
        at = slice(part * width // parts, (part + 1) * width // parts)
        picked_ref[part] = picked[:, at].astype(jnp.bfloat16)
    keep = channels // segments
    for step, block in enumerate(blocks):
        at = pl.multiple_of((lax.axis_index("tm") ^ step) * keep, keep)
        block[...] = encoded_ref[pl.ds(at, keep), :].astype(jnp.bfloat16)


def whiten_kernel(segments, *refs):
    blocks, (real_ref, imag_ref, both_ref, valid_ref, high, low) = refs[:segments], refs[segments:]
    rows = jnp.concatenate([ref[...].astype(jnp.float32) for ref in blocks], axis=0)
    nbins = rows.shape[1] // 2
    real, imag = rows[:, :nbins], rows[:, nbins:]
    for at, re, im in whitening(real, imag, high, low):
        real_ref[:, at] = re
        imag_ref[:, at] = im
        both_ref[:, at] = re + im
    valid_ref[...] = usable_rows(real)


def stack_kernel(
    segments, slabs_ref, rcv_re, rcv_im, rcv_both, rcv_valid, table_ref, out_ref,
    src_re, src_diff, src_sum, high, low, cross_a, cross_b, total_re, total_im
):
    parts, count, share = slabs_ref.shape[1:]
    nbins = parts * share // 2
    keep = rcv_re.shape[0] // segments
    chunk = min(keep, 16)
    slabs = []
    for step in range(segments):
        slab = slabs_ref[lax.axis_index("tm") ^ step].astype(jnp.float32)
        slabs.append(jnp.concatenate([slab[part] for part in range(parts)], axis=1))
    slabs = jnp.concatenate(slabs, axis=0)
    real, imag = slabs[:, :nbins], slabs[:, nbins:]
    for at, re, im in whitening(real, imag, high, low):
        src_re[:, at] = re
        src_diff[:, at] = im - re
        src_sum[:, at] = im + re
    src_valid = usable_rows(real)
    total_re[...] = jnp.zeros_like(total_re)
    total_im[...] = jnp.zeros_like(total_im)
    cross_b[...] = jnp.zeros_like(cross_b)

    def multiply(block, cross):
        for sub in range(BLOCK // LANES):
            at = pl.ds(pl.multiple_of(block * BLOCK + sub * LANES, LANES), LANES)
            for first in range(0, keep, chunk):
                rows = [slice(t * keep + first, t * keep + first + chunk) for t in range(segments)]
                r_re = [rcv_re[row, at] for row in rows]
                r_im = [rcv_im[row, at] for row in rows]
                r_both = [rcv_both[row, at] for row in rows]
                for source in range(count):
                    p, q, w = 0.0, 0.0, 0.0
                    for t in range(segments):
                        row = slice(t * count + source, t * count + source + 1)
                        p = p + src_re[row, at] * r_both[t]
                        q = q + src_diff[row, at] * r_im[t]
                        w = w + src_sum[row, at] * r_re[t]
                    to = slice(source * keep + first, source * keep + first + chunk)
                    cross[to, sub * LANES : (sub + 1) * LANES] = (p + q).astype(cross.dtype)
                    cross[to, BLOCK + sub * LANES : BLOCK + (sub + 1) * LANES] = (w - p).astype(
                        cross.dtype
                    )

    def project(block, cross):
        value = cross[...].astype(jnp.bfloat16)
        re_at = pl.ds(pl.multiple_of(block * BLOCK, BLOCK), BLOCK)
        im_at = pl.ds(pl.multiple_of(nbins + block * BLOCK, BLOCK), BLOCK)
        total_re[...] += jnp.dot(
            value[:, :BLOCK], table_ref[re_at, :], preferred_element_type=jnp.float32
        )
        total_im[...] += jnp.dot(
            value[:, BLOCK:], table_ref[im_at, :], preferred_element_type=jnp.float32
        )

    def two_blocks(pair, carry):
        multiply(2 * pair, cross_a)
        project(jnp.maximum(2 * pair - 1, 0), cross_b)
        multiply(2 * pair + 1, cross_b)
        project(2 * pair, cross_a)
        return carry

    pairs = nbins // (2 * BLOCK)
    lax.fori_loop(0, pairs, two_blocks, 0)
    project(2 * pairs - 1, cross_b)

    lags = out_ref.shape[1]
    scale = 2.0 / math.sqrt(nbins)
    mirror = LAG - FIRST_LAG - iota((keep, LANES), 1)
    for source in range(count):
        common = 0.0
        for t in range(segments):
            row = t * count + source
            common = common + src_valid[row : row + 1] * rcv_valid[t * keep : (t + 1) * keep, :]
        weight = scale / jnp.maximum(common, 1.0)
        to = slice(source * keep, (source + 1) * keep)
        even, odd = total_re[to], total_im[to]
        ahead = even + odd
        behind = even - odd
        low_part = jnp.take_along_axis(
            behind[:, :LANES], jnp.clip(mirror, 0, LANES - 1), axis=1
        )
        high_part = jnp.take_along_axis(
            behind[:, LANES:], jnp.clip(mirror - LANES, 0, LANES - 1), axis=1
        )
        out_ref[to, :LANES] = jnp.where(mirror < LANES, low_part, high_part) * weight
        for first in range(0, lags - LANES, LANES):
            last = min(first + LANES, lags - LANES)
            value = ahead[:, first : first + LANES] * weight
            out_ref[to, LANES + first : LANES + last] = value[:, : last - first]


def encode(rcv_size, tm_size, spectra, valid, sources):
    channels, width = spectra.shape
    keep, count = channels // tm_size, sources.size
    picked = jax.ShapeDtypeStruct((rcv_size, count, width // rcv_size), jnp.bfloat16)
    block = jax.ShapeDtypeStruct((keep, width), jnp.bfloat16)
    return pl.pallas_call(
        functools.partial(encode_kernel, tm_size),
        out_shape=(picked,) + (block,) * tm_size,
        in_specs=[HBM] * 3,
        out_specs=(VMEM,) * (1 + tm_size),
        scratch_shapes=[
            pltpu.VMEM((channels, width), jnp.float32),
            pltpu.VMEM((channels, width), jnp.bfloat16),
            pltpu.VMEM((1, channels), jnp.int32),
            pltpu.SMEM(sources.shape, jnp.int32),
            pltpu.SemaphoreType.DMA((3,)),
        ],
        compiler_params=pltpu.CompilerParams(vmem_limit_bytes=60 * MEBI),
        name="encode_and_pick",
    )(spectra, valid, sources)


def whiten_blocks(blocks):
    segments, (keep, width) = len(blocks), blocks[0].shape
    count, nbins = segments * keep, width // 2
    padded = pltpu.VMEM((count, nbins + 2 * LANES), jnp.bfloat16)
    part = jax.ShapeDtypeStruct((count, nbins), jnp.float32)
    return pl.pallas_call(
        functools.partial(whiten_kernel, segments),
        out_shape=(part, part, part, jax.ShapeDtypeStruct((count, LANES), jnp.float32)),
        in_specs=[VMEM] * segments,
        out_specs=(VMEM,) * 4,
        scratch_shapes=[padded, padded],
        compiler_params=pltpu.CompilerParams(vmem_limit_bytes=24 * MEBI),
        cost_estimate=pl.CostEstimate(
            flops=count * width * 1024, bytes_accessed=count * width * 4, transcendentals=0
        ),
        name="whiten_receivers",
    )(*blocks)


def stack_all(slabs, receivers, table):
    segments, parts, nsrc, share = slabs.shape
    nbins = parts * share // 2
    keep = receivers[0].shape[0] // segments
    count, rows = segments * nsrc, nsrc * keep
    padded = pltpu.VMEM((count, nbins + 2 * LANES), jnp.bfloat16)
    part = pltpu.VMEM((count, nbins), jnp.float32)
    cross = pltpu.VMEM((rows, 2 * BLOCK), jnp.bfloat16 if keep % 16 == 0 else jnp.float32)
    total = pltpu.VMEM((rows, BLOCK), jnp.float32)
    return pl.pallas_call(
        functools.partial(stack_kernel, segments),
        out_shape=jax.ShapeDtypeStruct((rows, 2 * LAG + 1), jnp.float32),
        in_specs=[VMEM] * 6,
        out_specs=VMEM,
        scratch_shapes=[part, part, part, padded, padded, cross, cross, total, total],
        compiler_params=pltpu.CompilerParams(vmem_limit_bytes=40 * MEBI),
        cost_estimate=pl.CostEstimate(
            flops=4 * rows * nbins * 2 * LAG, bytes_accessed=nbins * 2048, transcendentals=0
        ),
        name="stack_sources",
    )(slabs, *receivers, table)


def swapped(value, axis, size, step):
    return lax.ppermute(value, axis, [(i, i ^ step) for i in range(size)])


def exchanged(value, axis):
    return lax.all_to_all(value, axis, 0, 0, tiled=True)


def shards(rcv_size, tm_size, spectra, valid, sources):
    channels, _, width = spectra.shape
    keep = channels // tm_size
    rounds, per_round = sources.shape
    picked, *receivers = encode(
        rcv_size, tm_size, spectra[:, 0, :], valid.reshape(1, channels), sources
    )
    receivers = receivers[:1] + [
        swapped(receivers[step], "tm", tm_size, step) for step in range(1, tm_size)
    ]
    mine = jnp.sum(exchanged(picked, "rcv"), axis=0, dtype=jnp.float32).astype(picked.dtype)
    chosen = exchanged(jnp.broadcast_to(mine[None], picked.shape), "rcv")
    chosen, receivers = lax.optimization_barrier((chosen, receivers))
    chosen = exchanged(jnp.broadcast_to(chosen[None], (tm_size,) + chosen.shape), "tm")
    if chosen.shape[-1] % LANES:
        chosen = jnp.swapaxes(chosen, 1, 2).reshape(tm_size, 1, rounds * per_round, width)
    whitened = whiten_blocks(receivers)
    stack = stack_all(chosen, whitened, jnp.asarray(lag_table(width // 2)))
    return stack.reshape(rounds, per_round, keep, 2 * LAG + 1)


def solution(mesh):
    body = functools.partial(shards, mesh.shape["rcv"], mesh.shape["tm"])
    in_specs = (P("rcv", "tm", None), P("rcv", "tm"), P())
    out_specs = P(None, None, ("rcv", "tm"), None)
    return jax.shard_map(body, mesh=mesh, in_specs=in_specs, out_specs=out_specs, check_vma=False)
```

time: 37.2 us -> 46 us (1.24)
  local copies, waits for them, and re-layouts: 2.95 us -> 8.63 us
  starting transfers between devices: 13.7 us -> 16.9 us
  waiting for transfers between devices: 7.64 us -> 9.27 us
  Pallas kernels: 11.7 us -> 10.6 us
  other arithmetic: 0.84 us -> 0.02 us
    all_to_all x0 -> x3, starting transfers between devices: none -> 13.4 us  [exchanged(): return lax.all_to_all(value, axis, 0, 0, tiled=True)]
    ppermute x10 -> x3, starting transfers between devices: 13.7 us -> 3.49 us  [swapped(): return lax.ppermute(value, axis, [(i, i ^ step) for i in range(size)])]
    unnamed x5 -> x24, local copies, waits for them, and re-layouts: 0.02 us -> 7.19 us
    all_to_all x0 -> x3, waiting for transfers between devices: none -> 6.72 us  [exchanged(): return lax.all_to_all(value, axis, 0, 0, tiled=True)]
    ppermute x10 -> x3, waiting for transfers between devices: 7.64 us -> 2.54 us  [swapped(): return lax.ppermute(value, axis, [(i, i ^ step) for i in range(size)])]
    dynamic_slice x3 -> x0, local copies, waits for them, and re-layouts: 2.93 us -> none  [block_for(): return lax.dynamic_slice_in_dim(block, (mine ^ step) * keep, keep, 0)]
    broadcast_in_dim x0 -> x2, local copies, waits for them, and re-layouts: none -> 1.44 us  [the longest x1 0.79 us: shards(): jnp.broadcast_to(chosen[None], (tm_size,) + chosen.shape)]
    pallas_call x3 -> x2, Pallas kernels: 10.7 us -> 9.58 us  [the longest x1 7.31 us: stack_all(): pl.pallas_call(functools.partial(stack_kernel, segments), out_shape=jax.S...]
  transfers between devices with their start and end apart: 10 -> 6, of which waited for: 5 -> 4; matrix products, arithmetic and copies ran while one was open for 8% -> 1% of each run, Pallas kernels for 14% -> 2%
where the time goes in v2:
time: 46 us; the launch traced here: 45.5 us
  starting transfers between devices  16.9 us (37%)
  Pallas kernels  10.6 us (23%)
  waiting for transfers between devices  9.27 us (20%)
  local copies, waits for them, and re-layouts  8.63 us (19%)
    all_to_all x3, starting transfers between devices, exchanged(): return lax.all_to_all(value, axis, 0, 0, tiled=True)  13.4 us
    pallas_call x1, Pallas kernels, stack_all(): pl.pallas_call(functools.partial(stack_kernel, segments), out_shape=jax.S...  7.31 us
    unnamed x24, local copies, waits for them, and re-layouts  7.19 us
    all_to_all x3, waiting for transfers between devices, exchanged(): return lax.all_to_all(value, axis, 0, 0, tiled=True)  6.72 us
    ppermute x3, starting transfers between devices, swapped(): return lax.ppermute(value, axis, [(i, i ^ step) for i in range(size)])  3.49 us
    ppermute x3, waiting for transfers between devices, swapped(): return lax.ppermute(value, axis, [(i, i ^ step) for i in range(size)])  2.54 us
    pallas_call x1, Pallas kernels, encode(): pl.pallas_call(functools.partial(encode_kernel, tm_size), out_shape=(pick...  2.27 us
    pallas_call x1, Pallas kernels, whiten_blocks(): pl.pallas_call(functools.partial(whiten_kernel, segments), out_shape=(par...  0.98 us
  transfers between devices with their start and end apart: 6, of which 4 were waited for; matrix products, arithmetic and copies ran while one was open for 1% of the time, Pallas kernels for 2%

profile of v2, /device:TPU:0, one launch (start us, length us, event | category | flops | bytes accessed | tf_op | source)
XLA Modules:
  0.0 45.5 jit_solution(2914561282724004187)
XLA Ops:
  0.0 2.3 %encode_and_pick.1 = (bf16[8,16,384]{2,1,0:T(8,128)(2,1)}, bf16[32,3072]{1,0:T(8,128)(2,1)}, bf16[32,3072]{1,0:T(8,128)(2,1)}, bf16[32,3072]{1,0:T(8,128)(2,1)}, bf16[32,3072]{1,0:T(8,128)(2,1)}) custom-call(bf16[128,3072]{1,0:T(8,128)(2,1)} %bitcast.3, s32[1,128]{1,0:T(1,128)} %bitcast.4, s32[2,8]{1,0:T(2,128)} %sources_ref.1), custom_call_target="tpu_custom_call" | custom-call | tf_op jit(solution)/shard_map/encode_and_pick/pallas_call | solution.py:230
  2.3 6.3 %all-to-all-start = ((bf16[8,16,384]{2,1,0:T(8,128)(2,1)}), bf16[8,16,384]{2,1,0:T(8,128)(2,1)S(1)}, u32[]{:S(2)}, u32[]{:S(2)}) async-start(bf16[8,16,384]{2,1,0:T(8,128)(2,1)} %get-tuple-element.19), calls=%async_computation | async-start | bytes 196608 | tf_op jit(solution)/shard_map/all_to_all | solution.py:294
  8.6 1.5 %collective-permute-start = (bf16[32,3072]{1,0:T(8,128)(2,1)}, bf16[32,3072]{1,0:T(8,128)(2,1)S(1)}, u32[]{:S(2)}, u32[]{:S(2)}) collective-permute-start(bf16[32,3072]{1,0:T(8,128)(2,1)} %get-tuple-element.21), channel_id=1, source_target_pairs={{0,1},{1,0},{2,3},{3,2},{4,5},{5,4},{6,7},{7,6},{8,9},{9,8},{10,11... | collective-permute-start | bytes 589832 | tf_op jit(solution)/shard_map/ppermute | solution.py:290
  10.1 1.5 %collective-permute-start.1 = (bf16[32,3072]{1,0:T(8,128)(2,1)}, bf16[32,3072]{1,0:T(8,128)(2,1)S(1)}, u32[]{:S(2)}, u32[]{:S(2)}) collective-permute-start(bf16[32,3072]{1,0:T(8,128)(2,1)} %get-tuple-element.22), channel_id=1, source_target_pairs={{0,2},{1,3},{2,0},{3,1},{4,6},{5,7},{6,4},{7,5},{8,10},{9,11},{10,... | collective-permute-start | bytes 589832 | tf_op jit(solution)/shard_map/ppermute | solution.py:290
  11.6 0.0 copy-start
  11.6 0.5 %collective-permute-start.2 = (bf16[32,3072]{1,0:T(8,128)(2,1)}, bf16[32,3072]{1,0:T(8,128)(2,1)S(1)}, u32[]{:S(2)}, u32[]{:S(2)}) collective-permute-start(bf16[32,3072]{1,0:T(8,128)(2,1)} %get-tuple-element.23), channel_id=1, source_target_pairs={{0,3},{1,2},{2,1},{3,0},{4,7},{5,6},{6,5},{7,4},{8,11},{9,10},{10,... | collective-permute-start | bytes 589832 | tf_op jit(solution)/shard_map/ppermute | solution.py:290
  12.1 2.9 %all-to-all-done = bf16[8,16,384]{2,1,0:T(8,128)(2,1)S(1)} async-done(((bf16[8,16,384]{2,1,0:T(8,128)(2,1)}), bf16[8,16,384]{2,1,0:T(8,128)(2,1)S(1)}, u32[]{:S(2)}, u32[]{:S(2)}) %all-to-all-start) | async-done | bytes 98336 | tf_op jit(solution)/shard_map/all_to_all | solution.py:294
  15.0 0.7 %broadcast_in_dim.4 = bf16[8,16,384]{2,1,0:T(8,128)(2,1)} broadcast(bf16[16,384]{1,0:T(8,128)(2,1)S(1)} %reduce_sum.12), dimensions={1,2} | broadcast | bytes 110592 | tf_op jit(solution)/shard_map/broadcast_in_dim | solution.py:308
  15.6 3.4 %all-to-all-start.1 = ((bf16[8,16,384]{2,1,0:T(8,128)(2,1)}), bf16[8,16,384]{2,1,0:T(8,128)(2,1)S(1)}, u32[]{:S(2)}, u32[]{:S(2)}) async-start(bf16[8,16,384]{2,1,0:T(8,128)(2,1)} %broadcast_in_dim.4), calls=%async_computation.1 | async-start | bytes 196608 | tf_op jit(solution)/shard_map/all_to_all | solution.py:294
  19.0 0.0 collective-permute-done.refs_1_
  19.0 0.0 copy-start.6
  19.0 2.5 %collective-permute-done.1.refs_2_ = bf16[32,3072]{1,0:T(8,128)(2,1)S(1)} collective-permute-done((bf16[32,3072]{1,0:T(8,128)(2,1)}, bf16[32,3072]{1,0:T(8,128)(2,1)S(1)}, u32[]{:S(2)}, u32[]{:S(2)}) %collective-permute-start.1) | collective-permute-done | bytes 196640 | tf_op jit(solution)/shard_map/ppermute | solution.py:290
  21.6 0.0 collective-permute-done.2.refs_3_
  21.6 3.7 %all-to-all-done.1 = bf16[8,16,384]{2,1,0:T(8,128)(2,1)S(1)} async-done(((bf16[8,16,384]{2,1,0:T(8,128)(2,1)}), bf16[8,16,384]{2,1,0:T(8,128)(2,1)S(1)}, u32[]{:S(2)}, u32[]{:S(2)}) %all-to-all-start.1) | async-done | bytes 98336 | tf_op jit(solution)/shard_map/all_to_all | solution.py:294
  25.3 0.8 %broadcast_in_dim.5 = bf16[4,8,16,384]{3,2,1,0:T(8,128)(2,1)} broadcast(bf16[8,16,384]{2,1,0:T(8,128)(2,1)S(1)} %all-to-all-done.1), dimensions={1,2,3} | broadcast | bytes 491520 | tf_op jit(solution)/shard_map/broadcast_in_dim | solution.py:310
  26.1 0.0 copy-done.6
  26.1 0.0 copy-done.8
  26.1 0.0 copy-done.10
  26.1 3.7 %all-to-all-start.2 = ((bf16[4,8,16,384]{3,2,1,0:T(8,128)(2,1)}), bf16[4,8,16,384]{3,2,1,0:T(8,128)(2,1)S(1)}, u32[]{:S(2)}, u32[]{:S(2)}) async-start(bf16[4,8,16,384]{3,2,1,0:T(8,128)(2,1)} %broadcast_in_dim.5), calls=%async_computation.2 | async-start | bytes 786432 | tf_op jit(solution)/shard_map/all_to_all | solution.py:294
  29.8 0.9 %copy-done.5 = bf16[32,3072]{1,0:T(8,128)(2,1)S(1)} copy-done((bf16[32,3072]{1,0:T(8,128)(2,1)S(1)}, bf16[32,3072]{1,0:T(8,128)(2,1)}, u32[]{:S(2)}) %copy-start.5) | copy-done | bytes 196632
  30.7 0.9 %copy-done.7 = bf16[32,3072]{1,0:T(8,128)(2,1)S(1)} copy-done((bf16[32,3072]{1,0:T(8,128)(2,1)S(1)}, bf16[32,3072]{1,0:T(8,128)(2,1)}, u32[]{:S(2)}) %copy-start.7) | copy-done | bytes 196632
  31.7 0.9 %copy-done.9 = bf16[32,3072]{1,0:T(8,128)(2,1)S(1)} copy-done((bf16[32,3072]{1,0:T(8,128)(2,1)S(1)}, bf16[32,3072]{1,0:T(8,128)(2,1)}, u32[]{:S(2)}) %copy-start.9) | copy-done | bytes 196632
  32.6 0.9 %copy-done.11 = bf16[32,3072]{1,0:T(8,128)(2,1)S(1)} copy-done((bf16[32,3072]{1,0:T(8,128)(2,1)S(1)}, bf16[32,3072]{1,0:T(8,128)(2,1)}, u32[]{:S(2)}) %copy-start.11) | copy-done | bytes 196632
  33.5 1.0 %whiten_receivers.1 = (f32[128,1536]{1,0:T(8,128)S(1)}, f32[128,1536]{1,0:T(8,128)S(1)}, f32[128,1536]{1,0:T(8,128)S(1)}, f32[128,128]{1,0:T(8,128)S(1)}) custom-call(bf16[32,3072]{1,0:T(8,128)(2,1)S(1)} %copy-done.5, bf16[32,3072]{1,0:T(8,128)(2,1)S(1)} %copy-done.7, bf16[32,3072]{1,0:T(8,128)(2,1)S(1)} %copy-done.9, bf16[32,3072]{1,0:T(8,128)(2,1)S(1)} %copy-done.11), custom_call_target="tpu_custom_call" | custom-call | flops 402653184 | bytes 1572864 | tf_op jit(solution)/shard_map/whiten_receivers/pallas_call | solution.py:252
  34.5 0.0 copy-start.1
  34.5 0.9 %copy-done.1 = f32[128,1536]{1,0:T(8,128)} copy-done((f32[128,1536]{1,0:T(8,128)}, f32[128,1536]{1,0:T(8,128)S(1)}, u32[]{:S(2)}) %copy-start.1) | copy-done | bytes 786456
  35.4 0.6 %copy-done.3 = f32[128,128]{1,0:T(8,128)} copy-done((f32[128,128]{1,0:T(8,128)}, f32[128,128]{1,0:T(8,128)S(1)}, u32[]{:S(2)}) %copy-start.3) | copy-done | bytes 65560
  36.0 0.2 all-to-all-done.2.slabs_ref
  36.2 0.0 copy-done
  36.2 1.1 %copy-done.2 = f32[128,1536]{1,0:T(8,128)S(1)} copy-done((f32[128,1536]{1,0:T(8,128)S(1)}, f32[128,1536]{1,0:T(8,128)}, u32[]{:S(2)}) %copy-start.2) | copy-done | bytes 786456
  37.3 0.8 %copy-done.4 = f32[128,128]{1,0:T(8,128)S(1)} copy-done((f32[128,128]{1,0:T(8,128)S(1)}, f32[128,128]{1,0:T(8,128)}, u32[]{:S(2)}) %copy-start.4) | copy-done | bytes 65560
  38.2 7.3 %stack_sources.1 = f32[512,301]{1,0:T(8,128)} custom-call(bf16[4,8,16,384]{3,2,1,0:T(8,128)(2,1)S(1)} %all-to-all-done.2.slabs_ref, f32[128,1536]{1,0:T(8,128)S(1)} %get-tuple-element.29.rcv_re, f32[128,1536]{1,0:T(8,128)S(1)} %get-tuple-element.30.rcv_im, f32[128,1536]{1,0:T(8,128)S(1)} %copy-done.2, f32[128,128]{1,0:T(8,128)S(1)} %copy-done.4, ...), custom_call_target="tpu_custom_call" | custom-call | flops 943718400 | bytes 3145728 | tf_op jit(solution)/shard_map/stack_sources/pallas_call | solution.py:275
  (10 shorter events, 0.0 us)
Async XLA Ops:
  2.3 12.7 %all-to-all-start = ((bf16[8,16,384]{2,1,0:T(8,128)(2,1)}), bf16[8,16,384]{2,1,0:T(8,128)(2,1)S(1)}, u32[]{:S(2)}, u32[]{:S(2)}) async-start(bf16[8,16,384]{2,1,0:T(8,128)(2,1)} %get-tuple-element.19), calls=%async_computation | async-start | bytes 196608 | tf_op jit(solution)/shard_map/all_to_all | solution.py:294
  8.6 10.4 %collective-permute-start = (bf16[32,3072]{1,0:T(8,128)(2,1)}, bf16[32,3072]{1,0:T(8,128)(2,1)S(1)}, u32[]{:S(2)}, u32[]{:S(2)}) collective-permute-start(bf16[32,3072]{1,0:T(8,128)(2,1)} %get-tuple-element.21), channel_id=1, source_target_pairs={{0,1},{1,0},{2,3},{3,2},{4,5},{5,4},{6,7},{7,6},{8,9},{9,8},{10,11... | collective-permute-start | bytes 589832 | tf_op jit(solution)/shard_map/ppermute | solution.py:290
  10.1 11.5 %collective-permute-start.1 = (bf16[32,3072]{1,0:T(8,128)(2,1)}, bf16[32,3072]{1,0:T(8,128)(2,1)S(1)}, u32[]{:S(2)}, u32[]{:S(2)}) collective-permute-start(bf16[32,3072]{1,0:T(8,128)(2,1)} %get-tuple-element.22), channel_id=1, source_target_pairs={{0,2},{1,3},{2,0},{3,1},{4,6},{5,7},{6,4},{7,5},{8,10},{9,11},{10,... | collective-permute-start | bytes 589832 | tf_op jit(solution)/shard_map/ppermute | solution.py:290
  11.6 24.5 %copy-start = (bf16[3072,256]{1,0:T(8,128)(2,1)S(1)}, bf16[3072,256]{1,0:T(8,128)(2,1)}, u32[]{:S(2)}) copy-start(bf16[3072,256]{1,0:T(8,128)(2,1)} %constant.5.clone.table_ref) | copy-start | bytes 4718596
  11.6 9.9 %collective-permute-start.2 = (bf16[32,3072]{1,0:T(8,128)(2,1)}, bf16[32,3072]{1,0:T(8,128)(2,1)S(1)}, u32[]{:S(2)}, u32[]{:S(2)}) collective-permute-start(bf16[32,3072]{1,0:T(8,128)(2,1)} %get-tuple-element.23), channel_id=1, source_target_pairs={{0,3},{1,2},{2,1},{3,0},{4,7},{5,6},{6,5},{7,4},{8,11},{9,10},{10,... | collective-permute-start | bytes 589832 | tf_op jit(solution)/shard_map/ppermute | solution.py:290
  15.6 9.6 %all-to-all-start.1 = ((bf16[8,16,384]{2,1,0:T(8,128)(2,1)}), bf16[8,16,384]{2,1,0:T(8,128)(2,1)S(1)}, u32[]{:S(2)}, u32[]{:S(2)}) async-start(bf16[8,16,384]{2,1,0:T(8,128)(2,1)} %broadcast_in_dim.4), calls=%async_computation.1 | async-start | bytes 196608 | tf_op jit(solution)/shard_map/all_to_all | solution.py:294
  19.0 7.1 %copy-start.6 = (bf16[32,3072]{1,0:T(8,128)(2,1)}, bf16[32,3072]{1,0:T(8,128)(2,1)S(1)}, u32[]{:S(2)}) copy-start(bf16[32,3072]{1,0:T(8,128)(2,1)S(1)} %collective-permute-done.refs_1_) | copy-start | bytes 589828
  21.6 4.5 %copy-start.8 = (bf16[32,3072]{1,0:T(8,128)(2,1)}, bf16[32,3072]{1,0:T(8,128)(2,1)S(1)}, u32[]{:S(2)}) copy-start(bf16[32,3072]{1,0:T(8,128)(2,1)S(1)} %collective-permute-done.1.refs_2_) | copy-start | bytes 589828
  21.6 4.5 %copy-start.10 = (bf16[32,3072]{1,0:T(8,128)(2,1)}, bf16[32,3072]{1,0:T(8,128)(2,1)S(1)}, u32[]{:S(2)}) copy-start(bf16[32,3072]{1,0:T(8,128)(2,1)S(1)} %collective-permute-done.2.refs_3_) | copy-start | bytes 589828
  26.1 10.1 %all-to-all-start.2 = ((bf16[4,8,16,384]{3,2,1,0:T(8,128)(2,1)}), bf16[4,8,16,384]{3,2,1,0:T(8,128)(2,1)S(1)}, u32[]{:S(2)}, u32[]{:S(2)}) async-start(bf16[4,8,16,384]{3,2,1,0:T(8,128)(2,1)} %broadcast_in_dim.5), calls=%async_computation.2 | async-start | bytes 786432 | tf_op jit(solution)/shard_map/all_to_all | solution.py:294
  29.8 0.9 %copy-start.5 = (bf16[32,3072]{1,0:T(8,128)(2,1)S(1)}, bf16[32,3072]{1,0:T(8,128)(2,1)}, u32[]{:S(2)}) copy-start(bf16[32,3072]{1,0:T(8,128)(2,1)} %get-tuple-element.25.refs_0_) | copy-start | bytes 589828
  30.7 0.9 %copy-start.7 = (bf16[32,3072]{1,0:T(8,128)(2,1)S(1)}, bf16[32,3072]{1,0:T(8,128)(2,1)}, u32[]{:S(2)}) copy-start(bf16[32,3072]{1,0:T(8,128)(2,1)} %copy-done.6) | copy-start | bytes 589828
  31.7 0.9 %copy-start.9 = (bf16[32,3072]{1,0:T(8,128)(2,1)S(1)}, bf16[32,3072]{1,0:T(8,128)(2,1)}, u32[]{:S(2)}) copy-start(bf16[32,3072]{1,0:T(8,128)(2,1)} %copy-done.8) | copy-start | bytes 589828
  32.6 0.9 %copy-start.11 = (bf16[32,3072]{1,0:T(8,128)(2,1)S(1)}, bf16[32,3072]{1,0:T(8,128)(2,1)}, u32[]{:S(2)}) copy-start(bf16[32,3072]{1,0:T(8,128)(2,1)} %copy-done.10) | copy-start | bytes 589828
  34.5 0.9 %copy-start.1 = (f32[128,1536]{1,0:T(8,128)}, f32[128,1536]{1,0:T(8,128)S(1)}, u32[]{:S(2)}) copy-start(f32[128,1536]{1,0:T(8,128)S(1)} %get-tuple-element.31.rcv_both) | copy-start | bytes 2359300
  35.4 0.6 %copy-start.3 = (f32[128,128]{1,0:T(8,128)}, f32[128,128]{1,0:T(8,128)S(1)}, u32[]{:S(2)}) copy-start(f32[128,128]{1,0:T(8,128)S(1)} %get-tuple-element.32.rcv_valid) | copy-start | bytes 196612
  36.2 1.1 %copy-start.2 = (f32[128,1536]{1,0:T(8,128)S(1)}, f32[128,1536]{1,0:T(8,128)}, u32[]{:S(2)}) copy-start(f32[128,1536]{1,0:T(8,128)} %copy-done.1) | copy-start | bytes 2359300
  37.3 0.8 %copy-start.4 = (f32[128,128]{1,0:T(8,128)S(1)}, f32[128,128]{1,0:T(8,128)}, u32[]{:S(2)}) copy-start(f32[128,128]{1,0:T(8,128)} %copy-done.3) | copy-start | bytes 196612

commit v3 on v2

v3 whole, which is shorter than its diff:
```python
import functools
import math

import jax
import jax.numpy as jnp
import numpy as np
from jax import lax
from jax.experimental import pallas as pl
from jax.experimental.pallas import tpu as pltpu
from jax.sharding import PartitionSpec as P

NT = 4096
LAG = 150
HALF_WIN = 64
EPSILON = 1e-06

UNUSABLE = 64.0
USABLE_BELOW = 32.0

LANES = 128
BLOCK = 256
MEBI = 1 << 20
FIRST_LAG = LANES - LAG
VMEM = pl.BlockSpec(memory_space=pltpu.VMEM)
HBM = pl.BlockSpec(memory_space=pltpu.HBM)


def lag_table(nbins):
    winding = np.mod(
        np.arange(1, nbins + 1, dtype=np.int64)[:, None]
        * np.arange(FIRST_LAG, FIRST_LAG + BLOCK, dtype=np.int64)[None, :],
        NT,
    )
    theta = winding * (2.0 * math.pi / NT)
    return np.concatenate([np.cos(theta), -np.sin(theta)], axis=0).astype(jnp.bfloat16)


def iota(shape, dim):
    return lax.broadcasted_iota(jnp.int32, shape, dim)


def whitening(real, imag, high, low):
    count, nbins = real.shape
    blocks = nbins // BLOCK
    span = BLOCK + 2 * LANES
    amplitude = jnp.sqrt(real * real + imag * imag)
    rounded = amplitude.astype(jnp.bfloat16)
    edge = jnp.zeros((count, LANES), jnp.bfloat16)
    for part, value in (
        (high, rounded),
        (low, (amplitude - rounded.astype(jnp.float32)).astype(jnp.bfloat16)),
    ):
        part[:, :LANES] = edge
        part[:, LANES : LANES + nbins] = value
        part[:, LANES + nbins :] = edge
    near = jnp.abs(iota((span, BLOCK), 0) - LANES - iota((span, BLOCK), 1)) <= HALF_WIN
    band = jnp.where(near, 1.0, 0.0).astype(jnp.bfloat16)
    pieces = [
        part[:, block * BLOCK : block * BLOCK + span] for block in range(blocks) for part in (high, low)
    ]
    windows = jnp.dot(
        jnp.concatenate(pieces, axis=0), band, preferred_element_type=jnp.float32
    )
    for block in range(blocks):
        first = block * BLOCK
        at = 2 * block * count
        window = windows[at : at + count] + windows[at + count : at + 2 * count]
        index = first + iota((1, BLOCK), 1)
        counted = jnp.minimum(index, HALF_WIN) + jnp.minimum(nbins - 1 - index, HALF_WIN) + 1
        factor = 1.0 / (window / counted.astype(jnp.float32) + EPSILON)
        re = real[:, first : first + BLOCK]
        im = imag[:, first : first + BLOCK]
        usable = re < USABLE_BELOW
        re = jnp.where(usable, re * factor, 0.0).astype(jnp.bfloat16).astype(jnp.float32)
        im = jnp.where(usable, im * factor, 0.0).astype(jnp.bfloat16).astype(jnp.float32)
        yield slice(first, first + BLOCK), re, im


def usable_rows(real):
    return jnp.where(real[:, :LANES] < USABLE_BELOW, 1.0, 0.0)


def encode_kernel(
    segments, spectra_ref, valid_ref, sources_ref, own_ref, other_ref, *refs
):
    blocks, (encoded_ref, spectra, valid, sources, arrived) = refs[:segments], refs[segments:]
    copies = [
        pltpu.make_async_copy(spectra_ref, spectra, arrived.at[0]),
        pltpu.make_async_copy(sources_ref, sources, arrived.at[1]),
        pltpu.make_async_copy(valid_ref, valid, arrived.at[2]),
    ]
    for copy in copies:
        copy.start()
    channels, width = spectra_ref.shape
    nbins = width // 2
    rounds, per_round = sources.shape
    half = rounds * per_round // 2
    index = lax.axis_index("rcv")
    copies[1].wait()
    copies[2].wait()
    diagonal = iota((channels, channels), 0) == iota((channels, channels), 1)
    usable = jnp.sum(jnp.where(diagonal, valid[...], 0), axis=1, keepdims=True) != 0
    row = iota((2 * half, channels), 0)
    local = jnp.zeros((2 * half, channels), jnp.int32)
    for place in range(2 * half):
        number = (index % 2 if place < half else 1 - index % 2) * half + place % half
        here = sources[number // per_round, number % per_round] - index * channels
        local = jnp.where(row == place, here, local)
    onehot = jnp.where(local == iota((2 * half, channels), 1), 1.0, 0.0).astype(jnp.bfloat16)
    copies[0].wait()
    encoded = jnp.where(usable, spectra[...].astype(jnp.float32), UNUSABLE).astype(jnp.bfloat16)
    picked = jnp.dot(onehot, encoded, preferred_element_type=jnp.float32)
    for first, ref in ((0, own_ref), (half, other_ref)):
        rows = picked[first : first + half]
        ref[...] = jnp.concatenate([rows[:, :nbins], rows[:, nbins:]], axis=0).astype(ref.dtype)
    encoded_ref[...] = encoded.astype(encoded_ref.dtype)
    keep = channels // segments
    for step, block in enumerate(blocks):
        at = pl.multiple_of((lax.axis_index("tm") ^ step) * keep, keep)
        block[...] = encoded_ref[pl.ds(at, keep), :].astype(block.dtype)


def whiten_kernel(segments, *refs):
    blocks, (real_ref, imag_ref, valid_ref, high, low) = refs[:segments], refs[segments:]
    rows = jnp.concatenate([ref[...].astype(jnp.float32) for ref in blocks], axis=0)
    nbins = rows.shape[1] // 2
    real, imag = rows[:, :nbins], rows[:, nbins:]
    for at, re, im in whitening(real, imag, high, low):
        real_ref[:, at] = re
        imag_ref[:, at] = im
    valid_ref[...] = usable_rows(real)


def stack_kernel(
    segments, slabs_ref, rcv_re, rcv_im, rcv_valid, table_ref, *refs
):
    *rest, out_ref, src_re, src_im, high, low, cross_a, cross_b, total_re, total_im = refs[
        : 10 if len(refs) == 12 else 9
    ]
    half = slabs_ref.shape[0] // (2 * segments)
    nbins = slabs_ref.shape[1]
    keep = rcv_re.shape[0] // segments
    rows = half * keep
    if rest:
        result, written = refs[10:]
        part = lax.axis_index("rcv") % 2
        first_copy = pltpu.make_async_copy(
            rest[0], out_ref.at[pl.ds(pl.multiple_of(part * rows, rows), rows)], written.at[0]
        )
        first_copy.start()
    else:
        result = out_ref
    slabs = slabs_ref[...].astype(jnp.float32)
    real = jnp.concatenate(
        [slabs[2 * half * t : 2 * half * t + half] for t in range(segments)], axis=0
    )
    imag = jnp.concatenate(
        [slabs[2 * half * t + half : 2 * half * (t + 1)] for t in range(segments)], axis=0
    )
    for at, re, im in whitening(real, imag, high, low):
        src_re[:, at] = re
        src_im[:, at] = im
    src_valid = usable_rows(real)
    total_re[...] = jnp.zeros_like(total_re)
    total_im[...] = jnp.zeros_like(total_im)
    cross_b[...] = jnp.zeros_like(cross_b)

    def multiply(block, cross):
        for sub in range(BLOCK // LANES):
            at = pl.ds(pl.multiple_of(block * BLOCK + sub * LANES, LANES), LANES)
            r_re = [rcv_re[t * keep : (t + 1) * keep, at] for t in range(segments)]
            r_im = [rcv_im[t * keep : (t + 1) * keep, at] for t in range(segments)]
            for source in range(half):
                real, imag = 0.0, 0.0
                for t in range(segments):
                    row = slice(t * half + source, t * half + source + 1)
                    s_re, s_im = src_re[row, at], src_im[row, at]
                    real = real + s_re * r_re[t] + s_im * r_im[t]
                    imag = imag + s_im * r_re[t] - s_re * r_im[t]
                to = slice(source * keep, (source + 1) * keep)
                cross[to, sub * LANES : (sub + 1) * LANES] = real.astype(cross.dtype)
                cross[to, BLOCK + sub * LANES : BLOCK + (sub + 1) * LANES] = imag.astype(
                    cross.dtype
                )

    def project(block, cross):
        value = cross[...].astype(jnp.bfloat16)
        re_at = pl.ds(pl.multiple_of(block * BLOCK, BLOCK), BLOCK)
        im_at = pl.ds(pl.multiple_of(nbins + block * BLOCK, BLOCK), BLOCK)
        total_re[...] += jnp.dot(
            value[:, :BLOCK], table_ref[re_at, :], preferred_element_type=jnp.float32
        )
        total_im[...] += jnp.dot(
            value[:, BLOCK:], table_ref[im_at, :], preferred_element_type=jnp.float32
        )

    def two_blocks(pair, carry):
        multiply(2 * pair, cross_a)
        project(jnp.maximum(2 * pair - 1, 0), cross_b)
        multiply(2 * pair + 1, cross_b)
        project(2 * pair, cross_a)
        return carry

    pairs = nbins // (2 * BLOCK)
    lax.fori_loop(0, pairs, two_blocks, 0)
    project(2 * pairs - 1, cross_b)

    lags = result.shape[1]
    scale = 2.0 / math.sqrt(nbins)
    mirror = LAG - FIRST_LAG - iota((keep, LANES), 1)
    for source in range(half):
        common = 0.0
        for t in range(segments):
            row = t * half + source
            common = common + src_valid[row : row + 1] * rcv_valid[t * keep : (t + 1) * keep, :]
        weight = scale / jnp.maximum(common, 1.0)
        to = slice(source * keep, (source + 1) * keep)
        even, odd = total_re[to], total_im[to]
        ahead = even + odd
        behind = even - odd
        low_part = jnp.take_along_axis(
            behind[:, :LANES], jnp.clip(mirror, 0, LANES - 1), axis=1
        )
        high_part = jnp.take_along_axis(
            behind[:, LANES:], jnp.clip(mirror - LANES, 0, LANES - 1), axis=1
        )
        result[to, :LANES] = jnp.where(mirror < LANES, low_part, high_part) * weight
        for first in range(0, lags - LANES, LANES):
            last = min(first + LANES, lags - LANES)
            value = ahead[:, first : first + LANES] * weight
            result[to, LANES + first : LANES + last] = value[:, : last - first]
    if rest:
        second_copy = pltpu.make_async_copy(
            result,
            out_ref.at[pl.ds(pl.multiple_of((1 - part) * rows, rows), rows)],
            written.at[1],
        )
        second_copy.start()
        first_copy.wait()
        second_copy.wait()


def encode(segments, spectra, valid, sources):
    channels, width = spectra.shape
    keep = channels // segments
    slab = jax.ShapeDtypeStruct((sources.size, width // 2), jnp.bfloat16)
    block = jax.ShapeDtypeStruct((keep, width), jnp.bfloat16)
    pinned = [pltpu.with_memory_space_constraint(x, pltpu.HBM) for x in (spectra, valid, sources)]
    return pl.pallas_call(
        functools.partial(encode_kernel, segments),
        out_shape=(slab, slab) + (block,) * segments,
        in_specs=[HBM] * 3,
        out_specs=(VMEM,) * (2 + segments),
        scratch_shapes=[
            pltpu.VMEM((channels, width), jnp.bfloat16 if keep % 16 == 0 else jnp.float32),
            pltpu.VMEM((channels, width), jnp.bfloat16),
            pltpu.VMEM((1, channels), jnp.int32),
            pltpu.SMEM(sources.shape, jnp.int32),
            pltpu.SemaphoreType.DMA((3,)),
        ],
        compiler_params=pltpu.CompilerParams(vmem_limit_bytes=12 * MEBI),
        name="encode_and_pick",
    )(*pinned)


def whiten_blocks(blocks):
    segments, (keep, width) = len(blocks), blocks[0].shape
    count, nbins = segments * keep, width // 2
    padded = pltpu.VMEM((count, nbins + 2 * LANES), jnp.bfloat16)
    part = jax.ShapeDtypeStruct((count, nbins), jnp.float32)
    return pl.pallas_call(
        functools.partial(whiten_kernel, segments),
        out_shape=(part, part, jax.ShapeDtypeStruct((count, LANES), jnp.float32)),
        in_specs=[VMEM] * segments,
        out_specs=(VMEM,) * 3,
        scratch_shapes=[padded, padded],
        compiler_params=pltpu.CompilerParams(vmem_limit_bytes=20 * MEBI),
        cost_estimate=pl.CostEstimate(
            flops=count * width * 1024, bytes_accessed=count * width * 4, transcendentals=0
        ),
        name="whiten_receivers",
    )(*blocks)


def stack_half(segments, slabs, receivers, table, rest=()):
    half, nbins = slabs.shape[0] // (2 * segments), slabs.shape[1]
    keep = receivers[0].shape[0] // segments
    count, rows, lags = segments * half, half * keep, 2 * LAG + 1
    padded = pltpu.VMEM((count, nbins + 2 * LANES), jnp.bfloat16)
    part = pltpu.VMEM((count, nbins), jnp.float32)
    cross = pltpu.VMEM((rows, 2 * BLOCK), jnp.bfloat16 if keep % 16 == 0 else jnp.float32)
    total = pltpu.VMEM((rows, BLOCK), jnp.float32)
    scratch = [part, part, padded, padded, cross, cross, total, total]
    if rest:
        scratch += [pltpu.VMEM((rows, lags), jnp.float32), pltpu.SemaphoreType.DMA((2,))]
    return pl.pallas_call(
        functools.partial(stack_kernel, segments),
        out_shape=jax.ShapeDtypeStruct((2 * rows if rest else rows, lags), jnp.float32),
        in_specs=[VMEM] * (5 + len(rest)),
        out_specs=HBM if rest else VMEM,
        scratch_shapes=scratch,
        compiler_params=pltpu.CompilerParams(vmem_limit_bytes=20 * MEBI),
        cost_estimate=pl.CostEstimate(
            flops=4 * rows * nbins * 2 * LAG, bytes_accessed=nbins * 2048, transcendentals=0
        ),
        name="stack_other_half" if rest else "stack_own_half",
    )(slabs, *receivers, table, *rest)


def swapped(value, axis, size, step):
    return lax.ppermute(value, axis, [(i, i ^ step) for i in range(size)])


def shards(rcv_size, tm_size, spectra, valid, sources):
    channels, _, width = spectra.shape
    keep = channels // tm_size
    rounds, per_round = sources.shape
    own, other, *receivers = encode(
        tm_size, spectra[:, 0, :], valid.reshape(1, channels), sources
    )
    own = own + swapped(other, "rcv", rcv_size, 1)
    receivers = receivers[:1] + [
        swapped(receivers[step], "tm", tm_size, step) for step in range(1, tm_size)
    ]
    step = 2
    while step < rcv_size:
        own = own + swapped(own, "rcv", rcv_size, step)
        step *= 2
    own, receivers = lax.optimization_barrier((own, receivers))
    own = [own] + [swapped(own, "tm", tm_size, step) for step in range(1, tm_size)]
    whitened = whiten_blocks(receivers)
    own, whitened = lax.optimization_barrier((own, whitened))
    own = jnp.concatenate(own, axis=0)
    other = swapped(own, "rcv", rcv_size, 1)

    table = jnp.asarray(lag_table(width // 2))
    first = stack_half(tm_size, own, whitened, table)
    stack = stack_half(tm_size, other, whitened, table, (first,))
    return stack.reshape(rounds, per_round, keep, 2 * LAG + 1)


def solution(mesh):
    body = functools.partial(shards, mesh.shape["rcv"], mesh.shape["tm"])
    in_specs = (P("rcv", "tm", None), P("rcv", "tm"), P())
    out_specs = P(None, None, ("rcv", "tm"), None)
    return jax.shard_map(body, mesh=mesh, in_specs=in_specs, out_specs=out_specs, check_vma=False)
```

time: 46 us -> 32.6 us (0.71)
  local copies, waits for them, and re-layouts: 8.63 us -> 0.02 us
  starting transfers between devices: 16.9 us -> 13.4 us
  waiting for transfers between devices: 9.27 us -> 8.29 us
    all_to_all x3 -> x0, starting transfers between devices: 13.4 us -> none  [exchanged(): return lax.all_to_all(value, axis, 0, 0, tiled=True)]
    ppermute x3 -> x10, starting transfers between devices: 3.49 us -> 13.4 us  [swapped(): return lax.ppermute(value, axis, [(i, i ^ step) for i in range(size)])]
    unnamed x24 -> x5, local copies, waits for them, and re-layouts: 7.19 us -> 0.02 us
    all_to_all x3 -> x0, waiting for transfers between devices: 6.72 us -> none  [exchanged(): return lax.all_to_all(value, axis, 0, 0, tiled=True)]
    ppermute x3 -> x10, waiting for transfers between devices: 2.54 us -> 8.29 us  [swapped(): return lax.ppermute(value, axis, [(i, i ^ step) for i in range(size)])]
    broadcast_in_dim x2 -> x0, local copies, waits for them, and re-layouts: 1.44 us -> none  [the longest x1 0.79 us: shards(): jnp.broadcast_to(chosen[None], (tm_size,) + chosen.shape)]
    pallas_call x2 -> x3, Pallas kernels: 9.58 us -> 9.59 us  [the longest x2 7.77 us: stack_half(): pl.pallas_call(functools.partial(stack_kernel, segments), out_shape=jax.S...]
  transfers between devices with their start and end apart: 6 -> 10, of which waited for: 4 -> 6; matrix products, arithmetic and copies ran while one was open for 1% -> 0% of each run, Pallas kernels for 2% -> 14%
where the time goes in v3:
time: 32.6 us; the launch traced here: 32.4 us
  starting transfers between devices  13.4 us (41%)
  Pallas kernels  10.6 us (33%)
  waiting for transfers between devices  8.29 us (25%)
    ppermute x10, starting transfers between devices, swapped(): return lax.ppermute(value, axis, [(i, i ^ step) for i in range(size)])  13.4 us
    ppermute x10, waiting for transfers between devices, swapped(): return lax.ppermute(value, axis, [(i, i ^ step) for i in range(size)])  8.29 us
    pallas_call x2, Pallas kernels, stack_half(): pl.pallas_call(functools.partial(stack_kernel, segments), out_shape=jax.S...  7.77 us
    pallas_call x1, Pallas kernels, encode(): pl.pallas_call(functools.partial(encode_kernel, segments), out_shape=(sla...  1.82 us
    pallas_call x1, Pallas kernels, whiten_blocks(): pl.pallas_call(functools.partial(whiten_kernel, segments), out_shape=(par...  0.96 us
  transfers between devices with their start and end apart: 10, of which 6 were waited for; matrix products, arithmetic and copies ran while one was open for 0% of the time, Pallas kernels for 14%

profile of v3, /device:TPU:0, one launch (start us, length us, event | category | flops | bytes accessed | tf_op | source)
XLA Modules:
  0.0 32.4 jit_solution(6602058852986447328)
XLA Ops:
  0.0 0.0 copy-start
  0.0 1.8 %encode_and_pick.1 = (bf16[16,1536]{1,0:T(8,128)(2,1)S(1)}, bf16[16,1536]{1,0:T(8,128)(2,1)S(1)}, bf16[32,3072]{1,0:T(8,128)(2,1)S(1)}, bf16[32,3072]{1,0:T(8,12...) custom-call(bf16[128,3072]{1,0:T(8,128)(2,1)} %bitcast.3, s32[1,128]{1,0:T(1,128)} %bitcast.4, ...), custom_call_target="tpu_custom_call" | custom-call | tf_op jit(solution)/shard_map/encode_and_pick/pallas_call | solution.py:249
  1.8 3.0 %collective-permute-start.3 = (bf16[32,3072]{1,0:T(8,128)(2,1)S(1)}, bf16[32,3072]{1,0:T(8,128)(2,1)S(1)}, u32[]{:S(2)}, u32[]{:S(2)}) collective-permute-start(bf16[32,3072]{1,0:T(8,128)(2,1)S(1)} %get-tuple-element.29), channel_id=1, source_target_pairs={{0,1},{1,0},{2,3},{3,2},{4,5},{5,4},{6,7},{7,6},{8,9},{9,8},{10,11... | collective-permute-start | bytes 589832 | tf_op jit(solution)/shard_map/ppermute | solution.py:311
  4.8 1.5 %collective-permute-start.4 = (bf16[32,3072]{1,0:T(8,128)(2,1)S(1)}, bf16[32,3072]{1,0:T(8,128)(2,1)S(1)}, u32[]{:S(2)}, u32[]{:S(2)}) collective-permute-start(bf16[32,3072]{1,0:T(8,128)(2,1)S(1)} %get-tuple-element.30), channel_id=1, source_target_pairs={{0,2},{1,3},{2,0},{3,1},{4,6},{5,7},{6,4},{7,5},{8,10},{9,11},{10,... | collective-permute-start | bytes 589832 | tf_op jit(solution)/shard_map/ppermute | solution.py:311
  6.4 0.0 collective-permute-start.5
  6.4 0.0 collective-permute-start
  6.4 1.2 %collective-permute-done = bf16[16,1536]{1,0:T(8,128)(2,1)S(1)} collective-permute-done((bf16[16,1536]{1,0:T(8,128)(2,1)S(1)}, bf16[16,1536]{1,0:T(8,128)(2,1)S(1)}, u32[]{:S(2)}, u32[]{:S(2)}) %collective-permute-start) | collective-permute-done | bytes 49184 | tf_op jit(solution)/shard_map/ppermute | solution.py:311
  7.6 2.1 %collective-permute-start.1 = (bf16[16,1536]{1,0:T(8,128)(2,1)S(1)}, bf16[16,1536]{1,0:T(8,128)(2,1)S(1)}, u32[]{:S(2)}, u32[]{:S(2)}) collective-permute-start(bf16[16,1536]{1,0:T(8,128)(2,1)S(1)} %add.9), channel_id=1, source_target_pairs={{0,8},{4,12},{8,0},{12,4},{16,24},{20,28},{24,16},{28,20},{1,9},{5... | collective-permute-start | bytes 147464 | tf_op jit(solution)/shard_map/ppermute | solution.py:311
  9.7 2.1 %collective-permute-done.1 = bf16[16,1536]{1,0:T(8,128)(2,1)S(1)} collective-permute-done((bf16[16,1536]{1,0:T(8,128)(2,1)S(1)}, bf16[16,1536]{1,0:T(8,128)(2,1)S(1)}, u32[]{:S(2)}, u32[]{:S(2)}) %collective-permute-start.1) | collective-permute-done | bytes 49184 | tf_op jit(solution)/shard_map/ppermute | solution.py:311
  11.8 3.1 %collective-permute-start.2 = (bf16[16,1536]{1,0:T(8,128)(2,1)S(1)}, bf16[16,1536]{1,0:T(8,128)(2,1)S(1)}, u32[]{:S(2)}, u32[]{:S(2)}) collective-permute-start(bf16[16,1536]{1,0:T(8,128)(2,1)S(1)} %add.10), channel_id=1, source_target_pairs={{0,16},{4,20},{8,24},{12,28},{16,0},{20,4},{24,8},{28,12},{1,17},{... | collective-permute-start | bytes 147464 | tf_op jit(solution)/shard_map/ppermute | solution.py:311
  14.9 2.3 %collective-permute-done.2 = bf16[16,1536]{1,0:T(8,128)(2,1)S(1)} collective-permute-done((bf16[16,1536]{1,0:T(8,128)(2,1)S(1)}, bf16[16,1536]{1,0:T(8,128)(2,1)S(1)}, u32[]{:S(2)}, u32[]{:S(2)}) %collective-permute-start.2) | collective-permute-done | bytes 49184 | tf_op jit(solution)/shard_map/ppermute | solution.py:311
  17.2 0.0 collective-permute-done.3.refs_1_
  17.2 0.0 collective-permute-done.4.refs_2_
  17.2 0.0 collective-permute-done.5.refs_3_
  17.2 2.6 %collective-permute-start.8 = (bf16[16,1536]{1,0:T(8,128)(2,1)S(1)}, bf16[16,1536]{1,0:T(8,128)(2,1)S(1)}, u32[]{:S(2)}, u32[]{:S(2)}) collective-permute-start(bf16[16,1536]{1,0:T(8,128)(2,1)S(1)} %add.11), channel_id=1, source_target_pairs={{0,3},{1,2},{2,1},{3,0},{4,7},{5,6},{6,5},{7,4},{8,11},{9,10},{10,... | collective-permute-start | bytes 147464 | tf_op jit(solution)/shard_map/ppermute | solution.py:311
  19.9 0.5 %collective-permute-start.7 = (bf16[16,1536]{1,0:T(8,128)(2,1)S(1)}, bf16[16,1536]{1,0:T(8,128)(2,1)S(1)}, u32[]{:S(2)}, u32[]{:S(2)}) collective-permute-start(bf16[16,1536]{1,0:T(8,128)(2,1)S(1)} %add.11), channel_id=1, source_target_pairs={{0,2},{1,3},{2,0},{3,1},{4,6},{5,7},{6,4},{7,5},{8,10},{9,11},{10,... | collective-permute-start | bytes 147464 | tf_op jit(solution)/shard_map/ppermute | solution.py:311
  20.4 0.4 %collective-permute-start.6 = (bf16[16,1536]{1,0:T(8,128)(2,1)S(1)}, bf16[16,1536]{1,0:T(8,128)(2,1)S(1)}, u32[]{:S(2)}, u32[]{:S(2)}) collective-permute-start(bf16[16,1536]{1,0:T(8,128)(2,1)S(1)} %add.11), channel_id=1, source_target_pairs={{0,1},{1,0},{2,3},{3,2},{4,5},{5,4},{6,7},{7,6},{8,9},{9,8},{10,11... | collective-permute-start | bytes 147464 | tf_op jit(solution)/shard_map/ppermute | solution.py:311
  20.8 1.0 %whiten_receivers.1 = (f32[128,1536]{1,0:T(8,128)S(1)}, f32[128,1536]{1,0:T(8,128)S(1)}, f32[128,128]{1,0:T(8,128)S(1)}) custom-call(bf16[32,3072]{1,0:T(8,128)(2,1)S(1)} %get-tuple-element.33.refs_0_, bf16[32,3072]{1,0:T(8,128)(2,1)S(1)} %collective-permute-done.3.refs_1_, bf16[32,3072]{1,0:T(8,128)(2,1)S(1)} %collective-permute-done.4.refs_2_, ...), custom_call_target="tpu_custom_call" | custom-call | flops 402653184 | bytes 1572864 | tf_op jit(solution)/shard_map/whiten_receivers/pallas_call | solution.py:271
  21.8 0.8 %collective-permute-done.8 = bf16[16,1536]{1,0:T(8,128)(2,1)S(1)} collective-permute-done((bf16[16,1536]{1,0:T(8,128)(2,1)S(1)}, bf16[16,1536]{1,0:T(8,128)(2,1)S(1)}, u32[]{:S(2)}, u32[]{:S(2)}) %collective-permute-start.8) | collective-permute-done | bytes 49184 | tf_op jit(solution)/shard_map/ppermute | solution.py:311
  22.6 1.4 %collective-permute-done.7 = bf16[16,1536]{1,0:T(8,128)(2,1)S(1)} collective-permute-done((bf16[16,1536]{1,0:T(8,128)(2,1)S(1)}, bf16[16,1536]{1,0:T(8,128)(2,1)S(1)}, u32[]{:S(2)}, u32[]{:S(2)}) %collective-permute-start.7) | collective-permute-done | bytes 49184 | tf_op jit(solution)/shard_map/ppermute | solution.py:311
  24.0 0.5 %collective-permute-done.6 = bf16[16,1536]{1,0:T(8,128)(2,1)S(1)} collective-permute-done((bf16[16,1536]{1,0:T(8,128)(2,1)S(1)}, bf16[16,1536]{1,0:T(8,128)(2,1)S(1)}, u32[]{:S(2)}, u32[]{:S(2)}) %collective-permute-start.6) | collective-permute-done | bytes 49184 | tf_op jit(solution)/shard_map/ppermute | solution.py:311
  24.5 0.1 collective-permute-start.9
  24.6 0.0 copy-done
  24.6 3.5 %stack_own_half.1.refs_0_ = f32[256,301]{1,0:T(8,128)S(1)} custom-call(bf16[64,1536]{1,0:T(8,128)(2,1)S(1)} %constant_dynamic-update-slice_fusion.slabs_ref, f32[128,1536]{1,0:T(8,128)S(1)} %get-tuple-element.44.rcv_re, f32[128,1536]{1,0:T(8,128)S(1)} %get-tuple-element.45.rcv_im, f32[128,128]{1,0:T(8,128)S(1)} %get-tuple-element.46.rcv_valid, ...), custom_call_target="tpu_custom_call" | custom-call | flops 471859200 | bytes 3145728 | tf_op jit(solution)/shard_map/stack_own_half/pallas_call | solution.py:296
  28.1 0.0 collective-permute-done.9.slabs_ref
  28.1 4.3 %stack_other_half.1 = f32[512,301]{1,0:T(8,128)} custom-call(bf16[64,1536]{1,0:T(8,128)(2,1)S(1)} %collective-permute-done.9.slabs_ref, f32[128,1536]{1,0:T(8,128)S(1)} %get-tuple-element.44.rcv_re, f32[128,1536]{1,0:T(8,128)S(1)} %get-tuple-element.45.rcv_im, f32[128,128]{1,0:T(8,128)S(1)} %get-tuple-element.46.rcv_valid, bf16[3072,256]{1,0:T(8,128)(2,1)S(1)} %copy-done, ...), custom_call_target="tpu_custom_call" | custom-call | flops 471859200 | bytes 3145728 | tf_op jit(solution)/shard_map/stack_other_half/pallas_call | solution.py:296
  (7 shorter events, 0.1 us)
Async XLA Ops:
  0.0 24.6 %copy-start = (bf16[3072,256]{1,0:T(8,128)(2,1)S(1)}, bf16[3072,256]{1,0:T(8,128)(2,1)}, u32[]{:S(2)}) copy-start(bf16[3072,256]{1,0:T(8,128)(2,1)} %constant.2.clone.table_ref) | copy-start | bytes 4718596
  1.8 15.4 %collective-permute-start.3 = (bf16[32,3072]{1,0:T(8,128)(2,1)S(1)}, bf16[32,3072]{1,0:T(8,128)(2,1)S(1)}, u32[]{:S(2)}, u32[]{:S(2)}) collective-permute-start(bf16[32,3072]{1,0:T(8,128)(2,1)S(1)} %get-tuple-element.29), channel_id=1, source_target_pairs={{0,1},{1,0},{2,3},{3,2},{4,5},{5,4},{6,7},{7,6},{8,9},{9,8},{10,11... | collective-permute-start | bytes 589832 | tf_op jit(solution)/shard_map/ppermute | solution.py:311
  4.8 12.4 %collective-permute-start.4 = (bf16[32,3072]{1,0:T(8,128)(2,1)S(1)}, bf16[32,3072]{1,0:T(8,128)(2,1)S(1)}, u32[]{:S(2)}, u32[]{:S(2)}) collective-permute-start(bf16[32,3072]{1,0:T(8,128)(2,1)S(1)} %get-tuple-element.30), channel_id=1, source_target_pairs={{0,2},{1,3},{2,0},{3,1},{4,6},{5,7},{6,4},{7,5},{8,10},{9,11},{10,... | collective-permute-start | bytes 589832 | tf_op jit(solution)/shard_map/ppermute | solution.py:311
  6.4 10.9 %collective-permute-start.5 = (bf16[32,3072]{1,0:T(8,128)(2,1)S(1)}, bf16[32,3072]{1,0:T(8,128)(2,1)S(1)}, u32[]{:S(2)}, u32[]{:S(2)}) collective-permute-start(bf16[32,3072]{1,0:T(8,128)(2,1)S(1)} %get-tuple-element.31), channel_id=1, source_target_pairs={{0,3},{1,2},{2,1},{3,0},{4,7},{5,6},{6,5},{7,4},{8,11},{9,10},{10,... | collective-permute-start | bytes 589832 | tf_op jit(solution)/shard_map/ppermute | solution.py:311
  6.4 1.2 %collective-permute-start = (bf16[16,1536]{1,0:T(8,128)(2,1)S(1)}, bf16[16,1536]{1,0:T(8,128)(2,1)S(1)}, u32[]{:S(2)}, u32[]{:S(2)}) collective-permute-start(bf16[16,1536]{1,0:T(8,128)(2,1)S(1)} %get-tuple-element.27), channel_id=1, source_target_pairs={{0,4},{4,0},{8,12},{12,8},{16,20},{20,16},{24,28},{28,24},{1,5},{5... | collective-permute-start | bytes 147464 | tf_op jit(solution)/shard_map/ppermute | solution.py:311
  7.6 4.2 %collective-permute-start.1 = (bf16[16,1536]{1,0:T(8,128)(2,1)S(1)}, bf16[16,1536]{1,0:T(8,128)(2,1)S(1)}, u32[]{:S(2)}, u32[]{:S(2)}) collective-permute-start(bf16[16,1536]{1,0:T(8,128)(2,1)S(1)} %add.9), channel_id=1, source_target_pairs={{0,8},{4,12},{8,0},{12,4},{16,24},{20,28},{24,16},{28,20},{1,9},{5... | collective-permute-start | bytes 147464 | tf_op jit(solution)/shard_map/ppermute | solution.py:311
  11.8 5.4 %collective-permute-start.2 = (bf16[16,1536]{1,0:T(8,128)(2,1)S(1)}, bf16[16,1536]{1,0:T(8,128)(2,1)S(1)}, u32[]{:S(2)}, u32[]{:S(2)}) collective-permute-start(bf16[16,1536]{1,0:T(8,128)(2,1)S(1)} %add.10), channel_id=1, source_target_pairs={{0,16},{4,20},{8,24},{12,28},{16,0},{20,4},{24,8},{28,12},{1,17},{... | collective-permute-start | bytes 147464 | tf_op jit(solution)/shard_map/ppermute | solution.py:311
  17.2 5.3 %collective-permute-start.8 = (bf16[16,1536]{1,0:T(8,128)(2,1)S(1)}, bf16[16,1536]{1,0:T(8,128)(2,1)S(1)}, u32[]{:S(2)}, u32[]{:S(2)}) collective-permute-start(bf16[16,1536]{1,0:T(8,128)(2,1)S(1)} %add.11), channel_id=1, source_target_pairs={{0,3},{1,2},{2,1},{3,0},{4,7},{5,6},{6,5},{7,4},{8,11},{9,10},{10,... | collective-permute-start | bytes 147464 | tf_op jit(solution)/shard_map/ppermute | solution.py:311
  19.9 4.1 %collective-permute-start.7 = (bf16[16,1536]{1,0:T(8,128)(2,1)S(1)}, bf16[16,1536]{1,0:T(8,128)(2,1)S(1)}, u32[]{:S(2)}, u32[]{:S(2)}) collective-permute-start(bf16[16,1536]{1,0:T(8,128)(2,1)S(1)} %add.11), channel_id=1, source_target_pairs={{0,2},{1,3},{2,0},{3,1},{4,6},{5,7},{6,4},{7,5},{8,10},{9,11},{10,... | collective-permute-start | bytes 147464 | tf_op jit(solution)/shard_map/ppermute | solution.py:311
  20.4 4.1 %collective-permute-start.6 = (bf16[16,1536]{1,0:T(8,128)(2,1)S(1)}, bf16[16,1536]{1,0:T(8,128)(2,1)S(1)}, u32[]{:S(2)}, u32[]{:S(2)}) collective-permute-start(bf16[16,1536]{1,0:T(8,128)(2,1)S(1)} %add.11), channel_id=1, source_target_pairs={{0,1},{1,0},{2,3},{3,2},{4,5},{5,4},{6,7},{7,6},{8,9},{9,8},{10,11... | collective-permute-start | bytes 147464 | tf_op jit(solution)/shard_map/ppermute | solution.py:311
  24.5 3.6 %collective-permute-start.9 = (bf16[64,1536]{1,0:T(8,128)(2,1)S(1)}, bf16[64,1536]{1,0:T(8,128)(2,1)S(1)}, u32[]{:S(2)}, u32[]{:S(2)}) collective-permute-start(bf16[64,1536]{1,0:T(8,128)(2,1)S(1)} %constant_dynamic-update-slice_fusion.slabs_ref), channel_id=1, source_target_pairs={{0,4},{4,0},{8,12},{12,8},{16,20},{20,16},{24,28},{28,24},{1,5},{5... | collective-permute-start | bytes 589832 | tf_op jit(solution)/shard_map/ppermute | solution.py:311

commit v4 on v3

--- a/solution.py
+++ b/solution.py
@@ -14,8 +14,8 @@
 HALF_WIN = 64
 EPSILON = 1e-06
 
-UNUSABLE = 64.0
-USABLE_BELOW = 32.0
+UNUSABLE = 1024.0
+USABLE_BELOW = 512.0
 
 LANES = 128
 BLOCK = 256
@@ -39,7 +39,7 @@
     return lax.broadcasted_iota(jnp.int32, shape, dim)
 
 
-def whitening(real, imag, high, low):
+def whitening(real, imag, high, low, unusable=0.0):
     count, nbins = real.shape
     blocks = nbins // BLOCK
     span = BLOCK + 2 * LANES
@@ -71,8 +71,8 @@
         re = real[:, first : first + BLOCK]
         im = imag[:, first : first + BLOCK]
         usable = re < USABLE_BELOW
-        re = jnp.where(usable, re * factor, 0.0).astype(jnp.bfloat16).astype(jnp.float32)
-        im = jnp.where(usable, im * factor, 0.0).astype(jnp.bfloat16).astype(jnp.float32)
+        re = jnp.where(usable, re * factor, unusable).astype(jnp.bfloat16).astype(jnp.float32)
+        im = jnp.where(usable, im * factor, unusable).astype(jnp.bfloat16).astype(jnp.float32)
         yield slice(first, first + BLOCK), re, im
 
 
@@ -83,7 +83,8 @@
 def encode_kernel(
     segments, spectra_ref, valid_ref, sources_ref, own_ref, other_ref, *refs
 ):
-    blocks, (encoded_ref, spectra, valid, sources, arrived) = refs[:segments], refs[segments:]
+    blocks, refs = refs[:segments], refs[segments:]
+    encoded_ref, spectra, valid, sources, high, low, arrived = refs
     copies = [
         pltpu.make_async_copy(spectra_ref, spectra, arrived.at[0]),
         pltpu.make_async_copy(sources_ref, sources, arrived.at[1]),
@@ -110,9 +111,10 @@
     copies[0].wait()
     encoded = jnp.where(usable, spectra[...].astype(jnp.float32), UNUSABLE).astype(jnp.bfloat16)
     picked = jnp.dot(onehot, encoded, preferred_element_type=jnp.float32)
-    for first, ref in ((0, own_ref), (half, other_ref)):
-        rows = picked[first : first + half]
-        ref[...] = jnp.concatenate([rows[:, :nbins], rows[:, nbins:]], axis=0).astype(ref.dtype)
+    for at, re, im in whitening(picked[:, :nbins], picked[:, nbins:], high, low, UNUSABLE):
+        for first, ref in ((0, own_ref), (half, other_ref)):
+            rows = slice(first, first + half)
+            ref[:, at] = jnp.concatenate([re[rows], im[rows]], axis=0).astype(ref.dtype)
     encoded_ref[...] = encoded.astype(encoded_ref.dtype)
     keep = channels // segments
     for step, block in enumerate(blocks):
@@ -134,20 +136,22 @@
 def stack_kernel(
     segments, slabs_ref, rcv_re, rcv_im, rcv_valid, table_ref, *refs
 ):
-    *rest, out_ref, src_re, src_im, high, low, cross_a, cross_b, total_re, total_im = refs[
-        : 10 if len(refs) == 12 else 9
+    *rest, out_ref, src_re, src_im, cross_a, cross_b, total_re, total_im = refs[
+        : 8 if len(refs) == 10 else 7
     ]
     half = slabs_ref.shape[0] // (2 * segments)
     nbins = slabs_ref.shape[1]
     keep = rcv_re.shape[0] // segments
     rows = half * keep
     if rest:
-        result, written = refs[10:]
+        result, written = refs[8:]
         part = lax.axis_index("rcv") % 2
-        first_copy = pltpu.make_async_copy(
-            rest[0], out_ref.at[pl.ds(pl.multiple_of(part * rows, rows), rows)], written.at[0]
-        )
-        first_copy.start()
+        pieces = max(1, half // 4)
+        at = pl.multiple_of(part * rows, rows)
+        copies = [
+            pltpu.make_async_copy(rest[0], out_ref.at[pl.ds(at, rows)], written.at[0])
+        ]
+        copies[0].start()
     else:
         result = out_ref
     slabs = slabs_ref[...].astype(jnp.float32)
@@ -157,9 +161,9 @@
     imag = jnp.concatenate(
         [slabs[2 * half * t + half : 2 * half * (t + 1)] for t in range(segments)], axis=0
     )
-    for at, re, im in whitening(real, imag, high, low):
-        src_re[:, at] = re
-        src_im[:, at] = im
+    usable = real < USABLE_BELOW
+    src_re[...] = jnp.where(usable, real, 0.0)
+    src_im[...] = jnp.where(usable, imag, 0.0)
     src_valid = usable_rows(real)
     total_re[...] = jnp.zeros_like(total_re)
     total_im[...] = jnp.zeros_like(total_im)
@@ -171,12 +175,13 @@
             r_re = [rcv_re[t * keep : (t + 1) * keep, at] for t in range(segments)]
             r_im = [rcv_im[t * keep : (t + 1) * keep, at] for t in range(segments)]
             for source in range(half):
-                real, imag = 0.0, 0.0
+                real, imag = [], []
                 for t in range(segments):
                     row = slice(t * half + source, t * half + source + 1)
                     s_re, s_im = src_re[row, at], src_im[row, at]
-                    real = real + s_re * r_re[t] + s_im * r_im[t]
-                    imag = imag + s_im * r_re[t] - s_re * r_im[t]
+                    real.append(s_re * r_re[t] + s_im * r_im[t])
+                    imag.append(s_im * r_re[t] - s_re * r_im[t])
+                real, imag = functools.reduce(jnp.add, real), functools.reduce(jnp.add, imag)
                 to = slice(source * keep, (source + 1) * keep)
                 cross[to, sub * LANES : (sub + 1) * LANES] = real.astype(cross.dtype)
                 cross[to, BLOCK + sub * LANES : BLOCK + (sub + 1) * LANES] = imag.astype(
@@ -229,15 +234,20 @@
             last = min(first + LANES, lags - LANES)
             value = ahead[:, first : first + LANES] * weight
             result[to, LANES + first : LANES + last] = value[:, : last - first]
+        if rest and (source + 1) % pieces == 0:
+            first, count = (source + 1 - pieces) * keep, pieces * keep
+            at = pl.multiple_of((1 - part) * rows + first, count)
+            copies.append(
+                pltpu.make_async_copy(
+                    result.at[pl.ds(first, count)],
+                    out_ref.at[pl.ds(at, count)],
+                    written.at[1 + source // pieces],
+                )
+            )
+            copies[-1].start()
     if rest:
-        second_copy = pltpu.make_async_copy(
-            result,
-            out_ref.at[pl.ds(pl.multiple_of((1 - part) * rows, rows), rows)],
-            written.at[1],
-        )
-        second_copy.start()
-        first_copy.wait()
-        second_copy.wait()
+        for copy in copies:
+            copy.wait()
 
 
 def encode(segments, spectra, valid, sources):
@@ -245,6 +255,7 @@
     keep = channels // segments
     slab = jax.ShapeDtypeStruct((sources.size, width // 2), jnp.bfloat16)
     block = jax.ShapeDtypeStruct((keep, width), jnp.bfloat16)
+    padded = pltpu.VMEM((sources.size, width // 2 + 2 * LANES), jnp.bfloat16)
     pinned = [pltpu.with_memory_space_constraint(x, pltpu.HBM) for x in (spectra, valid, sources)]
     return pl.pallas_call(
         functools.partial(encode_kernel, segments),
@@ -256,6 +267,8 @@
             pltpu.VMEM((channels, width), jnp.bfloat16),
             pltpu.VMEM((1, channels), jnp.int32),
             pltpu.SMEM(sources.shape, jnp.int32),
+            padded,
+            padded,
             pltpu.SemaphoreType.DMA((3,)),
         ],
         compiler_params=pltpu.CompilerParams(vmem_limit_bytes=12 * MEBI),
@@ -286,13 +299,12 @@
     half, nbins = slabs.shape[0] // (2 * segments), slabs.shape[1]
     keep = receivers[0].shape[0] // segments
     count, rows, lags = segments * half, half * keep, 2 * LAG + 1
-    padded = pltpu.VMEM((count, nbins + 2 * LANES), jnp.bfloat16)
     part = pltpu.VMEM((count, nbins), jnp.float32)
     cross = pltpu.VMEM((rows, 2 * BLOCK), jnp.bfloat16 if keep % 16 == 0 else jnp.float32)
     total = pltpu.VMEM((rows, BLOCK), jnp.float32)
-    scratch = [part, part, padded, padded, cross, cross, total, total]
+    scratch = [part, part, cross, cross, total, total]
     if rest:
-        scratch += [pltpu.VMEM((rows, lags), jnp.float32), pltpu.SemaphoreType.DMA((2,))]
+        scratch += [pltpu.VMEM((rows, lags), jnp.float32), pltpu.SemaphoreType.DMA((1 + half,))]
     return pl.pallas_call(
         functools.partial(stack_kernel, segments),
         out_shape=jax.ShapeDtypeStruct((2 * rows if rest else rows, lags), jnp.float32),
@@ -318,16 +330,18 @@
     own, other, *receivers = encode(
         tm_size, spectra[:, 0, :], valid.reshape(1, channels), sources
     )
-    own = own + swapped(other, "rcv", rcv_size, 1)
-    receivers = receivers[:1] + [
-        swapped(receivers[step], "tm", tm_size, step) for step in range(1, tm_size)
-    ]
-    step = 2
+    moving, step, place = other, 1, tm_size - 1
     while step < rcv_size:
-        own = own + swapped(own, "rcv", rcv_size, step)
-        step *= 2
-    own, receivers = lax.optimization_barrier((own, receivers))
-    own = [own] + [swapped(own, "tm", tm_size, step) for step in range(1, tm_size)]
+        now = 1 if 2 * step < rcv_size else place
+        for place in range(place, place - now, -1):
+            receivers[place] = swapped(receivers[place], "tm", tm_size, place)
+        place -= 1
+        own = own + swapped(moving, "rcv", rcv_size, step)
+        own, receivers[1 : place + 1] = lax.optimization_barrier((own, receivers[1 : place + 1]))
+        moving, step = own, 2 * step
+    own = [own] + [swapped(own, "tm", tm_size, step) for step in range(tm_size - 1, 1, -1)] + [own]
+    own[-1], receivers = lax.optimization_barrier((own[-1], receivers))
+    own = own[:1] + [swapped(own[-1], "tm", tm_size, 1)] + own[-2:0:-1]
     whitened = whiten_blocks(receivers)
     own, whitened = lax.optimization_barrier((own, whitened))
     own = jnp.concatenate(own, axis=0)

time: 32.6 us -> 30.5 us (0.936)
  waiting for transfers between devices: 8.29 us -> 5.72 us
  starting transfers between devices: 13.4 us -> 14.2 us
  Pallas kernels: 10.6 us -> 10.2 us
    ppermute x10, waiting for transfers between devices: 8.29 us -> 5.72 us  [swapped(): return lax.ppermute(value, axis, [(i, i ^ step) for i in range(size)])]
    ppermute x10, starting transfers between devices: 13.4 us -> 14.2 us  [swapped(): return lax.ppermute(value, axis, [(i, i ^ step) for i in range(size)])]
    pallas_call x2, Pallas kernels: 7.77 us -> 7.24 us  [stack_half(): pl.pallas_call(functools.partial(stack_kernel, segments), out_shape=jax.S...]
  transfers between devices with their start and end apart: 10 -> 10, of which waited for: 6 -> 5; matrix products, arithmetic and copies ran while one was open for 0% -> 0% of each run, Pallas kernels for 14% -> 14%
where the time goes in v4:
time: 30.5 us; the launch traced here: 30.3 us
  starting transfers between devices  14.2 us (47%)
  Pallas kernels  10.2 us (33%)
  waiting for transfers between devices  5.72 us (19%)
    ppermute x10, starting transfers between devices, swapped(): return lax.ppermute(value, axis, [(i, i ^ step) for i in range(size)])  14.2 us
    pallas_call x2, Pallas kernels, stack_half(): pl.pallas_call(functools.partial(stack_kernel, segments), out_shape=jax.S...  7.24 us
    ppermute x10, waiting for transfers between devices, swapped(): return lax.ppermute(value, axis, [(i, i ^ step) for i in range(size)])  5.72 us
    pallas_call x1, Pallas kernels, encode(): pl.pallas_call(functools.partial(encode_kernel, segments), out_shape=(sla...  2.02 us
    pallas_call x1, Pallas kernels, whiten_blocks(): pl.pallas_call(functools.partial(whiten_kernel, segments), out_shape=(par...  0.96 us
  transfers between devices with their start and end apart: 10, of which 5 were waited for; matrix products, arithmetic and copies ran while one was open for 0% of the time, Pallas kernels for 14%

profile of v4, /device:TPU:0, one launch (start us, length us, event | category | flops | bytes accessed | tf_op | source)
XLA Modules:
  0.0 30.3 jit_solution(3948770027331466852)
XLA Ops:
  0.0 0.0 copy-start
  0.0 2.0 %encode_and_pick.1 = (bf16[16,1536]{1,0:T(8,128)(2,1)S(1)}, bf16[16,1536]{1,0:T(8,128)(2,1)S(1)}, bf16[32,3072]{1,0:T(8,128)(2,1)S(1)}, bf16[32,3072]{1,0:T(8,12...) custom-call(bf16[128,3072]{1,0:T(8,128)(2,1)} %bitcast.3, s32[1,128]{1,0:T(1,128)} %bitcast.4, ...), custom_call_target="tpu_custom_call" | custom-call | tf_op jit(solution)/shard_map/encode_and_pick/pallas_call | solution.py:260
  2.0 0.5 %collective-permute-start = (bf16[16,1536]{1,0:T(8,128)(2,1)S(1)}, bf16[16,1536]{1,0:T(8,128)(2,1)S(1)}, u32[]{:S(2)}, u32[]{:S(2)}) collective-permute-start(bf16[16,1536]{1,0:T(8,128)(2,1)S(1)} %get-tuple-element.32), channel_id=1, source_target_pairs={{0,4},{4,0},{8,12},{12,8},{16,20},{20,16},{24,28},{28,24},{1,5},{5... | collective-permute-start | bytes 147464 | tf_op jit(solution)/shard_map/ppermute | solution.py:323
  2.5 0.9 %collective-permute-done = bf16[16,1536]{1,0:T(8,128)(2,1)S(1)} collective-permute-done((bf16[16,1536]{1,0:T(8,128)(2,1)S(1)}, bf16[16,1536]{1,0:T(8,128)(2,1)S(1)}, u32[]{:S(2)}, u32[]{:S(2)}) %collective-permute-start) | collective-permute-done | bytes 49184 | tf_op jit(solution)/shard_map/ppermute | solution.py:323
  3.4 3.0 %collective-permute-start.1 = (bf16[16,1536]{1,0:T(8,128)(2,1)S(1)}, bf16[16,1536]{1,0:T(8,128)(2,1)S(1)}, u32[]{:S(2)}, u32[]{:S(2)}) collective-permute-start(bf16[16,1536]{1,0:T(8,128)(2,1)S(1)} %add.9), channel_id=1, source_target_pairs={{0,8},{4,12},{8,0},{12,4},{16,24},{20,28},{24,16},{28,20},{1,9},{5... | collective-permute-start | bytes 147464 | tf_op jit(solution)/shard_map/ppermute | solution.py:323
  6.4 2.4 %collective-permute-start.5 = (bf16[32,3072]{1,0:T(8,128)(2,1)S(1)}, bf16[32,3072]{1,0:T(8,128)(2,1)S(1)}, u32[]{:S(2)}, u32[]{:S(2)}) collective-permute-start(bf16[32,3072]{1,0:T(8,128)(2,1)S(1)} %get-tuple-element.41), channel_id=1, source_target_pairs={{0,3},{1,2},{2,1},{3,0},{4,7},{5,6},{6,5},{7,4},{8,11},{9,10},{10,... | collective-permute-start | bytes 589832 | tf_op jit(solution)/shard_map/ppermute | solution.py:323
  8.9 0.5 %collective-permute-start.4 = (bf16[32,3072]{1,0:T(8,128)(2,1)S(1)}, bf16[32,3072]{1,0:T(8,128)(2,1)S(1)}, u32[]{:S(2)}, u32[]{:S(2)}) collective-permute-start(bf16[32,3072]{1,0:T(8,128)(2,1)S(1)} %get-tuple-element.40), channel_id=1, source_target_pairs={{0,2},{1,3},{2,0},{3,1},{4,6},{5,7},{6,4},{7,5},{8,10},{9,11},{10,... | collective-permute-start | bytes 589832 | tf_op jit(solution)/shard_map/ppermute | solution.py:323
  9.4 0.0 collective-permute-done.1
  9.4 1.1 %collective-permute-start.3 = (bf16[32,3072]{1,0:T(8,128)(2,1)S(1)}, bf16[32,3072]{1,0:T(8,128)(2,1)S(1)}, u32[]{:S(2)}, u32[]{:S(2)}) collective-permute-start(bf16[32,3072]{1,0:T(8,128)(2,1)S(1)} %get-tuple-element.39), channel_id=1, source_target_pairs={{0,1},{1,0},{2,3},{3,2},{4,5},{5,4},{6,7},{7,6},{8,9},{9,8},{10,11... | collective-permute-start | bytes 589832 | tf_op jit(solution)/shard_map/ppermute | solution.py:323
  10.5 2.6 %collective-permute-start.2 = (bf16[16,1536]{1,0:T(8,128)(2,1)S(1)}, bf16[16,1536]{1,0:T(8,128)(2,1)S(1)}, u32[]{:S(2)}, u32[]{:S(2)}) collective-permute-start(bf16[16,1536]{1,0:T(8,128)(2,1)S(1)} %add.10), channel_id=1, source_target_pairs={{0,16},{4,20},{8,24},{12,28},{16,0},{20,4},{24,8},{28,12},{1,17},{... | collective-permute-start | bytes 147464 | tf_op jit(solution)/shard_map/ppermute | solution.py:323
  13.1 2.4 %collective-permute-done.2 = bf16[16,1536]{1,0:T(8,128)(2,1)S(1)} collective-permute-done((bf16[16,1536]{1,0:T(8,128)(2,1)S(1)}, bf16[16,1536]{1,0:T(8,128)(2,1)S(1)}, u32[]{:S(2)}, u32[]{:S(2)}) %collective-permute-start.2) | collective-permute-done | bytes 49184 | tf_op jit(solution)/shard_map/ppermute | solution.py:323
  15.5 2.0 %collective-permute-start.8 = (bf16[16,1536]{1,0:T(8,128)(2,1)S(1)}, bf16[16,1536]{1,0:T(8,128)(2,1)S(1)}, u32[]{:S(2)}, u32[]{:S(2)}) collective-permute-start(bf16[16,1536]{1,0:T(8,128)(2,1)S(1)} %add.11), channel_id=1, source_target_pairs={{0,3},{1,2},{2,1},{3,0},{4,7},{5,6},{6,5},{7,4},{8,11},{9,10},{10,... | collective-permute-start | bytes 147464 | tf_op jit(solution)/shard_map/ppermute | solution.py:323
  17.5 0.5 %collective-permute-start.7 = (bf16[16,1536]{1,0:T(8,128)(2,1)S(1)}, bf16[16,1536]{1,0:T(8,128)(2,1)S(1)}, u32[]{:S(2)}, u32[]{:S(2)}) collective-permute-start(bf16[16,1536]{1,0:T(8,128)(2,1)S(1)} %add.11), channel_id=1, source_target_pairs={{0,2},{1,3},{2,0},{3,1},{4,6},{5,7},{6,4},{7,5},{8,10},{9,11},{10,... | collective-permute-start | bytes 147464 | tf_op jit(solution)/shard_map/ppermute | solution.py:323
  18.0 0.0 collective-permute-done.5.refs_3_
  18.0 0.8 %collective-permute-done.4.refs_2_ = bf16[32,3072]{1,0:T(8,128)(2,1)S(1)} collective-permute-done((bf16[32,3072]{1,0:T(8,128)(2,1)S(1)}, bf16[32,3072]{1,0:T(8,128)(2,1)S(1)}, u32[]{:S(2)}, u32[]{:S(2)}) %collective-permute-start.4) | collective-permute-done | bytes 196640 | tf_op jit(solution)/shard_map/ppermute | solution.py:323
  18.9 0.0 collective-permute-done.3.refs_1_
  18.9 1.5 %collective-permute-start.6 = (bf16[16,1536]{1,0:T(8,128)(2,1)S(1)}, bf16[16,1536]{1,0:T(8,128)(2,1)S(1)}, u32[]{:S(2)}, u32[]{:S(2)}) collective-permute-start(bf16[16,1536]{1,0:T(8,128)(2,1)S(1)} %add.11), channel_id=1, source_target_pairs={{0,1},{1,0},{2,3},{3,2},{4,5},{5,4},{6,7},{7,6},{8,9},{9,8},{10,11... | collective-permute-start | bytes 147464 | tf_op jit(solution)/shard_map/ppermute | solution.py:323
  20.4 1.0 %whiten_receivers.1 = (f32[128,1536]{1,0:T(8,128)S(1)}, f32[128,1536]{1,0:T(8,128)S(1)}, f32[128,128]{1,0:T(8,128)S(1)}) custom-call(bf16[32,3072]{1,0:T(8,128)(2,1)S(1)} %get-tuple-element.43.refs_0_, bf16[32,3072]{1,0:T(8,128)(2,1)S(1)} %collective-permute-done.3.refs_1_, bf16[32,3072]{1,0:T(8,128)(2,1)S(1)} %collective-permute-done.4.refs_2_, ...), custom_call_target="tpu_custom_call" | custom-call | flops 402653184 | bytes 1572864 | tf_op jit(solution)/shard_map/whiten_receivers/pallas_call | solution.py:284
  21.3 0.0 collective-permute-done.8
  21.3 0.3 collective-permute-done.7
  21.6 1.3 %collective-permute-done.6 = bf16[16,1536]{1,0:T(8,128)(2,1)S(1)} collective-permute-done((bf16[16,1536]{1,0:T(8,128)(2,1)S(1)}, bf16[16,1536]{1,0:T(8,128)(2,1)S(1)}, u32[]{:S(2)}, u32[]{:S(2)}) %collective-permute-start.6) | collective-permute-done | bytes 49184 | tf_op jit(solution)/shard_map/ppermute | solution.py:323
  23.0 0.1 collective-permute-start.9
  23.1 0.0 copy-done
  23.1 3.3 %stack_own_half.1.refs_0_ = f32[256,301]{1,0:T(8,128)S(1)} custom-call(bf16[64,1536]{1,0:T(8,128)(2,1)S(1)} %constant_dynamic-update-slice_fusion.slabs_ref, f32[128,1536]{1,0:T(8,128)S(1)} %get-tuple-element.54.rcv_re, f32[128,1536]{1,0:T(8,128)S(1)} %get-tuple-element.55.rcv_im, f32[128,128]{1,0:T(8,128)S(1)} %get-tuple-element.56.rcv_valid, ...), custom_call_target="tpu_custom_call" | custom-call | flops 471859200 | bytes 3145728 | tf_op jit(solution)/shard_map/stack_own_half/pallas_call | solution.py:308
  26.3 0.0 collective-permute-done.9.slabs_ref
  26.4 4.0 %stack_other_half.1 = f32[512,301]{1,0:T(8,128)} custom-call(bf16[64,1536]{1,0:T(8,128)(2,1)S(1)} %collective-permute-done.9.slabs_ref, f32[128,1536]{1,0:T(8,128)S(1)} %get-tuple-element.54.rcv_re, f32[128,1536]{1,0:T(8,128)S(1)} %get-tuple-element.55.rcv_im, f32[128,128]{1,0:T(8,128)S(1)} %get-tuple-element.56.rcv_valid, bf16[3072,256]{1,0:T(8,128)(2,1)S(1)} %copy-done, ...), custom_call_target="tpu_custom_call" | custom-call | flops 471859200 | bytes 3145728 | tf_op jit(solution)/shard_map/stack_other_half/pallas_call | solution.py:308
  (7 shorter events, 0.1 us)
Async XLA Ops:
  0.0 23.1 %copy-start = (bf16[3072,256]{1,0:T(8,128)(2,1)S(1)}, bf16[3072,256]{1,0:T(8,128)(2,1)}, u32[]{:S(2)}) copy-start(bf16[3072,256]{1,0:T(8,128)(2,1)} %constant.2.clone.table_ref) | copy-start | bytes 4718596
  2.0 1.4 %collective-permute-start = (bf16[16,1536]{1,0:T(8,128)(2,1)S(1)}, bf16[16,1536]{1,0:T(8,128)(2,1)S(1)}, u32[]{:S(2)}, u32[]{:S(2)}) collective-permute-start(bf16[16,1536]{1,0:T(8,128)(2,1)S(1)} %get-tuple-element.32), channel_id=1, source_target_pairs={{0,4},{4,0},{8,12},{12,8},{16,20},{20,16},{24,28},{28,24},{1,5},{5... | collective-permute-start | bytes 147464 | tf_op jit(solution)/shard_map/ppermute | solution.py:323
  3.4 5.9 %collective-permute-start.1 = (bf16[16,1536]{1,0:T(8,128)(2,1)S(1)}, bf16[16,1536]{1,0:T(8,128)(2,1)S(1)}, u32[]{:S(2)}, u32[]{:S(2)}) collective-permute-start(bf16[16,1536]{1,0:T(8,128)(2,1)S(1)} %add.9), channel_id=1, source_target_pairs={{0,8},{4,12},{8,0},{12,4},{16,24},{20,28},{24,16},{28,20},{1,9},{5... | collective-permute-start | bytes 147464 | tf_op jit(solution)/shard_map/ppermute | solution.py:323
  6.4 11.6 %collective-permute-start.5 = (bf16[32,3072]{1,0:T(8,128)(2,1)S(1)}, bf16[32,3072]{1,0:T(8,128)(2,1)S(1)}, u32[]{:S(2)}, u32[]{:S(2)}) collective-permute-start(bf16[32,3072]{1,0:T(8,128)(2,1)S(1)} %get-tuple-element.41), channel_id=1, source_target_pairs={{0,3},{1,2},{2,1},{3,0},{4,7},{5,6},{6,5},{7,4},{8,11},{9,10},{10,... | collective-permute-start | bytes 589832 | tf_op jit(solution)/shard_map/ppermute | solution.py:323
  8.9 10.0 %collective-permute-start.4 = (bf16[32,3072]{1,0:T(8,128)(2,1)S(1)}, bf16[32,3072]{1,0:T(8,128)(2,1)S(1)}, u32[]{:S(2)}, u32[]{:S(2)}) collective-permute-start(bf16[32,3072]{1,0:T(8,128)(2,1)S(1)} %get-tuple-element.40), channel_id=1, source_target_pairs={{0,2},{1,3},{2,0},{3,1},{4,6},{5,7},{6,4},{7,5},{8,10},{9,11},{10,... | collective-permute-start | bytes 589832 | tf_op jit(solution)/shard_map/ppermute | solution.py:323
  9.4 9.4 %collective-permute-start.3 = (bf16[32,3072]{1,0:T(8,128)(2,1)S(1)}, bf16[32,3072]{1,0:T(8,128)(2,1)S(1)}, u32[]{:S(2)}, u32[]{:S(2)}) collective-permute-start(bf16[32,3072]{1,0:T(8,128)(2,1)S(1)} %get-tuple-element.39), channel_id=1, source_target_pairs={{0,1},{1,0},{2,3},{3,2},{4,5},{5,4},{6,7},{7,6},{8,9},{9,8},{10,11... | collective-permute-start | bytes 589832 | tf_op jit(solution)/shard_map/ppermute | solution.py:323
  10.5 5.0 %collective-permute-start.2 = (bf16[16,1536]{1,0:T(8,128)(2,1)S(1)}, bf16[16,1536]{1,0:T(8,128)(2,1)S(1)}, u32[]{:S(2)}, u32[]{:S(2)}) collective-permute-start(bf16[16,1536]{1,0:T(8,128)(2,1)S(1)} %add.10), channel_id=1, source_target_pairs={{0,16},{4,20},{8,24},{12,28},{16,0},{20,4},{24,8},{28,12},{1,17},{... | collective-permute-start | bytes 147464 | tf_op jit(solution)/shard_map/ppermute | solution.py:323
  15.5 5.8 %collective-permute-start.8 = (bf16[16,1536]{1,0:T(8,128)(2,1)S(1)}, bf16[16,1536]{1,0:T(8,128)(2,1)S(1)}, u32[]{:S(2)}, u32[]{:S(2)}) collective-permute-start(bf16[16,1536]{1,0:T(8,128)(2,1)S(1)} %add.11), channel_id=1, source_target_pairs={{0,3},{1,2},{2,1},{3,0},{4,7},{5,6},{6,5},{7,4},{8,11},{9,10},{10,... | collective-permute-start | bytes 147464 | tf_op jit(solution)/shard_map/ppermute | solution.py:323
  17.5 4.1 %collective-permute-start.7 = (bf16[16,1536]{1,0:T(8,128)(2,1)S(1)}, bf16[16,1536]{1,0:T(8,128)(2,1)S(1)}, u32[]{:S(2)}, u32[]{:S(2)}) collective-permute-start(bf16[16,1536]{1,0:T(8,128)(2,1)S(1)} %add.11), channel_id=1, source_target_pairs={{0,2},{1,3},{2,0},{3,1},{4,6},{5,7},{6,4},{7,5},{8,10},{9,11},{10,... | collective-permute-start | bytes 147464 | tf_op jit(solution)/shard_map/ppermute | solution.py:323
  18.9 4.1 %collective-permute-start.6 = (bf16[16,1536]{1,0:T(8,128)(2,1)S(1)}, bf16[16,1536]{1,0:T(8,128)(2,1)S(1)}, u32[]{:S(2)}, u32[]{:S(2)}) collective-permute-start(bf16[16,1536]{1,0:T(8,128)(2,1)S(1)} %add.11), channel_id=1, source_target_pairs={{0,1},{1,0},{2,3},{3,2},{4,5},{5,4},{6,7},{7,6},{8,9},{9,8},{10,11... | collective-permute-start | bytes 147464 | tf_op jit(solution)/shard_map/ppermute | solution.py:323
  23.0 3.4 %collective-permute-start.9 = (bf16[64,1536]{1,0:T(8,128)(2,1)S(1)}, bf16[64,1536]{1,0:T(8,128)(2,1)S(1)}, u32[]{:S(2)}, u32[]{:S(2)}) collective-permute-start(bf16[64,1536]{1,0:T(8,128)(2,1)S(1)} %constant_dynamic-update-slice_fusion.slabs_ref), channel_id=1, source_target_pairs={{0,4},{4,0},{8,12},{12,8},{16,20},{20,16},{24,28},{28,24},{1,5},{5... | collective-permute-start | bytes 589832 | tf_op jit(solution)/shard_map/ppermute | solution.py:323

commit v5 on v4

--- a/solution.py
+++ b/solution.py
@@ -330,18 +330,17 @@
     own, other, *receivers = encode(
         tm_size, spectra[:, 0, :], valid.reshape(1, channels), sources
     )
-    moving, step, place = other, 1, tm_size - 1
+    receivers[1:] = [
+        swapped(receivers[place], "tm", tm_size, place) for place in range(1, tm_size)
+    ]
+    own = own + swapped(other, "rcv", rcv_size, 1)
+    step = 2
     while step < rcv_size:
-        now = 1 if 2 * step < rcv_size else place
-        for place in range(place, place - now, -1):
-            receivers[place] = swapped(receivers[place], "tm", tm_size, place)
-        place -= 1
-        own = own + swapped(moving, "rcv", rcv_size, step)
-        own, receivers[1 : place + 1] = lax.optimization_barrier((own, receivers[1 : place + 1]))
-        moving, step = own, 2 * step
-    own = [own] + [swapped(own, "tm", tm_size, step) for step in range(tm_size - 1, 1, -1)] + [own]
-    own[-1], receivers = lax.optimization_barrier((own[-1], receivers))
-    own = own[:1] + [swapped(own[-1], "tm", tm_size, 1)] + own[-2:0:-1]
+        wide = min(4, rcv_size // step)
+        others = [swapped(own, "rcv", rcv_size, place * step) for place in range(wide - 1, 0, -1)]
+        own = functools.reduce(jnp.add, others, own)
+        step *= wide
+    own = [own] + [swapped(own, "tm", tm_size, place) for place in range(1, tm_size)]
     whitened = whiten_blocks(receivers)
     own, whitened = lax.optimization_barrier((own, whitened))
     own = jnp.concatenate(own, axis=0)

time: 30.5 us -> 30.5 us (level)
  waiting for transfers between devices: 5.72 us -> 6.69 us
  starting transfers between devices: 14.2 us -> 13.3 us
    ppermute x10 -> x11, waiting for transfers between devices: 5.72 us -> 6.69 us  [swapped(): return lax.ppermute(value, axis, [(i, i ^ step) for i in range(size)])]
    ppermute x10 -> x11, starting transfers between devices: 14.2 us -> 13.3 us  [swapped(): return lax.ppermute(value, axis, [(i, i ^ step) for i in range(size)])]
  transfers between devices with their start and end apart: 10 -> 11, of which waited for: 5 -> 5; matrix products, arithmetic and copies ran while one was open for 0% -> 0% of each run, Pallas kernels for 14% -> 14%
where the time goes in v5:
time: 30.5 us; the launch traced here: 30.4 us
  starting transfers between devices  13.3 us (44%)
  Pallas kernels  10.2 us (33%)
  waiting for transfers between devices  6.69 us (22%)
    ppermute x11, starting transfers between devices, swapped(): return lax.ppermute(value, axis, [(i, i ^ step) for i in range(size)])  13.3 us
    pallas_call x2, Pallas kernels, stack_half(): pl.pallas_call(functools.partial(stack_kernel, segments), out_shape=jax.S...  7.24 us
    ppermute x11, waiting for transfers between devices, swapped(): return lax.ppermute(value, axis, [(i, i ^ step) for i in range(size)])  6.69 us
    pallas_call x1, Pallas kernels, encode(): pl.pallas_call(functools.partial(encode_kernel, segments), out_shape=(sla...  2.02 us
    pallas_call x1, Pallas kernels, whiten_blocks(): pl.pallas_call(functools.partial(whiten_kernel, segments), out_shape=(par...  0.96 us
  transfers between devices with their start and end apart: 11, of which 5 were waited for; matrix products, arithmetic and copies ran while one was open for 0% of the time, Pallas kernels for 14%

profile of v5, /device:TPU:0, one launch (start us, length us, event | category | flops | bytes accessed | tf_op | source)
XLA Modules:
  0.0 30.4 jit_solution(8606076799797454826)
XLA Ops:
  0.0 0.0 copy-start
  0.0 2.0 %encode_and_pick.1 = (bf16[16,1536]{1,0:T(8,128)(2,1)S(1)}, bf16[16,1536]{1,0:T(8,128)(2,1)S(1)}, bf16[32,3072]{1,0:T(8,128)(2,1)S(1)}, bf16[32,3072]{1,0:T(8,12...) custom-call(bf16[128,3072]{1,0:T(8,128)(2,1)} %bitcast.3, s32[1,128]{1,0:T(1,128)} %bitcast.4, ...), custom_call_target="tpu_custom_call" | custom-call | tf_op jit(solution)/shard_map/encode_and_pick/pallas_call | solution.py:260
  2.0 0.5 %collective-permute-start = (bf16[16,1536]{1,0:T(8,128)(2,1)S(1)}, bf16[16,1536]{1,0:T(8,128)(2,1)S(1)}, u32[]{:S(2)}, u32[]{:S(2)}) collective-permute-start(bf16[16,1536]{1,0:T(8,128)(2,1)S(1)} %get-tuple-element.22), channel_id=1, source_target_pairs={{0,4},{4,0},{8,12},{12,8},{16,20},{20,16},{24,28},{28,24},{1,5},{5... | collective-permute-start | bytes 147464 | tf_op jit(solution)/shard_map/ppermute | solution.py:323
  2.5 0.9 %collective-permute-done = bf16[16,1536]{1,0:T(8,128)(2,1)S(1)} collective-permute-done((bf16[16,1536]{1,0:T(8,128)(2,1)S(1)}, bf16[16,1536]{1,0:T(8,128)(2,1)S(1)}, u32[]{:S(2)}, u32[]{:S(2)}) %collective-permute-start) | collective-permute-done | bytes 49184 | tf_op jit(solution)/shard_map/ppermute | solution.py:323
  3.4 3.0 %collective-permute-start.3 = (bf16[16,1536]{1,0:T(8,128)(2,1)S(1)}, bf16[16,1536]{1,0:T(8,128)(2,1)S(1)}, u32[]{:S(2)}, u32[]{:S(2)}) collective-permute-start(bf16[16,1536]{1,0:T(8,128)(2,1)S(1)} %add.12), channel_id=1, source_target_pairs={{0,8},{4,12},{8,0},{12,4},{16,24},{20,28},{24,16},{28,20},{1,9},{5... | collective-permute-start | bytes 147464 | tf_op jit(solution)/shard_map/ppermute | solution.py:323
  6.4 2.6 %collective-permute-start.2 = (bf16[16,1536]{1,0:T(8,128)(2,1)S(1)}, bf16[16,1536]{1,0:T(8,128)(2,1)S(1)}, u32[]{:S(2)}, u32[]{:S(2)}) collective-permute-start(bf16[16,1536]{1,0:T(8,128)(2,1)S(1)} %add.12), channel_id=1, source_target_pairs={{0,16},{4,20},{8,24},{12,28},{16,0},{20,4},{24,8},{28,12},{1,17},{... | collective-permute-start | bytes 147464 | tf_op jit(solution)/shard_map/ppermute | solution.py:323
  9.0 0.0 collective-permute-start.1
  9.0 1.7 %collective-permute-start.7 = (bf16[32,3072]{1,0:T(8,128)(2,1)S(1)}, bf16[32,3072]{1,0:T(8,128)(2,1)S(1)}, u32[]{:S(2)}, u32[]{:S(2)}) collective-permute-start(bf16[32,3072]{1,0:T(8,128)(2,1)S(1)} %get-tuple-element.24), channel_id=1, source_target_pairs={{0,1},{1,0},{2,3},{3,2},{4,5},{5,4},{6,7},{7,6},{8,9},{9,8},{10,11... | collective-permute-start | bytes 589832 | tf_op jit(solution)/shard_map/ppermute | solution.py:323
  10.7 1.5 %collective-permute-start.8 = (bf16[32,3072]{1,0:T(8,128)(2,1)S(1)}, bf16[32,3072]{1,0:T(8,128)(2,1)S(1)}, u32[]{:S(2)}, u32[]{:S(2)}) collective-permute-start(bf16[32,3072]{1,0:T(8,128)(2,1)S(1)} %get-tuple-element.25), channel_id=1, source_target_pairs={{0,2},{1,3},{2,0},{3,1},{4,6},{5,7},{6,4},{7,5},{8,10},{9,11},{10,... | collective-permute-start | bytes 589832 | tf_op jit(solution)/shard_map/ppermute | solution.py:323
  12.3 0.0 collective-permute-done.3
  12.3 0.3 collective-permute-start.9
  12.5 0.0 collective-permute-done.2
  12.5 2.4 %collective-permute-done.1 = bf16[16,1536]{1,0:T(8,128)(2,1)S(1)} collective-permute-done((bf16[16,1536]{1,0:T(8,128)(2,1)S(1)}, bf16[16,1536]{1,0:T(8,128)(2,1)S(1)}, u32[]{:S(2)}, u32[]{:S(2)}) %collective-permute-start.1) | collective-permute-done | bytes 49184 | tf_op jit(solution)/shard_map/ppermute | solution.py:323
  14.9 2.5 %collective-permute-start.6 = (bf16[16,1536]{1,0:T(8,128)(2,1)S(1)}, bf16[16,1536]{1,0:T(8,128)(2,1)S(1)}, u32[]{:S(2)}, u32[]{:S(2)}) collective-permute-start(bf16[16,1536]{1,0:T(8,128)(2,1)S(1)} %add_add_fusion), channel_id=1, source_target_pairs={{0,3},{1,2},{2,1},{3,0},{4,7},{5,6},{6,5},{7,4},{8,11},{9,10},{10,... | collective-permute-start | bytes 147464 | tf_op jit(solution)/shard_map/ppermute | solution.py:323
  17.4 0.5 %collective-permute-start.5 = (bf16[16,1536]{1,0:T(8,128)(2,1)S(1)}, bf16[16,1536]{1,0:T(8,128)(2,1)S(1)}, u32[]{:S(2)}, u32[]{:S(2)}) collective-permute-start(bf16[16,1536]{1,0:T(8,128)(2,1)S(1)} %add_add_fusion), channel_id=1, source_target_pairs={{0,2},{1,3},{2,0},{3,1},{4,6},{5,7},{6,4},{7,5},{8,10},{9,11},{10,... | collective-permute-start | bytes 147464 | tf_op jit(solution)/shard_map/ppermute | solution.py:323
  17.9 0.0 collective-permute-done.7.refs_1_
  17.9 0.6 %collective-permute-start.4 = (bf16[16,1536]{1,0:T(8,128)(2,1)S(1)}, bf16[16,1536]{1,0:T(8,128)(2,1)S(1)}, u32[]{:S(2)}, u32[]{:S(2)}) collective-permute-start(bf16[16,1536]{1,0:T(8,128)(2,1)S(1)} %add_add_fusion), channel_id=1, source_target_pairs={{0,1},{1,0},{2,3},{3,2},{4,5},{5,4},{6,7},{7,6},{8,9},{9,8},{10,11... | collective-permute-start | bytes 147464 | tf_op jit(solution)/shard_map/ppermute | solution.py:323
  18.6 2.9 %collective-permute-done.8.refs_2_ = bf16[32,3072]{1,0:T(8,128)(2,1)S(1)} collective-permute-done((bf16[32,3072]{1,0:T(8,128)(2,1)S(1)}, bf16[32,3072]{1,0:T(8,128)(2,1)S(1)}, u32[]{:S(2)}, u32[]{:S(2)}) %collective-permute-start.8) | collective-permute-done | bytes 196640 | tf_op jit(solution)/shard_map/ppermute | solution.py:323
  21.5 0.3 collective-permute-done.9.refs_3_
  21.8 1.0 %whiten_receivers.1 = (f32[128,1536]{1,0:T(8,128)S(1)}, f32[128,1536]{1,0:T(8,128)S(1)}, f32[128,128]{1,0:T(8,128)S(1)}) custom-call(bf16[32,3072]{1,0:T(8,128)(2,1)S(1)} %get-tuple-element.23.refs_0_, bf16[32,3072]{1,0:T(8,128)(2,1)S(1)} %collective-permute-done.7.refs_1_, bf16[32,3072]{1,0:T(8,128)(2,1)S(1)} %collective-permute-done.8.refs_2_, ...), custom_call_target="tpu_custom_call" | custom-call | flops 402653184 | bytes 1572864 | tf_op jit(solution)/shard_map/whiten_receivers/pallas_call | solution.py:284
  22.7 0.0 collective-permute-done.6
  22.7 0.2 collective-permute-done.5
  23.0 0.0 collective-permute-done.4
  23.0 0.1 collective-permute-start.10
  23.1 0.0 copy-done
  23.1 3.3 %stack_own_half.1.refs_0_ = f32[256,301]{1,0:T(8,128)S(1)} custom-call(bf16[64,1536]{1,0:T(8,128)(2,1)S(1)} %constant_dynamic-update-slice_fusion.slabs_ref, f32[128,1536]{1,0:T(8,128)S(1)} %get-tuple-element.34.rcv_re, f32[128,1536]{1,0:T(8,128)S(1)} %get-tuple-element.35.rcv_im, f32[128,128]{1,0:T(8,128)S(1)} %get-tuple-element.36.rcv_valid, ...), custom_call_target="tpu_custom_call" | custom-call | flops 471859200 | bytes 3145728 | tf_op jit(solution)/shard_map/stack_own_half/pallas_call | solution.py:308
  26.4 0.0 collective-permute-done.10.slabs_ref
  26.4 4.0 %stack_other_half.1 = f32[512,301]{1,0:T(8,128)} custom-call(bf16[64,1536]{1,0:T(8,128)(2,1)S(1)} %collective-permute-done.10.slabs_ref, f32[128,1536]{1,0:T(8,128)S(1)} %get-tuple-element.34.rcv_re, f32[128,1536]{1,0:T(8,128)S(1)} %get-tuple-element.35.rcv_im, f32[128,128]{1,0:T(8,128)S(1)} %get-tuple-element.36.rcv_valid, bf16[3072,256]{1,0:T(8,128)(2,1)S(1)} %copy-done, ...), custom_call_target="tpu_custom_call" | custom-call | flops 471859200 | bytes 3145728 | tf_op jit(solution)/shard_map/stack_other_half/pallas_call | solution.py:308
  (6 shorter events, 0.1 us)
Async XLA Ops:
  0.0 23.1 %copy-start = (bf16[3072,256]{1,0:T(8,128)(2,1)S(1)}, bf16[3072,256]{1,0:T(8,128)(2,1)}, u32[]{:S(2)}) copy-start(bf16[3072,256]{1,0:T(8,128)(2,1)} %constant.2.clone.table_ref) | copy-start | bytes 4718596
  2.0 1.4 %collective-permute-start = (bf16[16,1536]{1,0:T(8,128)(2,1)S(1)}, bf16[16,1536]{1,0:T(8,128)(2,1)S(1)}, u32[]{:S(2)}, u32[]{:S(2)}) collective-permute-start(bf16[16,1536]{1,0:T(8,128)(2,1)S(1)} %get-tuple-element.22), channel_id=1, source_target_pairs={{0,4},{4,0},{8,12},{12,8},{16,20},{20,16},{24,28},{28,24},{1,5},{5... | collective-permute-start | bytes 147464 | tf_op jit(solution)/shard_map/ppermute | solution.py:323
  3.4 8.8 %collective-permute-start.3 = (bf16[16,1536]{1,0:T(8,128)(2,1)S(1)}, bf16[16,1536]{1,0:T(8,128)(2,1)S(1)}, u32[]{:S(2)}, u32[]{:S(2)}) collective-permute-start(bf16[16,1536]{1,0:T(8,128)(2,1)S(1)} %add.12), channel_id=1, source_target_pairs={{0,8},{4,12},{8,0},{12,4},{16,24},{20,28},{24,16},{28,20},{1,9},{5... | collective-permute-start | bytes 147464 | tf_op jit(solution)/shard_map/ppermute | solution.py:323
  6.4 6.1 %collective-permute-start.2 = (bf16[16,1536]{1,0:T(8,128)(2,1)S(1)}, bf16[16,1536]{1,0:T(8,128)(2,1)S(1)}, u32[]{:S(2)}, u32[]{:S(2)}) collective-permute-start(bf16[16,1536]{1,0:T(8,128)(2,1)S(1)} %add.12), channel_id=1, source_target_pairs={{0,16},{4,20},{8,24},{12,28},{16,0},{20,4},{24,8},{28,12},{1,17},{... | collective-permute-start | bytes 147464 | tf_op jit(solution)/shard_map/ppermute | solution.py:323
  9.0 5.9 %collective-permute-start.1 = (bf16[16,1536]{1,0:T(8,128)(2,1)S(1)}, bf16[16,1536]{1,0:T(8,128)(2,1)S(1)}, u32[]{:S(2)}, u32[]{:S(2)}) collective-permute-start(bf16[16,1536]{1,0:T(8,128)(2,1)S(1)} %add.12), channel_id=1, source_target_pairs={{0,24},{4,28},{8,16},{12,20},{16,8},{20,12},{24,0},{28,4},{1,25},{... | collective-permute-start | bytes 147464 | tf_op jit(solution)/shard_map/ppermute | solution.py:323
  9.0 8.9 %collective-permute-start.7 = (bf16[32,3072]{1,0:T(8,128)(2,1)S(1)}, bf16[32,3072]{1,0:T(8,128)(2,1)S(1)}, u32[]{:S(2)}, u32[]{:S(2)}) collective-permute-start(bf16[32,3072]{1,0:T(8,128)(2,1)S(1)} %get-tuple-element.24), channel_id=1, source_target_pairs={{0,1},{1,0},{2,3},{3,2},{4,5},{5,4},{6,7},{7,6},{8,9},{9,8},{10,11... | collective-permute-start | bytes 589832 | tf_op jit(solution)/shard_map/ppermute | solution.py:323
  10.7 10.7 %collective-permute-start.8 = (bf16[32,3072]{1,0:T(8,128)(2,1)S(1)}, bf16[32,3072]{1,0:T(8,128)(2,1)S(1)}, u32[]{:S(2)}, u32[]{:S(2)}) collective-permute-start(bf16[32,3072]{1,0:T(8,128)(2,1)S(1)} %get-tuple-element.25), channel_id=1, source_target_pairs={{0,2},{1,3},{2,0},{3,1},{4,6},{5,7},{6,4},{7,5},{8,10},{9,11},{10,... | collective-permute-start | bytes 589832 | tf_op jit(solution)/shard_map/ppermute | solution.py:323
  12.3 9.5 %collective-permute-start.9 = (bf16[32,3072]{1,0:T(8,128)(2,1)S(1)}, bf16[32,3072]{1,0:T(8,128)(2,1)S(1)}, u32[]{:S(2)}, u32[]{:S(2)}) collective-permute-start(bf16[32,3072]{1,0:T(8,128)(2,1)S(1)} %get-tuple-element.26), channel_id=1, source_target_pairs={{0,3},{1,2},{2,1},{3,0},{4,7},{5,6},{6,5},{7,4},{8,11},{9,10},{10,... | collective-permute-start | bytes 589832 | tf_op jit(solution)/shard_map/ppermute | solution.py:323
  14.9 7.8 %collective-permute-start.6 = (bf16[16,1536]{1,0:T(8,128)(2,1)S(1)}, bf16[16,1536]{1,0:T(8,128)(2,1)S(1)}, u32[]{:S(2)}, u32[]{:S(2)}) collective-permute-start(bf16[16,1536]{1,0:T(8,128)(2,1)S(1)} %add_add_fusion), channel_id=1, source_target_pairs={{0,3},{1,2},{2,1},{3,0},{4,7},{5,6},{6,5},{7,4},{8,11},{9,10},{10,... | collective-permute-start | bytes 147464 | tf_op jit(solution)/shard_map/ppermute | solution.py:323
  17.4 5.5 %collective-permute-start.5 = (bf16[16,1536]{1,0:T(8,128)(2,1)S(1)}, bf16[16,1536]{1,0:T(8,128)(2,1)S(1)}, u32[]{:S(2)}, u32[]{:S(2)}) collective-permute-start(bf16[16,1536]{1,0:T(8,128)(2,1)S(1)} %add_add_fusion), channel_id=1, source_target_pairs={{0,2},{1,3},{2,0},{3,1},{4,6},{5,7},{6,4},{7,5},{8,10},{9,11},{10,... | collective-permute-start | bytes 147464 | tf_op jit(solution)/shard_map/ppermute | solution.py:323
  17.9 5.0 %collective-permute-start.4 = (bf16[16,1536]{1,0:T(8,128)(2,1)S(1)}, bf16[16,1536]{1,0:T(8,128)(2,1)S(1)}, u32[]{:S(2)}, u32[]{:S(2)}) collective-permute-start(bf16[16,1536]{1,0:T(8,128)(2,1)S(1)} %add_add_fusion), channel_id=1, source_target_pairs={{0,1},{1,0},{2,3},{3,2},{4,5},{5,4},{6,7},{7,6},{8,9},{9,8},{10,11... | collective-permute-start | bytes 147464 | tf_op jit(solution)/shard_map/ppermute | solution.py:323
  23.0 3.4 %collective-permute-start.10 = (bf16[64,1536]{1,0:T(8,128)(2,1)S(1)}, bf16[64,1536]{1,0:T(8,128)(2,1)S(1)}, u32[]{:S(2)}, u32[]{:S(2)}) collective-permute-start(bf16[64,1536]{1,0:T(8,128)(2,1)S(1)} %constant_dynamic-update-slice_fusion.slabs_ref), channel_id=1, source_target_pairs={{0,4},{4,0},{8,12},{12,8},{16,20},{20,16},{24,28},{28,24},{1,5},{5... | collective-permute-start | bytes 589832 | tf_op jit(solution)/shard_map/ppermute | solution.py:323

commit v6 on v5

--- a/solution.py
+++ b/solution.py
@@ -330,15 +330,19 @@
     own, other, *receivers = encode(
         tm_size, spectra[:, 0, :], valid.reshape(1, channels), sources
     )
-    receivers[1:] = [
-        swapped(receivers[place], "tm", tm_size, place) for place in range(1, tm_size)
-    ]
+    receivers[-1] = swapped(receivers[-1], "tm", tm_size, tm_size - 1)
     own = own + swapped(other, "rcv", rcv_size, 1)
     step = 2
     while step < rcv_size:
         wide = min(4, rcv_size // step)
-        others = [swapped(own, "rcv", rcv_size, place * step) for place in range(wide - 1, 0, -1)]
-        own = functools.reduce(jnp.add, others, own)
+        parts = [swapped(own, "rcv", rcv_size, place * step) for place in range(wide - 1, 0, -1)]
+        if step == 2:
+            parts[-1], later = lax.optimization_barrier((parts[-1], receivers[1:-1]))
+            receivers[1:-1] = [
+                swapped(block, "tm", tm_size, place) for place, block in enumerate(later, 1)
+            ]
+            parts[0], receivers[-1] = lax.optimization_barrier((parts[0], receivers[-1]))
+        own = functools.reduce(jnp.add, parts[::-1], own)
         step *= wide
     own = [own] + [swapped(own, "tm", tm_size, place) for place in range(1, tm_size)]
     whitened = whiten_blocks(receivers)

time: 30.5 us -> 30.6 us (level)
  waiting for transfers between devices: 6.69 us -> 7.21 us
  starting transfers between devices: 13.3 us -> 12.9 us
    ppermute x11, waiting for transfers between devices: 6.69 us -> 7.21 us  [swapped(): return lax.ppermute(value, axis, [(i, i ^ step) for i in range(size)])]
    ppermute x11, starting transfers between devices: 13.3 us -> 12.9 us  [swapped(): return lax.ppermute(value, axis, [(i, i ^ step) for i in range(size)])]
where the time goes in v6:
time: 30.6 us; the launch traced here: 30.4 us
  starting transfers between devices  12.9 us (42%)
  Pallas kernels  10.2 us (33%)
  waiting for transfers between devices  7.21 us (24%)
    ppermute x11, starting transfers between devices, swapped(): return lax.ppermute(value, axis, [(i, i ^ step) for i in range(size)])  12.9 us
    pallas_call x2, Pallas kernels, stack_half(): pl.pallas_call(functools.partial(stack_kernel, segments), out_shape=jax.S...  7.24 us
    ppermute x11, waiting for transfers between devices, swapped(): return lax.ppermute(value, axis, [(i, i ^ step) for i in range(size)])  7.21 us
    pallas_call x1, Pallas kernels, encode(): pl.pallas_call(functools.partial(encode_kernel, segments), out_shape=(sla...  2.02 us
    pallas_call x1, Pallas kernels, whiten_blocks(): pl.pallas_call(functools.partial(whiten_kernel, segments), out_shape=(par...  0.97 us
  transfers between devices with their start and end apart: 11, of which 5 were waited for; matrix products, arithmetic and copies ran while one was open for 0% of the time, Pallas kernels for 14%

profile of v6, /device:TPU:0, one launch (start us, length us, event | category | flops | bytes accessed | tf_op | source)
XLA Modules:
  0.0 30.4 jit_solution(10792875559334675338)
XLA Ops:
  0.0 0.0 copy-start
  0.0 2.0 %encode_and_pick.1 = (bf16[16,1536]{1,0:T(8,128)(2,1)S(1)}, bf16[16,1536]{1,0:T(8,128)(2,1)S(1)}, bf16[32,3072]{1,0:T(8,128)(2,1)S(1)}, bf16[32,3072]{1,0:T(8,12...) custom-call(bf16[128,3072]{1,0:T(8,128)(2,1)} %bitcast.3, s32[1,128]{1,0:T(1,128)} %bitcast.4, ...), custom_call_target="tpu_custom_call" | custom-call | tf_op jit(solution)/shard_map/encode_and_pick/pallas_call | solution.py:260
  2.0 4.0 %collective-permute-start.4 = (bf16[32,3072]{1,0:T(8,128)(2,1)S(1)}, bf16[32,3072]{1,0:T(8,128)(2,1)S(1)}, u32[]{:S(2)}, u32[]{:S(2)}) collective-permute-start(bf16[32,3072]{1,0:T(8,128)(2,1)S(1)} %get-tuple-element.31), channel_id=1, source_target_pairs={{0,3},{1,2},{2,1},{3,0},{4,7},{5,6},{6,5},{7,4},{8,11},{9,10},{10,... | collective-permute-start | bytes 589832 | tf_op jit(solution)/shard_map/ppermute | solution.py:323
  6.0 0.0 collective-permute-start
  6.0 1.2 %collective-permute-done = bf16[16,1536]{1,0:T(8,128)(2,1)S(1)} collective-permute-done((bf16[16,1536]{1,0:T(8,128)(2,1)S(1)}, bf16[16,1536]{1,0:T(8,128)(2,1)S(1)}, u32[]{:S(2)}, u32[]{:S(2)}) %collective-permute-start) | collective-permute-done | bytes 49184 | tf_op jit(solution)/shard_map/ppermute | solution.py:323
  7.2 1.6 %collective-permute-start.1 = (bf16[16,1536]{1,0:T(8,128)(2,1)S(1)}, bf16[16,1536]{1,0:T(8,128)(2,1)S(1)}, u32[]{:S(2)}, u32[]{:S(2)}) collective-permute-start(bf16[16,1536]{1,0:T(8,128)(2,1)S(1)} %add.12), channel_id=1, source_target_pairs={{0,8},{4,12},{8,0},{12,4},{16,24},{20,28},{24,16},{28,20},{1,9},{5... | collective-permute-start | bytes 147464 | tf_op jit(solution)/shard_map/ppermute | solution.py:323
  8.9 2.5 %collective-permute-start.3 = (bf16[16,1536]{1,0:T(8,128)(2,1)S(1)}, bf16[16,1536]{1,0:T(8,128)(2,1)S(1)}, u32[]{:S(2)}, u32[]{:S(2)}) collective-permute-start(bf16[16,1536]{1,0:T(8,128)(2,1)S(1)} %add.12), channel_id=1, source_target_pairs={{0,24},{4,28},{8,16},{12,20},{16,8},{20,12},{24,0},{28,4},{1,25},{... | collective-permute-start | bytes 147464 | tf_op jit(solution)/shard_map/ppermute | solution.py:323
  11.4 0.1 collective-permute-start.2
  11.5 0.0 collective-permute-done.1
  11.5 0.5 %collective-permute-start.8 = (bf16[32,3072]{1,0:T(8,128)(2,1)S(1)}, bf16[32,3072]{1,0:T(8,128)(2,1)S(1)}, u32[]{:S(2)}, u32[]{:S(2)}) collective-permute-start(bf16[32,3072]{1,0:T(8,128)(2,1)S(1)} %get-tuple-element.34), channel_id=1, source_target_pairs={{0,1},{1,0},{2,3},{3,2},{4,5},{5,4},{6,7},{7,6},{8,9},{9,8},{10,11... | collective-permute-start | bytes 589832 | tf_op jit(solution)/shard_map/ppermute | solution.py:323
  12.0 0.5 %collective-permute-start.9 = (bf16[32,3072]{1,0:T(8,128)(2,1)S(1)}, bf16[32,3072]{1,0:T(8,128)(2,1)S(1)}, u32[]{:S(2)}, u32[]{:S(2)}) collective-permute-start(bf16[32,3072]{1,0:T(8,128)(2,1)S(1)} %get-tuple-element.35), channel_id=1, source_target_pairs={{0,2},{1,3},{2,0},{3,1},{4,6},{5,7},{6,4},{7,5},{8,10},{9,11},{10,... | collective-permute-start | bytes 589832 | tf_op jit(solution)/shard_map/ppermute | solution.py:323
  12.5 2.5 %collective-permute-done.3 = bf16[16,1536]{1,0:T(8,128)(2,1)S(1)} collective-permute-done((bf16[16,1536]{1,0:T(8,128)(2,1)S(1)}, bf16[16,1536]{1,0:T(8,128)(2,1)S(1)}, u32[]{:S(2)}, u32[]{:S(2)}) %collective-permute-start.3) | collective-permute-done | bytes 49184 | tf_op jit(solution)/shard_map/ppermute | solution.py:323
  15.0 0.0 collective-permute-done.4.refs_3_
  15.0 1.9 %collective-permute-done.2 = bf16[16,1536]{1,0:T(8,128)(2,1)S(1)} collective-permute-done((bf16[16,1536]{1,0:T(8,128)(2,1)S(1)}, bf16[16,1536]{1,0:T(8,128)(2,1)S(1)}, u32[]{:S(2)}, u32[]{:S(2)}) %collective-permute-start.2) | collective-permute-done | bytes 49184 | tf_op jit(solution)/shard_map/ppermute | solution.py:323
  16.9 0.5 %collective-permute-start.7 = (bf16[16,1536]{1,0:T(8,128)(2,1)S(1)}, bf16[16,1536]{1,0:T(8,128)(2,1)S(1)}, u32[]{:S(2)}, u32[]{:S(2)}) collective-permute-start(bf16[16,1536]{1,0:T(8,128)(2,1)S(1)} %add_add_fusion), channel_id=1, source_target_pairs={{0,3},{1,2},{2,1},{3,0},{4,7},{5,6},{6,5},{7,4},{8,11},{9,10},{10,... | collective-permute-start | bytes 147464 | tf_op jit(solution)/shard_map/ppermute | solution.py:323
  17.4 1.5 %collective-permute-start.6 = (bf16[16,1536]{1,0:T(8,128)(2,1)S(1)}, bf16[16,1536]{1,0:T(8,128)(2,1)S(1)}, u32[]{:S(2)}, u32[]{:S(2)}) collective-permute-start(bf16[16,1536]{1,0:T(8,128)(2,1)S(1)} %add_add_fusion), channel_id=1, source_target_pairs={{0,2},{1,3},{2,0},{3,1},{4,6},{5,7},{6,4},{7,5},{8,10},{9,11},{10,... | collective-permute-start | bytes 147464 | tf_op jit(solution)/shard_map/ppermute | solution.py:323
  19.0 1.5 %collective-permute-start.5 = (bf16[16,1536]{1,0:T(8,128)(2,1)S(1)}, bf16[16,1536]{1,0:T(8,128)(2,1)S(1)}, u32[]{:S(2)}, u32[]{:S(2)}) collective-permute-start(bf16[16,1536]{1,0:T(8,128)(2,1)S(1)} %add_add_fusion), channel_id=1, source_target_pairs={{0,1},{1,0},{2,3},{3,2},{4,5},{5,4},{6,7},{7,6},{8,9},{9,8},{10,11... | collective-permute-start | bytes 147464 | tf_op jit(solution)/shard_map/ppermute | solution.py:323
  20.4 0.0 collective-permute-done.8.refs_1_
  20.4 0.0 collective-permute-done.9.refs_2_
  20.5 1.0 %whiten_receivers.1 = (f32[128,1536]{1,0:T(8,128)S(1)}, f32[128,1536]{1,0:T(8,128)S(1)}, f32[128,128]{1,0:T(8,128)S(1)}) custom-call(bf16[32,3072]{1,0:T(8,128)(2,1)S(1)} %get-tuple-element.33.refs_0_, bf16[32,3072]{1,0:T(8,128)(2,1)S(1)} %collective-permute-done.8.refs_1_, bf16[32,3072]{1,0:T(8,128)(2,1)S(1)} %collective-permute-done.9.refs_2_, ...), custom_call_target="tpu_custom_call" | custom-call | flops 402653184 | bytes 1572864 | tf_op jit(solution)/shard_map/whiten_receivers/pallas_call | solution.py:284
  21.4 0.6 %collective-permute-done.7 = bf16[16,1536]{1,0:T(8,128)(2,1)S(1)} collective-permute-done((bf16[16,1536]{1,0:T(8,128)(2,1)S(1)}, bf16[16,1536]{1,0:T(8,128)(2,1)S(1)}, u32[]{:S(2)}, u32[]{:S(2)}) %collective-permute-start.7) | collective-permute-done | bytes 49184 | tf_op jit(solution)/shard_map/ppermute | solution.py:323
  22.1 0.0 collective-permute-done.6
  22.1 1.0 %collective-permute-done.5 = bf16[16,1536]{1,0:T(8,128)(2,1)S(1)} collective-permute-done((bf16[16,1536]{1,0:T(8,128)(2,1)S(1)}, bf16[16,1536]{1,0:T(8,128)(2,1)S(1)}, u32[]{:S(2)}, u32[]{:S(2)}) %collective-permute-start.5) | collective-permute-done | bytes 49184 | tf_op jit(solution)/shard_map/ppermute | solution.py:323
  23.1 0.1 collective-permute-start.10
  23.2 0.0 copy-done
  23.2 3.3 %stack_own_half.1.refs_0_ = f32[256,301]{1,0:T(8,128)S(1)} custom-call(bf16[64,1536]{1,0:T(8,128)(2,1)S(1)} %constant_dynamic-update-slice_fusion.slabs_ref, f32[128,1536]{1,0:T(8,128)S(1)} %get-tuple-element.44.rcv_re, f32[128,1536]{1,0:T(8,128)S(1)} %get-tuple-element.45.rcv_im, f32[128,128]{1,0:T(8,128)S(1)} %get-tuple-element.46.rcv_valid, ...), custom_call_target="tpu_custom_call" | custom-call | flops 471859200 | bytes 3145728 | tf_op jit(solution)/shard_map/stack_own_half/pallas_call | solution.py:308
  26.4 0.0 collective-permute-done.10.slabs_ref
  26.4 4.0 %stack_other_half.1 = f32[512,301]{1,0:T(8,128)} custom-call(bf16[64,1536]{1,0:T(8,128)(2,1)S(1)} %collective-permute-done.10.slabs_ref, f32[128,1536]{1,0:T(8,128)S(1)} %get-tuple-element.44.rcv_re, f32[128,1536]{1,0:T(8,128)S(1)} %get-tuple-element.45.rcv_im, f32[128,128]{1,0:T(8,128)S(1)} %get-tuple-element.46.rcv_valid, bf16[3072,256]{1,0:T(8,128)(2,1)S(1)} %copy-done, ...), custom_call_target="tpu_custom_call" | custom-call | flops 471859200 | bytes 3145728 | tf_op jit(solution)/shard_map/stack_other_half/pallas_call | solution.py:308
  (6 shorter events, 0.0 us)
Async XLA Ops:
  0.0 23.2 %copy-start = (bf16[3072,256]{1,0:T(8,128)(2,1)S(1)}, bf16[3072,256]{1,0:T(8,128)(2,1)}, u32[]{:S(2)}) copy-start(bf16[3072,256]{1,0:T(8,128)(2,1)} %constant.2.clone.table_ref) | copy-start | bytes 4718596
  2.0 12.9 %collective-permute-start.4 = (bf16[32,3072]{1,0:T(8,128)(2,1)S(1)}, bf16[32,3072]{1,0:T(8,128)(2,1)S(1)}, u32[]{:S(2)}, u32[]{:S(2)}) collective-permute-start(bf16[32,3072]{1,0:T(8,128)(2,1)S(1)} %get-tuple-element.31), channel_id=1, source_target_pairs={{0,3},{1,2},{2,1},{3,0},{4,7},{5,6},{6,5},{7,4},{8,11},{9,10},{10,... | collective-permute-start | bytes 589832 | tf_op jit(solution)/shard_map/ppermute | solution.py:323
  6.0 1.2 %collective-permute-start = (bf16[16,1536]{1,0:T(8,128)(2,1)S(1)}, bf16[16,1536]{1,0:T(8,128)(2,1)S(1)}, u32[]{:S(2)}, u32[]{:S(2)}) collective-permute-start(bf16[16,1536]{1,0:T(8,128)(2,1)S(1)} %get-tuple-element.27), channel_id=1, source_target_pairs={{0,4},{4,0},{8,12},{12,8},{16,20},{20,16},{24,28},{28,24},{1,5},{5... | collective-permute-start | bytes 147464 | tf_op jit(solution)/shard_map/ppermute | solution.py:323
  7.2 4.2 %collective-permute-start.1 = (bf16[16,1536]{1,0:T(8,128)(2,1)S(1)}, bf16[16,1536]{1,0:T(8,128)(2,1)S(1)}, u32[]{:S(2)}, u32[]{:S(2)}) collective-permute-start(bf16[16,1536]{1,0:T(8,128)(2,1)S(1)} %add.12), channel_id=1, source_target_pairs={{0,8},{4,12},{8,0},{12,4},{16,24},{20,28},{24,16},{28,20},{1,9},{5... | collective-permute-start | bytes 147464 | tf_op jit(solution)/shard_map/ppermute | solution.py:323
  8.9 6.1 %collective-permute-start.3 = (bf16[16,1536]{1,0:T(8,128)(2,1)S(1)}, bf16[16,1536]{1,0:T(8,128)(2,1)S(1)}, u32[]{:S(2)}, u32[]{:S(2)}) collective-permute-start(bf16[16,1536]{1,0:T(8,128)(2,1)S(1)} %add.12), channel_id=1, source_target_pairs={{0,24},{4,28},{8,16},{12,20},{16,8},{20,12},{24,0},{28,4},{1,25},{... | collective-permute-start | bytes 147464 | tf_op jit(solution)/shard_map/ppermute | solution.py:323
  11.4 5.5 %collective-permute-start.2 = (bf16[16,1536]{1,0:T(8,128)(2,1)S(1)}, bf16[16,1536]{1,0:T(8,128)(2,1)S(1)}, u32[]{:S(2)}, u32[]{:S(2)}) collective-permute-start(bf16[16,1536]{1,0:T(8,128)(2,1)S(1)} %add.12), channel_id=1, source_target_pairs={{0,16},{4,20},{8,24},{12,28},{16,0},{20,4},{24,8},{28,12},{1,17},{... | collective-permute-start | bytes 147464 | tf_op jit(solution)/shard_map/ppermute | solution.py:323
  11.5 9.0 %collective-permute-start.8 = (bf16[32,3072]{1,0:T(8,128)(2,1)S(1)}, bf16[32,3072]{1,0:T(8,128)(2,1)S(1)}, u32[]{:S(2)}, u32[]{:S(2)}) collective-permute-start(bf16[32,3072]{1,0:T(8,128)(2,1)S(1)} %get-tuple-element.34), channel_id=1, source_target_pairs={{0,1},{1,0},{2,3},{3,2},{4,5},{5,4},{6,7},{7,6},{8,9},{9,8},{10,11... | collective-permute-start | bytes 589832 | tf_op jit(solution)/shard_map/ppermute | solution.py:323
  12.0 8.4 %collective-permute-start.9 = (bf16[32,3072]{1,0:T(8,128)(2,1)S(1)}, bf16[32,3072]{1,0:T(8,128)(2,1)S(1)}, u32[]{:S(2)}, u32[]{:S(2)}) collective-permute-start(bf16[32,3072]{1,0:T(8,128)(2,1)S(1)} %get-tuple-element.35), channel_id=1, source_target_pairs={{0,2},{1,3},{2,0},{3,1},{4,6},{5,7},{6,4},{7,5},{8,10},{9,11},{10,... | collective-permute-start | bytes 589832 | tf_op jit(solution)/shard_map/ppermute | solution.py:323
  16.9 5.2 %collective-permute-start.7 = (bf16[16,1536]{1,0:T(8,128)(2,1)S(1)}, bf16[16,1536]{1,0:T(8,128)(2,1)S(1)}, u32[]{:S(2)}, u32[]{:S(2)}) collective-permute-start(bf16[16,1536]{1,0:T(8,128)(2,1)S(1)} %add_add_fusion), channel_id=1, source_target_pairs={{0,3},{1,2},{2,1},{3,0},{4,7},{5,6},{6,5},{7,4},{8,11},{9,10},{10,... | collective-permute-start | bytes 147464 | tf_op jit(solution)/shard_map/ppermute | solution.py:323
  17.4 4.6 %collective-permute-start.6 = (bf16[16,1536]{1,0:T(8,128)(2,1)S(1)}, bf16[16,1536]{1,0:T(8,128)(2,1)S(1)}, u32[]{:S(2)}, u32[]{:S(2)}) collective-permute-start(bf16[16,1536]{1,0:T(8,128)(2,1)S(1)} %add_add_fusion), channel_id=1, source_target_pairs={{0,2},{1,3},{2,0},{3,1},{4,6},{5,7},{6,4},{7,5},{8,10},{9,11},{10,... | collective-permute-start | bytes 147464 | tf_op jit(solution)/shard_map/ppermute | solution.py:323
  19.0 4.1 %collective-permute-start.5 = (bf16[16,1536]{1,0:T(8,128)(2,1)S(1)}, bf16[16,1536]{1,0:T(8,128)(2,1)S(1)}, u32[]{:S(2)}, u32[]{:S(2)}) collective-permute-start(bf16[16,1536]{1,0:T(8,128)(2,1)S(1)} %add_add_fusion), channel_id=1, source_target_pairs={{0,1},{1,0},{2,3},{3,2},{4,5},{5,4},{6,7},{7,6},{8,9},{9,8},{10,11... | collective-permute-start | bytes 147464 | tf_op jit(solution)/shard_map/ppermute | solution.py:323
  23.1 3.4 %collective-permute-start.10 = (bf16[64,1536]{1,0:T(8,128)(2,1)S(1)}, bf16[64,1536]{1,0:T(8,128)(2,1)S(1)}, u32[]{:S(2)}, u32[]{:S(2)}) collective-permute-start(bf16[64,1536]{1,0:T(8,128)(2,1)S(1)} %constant_dynamic-update-slice_fusion.slabs_ref), channel_id=1, source_target_pairs={{0,4},{4,0},{8,12},{12,8},{16,20},{20,16},{24,28},{28,24},{1,5},{5... | collective-permute-start | bytes 589832 | tf_op jit(solution)/shard_map/ppermute | solution.py:323

commit v7 on v6

--- a/solution.py
+++ b/solution.py
@@ -33,6 +33,10 @@
     )
     theta = winding * (2.0 * math.pi / NT)
     return np.concatenate([np.cos(theta), -np.sin(theta)], axis=0).astype(jnp.bfloat16)
+
+
+def kind_for(rows):
+    return jnp.bfloat16 if rows % 16 == 0 else jnp.float32
 
 
 def iota(shape, dim):
@@ -128,9 +132,13 @@
     nbins = rows.shape[1] // 2
     real, imag = rows[:, :nbins], rows[:, nbins:]
     for at, re, im in whitening(real, imag, high, low):
-        real_ref[:, at] = re
-        imag_ref[:, at] = im
+        real_ref[:, at] = re.astype(real_ref.dtype)
+        imag_ref[:, at] = im.astype(imag_ref.dtype)
     valid_ref[...] = usable_rows(real)
+
+
+def total_groups(segments, kind):
+    return -(-segments // 2) if kind == jnp.bfloat16 and segments % 2 == 0 else 1
 
 
 def stack_kernel(
@@ -169,6 +177,13 @@
     total_im[...] = jnp.zeros_like(total_im)
     cross_b[...] = jnp.zeros_like(cross_b)
 
+    kind = rcv_re.dtype
+    groups = total_groups(segments, kind)
+
+    def spread(row):
+        tile = jnp.broadcast_to(row, (min(keep, 16), LANES)).astype(kind)
+        return jnp.concatenate([tile] * (keep // tile.shape[0]), axis=0)
+
     def multiply(block, cross):
         for sub in range(BLOCK // LANES):
             at = pl.ds(pl.multiple_of(block * BLOCK + sub * LANES, LANES), LANES)
@@ -178,26 +193,27 @@
                 real, imag = [], []
                 for t in range(segments):
                     row = slice(t * half + source, t * half + source + 1)
-                    s_re, s_im = src_re[row, at], src_im[row, at]
+                    s_re, s_im = spread(src_re[row, at]), spread(src_im[row, at])
                     real.append(s_re * r_re[t] + s_im * r_im[t])
                     imag.append(s_im * r_re[t] - s_re * r_im[t])
-                real, imag = functools.reduce(jnp.add, real), functools.reduce(jnp.add, imag)
                 to = slice(source * keep, (source + 1) * keep)
-                cross[to, sub * LANES : (sub + 1) * LANES] = real.astype(cross.dtype)
-                cross[to, BLOCK + sub * LANES : BLOCK + (sub + 1) * LANES] = imag.astype(
-                    cross.dtype
-                )
+                share = segments // groups
+                for place, part in enumerate((real, imag)):
+                    for group in range(groups):
+                        value = functools.reduce(jnp.add, part[group * share : (group + 1) * share])
+                        first = (place * groups + group) * BLOCK + sub * LANES
+                        cross[to, first : first + LANES] = value
 
     def project(block, cross):
         value = cross[...].astype(jnp.bfloat16)
         re_at = pl.ds(pl.multiple_of(block * BLOCK, BLOCK), BLOCK)
         im_at = pl.ds(pl.multiple_of(nbins + block * BLOCK, BLOCK), BLOCK)
-        total_re[...] += jnp.dot(
-            value[:, :BLOCK], table_ref[re_at, :], preferred_element_type=jnp.float32
-        )
-        total_im[...] += jnp.dot(
-            value[:, BLOCK:], table_ref[im_at, :], preferred_element_type=jnp.float32
-        )
+        for first, at, total in ((0, re_at, total_re), (groups * BLOCK, im_at, total_im)):
+            total[...] += jnp.dot(
+                value[:, first : first + groups * BLOCK],
+                jnp.concatenate([table_ref[at, :]] * groups, axis=0),
+                preferred_element_type=jnp.float32,
+            )
 
     def two_blocks(pair, carry):
         multiply(2 * pair, cross_a)
@@ -263,7 +279,7 @@
         in_specs=[HBM] * 3,
         out_specs=(VMEM,) * (2 + segments),
         scratch_shapes=[
-            pltpu.VMEM((channels, width), jnp.bfloat16 if keep % 16 == 0 else jnp.float32),
+            pltpu.VMEM((channels, width), kind_for(keep)),
             pltpu.VMEM((channels, width), jnp.bfloat16),
             pltpu.VMEM((1, channels), jnp.int32),
             pltpu.SMEM(sources.shape, jnp.int32),
@@ -280,7 +296,7 @@
     segments, (keep, width) = len(blocks), blocks[0].shape
     count, nbins = segments * keep, width // 2
     padded = pltpu.VMEM((count, nbins + 2 * LANES), jnp.bfloat16)
-    part = jax.ShapeDtypeStruct((count, nbins), jnp.float32)
+    part = jax.ShapeDtypeStruct((count, nbins), kind_for(keep))
     return pl.pallas_call(
         functools.partial(whiten_kernel, segments),
         out_shape=(part, part, jax.ShapeDtypeStruct((count, LANES), jnp.float32)),
@@ -299,8 +315,10 @@
     half, nbins = slabs.shape[0] // (2 * segments), slabs.shape[1]
     keep = receivers[0].shape[0] // segments
     count, rows, lags = segments * half, half * keep, 2 * LAG + 1
+    kind = receivers[0].dtype
+    groups = total_groups(segments, kind)
     part = pltpu.VMEM((count, nbins), jnp.float32)
-    cross = pltpu.VMEM((rows, 2 * BLOCK), jnp.bfloat16 if keep % 16 == 0 else jnp.float32)
+    cross = pltpu.VMEM((rows, 2 * groups * BLOCK), kind)
     total = pltpu.VMEM((rows, BLOCK), jnp.float32)
     scratch = [part, part, cross, cross, total, total]
     if rest:

time: 30.6 us -> 29.1 us (0.951)
  Pallas kernels: 10.2 us -> 8.64 us
    pallas_call x2, Pallas kernels: 7.24 us -> 5.71 us  [stack_half(): pl.pallas_call(functools.partial(stack_kernel, segments), out_shape=jax.S...]
  transfers between devices with their start and end apart: 11 -> 11, of which waited for: 5 -> 5; matrix products, arithmetic and copies ran while one was open for 0% -> 0% of each run, Pallas kernels for 14% -> 12%
where the time goes in v7:
time: 29.1 us; the launch traced here: 28.9 us
  starting transfers between devices  12.9 us (44%)
  Pallas kernels  8.64 us (30%)
  waiting for transfers between devices  7.26 us (25%)
    ppermute x11, starting transfers between devices, swapped(): return lax.ppermute(value, axis, [(i, i ^ step) for i in range(size)])  12.9 us
    ppermute x11, waiting for transfers between devices, swapped(): return lax.ppermute(value, axis, [(i, i ^ step) for i in range(size)])  7.26 us
    pallas_call x2, Pallas kernels, stack_half(): pl.pallas_call(functools.partial(stack_kernel, segments), out_shape=jax.S...  5.71 us
    pallas_call x1, Pallas kernels, encode(): pl.pallas_call(functools.partial(encode_kernel, segments), out_shape=(sla...  2.02 us
    pallas_call x1, Pallas kernels, whiten_blocks(): pl.pallas_call(functools.partial(whiten_kernel, segments), out_shape=(par...  0.92 us
  transfers between devices with their start and end apart: 11, of which 5 were waited for; matrix products, arithmetic and copies ran while one was open for 0% of the time, Pallas kernels for 12%

profile of v7, /device:TPU:0, one launch (start us, length us, event | category | flops | bytes accessed | tf_op | source)
XLA Modules:
  0.0 28.9 jit_solution(5934112606814573124)
XLA Ops:
  0.0 0.0 copy-start
  0.0 2.0 %encode_and_pick.1 = (bf16[16,1536]{1,0:T(8,128)(2,1)S(1)}, bf16[16,1536]{1,0:T(8,128)(2,1)S(1)}, bf16[32,3072]{1,0:T(8,128)(2,1)S(1)}, bf16[32,3072]{1,0:T(8,12...) custom-call(bf16[128,3072]{1,0:T(8,128)(2,1)} %bitcast.3, s32[1,128]{1,0:T(1,128)} %bitcast.4, ...), custom_call_target="tpu_custom_call" | custom-call | tf_op jit(solution)/shard_map/encode_and_pick/pallas_call | solution.py:276
  2.0 4.0 %collective-permute-start.4 = (bf16[32,3072]{1,0:T(8,128)(2,1)S(1)}, bf16[32,3072]{1,0:T(8,128)(2,1)S(1)}, u32[]{:S(2)}, u32[]{:S(2)}) collective-permute-start(bf16[32,3072]{1,0:T(8,128)(2,1)S(1)} %get-tuple-element.31), channel_id=1, source_target_pairs={{0,3},{1,2},{2,1},{3,0},{4,7},{5,6},{6,5},{7,4},{8,11},{9,10},{10,... | collective-permute-start | bytes 589832 | tf_op jit(solution)/shard_map/ppermute | solution.py:341
  6.0 0.0 collective-permute-start
  6.0 1.2 %collective-permute-done = bf16[16,1536]{1,0:T(8,128)(2,1)S(1)} collective-permute-done((bf16[16,1536]{1,0:T(8,128)(2,1)S(1)}, bf16[16,1536]{1,0:T(8,128)(2,1)S(1)}, u32[]{:S(2)}, u32[]{:S(2)}) %collective-permute-start) | collective-permute-done | bytes 49184 | tf_op jit(solution)/shard_map/ppermute | solution.py:341
  7.2 1.6 %collective-permute-start.1 = (bf16[16,1536]{1,0:T(8,128)(2,1)S(1)}, bf16[16,1536]{1,0:T(8,128)(2,1)S(1)}, u32[]{:S(2)}, u32[]{:S(2)}) collective-permute-start(bf16[16,1536]{1,0:T(8,128)(2,1)S(1)} %add.12), channel_id=1, source_target_pairs={{0,8},{4,12},{8,0},{12,4},{16,24},{20,28},{24,16},{28,20},{1,9},{5... | collective-permute-start | bytes 147464 | tf_op jit(solution)/shard_map/ppermute | solution.py:341
  8.9 2.5 %collective-permute-start.3 = (bf16[16,1536]{1,0:T(8,128)(2,1)S(1)}, bf16[16,1536]{1,0:T(8,128)(2,1)S(1)}, u32[]{:S(2)}, u32[]{:S(2)}) collective-permute-start(bf16[16,1536]{1,0:T(8,128)(2,1)S(1)} %add.12), channel_id=1, source_target_pairs={{0,24},{4,28},{8,16},{12,20},{16,8},{20,12},{24,0},{28,4},{1,25},{... | collective-permute-start | bytes 147464 | tf_op jit(solution)/shard_map/ppermute | solution.py:341
  11.4 0.1 collective-permute-start.2
  11.5 0.0 collective-permute-done.1
  11.5 0.5 %collective-permute-start.8 = (bf16[32,3072]{1,0:T(8,128)(2,1)S(1)}, bf16[32,3072]{1,0:T(8,128)(2,1)S(1)}, u32[]{:S(2)}, u32[]{:S(2)}) collective-permute-start(bf16[32,3072]{1,0:T(8,128)(2,1)S(1)} %get-tuple-element.34), channel_id=1, source_target_pairs={{0,1},{1,0},{2,3},{3,2},{4,5},{5,4},{6,7},{7,6},{8,9},{9,8},{10,11... | collective-permute-start | bytes 589832 | tf_op jit(solution)/shard_map/ppermute | solution.py:341
  12.0 0.5 %collective-permute-start.9 = (bf16[32,3072]{1,0:T(8,128)(2,1)S(1)}, bf16[32,3072]{1,0:T(8,128)(2,1)S(1)}, u32[]{:S(2)}, u32[]{:S(2)}) collective-permute-start(bf16[32,3072]{1,0:T(8,128)(2,1)S(1)} %get-tuple-element.35), channel_id=1, source_target_pairs={{0,2},{1,3},{2,0},{3,1},{4,6},{5,7},{6,4},{7,5},{8,10},{9,11},{10,... | collective-permute-start | bytes 589832 | tf_op jit(solution)/shard_map/ppermute | solution.py:341
  12.5 2.5 %collective-permute-done.3 = bf16[16,1536]{1,0:T(8,128)(2,1)S(1)} collective-permute-done((bf16[16,1536]{1,0:T(8,128)(2,1)S(1)}, bf16[16,1536]{1,0:T(8,128)(2,1)S(1)}, u32[]{:S(2)}, u32[]{:S(2)}) %collective-permute-start.3) | collective-permute-done | bytes 49184 | tf_op jit(solution)/shard_map/ppermute | solution.py:341
  15.0 0.0 collective-permute-done.4.refs_3_
  15.0 1.9 %collective-permute-done.2 = bf16[16,1536]{1,0:T(8,128)(2,1)S(1)} collective-permute-done((bf16[16,1536]{1,0:T(8,128)(2,1)S(1)}, bf16[16,1536]{1,0:T(8,128)(2,1)S(1)}, u32[]{:S(2)}, u32[]{:S(2)}) %collective-permute-start.2) | collective-permute-done | bytes 49184 | tf_op jit(solution)/shard_map/ppermute | solution.py:341
  16.9 0.5 %collective-permute-start.7 = (bf16[16,1536]{1,0:T(8,128)(2,1)S(1)}, bf16[16,1536]{1,0:T(8,128)(2,1)S(1)}, u32[]{:S(2)}, u32[]{:S(2)}) collective-permute-start(bf16[16,1536]{1,0:T(8,128)(2,1)S(1)} %add_add_fusion), channel_id=1, source_target_pairs={{0,3},{1,2},{2,1},{3,0},{4,7},{5,6},{6,5},{7,4},{8,11},{9,10},{10,... | collective-permute-start | bytes 147464 | tf_op jit(solution)/shard_map/ppermute | solution.py:341
  17.4 1.5 %collective-permute-start.6 = (bf16[16,1536]{1,0:T(8,128)(2,1)S(1)}, bf16[16,1536]{1,0:T(8,128)(2,1)S(1)}, u32[]{:S(2)}, u32[]{:S(2)}) collective-permute-start(bf16[16,1536]{1,0:T(8,128)(2,1)S(1)} %add_add_fusion), channel_id=1, source_target_pairs={{0,2},{1,3},{2,0},{3,1},{4,6},{5,7},{6,4},{7,5},{8,10},{9,11},{10,... | collective-permute-start | bytes 147464 | tf_op jit(solution)/shard_map/ppermute | solution.py:341
  19.0 1.5 %collective-permute-start.5 = (bf16[16,1536]{1,0:T(8,128)(2,1)S(1)}, bf16[16,1536]{1,0:T(8,128)(2,1)S(1)}, u32[]{:S(2)}, u32[]{:S(2)}) collective-permute-start(bf16[16,1536]{1,0:T(8,128)(2,1)S(1)} %add_add_fusion), channel_id=1, source_target_pairs={{0,1},{1,0},{2,3},{3,2},{4,5},{5,4},{6,7},{7,6},{8,9},{9,8},{10,11... | collective-permute-start | bytes 147464 | tf_op jit(solution)/shard_map/ppermute | solution.py:341
  20.4 0.0 collective-permute-done.8.refs_1_
  20.4 0.0 collective-permute-done.9.refs_2_
  20.5 0.9 %whiten_receivers.1 = (bf16[128,1536]{1,0:T(8,128)(2,1)S(1)}, bf16[128,1536]{1,0:T(8,128)(2,1)S(1)}, f32[128,128]{1,0:T(8,128)S(1)}) custom-call(bf16[32,3072]{1,0:T(8,128)(2,1)S(1)} %get-tuple-element.33.refs_0_, bf16[32,3072]{1,0:T(8,128)(2,1)S(1)} %collective-permute-done.8.refs_1_, bf16[32,3072]{1,0:T(8,128)(2,1)S(1)} %collective-permute-done.9.refs_2_, ...), custom_call_target="tpu_custom_call" | custom-call | flops 402653184 | bytes 1572864 | tf_op jit(solution)/shard_map/whiten_receivers/pallas_call | solution.py:300
  21.4 0.7 %collective-permute-done.7 = bf16[16,1536]{1,0:T(8,128)(2,1)S(1)} collective-permute-done((bf16[16,1536]{1,0:T(8,128)(2,1)S(1)}, bf16[16,1536]{1,0:T(8,128)(2,1)S(1)}, u32[]{:S(2)}, u32[]{:S(2)}) %collective-permute-start.7) | collective-permute-done | bytes 49184 | tf_op jit(solution)/shard_map/ppermute | solution.py:341
  22.1 0.0 collective-permute-done.6
  22.1 1.0 %collective-permute-done.5 = bf16[16,1536]{1,0:T(8,128)(2,1)S(1)} collective-permute-done((bf16[16,1536]{1,0:T(8,128)(2,1)S(1)}, bf16[16,1536]{1,0:T(8,128)(2,1)S(1)}, u32[]{:S(2)}, u32[]{:S(2)}) %collective-permute-start.5) | collective-permute-done | bytes 49184 | tf_op jit(solution)/shard_map/ppermute | solution.py:341
  23.1 0.1 collective-permute-start.10
  23.2 0.0 copy-done
  23.2 2.5 %stack_own_half.1.refs_0_ = f32[256,301]{1,0:T(8,128)S(1)} custom-call(bf16[64,1536]{1,0:T(8,128)(2,1)S(1)} %constant_dynamic-update-slice_fusion.slabs_ref, bf16[128,1536]{1,0:T(8,128)(2,1)S(1)} %get-tuple-element.44.rcv_re, bf16[128,1536]{1,0:T(8,128)(2,1)S(1)} %get-tuple-element.45.rcv_im, f32[128,128]{1,0:T(8,128)S(1)} %get-tuple-element.46.rcv_valid, ...), custom_call_target="tpu_custom_call" | custom-call | flops 471859200 | bytes 3145728 | tf_op jit(solution)/shard_map/stack_own_half/pallas_call | solution.py:326
  25.7 0.0 collective-permute-done.10.slabs_ref
  25.7 3.2 %stack_other_half.1 = f32[512,301]{1,0:T(8,128)} custom-call(bf16[64,1536]{1,0:T(8,128)(2,1)S(1)} %collective-permute-done.10.slabs_ref, bf16[128,1536]{1,0:T(8,128)(2,1)S(1)} %get-tuple-element.44.rcv_re, bf16[128,1536]{1,0:T(8,128)(2,1)S(1)} %get-tuple-element.45.rcv_im, f32[128,128]{1,0:T(8,128)S(1)} %get-tuple-element.46.rcv_valid, ...), custom_call_target="tpu_custom_call" | custom-call | flops 471859200 | bytes 3145728 | tf_op jit(solution)/shard_map/stack_other_half/pallas_call | solution.py:326
  (6 shorter events, 0.0 us)
Async XLA Ops:
  0.0 23.2 %copy-start = (bf16[3072,256]{1,0:T(8,128)(2,1)S(1)}, bf16[3072,256]{1,0:T(8,128)(2,1)}, u32[]{:S(2)}) copy-start(bf16[3072,256]{1,0:T(8,128)(2,1)} %constant.2.clone.table_ref) | copy-start | bytes 4718596
  2.0 12.9 %collective-permute-start.4 = (bf16[32,3072]{1,0:T(8,128)(2,1)S(1)}, bf16[32,3072]{1,0:T(8,128)(2,1)S(1)}, u32[]{:S(2)}, u32[]{:S(2)}) collective-permute-start(bf16[32,3072]{1,0:T(8,128)(2,1)S(1)} %get-tuple-element.31), channel_id=1, source_target_pairs={{0,3},{1,2},{2,1},{3,0},{4,7},{5,6},{6,5},{7,4},{8,11},{9,10},{10,... | collective-permute-start | bytes 589832 | tf_op jit(solution)/shard_map/ppermute | solution.py:341
  6.0 1.2 %collective-permute-start = (bf16[16,1536]{1,0:T(8,128)(2,1)S(1)}, bf16[16,1536]{1,0:T(8,128)(2,1)S(1)}, u32[]{:S(2)}, u32[]{:S(2)}) collective-permute-start(bf16[16,1536]{1,0:T(8,128)(2,1)S(1)} %get-tuple-element.27), channel_id=1, source_target_pairs={{0,4},{4,0},{8,12},{12,8},{16,20},{20,16},{24,28},{28,24},{1,5},{5... | collective-permute-start | bytes 147464 | tf_op jit(solution)/shard_map/ppermute | solution.py:341
  7.2 4.2 %collective-permute-start.1 = (bf16[16,1536]{1,0:T(8,128)(2,1)S(1)}, bf16[16,1536]{1,0:T(8,128)(2,1)S(1)}, u32[]{:S(2)}, u32[]{:S(2)}) collective-permute-start(bf16[16,1536]{1,0:T(8,128)(2,1)S(1)} %add.12), channel_id=1, source_target_pairs={{0,8},{4,12},{8,0},{12,4},{16,24},{20,28},{24,16},{28,20},{1,9},{5... | collective-permute-start | bytes 147464 | tf_op jit(solution)/shard_map/ppermute | solution.py:341
  8.9 6.1 %collective-permute-start.3 = (bf16[16,1536]{1,0:T(8,128)(2,1)S(1)}, bf16[16,1536]{1,0:T(8,128)(2,1)S(1)}, u32[]{:S(2)}, u32[]{:S(2)}) collective-permute-start(bf16[16,1536]{1,0:T(8,128)(2,1)S(1)} %add.12), channel_id=1, source_target_pairs={{0,24},{4,28},{8,16},{12,20},{16,8},{20,12},{24,0},{28,4},{1,25},{... | collective-permute-start | bytes 147464 | tf_op jit(solution)/shard_map/ppermute | solution.py:341
  11.4 5.5 %collective-permute-start.2 = (bf16[16,1536]{1,0:T(8,128)(2,1)S(1)}, bf16[16,1536]{1,0:T(8,128)(2,1)S(1)}, u32[]{:S(2)}, u32[]{:S(2)}) collective-permute-start(bf16[16,1536]{1,0:T(8,128)(2,1)S(1)} %add.12), channel_id=1, source_target_pairs={{0,16},{4,20},{8,24},{12,28},{16,0},{20,4},{24,8},{28,12},{1,17},{... | collective-permute-start | bytes 147464 | tf_op jit(solution)/shard_map/ppermute | solution.py:341
  11.5 9.0 %collective-permute-start.8 = (bf16[32,3072]{1,0:T(8,128)(2,1)S(1)}, bf16[32,3072]{1,0:T(8,128)(2,1)S(1)}, u32[]{:S(2)}, u32[]{:S(2)}) collective-permute-start(bf16[32,3072]{1,0:T(8,128)(2,1)S(1)} %get-tuple-element.34), channel_id=1, source_target_pairs={{0,1},{1,0},{2,3},{3,2},{4,5},{5,4},{6,7},{7,6},{8,9},{9,8},{10,11... | collective-permute-start | bytes 589832 | tf_op jit(solution)/shard_map/ppermute | solution.py:341
  12.0 8.4 %collective-permute-start.9 = (bf16[32,3072]{1,0:T(8,128)(2,1)S(1)}, bf16[32,3072]{1,0:T(8,128)(2,1)S(1)}, u32[]{:S(2)}, u32[]{:S(2)}) collective-permute-start(bf16[32,3072]{1,0:T(8,128)(2,1)S(1)} %get-tuple-element.35), channel_id=1, source_target_pairs={{0,2},{1,3},{2,0},{3,1},{4,6},{5,7},{6,4},{7,5},{8,10},{9,11},{10,... | collective-permute-start | bytes 589832 | tf_op jit(solution)/shard_map/ppermute | solution.py:341
  16.9 5.2 %collective-permute-start.7 = (bf16[16,1536]{1,0:T(8,128)(2,1)S(1)}, bf16[16,1536]{1,0:T(8,128)(2,1)S(1)}, u32[]{:S(2)}, u32[]{:S(2)}) collective-permute-start(bf16[16,1536]{1,0:T(8,128)(2,1)S(1)} %add_add_fusion), channel_id=1, source_target_pairs={{0,3},{1,2},{2,1},{3,0},{4,7},{5,6},{6,5},{7,4},{8,11},{9,10},{10,... | collective-permute-start | bytes 147464 | tf_op jit(solution)/shard_map/ppermute | solution.py:341
  17.4 4.6 %collective-permute-start.6 = (bf16[16,1536]{1,0:T(8,128)(2,1)S(1)}, bf16[16,1536]{1,0:T(8,128)(2,1)S(1)}, u32[]{:S(2)}, u32[]{:S(2)}) collective-permute-start(bf16[16,1536]{1,0:T(8,128)(2,1)S(1)} %add_add_fusion), channel_id=1, source_target_pairs={{0,2},{1,3},{2,0},{3,1},{4,6},{5,7},{6,4},{7,5},{8,10},{9,11},{10,... | collective-permute-start | bytes 147464 | tf_op jit(solution)/shard_map/ppermute | solution.py:341
  19.0 4.1 %collective-permute-start.5 = (bf16[16,1536]{1,0:T(8,128)(2,1)S(1)}, bf16[16,1536]{1,0:T(8,128)(2,1)S(1)}, u32[]{:S(2)}, u32[]{:S(2)}) collective-permute-start(bf16[16,1536]{1,0:T(8,128)(2,1)S(1)} %add_add_fusion), channel_id=1, source_target_pairs={{0,1},{1,0},{2,3},{3,2},{4,5},{5,4},{6,7},{7,6},{8,9},{9,8},{10,11... | collective-permute-start | bytes 147464 | tf_op jit(solution)/shard_map/ppermute | solution.py:341
  23.1 2.6 %collective-permute-start.10 = (bf16[64,1536]{1,0:T(8,128)(2,1)S(1)}, bf16[64,1536]{1,0:T(8,128)(2,1)S(1)}, u32[]{:S(2)}, u32[]{:S(2)}) collective-permute-start(bf16[64,1536]{1,0:T(8,128)(2,1)S(1)} %constant_dynamic-update-slice_fusion.slabs_ref), channel_id=1, source_target_pairs={{0,4},{4,0},{8,12},{12,8},{16,20},{20,16},{24,28},{28,24},{1,5},{5... | collective-permute-start | bytes 589832 | tf_op jit(solution)/shard_map/ppermute | solution.py:341

commit v8 on v7

--- a/solution.py
+++ b/solution.py
@@ -19,6 +19,7 @@
 
 LANES = 128
 BLOCK = 256
+CHUNK = 512
 MEBI = 1 << 20
 FIRST_LAG = LANES - LAG
 VMEM = pl.BlockSpec(memory_space=pltpu.VMEM)
@@ -144,15 +145,13 @@
 def stack_kernel(
     segments, slabs_ref, rcv_re, rcv_im, rcv_valid, table_ref, *refs
 ):
-    *rest, out_ref, src_re, src_im, cross_a, cross_b, total_re, total_im = refs[
-        : 8 if len(refs) == 10 else 7
-    ]
+    *rest, out_ref, src_re, src_im, cross = refs[: 5 if len(refs) == 7 else 4]
     half = slabs_ref.shape[0] // (2 * segments)
     nbins = slabs_ref.shape[1]
     keep = rcv_re.shape[0] // segments
     rows = half * keep
     if rest:
-        result, written = refs[8:]
+        result, written = refs[5:]
         part = lax.axis_index("rcv") % 2
         pieces = max(1, half // 4)
         at = pl.multiple_of(part * rows, rows)
@@ -170,30 +169,29 @@
         [slabs[2 * half * t + half : 2 * half * (t + 1)] for t in range(segments)], axis=0
     )
     usable = real < USABLE_BELOW
-    src_re[...] = jnp.where(usable, real, 0.0)
-    src_im[...] = jnp.where(usable, imag, 0.0)
+    for ref, value in ((src_re, real), (src_im, imag)):
+        value = jnp.where(usable, value, 0.0)
+        for block in range(nbins // LANES):
+            ref[block] = value[:, block * LANES : (block + 1) * LANES]
     src_valid = usable_rows(real)
-    total_re[...] = jnp.zeros_like(total_re)
-    total_im[...] = jnp.zeros_like(total_im)
-    cross_b[...] = jnp.zeros_like(cross_b)
-
     kind = rcv_re.dtype
     groups = total_groups(segments, kind)
 
-    def spread(row):
-        tile = jnp.broadcast_to(row, (min(keep, 16), LANES)).astype(kind)
-        return jnp.concatenate([tile] * (keep // tile.shape[0]), axis=0)
-
-    def multiply(block, cross):
-        for sub in range(BLOCK // LANES):
-            at = pl.ds(pl.multiple_of(block * BLOCK + sub * LANES, LANES), LANES)
+    def spread(ref, block, row):
+        tile = ref[block, pl.ds(row, 8, stride=0), :]
+        return jnp.concatenate([tile] * (keep // 8), axis=0).astype(kind)
+
+    def multiply(chunk):
+        for sub in range(CHUNK // LANES):
+            block = chunk * (CHUNK // LANES) + sub
+            at = slice(block * LANES, (block + 1) * LANES)
             r_re = [rcv_re[t * keep : (t + 1) * keep, at] for t in range(segments)]
             r_im = [rcv_im[t * keep : (t + 1) * keep, at] for t in range(segments)]
             for source in range(half):
                 real, imag = [], []
                 for t in range(segments):
-                    row = slice(t * half + source, t * half + source + 1)
-                    s_re, s_im = spread(src_re[row, at]), spread(src_im[row, at])
+                    row = t * half + source
+                    s_re, s_im = spread(src_re, block, row), spread(src_im, block, row)
                     real.append(s_re * r_re[t] + s_im * r_im[t])
                     imag.append(s_im * r_re[t] - s_re * r_im[t])
                 to = slice(source * keep, (source + 1) * keep)
@@ -201,30 +199,32 @@
                 for place, part in enumerate((real, imag)):
                     for group in range(groups):
                         value = functools.reduce(jnp.add, part[group * share : (group + 1) * share])
-                        first = (place * groups + group) * BLOCK + sub * LANES
-                        cross[to, first : first + LANES] = value
-
-    def project(block, cross):
-        value = cross[...].astype(jnp.bfloat16)
-        re_at = pl.ds(pl.multiple_of(block * BLOCK, BLOCK), BLOCK)
-        im_at = pl.ds(pl.multiple_of(nbins + block * BLOCK, BLOCK), BLOCK)
-        for first, at, total in ((0, re_at, total_re), (groups * BLOCK, im_at, total_im)):
-            total[...] += jnp.dot(
-                value[:, first : first + groups * BLOCK],
-                jnp.concatenate([table_ref[at, :]] * groups, axis=0),
-                preferred_element_type=jnp.float32,
+                        first = (place * groups + group) * CHUNK + sub * LANES
+                        cross[chunk, to, first : first + LANES] = value
+
+    def project(chunk):
+        value = cross[chunk].astype(jnp.bfloat16)
+        parts = []
+        for place in range(2):
+            first = place * nbins + chunk * CHUNK
+            table = table_ref[first : first + CHUNK]
+            parts.append(
+                jnp.dot(
+                    value[:, place * groups * CHUNK : (place + 1) * groups * CHUNK],
+                    jnp.concatenate([table] * groups, axis=0),
+                    preferred_element_type=jnp.float32,
+                )
             )
-
-    def two_blocks(pair, carry):
-        multiply(2 * pair, cross_a)
-        project(jnp.maximum(2 * pair - 1, 0), cross_b)
-        multiply(2 * pair + 1, cross_b)
-        project(2 * pair, cross_a)
-        return carry
-
-    pairs = nbins // (2 * BLOCK)
-    lax.fori_loop(0, pairs, two_blocks, 0)
-    project(2 * pairs - 1, cross_b)
+        return parts
+
+    parts = []
+    chunks = nbins // CHUNK
+    for chunk in range(chunks + 1):
+        if chunk < chunks:
+            multiply(chunk)
+        if chunk > 0:
+            parts.append(project(chunk - 1))
+    total_re, total_im = (functools.reduce(jnp.add, part) for part in zip(*parts))
 
     lags = result.shape[1]
     scale = 2.0 / math.sqrt(nbins)
@@ -317,10 +317,9 @@
     count, rows, lags = segments * half, half * keep, 2 * LAG + 1
     kind = receivers[0].dtype
     groups = total_groups(segments, kind)
-    part = pltpu.VMEM((count, nbins), jnp.float32)
-    cross = pltpu.VMEM((rows, 2 * groups * BLOCK), kind)
-    total = pltpu.VMEM((rows, BLOCK), jnp.float32)
-    scratch = [part, part, cross, cross, total, total]
+    part = pltpu.VMEM((nbins // LANES, count, LANES), jnp.float32)
+    cross = pltpu.VMEM((nbins // CHUNK, rows, 2 * groups * CHUNK), kind)
+    scratch = [part, part, cross]
     if rest:
         scratch += [pltpu.VMEM((rows, lags), jnp.float32), pltpu.SemaphoreType.DMA((1 + half,))]
     return pl.pallas_call(

time: 29.1 us -> 28 us (0.962)
  Pallas kernels: 8.64 us -> 7.52 us
    pallas_call x2, Pallas kernels: 5.71 us -> 4.58 us  [stack_half(): pl.pallas_call(functools.partial(stack_kernel, segments), out_shape=jax.S...]
  transfers between devices with their start and end apart: 11 -> 11, of which waited for: 5 -> 5; matrix products, arithmetic and copies ran while one was open for 0% -> 0% of each run, Pallas kernels for 12% -> 10%
where the time goes in v8:
time: 28 us; the launch traced here: 27.8 us
  starting transfers between devices  12.9 us (46%)
  Pallas kernels  7.52 us (27%)
  waiting for transfers between devices  7.26 us (26%)
    ppermute x11, starting transfers between devices, swapped(): return lax.ppermute(value, axis, [(i, i ^ step) for i in range(size)])  12.9 us
    ppermute x11, waiting for transfers between devices, swapped(): return lax.ppermute(value, axis, [(i, i ^ step) for i in range(size)])  7.26 us
    pallas_call x2, Pallas kernels, stack_half(): pl.pallas_call(functools.partial(stack_kernel, segments), out_shape=jax.S...  4.58 us
    pallas_call x1, Pallas kernels, encode(): pl.pallas_call(functools.partial(encode_kernel, segments), out_shape=(sla...  2.02 us
    pallas_call x1, Pallas kernels, whiten_blocks(): pl.pallas_call(functools.partial(whiten_kernel, segments), out_shape=(par...  0.92 us
  transfers between devices with their start and end apart: 11, of which 5 were waited for; matrix products, arithmetic and copies ran while one was open for 0% of the time, Pallas kernels for 10%

profile of v8, /device:TPU:0, one launch (start us, length us, event | category | flops | bytes accessed | tf_op | source)
XLA Modules:
  0.0 27.8 jit_solution(572829822473986712)
XLA Ops:
  0.0 0.0 copy-start
  0.0 2.0 %encode_and_pick.1 = (bf16[16,1536]{1,0:T(8,128)(2,1)S(1)}, bf16[16,1536]{1,0:T(8,128)(2,1)S(1)}, bf16[32,3072]{1,0:T(8,128)(2,1)S(1)}, bf16[32,3072]{1,0:T(8,12...) custom-call(bf16[128,3072]{1,0:T(8,128)(2,1)} %bitcast.3, s32[1,128]{1,0:T(1,128)} %bitcast.4, ...), custom_call_target="tpu_custom_call" | custom-call | tf_op jit(solution)/shard_map/encode_and_pick/pallas_call | solution.py:276
  2.0 4.0 %collective-permute-start.4 = (bf16[32,3072]{1,0:T(8,128)(2,1)S(1)}, bf16[32,3072]{1,0:T(8,128)(2,1)S(1)}, u32[]{:S(2)}, u32[]{:S(2)}) collective-permute-start(bf16[32,3072]{1,0:T(8,128)(2,1)S(1)} %get-tuple-element.31), channel_id=1, source_target_pairs={{0,3},{1,2},{2,1},{3,0},{4,7},{5,6},{6,5},{7,4},{8,11},{9,10},{10,... | collective-permute-start | bytes 589832 | tf_op jit(solution)/shard_map/ppermute | solution.py:340
  6.0 0.0 collective-permute-start
  6.0 1.2 %collective-permute-done = bf16[16,1536]{1,0:T(8,128)(2,1)S(1)} collective-permute-done((bf16[16,1536]{1,0:T(8,128)(2,1)S(1)}, bf16[16,1536]{1,0:T(8,128)(2,1)S(1)}, u32[]{:S(2)}, u32[]{:S(2)}) %collective-permute-start) | collective-permute-done | bytes 49184 | tf_op jit(solution)/shard_map/ppermute | solution.py:340
  7.2 1.6 %collective-permute-start.1 = (bf16[16,1536]{1,0:T(8,128)(2,1)S(1)}, bf16[16,1536]{1,0:T(8,128)(2,1)S(1)}, u32[]{:S(2)}, u32[]{:S(2)}) collective-permute-start(bf16[16,1536]{1,0:T(8,128)(2,1)S(1)} %add.12), channel_id=1, source_target_pairs={{0,8},{4,12},{8,0},{12,4},{16,24},{20,28},{24,16},{28,20},{1,9},{5... | collective-permute-start | bytes 147464 | tf_op jit(solution)/shard_map/ppermute | solution.py:340
  8.9 2.5 %collective-permute-start.3 = (bf16[16,1536]{1,0:T(8,128)(2,1)S(1)}, bf16[16,1536]{1,0:T(8,128)(2,1)S(1)}, u32[]{:S(2)}, u32[]{:S(2)}) collective-permute-start(bf16[16,1536]{1,0:T(8,128)(2,1)S(1)} %add.12), channel_id=1, source_target_pairs={{0,24},{4,28},{8,16},{12,20},{16,8},{20,12},{24,0},{28,4},{1,25},{... | collective-permute-start | bytes 147464 | tf_op jit(solution)/shard_map/ppermute | solution.py:340
  11.4 0.1 collective-permute-start.2
  11.5 0.0 collective-permute-done.1
  11.5 0.5 %collective-permute-start.8 = (bf16[32,3072]{1,0:T(8,128)(2,1)S(1)}, bf16[32,3072]{1,0:T(8,128)(2,1)S(1)}, u32[]{:S(2)}, u32[]{:S(2)}) collective-permute-start(bf16[32,3072]{1,0:T(8,128)(2,1)S(1)} %get-tuple-element.34), channel_id=1, source_target_pairs={{0,1},{1,0},{2,3},{3,2},{4,5},{5,4},{6,7},{7,6},{8,9},{9,8},{10,11... | collective-permute-start | bytes 589832 | tf_op jit(solution)/shard_map/ppermute | solution.py:340
  12.0 0.5 %collective-permute-start.9 = (bf16[32,3072]{1,0:T(8,128)(2,1)S(1)}, bf16[32,3072]{1,0:T(8,128)(2,1)S(1)}, u32[]{:S(2)}, u32[]{:S(2)}) collective-permute-start(bf16[32,3072]{1,0:T(8,128)(2,1)S(1)} %get-tuple-element.35), channel_id=1, source_target_pairs={{0,2},{1,3},{2,0},{3,1},{4,6},{5,7},{6,4},{7,5},{8,10},{9,11},{10,... | collective-permute-start | bytes 589832 | tf_op jit(solution)/shard_map/ppermute | solution.py:340
  12.5 2.5 %collective-permute-done.3 = bf16[16,1536]{1,0:T(8,128)(2,1)S(1)} collective-permute-done((bf16[16,1536]{1,0:T(8,128)(2,1)S(1)}, bf16[16,1536]{1,0:T(8,128)(2,1)S(1)}, u32[]{:S(2)}, u32[]{:S(2)}) %collective-permute-start.3) | collective-permute-done | bytes 49184 | tf_op jit(solution)/shard_map/ppermute | solution.py:340
  15.0 0.0 collective-permute-done.4.refs_3_
  15.0 1.9 %collective-permute-done.2 = bf16[16,1536]{1,0:T(8,128)(2,1)S(1)} collective-permute-done((bf16[16,1536]{1,0:T(8,128)(2,1)S(1)}, bf16[16,1536]{1,0:T(8,128)(2,1)S(1)}, u32[]{:S(2)}, u32[]{:S(2)}) %collective-permute-start.2) | collective-permute-done | bytes 49184 | tf_op jit(solution)/shard_map/ppermute | solution.py:340
  16.9 0.5 %collective-permute-start.7 = (bf16[16,1536]{1,0:T(8,128)(2,1)S(1)}, bf16[16,1536]{1,0:T(8,128)(2,1)S(1)}, u32[]{:S(2)}, u32[]{:S(2)}) collective-permute-start(bf16[16,1536]{1,0:T(8,128)(2,1)S(1)} %add_add_fusion), channel_id=1, source_target_pairs={{0,3},{1,2},{2,1},{3,0},{4,7},{5,6},{6,5},{7,4},{8,11},{9,10},{10,... | collective-permute-start | bytes 147464 | tf_op jit(solution)/shard_map/ppermute | solution.py:340
  17.4 1.5 %collective-permute-start.6 = (bf16[16,1536]{1,0:T(8,128)(2,1)S(1)}, bf16[16,1536]{1,0:T(8,128)(2,1)S(1)}, u32[]{:S(2)}, u32[]{:S(2)}) collective-permute-start(bf16[16,1536]{1,0:T(8,128)(2,1)S(1)} %add_add_fusion), channel_id=1, source_target_pairs={{0,2},{1,3},{2,0},{3,1},{4,6},{5,7},{6,4},{7,5},{8,10},{9,11},{10,... | collective-permute-start | bytes 147464 | tf_op jit(solution)/shard_map/ppermute | solution.py:340
  19.0 1.5 %collective-permute-start.5 = (bf16[16,1536]{1,0:T(8,128)(2,1)S(1)}, bf16[16,1536]{1,0:T(8,128)(2,1)S(1)}, u32[]{:S(2)}, u32[]{:S(2)}) collective-permute-start(bf16[16,1536]{1,0:T(8,128)(2,1)S(1)} %add_add_fusion), channel_id=1, source_target_pairs={{0,1},{1,0},{2,3},{3,2},{4,5},{5,4},{6,7},{7,6},{8,9},{9,8},{10,11... | collective-permute-start | bytes 147464 | tf_op jit(solution)/shard_map/ppermute | solution.py:340
  20.4 0.0 collective-permute-done.8.refs_1_
  20.4 0.0 collective-permute-done.9.refs_2_
  20.5 0.9 %whiten_receivers.1 = (bf16[128,1536]{1,0:T(8,128)(2,1)S(1)}, bf16[128,1536]{1,0:T(8,128)(2,1)S(1)}, f32[128,128]{1,0:T(8,128)S(1)}) custom-call(bf16[32,3072]{1,0:T(8,128)(2,1)S(1)} %get-tuple-element.33.refs_0_, bf16[32,3072]{1,0:T(8,128)(2,1)S(1)} %collective-permute-done.8.refs_1_, bf16[32,3072]{1,0:T(8,128)(2,1)S(1)} %collective-permute-done.9.refs_2_, ...), custom_call_target="tpu_custom_call" | custom-call | flops 402653184 | bytes 1572864 | tf_op jit(solution)/shard_map/whiten_receivers/pallas_call | solution.py:300
  21.4 0.7 %collective-permute-done.7 = bf16[16,1536]{1,0:T(8,128)(2,1)S(1)} collective-permute-done((bf16[16,1536]{1,0:T(8,128)(2,1)S(1)}, bf16[16,1536]{1,0:T(8,128)(2,1)S(1)}, u32[]{:S(2)}, u32[]{:S(2)}) %collective-permute-start.7) | collective-permute-done | bytes 49184 | tf_op jit(solution)/shard_map/ppermute | solution.py:340
  22.1 0.0 collective-permute-done.6
  22.1 1.0 %collective-permute-done.5 = bf16[16,1536]{1,0:T(8,128)(2,1)S(1)} collective-permute-done((bf16[16,1536]{1,0:T(8,128)(2,1)S(1)}, bf16[16,1536]{1,0:T(8,128)(2,1)S(1)}, u32[]{:S(2)}, u32[]{:S(2)}) %collective-permute-start.5) | collective-permute-done | bytes 49184 | tf_op jit(solution)/shard_map/ppermute | solution.py:340
  23.1 0.1 collective-permute-start.10
  23.2 0.0 copy-done
  23.2 1.9 %stack_own_half.1.refs_0_ = f32[256,301]{1,0:T(8,128)S(1)} custom-call(bf16[64,1536]{1,0:T(8,128)(2,1)S(1)} %constant_dynamic-update-slice_fusion.slabs_ref, bf16[128,1536]{1,0:T(8,128)(2,1)S(1)} %get-tuple-element.44.rcv_re, bf16[128,1536]{1,0:T(8,128)(2,1)S(1)} %get-tuple-element.45.rcv_im, f32[128,128]{1,0:T(8,128)S(1)} %get-tuple-element.46.rcv_valid, ...), custom_call_target="tpu_custom_call" | custom-call | flops 471859200 | bytes 3145728 | tf_op jit(solution)/shard_map/stack_own_half/pallas_call | solution.py:325
  25.1 0.0 collective-permute-done.10.slabs_ref
  25.1 2.7 %stack_other_half.1 = f32[512,301]{1,0:T(8,128)} custom-call(bf16[64,1536]{1,0:T(8,128)(2,1)S(1)} %collective-permute-done.10.slabs_ref, bf16[128,1536]{1,0:T(8,128)(2,1)S(1)} %get-tuple-element.44.rcv_re, bf16[128,1536]{1,0:T(8,128)(2,1)S(1)} %get-tuple-element.45.rcv_im, f32[128,128]{1,0:T(8,128)S(1)} %get-tuple-element.46.rcv_valid, ...), custom_call_target="tpu_custom_call" | custom-call | flops 471859200 | bytes 3145728 | tf_op jit(solution)/shard_map/stack_other_half/pallas_call | solution.py:325
  (6 shorter events, 0.0 us)
Async XLA Ops:
  0.0 23.2 %copy-start = (bf16[3072,256]{1,0:T(8,128)(2,1)S(1)}, bf16[3072,256]{1,0:T(8,128)(2,1)}, u32[]{:S(2)}) copy-start(bf16[3072,256]{1,0:T(8,128)(2,1)} %constant.2.clone.table_ref) | copy-start | bytes 4718596
  2.0 12.9 %collective-permute-start.4 = (bf16[32,3072]{1,0:T(8,128)(2,1)S(1)}, bf16[32,3072]{1,0:T(8,128)(2,1)S(1)}, u32[]{:S(2)}, u32[]{:S(2)}) collective-permute-start(bf16[32,3072]{1,0:T(8,128)(2,1)S(1)} %get-tuple-element.31), channel_id=1, source_target_pairs={{0,3},{1,2},{2,1},{3,0},{4,7},{5,6},{6,5},{7,4},{8,11},{9,10},{10,... | collective-permute-start | bytes 589832 | tf_op jit(solution)/shard_map/ppermute | solution.py:340
  6.0 1.2 %collective-permute-start = (bf16[16,1536]{1,0:T(8,128)(2,1)S(1)}, bf16[16,1536]{1,0:T(8,128)(2,1)S(1)}, u32[]{:S(2)}, u32[]{:S(2)}) collective-permute-start(bf16[16,1536]{1,0:T(8,128)(2,1)S(1)} %get-tuple-element.27), channel_id=1, source_target_pairs={{0,4},{4,0},{8,12},{12,8},{16,20},{20,16},{24,28},{28,24},{1,5},{5... | collective-permute-start | bytes 147464 | tf_op jit(solution)/shard_map/ppermute | solution.py:340
  7.2 4.2 %collective-permute-start.1 = (bf16[16,1536]{1,0:T(8,128)(2,1)S(1)}, bf16[16,1536]{1,0:T(8,128)(2,1)S(1)}, u32[]{:S(2)}, u32[]{:S(2)}) collective-permute-start(bf16[16,1536]{1,0:T(8,128)(2,1)S(1)} %add.12), channel_id=1, source_target_pairs={{0,8},{4,12},{8,0},{12,4},{16,24},{20,28},{24,16},{28,20},{1,9},{5... | collective-permute-start | bytes 147464 | tf_op jit(solution)/shard_map/ppermute | solution.py:340
  8.9 6.1 %collective-permute-start.3 = (bf16[16,1536]{1,0:T(8,128)(2,1)S(1)}, bf16[16,1536]{1,0:T(8,128)(2,1)S(1)}, u32[]{:S(2)}, u32[]{:S(2)}) collective-permute-start(bf16[16,1536]{1,0:T(8,128)(2,1)S(1)} %add.12), channel_id=1, source_target_pairs={{0,24},{4,28},{8,16},{12,20},{16,8},{20,12},{24,0},{28,4},{1,25},{... | collective-permute-start | bytes 147464 | tf_op jit(solution)/shard_map/ppermute | solution.py:340
  11.4 5.5 %collective-permute-start.2 = (bf16[16,1536]{1,0:T(8,128)(2,1)S(1)}, bf16[16,1536]{1,0:T(8,128)(2,1)S(1)}, u32[]{:S(2)}, u32[]{:S(2)}) collective-permute-start(bf16[16,1536]{1,0:T(8,128)(2,1)S(1)} %add.12), channel_id=1, source_target_pairs={{0,16},{4,20},{8,24},{12,28},{16,0},{20,4},{24,8},{28,12},{1,17},{... | collective-permute-start | bytes 147464 | tf_op jit(solution)/shard_map/ppermute | solution.py:340
  11.5 9.0 %collective-permute-start.8 = (bf16[32,3072]{1,0:T(8,128)(2,1)S(1)}, bf16[32,3072]{1,0:T(8,128)(2,1)S(1)}, u32[]{:S(2)}, u32[]{:S(2)}) collective-permute-start(bf16[32,3072]{1,0:T(8,128)(2,1)S(1)} %get-tuple-element.34), channel_id=1, source_target_pairs={{0,1},{1,0},{2,3},{3,2},{4,5},{5,4},{6,7},{7,6},{8,9},{9,8},{10,11... | collective-permute-start | bytes 589832 | tf_op jit(solution)/shard_map/ppermute | solution.py:340
  12.0 8.4 %collective-permute-start.9 = (bf16[32,3072]{1,0:T(8,128)(2,1)S(1)}, bf16[32,3072]{1,0:T(8,128)(2,1)S(1)}, u32[]{:S(2)}, u32[]{:S(2)}) collective-permute-start(bf16[32,3072]{1,0:T(8,128)(2,1)S(1)} %get-tuple-element.35), channel_id=1, source_target_pairs={{0,2},{1,3},{2,0},{3,1},{4,6},{5,7},{6,4},{7,5},{8,10},{9,11},{10,... | collective-permute-start | bytes 589832 | tf_op jit(solution)/shard_map/ppermute | solution.py:340
  16.9 5.2 %collective-permute-start.7 = (bf16[16,1536]{1,0:T(8,128)(2,1)S(1)}, bf16[16,1536]{1,0:T(8,128)(2,1)S(1)}, u32[]{:S(2)}, u32[]{:S(2)}) collective-permute-start(bf16[16,1536]{1,0:T(8,128)(2,1)S(1)} %add_add_fusion), channel_id=1, source_target_pairs={{0,3},{1,2},{2,1},{3,0},{4,7},{5,6},{6,5},{7,4},{8,11},{9,10},{10,... | collective-permute-start | bytes 147464 | tf_op jit(solution)/shard_map/ppermute | solution.py:340
  17.4 4.6 %collective-permute-start.6 = (bf16[16,1536]{1,0:T(8,128)(2,1)S(1)}, bf16[16,1536]{1,0:T(8,128)(2,1)S(1)}, u32[]{:S(2)}, u32[]{:S(2)}) collective-permute-start(bf16[16,1536]{1,0:T(8,128)(2,1)S(1)} %add_add_fusion), channel_id=1, source_target_pairs={{0,2},{1,3},{2,0},{3,1},{4,6},{5,7},{6,4},{7,5},{8,10},{9,11},{10,... | collective-permute-start | bytes 147464 | tf_op jit(solution)/shard_map/ppermute | solution.py:340
  19.0 4.1 %collective-permute-start.5 = (bf16[16,1536]{1,0:T(8,128)(2,1)S(1)}, bf16[16,1536]{1,0:T(8,128)(2,1)S(1)}, u32[]{:S(2)}, u32[]{:S(2)}) collective-permute-start(bf16[16,1536]{1,0:T(8,128)(2,1)S(1)} %add_add_fusion), channel_id=1, source_target_pairs={{0,1},{1,0},{2,3},{3,2},{4,5},{5,4},{6,7},{7,6},{8,9},{9,8},{10,11... | collective-permute-start | bytes 147464 | tf_op jit(solution)/shard_map/ppermute | solution.py:340
  23.1 2.0 %collective-permute-start.10 = (bf16[64,1536]{1,0:T(8,128)(2,1)S(1)}, bf16[64,1536]{1,0:T(8,128)(2,1)S(1)}, u32[]{:S(2)}, u32[]{:S(2)}) collective-permute-start(bf16[64,1536]{1,0:T(8,128)(2,1)S(1)} %constant_dynamic-update-slice_fusion.slabs_ref), channel_id=1, source_target_pairs={{0,4},{4,0},{8,12},{12,8},{16,20},{20,16},{24,28},{28,24},{1,5},{5... | collective-permute-start | bytes 589832 | tf_op jit(solution)/shard_map/ppermute | solution.py:340

commit v9 on v8

--- a/solution.py
+++ b/solution.py
@@ -86,7 +86,7 @@
 
 
 def encode_kernel(
-    segments, spectra_ref, valid_ref, sources_ref, own_ref, other_ref, *refs
+    segments, spectra_ref, valid_ref, sources_ref, picked_ref, *refs
 ):
     blocks, refs = refs[:segments], refs[segments:]
     encoded_ref, spectra, valid, sources, high, low, arrived = refs
@@ -100,26 +100,24 @@
     channels, width = spectra_ref.shape
     nbins = width // 2
     rounds, per_round = sources.shape
-    half = rounds * per_round // 2
-    index = lax.axis_index("rcv")
+    count = rounds * per_round
+    first_channel = lax.axis_index("rcv") * channels
     copies[1].wait()
     copies[2].wait()
     diagonal = iota((channels, channels), 0) == iota((channels, channels), 1)
     usable = jnp.sum(jnp.where(diagonal, valid[...], 0), axis=1, keepdims=True) != 0
-    row = iota((2 * half, channels), 0)
-    local = jnp.zeros((2 * half, channels), jnp.int32)
-    for place in range(2 * half):
-        number = (index % 2 if place < half else 1 - index % 2) * half + place % half
-        here = sources[number // per_round, number % per_round] - index * channels
+    row = iota((count, channels), 0)
+    local = jnp.zeros((count, channels), jnp.int32)
+    for place in range(count):
+        here = sources[place // per_round, place % per_round] - first_channel
         local = jnp.where(row == place, here, local)
-    onehot = jnp.where(local == iota((2 * half, channels), 1), 1.0, 0.0).astype(jnp.bfloat16)
+    onehot = jnp.where(local == iota((count, channels), 1), 1.0, 0.0).astype(jnp.bfloat16)
     copies[0].wait()
     encoded = jnp.where(usable, spectra[...].astype(jnp.float32), UNUSABLE).astype(jnp.bfloat16)
     picked = jnp.dot(onehot, encoded, preferred_element_type=jnp.float32)
     for at, re, im in whitening(picked[:, :nbins], picked[:, nbins:], high, low, UNUSABLE):
-        for first, ref in ((0, own_ref), (half, other_ref)):
-            rows = slice(first, first + half)
-            ref[:, at] = jnp.concatenate([re[rows], im[rows]], axis=0).astype(ref.dtype)
+        picked_ref[:count, at] = re.astype(picked_ref.dtype)
+        picked_ref[count:, at] = im.astype(picked_ref.dtype)
     encoded_ref[...] = encoded.astype(encoded_ref.dtype)
     keep = channels // segments
     for step, block in enumerate(blocks):
@@ -143,24 +141,14 @@
 
 
 def stack_kernel(
-    segments, slabs_ref, rcv_re, rcv_im, rcv_valid, table_ref, *refs
+    segments, slabs_ref, rcv_re, rcv_im, rcv_valid, table_ref, out_ref,
+    src_re, src_im, cross, result, written
 ):
-    *rest, out_ref, src_re, src_im, cross = refs[: 5 if len(refs) == 7 else 4]
     half = slabs_ref.shape[0] // (2 * segments)
     nbins = slabs_ref.shape[1]
     keep = rcv_re.shape[0] // segments
-    rows = half * keep
-    if rest:
-        result, written = refs[5:]
-        part = lax.axis_index("rcv") % 2
-        pieces = max(1, half // 4)
-        at = pl.multiple_of(part * rows, rows)
-        copies = [
-            pltpu.make_async_copy(rest[0], out_ref.at[pl.ds(at, rows)], written.at[0])
-        ]
-        copies[0].start()
-    else:
-        result = out_ref
+    pieces = max(1, half // 8)
+    copies = []
     slabs = slabs_ref[...].astype(jnp.float32)
     real = jnp.concatenate(
         [slabs[2 * half * t : 2 * half * t + half] for t in range(segments)], axis=0
@@ -250,34 +238,30 @@
             last = min(first + LANES, lags - LANES)
             value = ahead[:, first : first + LANES] * weight
             result[to, LANES + first : LANES + last] = value[:, : last - first]
-        if rest and (source + 1) % pieces == 0:
-            first, count = (source + 1 - pieces) * keep, pieces * keep
-            at = pl.multiple_of((1 - part) * rows + first, count)
+        if (source + 1) % pieces == 0:
+            at = pl.ds((source + 1 - pieces) * keep, pieces * keep)
             copies.append(
                 pltpu.make_async_copy(
-                    result.at[pl.ds(first, count)],
-                    out_ref.at[pl.ds(at, count)],
-                    written.at[1 + source // pieces],
+                    result.at[at], out_ref.at[at], written.at[source // pieces]
                 )
             )
             copies[-1].start()
-    if rest:
-        for copy in copies:
-            copy.wait()
+    for copy in copies:
+        copy.wait()
 
 
 def encode(segments, spectra, valid, sources):
     channels, width = spectra.shape
     keep = channels // segments
-    slab = jax.ShapeDtypeStruct((sources.size, width // 2), jnp.bfloat16)
+    slab = jax.ShapeDtypeStruct((2 * sources.size, width // 2), jnp.bfloat16)
     block = jax.ShapeDtypeStruct((keep, width), jnp.bfloat16)
     padded = pltpu.VMEM((sources.size, width // 2 + 2 * LANES), jnp.bfloat16)
     pinned = [pltpu.with_memory_space_constraint(x, pltpu.HBM) for x in (spectra, valid, sources)]
     return pl.pallas_call(
         functools.partial(encode_kernel, segments),
-        out_shape=(slab, slab) + (block,) * segments,
+        out_shape=(slab,) + (block,) * segments,
         in_specs=[HBM] * 3,
-        out_specs=(VMEM,) * (2 + segments),
+        out_specs=(VMEM,) * (1 + segments),
         scratch_shapes=[
             pltpu.VMEM((channels, width), kind_for(keep)),
             pltpu.VMEM((channels, width), jnp.bfloat16),
@@ -311,29 +295,32 @@
     )(*blocks)
 
 
-def stack_half(segments, slabs, receivers, table, rest=()):
-    half, nbins = slabs.shape[0] // (2 * segments), slabs.shape[1]
+def stack_all(segments, slabs, receivers, table):
+    count, nbins = slabs.shape[0] // 2, slabs.shape[1]
     keep = receivers[0].shape[0] // segments
-    count, rows, lags = segments * half, half * keep, 2 * LAG + 1
+    sources = count // segments
+    rows, lags = sources * keep, 2 * LAG + 1
     kind = receivers[0].dtype
     groups = total_groups(segments, kind)
     part = pltpu.VMEM((nbins // LANES, count, LANES), jnp.float32)
-    cross = pltpu.VMEM((nbins // CHUNK, rows, 2 * groups * CHUNK), kind)
-    scratch = [part, part, cross]
-    if rest:
-        scratch += [pltpu.VMEM((rows, lags), jnp.float32), pltpu.SemaphoreType.DMA((1 + half,))]
     return pl.pallas_call(
         functools.partial(stack_kernel, segments),
-        out_shape=jax.ShapeDtypeStruct((2 * rows if rest else rows, lags), jnp.float32),
-        in_specs=[VMEM] * (5 + len(rest)),
-        out_specs=HBM if rest else VMEM,
-        scratch_shapes=scratch,
-        compiler_params=pltpu.CompilerParams(vmem_limit_bytes=20 * MEBI),
+        out_shape=jax.ShapeDtypeStruct((rows, lags), jnp.float32),
+        in_specs=[VMEM] * 5,
+        out_specs=HBM,
+        scratch_shapes=[
+            part,
+            part,
+            pltpu.VMEM((nbins // CHUNK, rows, 2 * groups * CHUNK), kind),
+            pltpu.VMEM((rows, lags), jnp.float32),
+            pltpu.SemaphoreType.DMA((sources,)),
+        ],
+        compiler_params=pltpu.CompilerParams(vmem_limit_bytes=28 * MEBI),
         cost_estimate=pl.CostEstimate(
             flops=4 * rows * nbins * 2 * LAG, bytes_accessed=nbins * 2048, transcendentals=0
         ),
-        name="stack_other_half" if rest else "stack_own_half",
-    )(slabs, *receivers, table, *rest)
+        name="stack_sources",
+    )(slabs, *receivers, table)
 
 
 def swapped(value, axis, size, step):
@@ -344,15 +331,26 @@
     channels, _, width = spectra.shape
     keep = channels // tm_size
     rounds, per_round = sources.shape
-    own, other, *receivers = encode(
+    picked, *receivers = encode(
         tm_size, spectra[:, 0, :], valid.reshape(1, channels), sources
     )
+    axes = ("rcv", "tm")
+    seconds = range(1, rcv_size, 2)
+
+    def among_seconds(value, rcv_step, tm_step):
+        pairs = [
+            (rcv * tm_size + tm, (rcv ^ rcv_step) * tm_size + (tm ^ tm_step))
+            for rcv in seconds
+            for tm in range(tm_size)
+        ]
+        return lax.ppermute(value, axes, pairs)
+
     receivers[-1] = swapped(receivers[-1], "tm", tm_size, tm_size - 1)
-    own = own + swapped(other, "rcv", rcv_size, 1)
+    own = picked + lax.ppermute(picked, "rcv", [(rcv - 1, rcv) for rcv in seconds])
     step = 2
     while step < rcv_size:
         wide = min(4, rcv_size // step)
-        parts = [swapped(own, "rcv", rcv_size, place * step) for place in range(wide - 1, 0, -1)]
+        parts = [among_seconds(own, place * step, 0) for place in range(wide - 1, 0, -1)]
         if step == 2:
             parts[-1], later = lax.optimization_barrier((parts[-1], receivers[1:-1]))
             receivers[1:-1] = [
@@ -361,15 +359,14 @@
             parts[0], receivers[-1] = lax.optimization_barrier((parts[0], receivers[-1]))
         own = functools.reduce(jnp.add, parts[::-1], own)
         step *= wide
-    own = [own] + [swapped(own, "tm", tm_size, place) for place in range(1, tm_size)]
+    own = [own] + [among_seconds(own, 0, place) for place in range(1, tm_size)]
     whitened = whiten_blocks(receivers)
     own, whitened = lax.optimization_barrier((own, whitened))
     own = jnp.concatenate(own, axis=0)
-    other = swapped(own, "rcv", rcv_size, 1)
-
-    table = jnp.asarray(lag_table(width // 2))
-    first = stack_half(tm_size, own, whitened, table)
-    stack = stack_half(tm_size, other, whitened, table, (first,))
+    handed = lax.ppermute(own, "rcv", [(rcv, rcv - 1) for rcv in seconds])
+    own = jnp.where(lax.axis_index("rcv") % 2 == 1, own, handed)
+
+    stack = stack_all(tm_size, own, whitened, jnp.asarray(lag_table(width // 2)))
     return stack.reshape(rounds, per_round, keep, 2 * LAG + 1)
 
 

time: 28 us -> 40 us (1.43)
  waiting for transfers between devices: 7.26 us -> 19.7 us
  starting transfers between devices: 12.9 us -> 12.5 us
    ppermute x0 -> x8, waiting for transfers between devices: none -> 16.9 us  [the longest x1 16.9 us: shards(): handed = lax.ppermute(own, 'rcv', [(rcv, rcv - 1) for rcv in seconds])]
    ppermute x11 -> x3, starting transfers between devices: 12.9 us -> 4.82 us  [swapped(): return lax.ppermute(value, axis, [(i, i ^ step) for i in range(size)])]
    ppermute x0 -> x8, starting transfers between devices: none -> 7.66 us  [the longest x6 4 us: among_seconds(): return lax.ppermute(value, axes, pairs)]
    ppermute x11 -> x3, waiting for transfers between devices: 7.26 us -> 2.73 us  [swapped(): return lax.ppermute(value, axis, [(i, i ^ step) for i in range(size)])]
    pallas_call x2 -> x1, Pallas kernels: 4.58 us -> 4.42 us  [stack_all(): pl.pallas_call(functools.partial(stack_kernel, segments), out_shape=jax.S...]
  transfers between devices with their start and end apart: 11 -> 11, of which waited for: 5 -> 4; matrix products, arithmetic and copies ran while one was open for 0% -> 0% of each run, Pallas kernels for 10% -> 2%
where the time goes in v9:
time: 40 us; the launch traced here: 39.7 us
  waiting for transfers between devices  19.7 us (49%)
  starting transfers between devices  12.5 us (31%)
  Pallas kernels  7.21 us (18%)
    ppermute x1, waiting for transfers between devices, shards(): handed = lax.ppermute(own, 'rcv', [(rcv, rcv - 1) for rcv in seconds])  16.9 us
    ppermute x3, starting transfers between devices, swapped(): return lax.ppermute(value, axis, [(i, i ^ step) for i in range(size)])  4.82 us
    pallas_call x1, Pallas kernels, stack_all(): pl.pallas_call(functools.partial(stack_kernel, segments), out_shape=jax.S...  4.42 us
    ppermute x6, starting transfers between devices, among_seconds(): return lax.ppermute(value, axes, pairs)  4 us
    ppermute x3, waiting for transfers between devices, swapped(): return lax.ppermute(value, axis, [(i, i ^ step) for i in range(size)])  2.73 us
    ppermute x1, starting transfers between devices, shards(): lax.ppermute(picked, 'rcv', [(rcv - 1, rcv) for rcv in seconds])  2.36 us
    pallas_call x1, Pallas kernels, encode(): pl.pallas_call(functools.partial(encode_kernel, segments), out_shape=(sla...  1.87 us
    ppermute x1, starting transfers between devices, shards(): handed = lax.ppermute(own, 'rcv', [(rcv, rcv - 1) for rcv in seconds])  1.29 us
  transfers between devices with their start and end apart: 11, of which 4 were waited for; matrix products, arithmetic and copies ran while one was open for 0% of the time, Pallas kernels for 2%

profile of v9, /device:TPU:0, one launch (start us, length us, event | category | flops | bytes accessed | tf_op | source)
XLA Modules:
  0.0 39.7 jit_solution(8256263208779593742)
XLA Ops:
  0.0 1.9 %encode_and_pick.1 = (bf16[32,1536]{1,0:T(8,128)(2,1)S(1)}, bf16[32,3072]{1,0:T(8,128)(2,1)S(1)}, bf16[32,3072]{1,0:T(8,128)(2,1)S(1)}, bf16[32,3072]{1,0:T(8,128)(2,1)S(1)}, bf16[32,3072]{1,0:T(8,128)(2,1)S(1)}) custom-call(bf16[128,3072]{1,0:T(8,128)(2,1)} %bitcast.3, s32[1,128]{1,0:T(1,128)} %bitcast.4, s32[2,8]{1,0:T(2,128)} %sources_ref.1), custom_call_target="tpu_custom_call" | custom-call | tf_op jit(solution)/shard_map/encode_and_pick/pallas_call | solution.py:260
  1.9 2.4 %collective-permute-start = (bf16[32,1536]{1,0:T(8,128)(2,1)S(1)}, bf16[32,1536]{1,0:T(8,128)(2,1)S(1)}, u32[]{:S(2)}, u32[]{:S(2)}) collective-permute-start(bf16[32,1536]{1,0:T(8,128)(2,1)S(1)} %get-tuple-element.25), channel_id=1, source_target_pairs={{0,4},{8,12},{16,20},{24,28},{1,5},{9,13},{17,21},{25,29},{2,6},{1... | collective-permute-start | bytes 294920 | tf_op jit(solution)/shard_map/ppermute | solution.py:349
  4.3 3.3 %collective-permute-start.4 = (bf16[32,3072]{1,0:T(8,128)(2,1)S(1)}, bf16[32,3072]{1,0:T(8,128)(2,1)S(1)}, u32[]{:S(2)}, u32[]{:S(2)}) collective-permute-start(bf16[32,3072]{1,0:T(8,128)(2,1)S(1)} %get-tuple-element.29), channel_id=1, source_target_pairs={{0,3},{1,2},{2,1},{3,0},{4,7},{5,6},{6,5},{7,4},{8,11},{9,10},{10,... | collective-permute-start | bytes 589832 | tf_op jit(solution)/shard_map/ppermute | solution.py:327
  7.6 0.0 collective-permute-done
  7.6 0.7 %collective-permute-start.1 = (bf16[32,1536]{1,0:T(8,128)(2,1)S(1)}, bf16[32,1536]{1,0:T(8,128)(2,1)S(1)}, u32[]{:S(2)}, u32[]{:S(2)}) collective-permute-start(bf16[32,1536]{1,0:T(8,128)(2,1)S(1)} %add.17), channel_id=1, source_target_pairs={{4,12},{5,13},{6,14},{7,15},{12,4},{13,5},{14,6},{15,7},{20,28},{2... | collective-permute-start | bytes 294920 | tf_op jit(solution)/shard_map/ppermute | solution.py:346
  8.3 0.7 %collective-permute-start.3 = (bf16[32,1536]{1,0:T(8,128)(2,1)S(1)}, bf16[32,1536]{1,0:T(8,128)(2,1)S(1)}, u32[]{:S(2)}, u32[]{:S(2)}) collective-permute-start(bf16[32,1536]{1,0:T(8,128)(2,1)S(1)} %add.17), channel_id=1, source_target_pairs={{4,28},{5,29},{6,30},{7,31},{12,20},{13,21},{14,22},{15,23},{20,12... | collective-permute-start | bytes 294920 | tf_op jit(solution)/shard_map/ppermute | solution.py:346
  9.0 0.7 %collective-permute-start.2 = (bf16[32,1536]{1,0:T(8,128)(2,1)S(1)}, bf16[32,1536]{1,0:T(8,128)(2,1)S(1)}, u32[]{:S(2)}, u32[]{:S(2)}) collective-permute-start(bf16[32,1536]{1,0:T(8,128)(2,1)S(1)} %add.17), channel_id=1, source_target_pairs={{4,20},{5,21},{6,22},{7,23},{12,28},{13,29},{14,30},{15,31},{20,4}... | collective-permute-start | bytes 294920 | tf_op jit(solution)/shard_map/ppermute | solution.py:346
  9.7 0.0 collective-permute-done.1
  9.7 0.6 %collective-permute-start.8 = (bf16[32,3072]{1,0:T(8,128)(2,1)S(1)}, bf16[32,3072]{1,0:T(8,128)(2,1)S(1)}, u32[]{:S(2)}, u32[]{:S(2)}) collective-permute-start(bf16[32,3072]{1,0:T(8,128)(2,1)S(1)} %get-tuple-element.32), channel_id=1, source_target_pairs={{0,1},{1,0},{2,3},{3,2},{4,5},{5,4},{6,7},{7,6},{8,9},{9,8},{10,11... | collective-permute-start | bytes 589832 | tf_op jit(solution)/shard_map/ppermute | solution.py:327
  10.3 0.9 %collective-permute-start.9 = (bf16[32,3072]{1,0:T(8,128)(2,1)S(1)}, bf16[32,3072]{1,0:T(8,128)(2,1)S(1)}, u32[]{:S(2)}, u32[]{:S(2)}) collective-permute-start(bf16[32,3072]{1,0:T(8,128)(2,1)S(1)} %get-tuple-element.33), channel_id=1, source_target_pairs={{0,2},{1,3},{2,0},{3,1},{4,6},{5,7},{6,4},{7,5},{8,10},{9,11},{10,... | collective-permute-start | bytes 589832 | tf_op jit(solution)/shard_map/ppermute | solution.py:327
  11.1 0.0 collective-permute-done.3
  11.1 0.9 %collective-permute-done.4.refs_3_ = bf16[32,3072]{1,0:T(8,128)(2,1)S(1)} collective-permute-done((bf16[32,3072]{1,0:T(8,128)(2,1)S(1)}, bf16[32,3072]{1,0:T(8,128)(2,1)S(1)}, u32[]{:S(2)}, u32[]{:S(2)}) %collective-permute-start.4) | collective-permute-done | bytes 196640 | tf_op jit(solution)/shard_map/ppermute | solution.py:327
  12.0 0.0 collective-permute-done.2
  12.1 0.7 %collective-permute-start.7 = (bf16[32,1536]{1,0:T(8,128)(2,1)S(1)}, bf16[32,1536]{1,0:T(8,128)(2,1)S(1)}, u32[]{:S(2)}, u32[]{:S(2)}) collective-permute-start(bf16[32,1536]{1,0:T(8,128)(2,1)S(1)} %add_add_fusion), channel_id=1, source_target_pairs={{4,7},{5,6},{6,5},{7,4},{12,15},{13,14},{14,13},{15,12},{20,23},{2... | collective-permute-start | bytes 294920 | tf_op jit(solution)/shard_map/ppermute | solution.py:346
  12.8 0.7 %collective-permute-start.6 = (bf16[32,1536]{1,0:T(8,128)(2,1)S(1)}, bf16[32,1536]{1,0:T(8,128)(2,1)S(1)}, u32[]{:S(2)}, u32[]{:S(2)}) collective-permute-start(bf16[32,1536]{1,0:T(8,128)(2,1)S(1)} %add_add_fusion), channel_id=1, source_target_pairs={{4,6},{5,7},{6,4},{7,5},{12,14},{13,15},{14,12},{15,13},{20,22},{2... | collective-permute-start | bytes 294920 | tf_op jit(solution)/shard_map/ppermute | solution.py:346
  13.4 0.7 %collective-permute-start.5 = (bf16[32,1536]{1,0:T(8,128)(2,1)S(1)}, bf16[32,1536]{1,0:T(8,128)(2,1)S(1)}, u32[]{:S(2)}, u32[]{:S(2)}) collective-permute-start(bf16[32,1536]{1,0:T(8,128)(2,1)S(1)} %add_add_fusion), channel_id=1, source_target_pairs={{4,5},{5,4},{6,7},{7,6},{12,13},{13,12},{14,15},{15,14},{20,21},{2... | collective-permute-start | bytes 294920 | tf_op jit(solution)/shard_map/ppermute | solution.py:346
  14.1 1.3 %collective-permute-done.8.refs_1_ = bf16[32,3072]{1,0:T(8,128)(2,1)S(1)} collective-permute-done((bf16[32,3072]{1,0:T(8,128)(2,1)S(1)}, bf16[32,3072]{1,0:T(8,128)(2,1)S(1)}, u32[]{:S(2)}, u32[]{:S(2)}) %collective-permute-start.8) | collective-permute-done | bytes 196640 | tf_op jit(solution)/shard_map/ppermute | solution.py:327
  15.4 0.5 %collective-permute-done.9.refs_2_ = bf16[32,3072]{1,0:T(8,128)(2,1)S(1)} collective-permute-done((bf16[32,3072]{1,0:T(8,128)(2,1)S(1)}, bf16[32,3072]{1,0:T(8,128)(2,1)S(1)}, u32[]{:S(2)}, u32[]{:S(2)}) %collective-permute-start.9) | collective-permute-done | bytes 196640 | tf_op jit(solution)/shard_map/ppermute | solution.py:327
  15.9 0.0 copy-start
  15.9 0.9 %whiten_receivers.1 = (bf16[128,1536]{1,0:T(8,128)(2,1)S(1)}, bf16[128,1536]{1,0:T(8,128)(2,1)S(1)}, f32[128,128]{1,0:T(8,128)S(1)}) custom-call(bf16[32,3072]{1,0:T(8,128)(2,1)S(1)} %get-tuple-element.31.refs_0_, bf16[32,3072]{1,0:T(8,128)(2,1)S(1)} %collective-permute-done.8.refs_1_, bf16[32,3072]{1,0:T(8,128)(2,1)S(1)} %collective-permute-done.9.refs_2_, ...), custom_call_target="tpu_custom_call" | custom-call | flops 402653184 | bytes 1572864 | tf_op jit(solution)/shard_map/whiten_receivers/pallas_call | solution.py:284
  16.9 0.0 collective-permute-done.7
  16.9 0.0 collective-permute-done.6
  16.9 0.0 collective-permute-done.5
  17.0 1.3 %collective-permute-start.10 = (bf16[128,1536]{1,0:T(8,128)(2,1)S(1)}, bf16[128,1536]{1,0:T(8,128)(2,1)S(1)}, u32[]{:S(2)}, u32[]{:S(2)}) collective-permute-start(bf16[128,1536]{1,0:T(8,128)(2,1)S(1)} %constant_dynamic-update-slice_fusion), channel_id=1, source_target_pairs={{4,0},{12,8},{20,16},{28,24},{5,1},{13,9},{21,17},{29,25},{6,2},{1... | collective-permute-start | bytes 1179656 | tf_op jit(solution)/shard_map/ppermute | solution.py:366
  18.3 16.9 %collective-permute-done.10 = bf16[128,1536]{1,0:T(8,128)(2,1)S(1)} collective-permute-done((bf16[128,1536]{1,0:T(8,128)(2,1)S(1)}, bf16[128,1536]{1,0:T(8,128)(2,1)S(1)}, u32[]{:S(2)}, u32[]{:S(2)}) %collective-permute-start.10) | collective-permute-done | bytes 393248 | tf_op jit(solution)/shard_map/ppermute | solution.py:366
  35.2 0.0 copy-done
  35.3 4.4 %stack_sources.1 = f32[512,301]{1,0:T(8,128)} custom-call(bf16[128,1536]{1,0:T(8,128)(2,1)S(1)} %broadcast_select_fusion.slabs_ref, bf16[128,1536]{1,0:T(8,128)(2,1)S(1)} %get-tuple-element.42.rcv_re, bf16[128,1536]{1,0:T(8,128)(2,1)S(1)} %get-tuple-element.43.rcv_im, f32[128,128]{1,0:T(8,128)S(1)} %get-tuple-element.44.rcv_valid, bf16[3072,256]{1,0:T(8,128)(2,1)S(1)} %copy-done), custom_call_target="tpu_custom_call" | custom-call | flops 943718400 | bytes 3145728 | tf_op jit(solution)/shard_map/stack_sources/pallas_call | solution.py:306
  (7 shorter events, 0.1 us)
Async XLA Ops:
  1.9 5.7 %collective-permute-start = (bf16[32,1536]{1,0:T(8,128)(2,1)S(1)}, bf16[32,1536]{1,0:T(8,128)(2,1)S(1)}, u32[]{:S(2)}, u32[]{:S(2)}) collective-permute-start(bf16[32,1536]{1,0:T(8,128)(2,1)S(1)} %get-tuple-element.25), channel_id=1, source_target_pairs={{0,4},{8,12},{16,20},{24,28},{1,5},{9,13},{17,21},{25,29},{2,6},{1... | collective-permute-start | bytes 294920 | tf_op jit(solution)/shard_map/ppermute | solution.py:349
  4.3 7.8 %collective-permute-start.4 = (bf16[32,3072]{1,0:T(8,128)(2,1)S(1)}, bf16[32,3072]{1,0:T(8,128)(2,1)S(1)}, u32[]{:S(2)}, u32[]{:S(2)}) collective-permute-start(bf16[32,3072]{1,0:T(8,128)(2,1)S(1)} %get-tuple-element.29), channel_id=1, source_target_pairs={{0,3},{1,2},{2,1},{3,0},{4,7},{5,6},{6,5},{7,4},{8,11},{9,10},{10,... | collective-permute-start | bytes 589832 | tf_op jit(solution)/shard_map/ppermute | solution.py:327
  7.6 2.0 %collective-permute-start.1 = (bf16[32,1536]{1,0:T(8,128)(2,1)S(1)}, bf16[32,1536]{1,0:T(8,128)(2,1)S(1)}, u32[]{:S(2)}, u32[]{:S(2)}) collective-permute-start(bf16[32,1536]{1,0:T(8,128)(2,1)S(1)} %add.17), channel_id=1, source_target_pairs={{4,12},{5,13},{6,14},{7,15},{12,4},{13,5},{14,6},{15,7},{20,28},{2... | collective-permute-start | bytes 294920 | tf_op jit(solution)/shard_map/ppermute | solution.py:346
  8.3 2.8 %collective-permute-start.3 = (bf16[32,1536]{1,0:T(8,128)(2,1)S(1)}, bf16[32,1536]{1,0:T(8,128)(2,1)S(1)}, u32[]{:S(2)}, u32[]{:S(2)}) collective-permute-start(bf16[32,1536]{1,0:T(8,128)(2,1)S(1)} %add.17), channel_id=1, source_target_pairs={{4,28},{5,29},{6,30},{7,31},{12,20},{13,21},{14,22},{15,23},{20,12... | collective-permute-start | bytes 294920 | tf_op jit(solution)/shard_map/ppermute | solution.py:346
  9.0 3.1 %collective-permute-start.2 = (bf16[32,1536]{1,0:T(8,128)(2,1)S(1)}, bf16[32,1536]{1,0:T(8,128)(2,1)S(1)}, u32[]{:S(2)}, u32[]{:S(2)}) collective-permute-start(bf16[32,1536]{1,0:T(8,128)(2,1)S(1)} %add.17), channel_id=1, source_target_pairs={{4,20},{5,21},{6,22},{7,23},{12,28},{13,29},{14,30},{15,31},{20,4}... | collective-permute-start | bytes 294920 | tf_op jit(solution)/shard_map/ppermute | solution.py:346
  9.7 5.7 %collective-permute-start.8 = (bf16[32,3072]{1,0:T(8,128)(2,1)S(1)}, bf16[32,3072]{1,0:T(8,128)(2,1)S(1)}, u32[]{:S(2)}, u32[]{:S(2)}) collective-permute-start(bf16[32,3072]{1,0:T(8,128)(2,1)S(1)} %get-tuple-element.32), channel_id=1, source_target_pairs={{0,1},{1,0},{2,3},{3,2},{4,5},{5,4},{6,7},{7,6},{8,9},{9,8},{10,11... | collective-permute-start | bytes 589832 | tf_op jit(solution)/shard_map/ppermute | solution.py:327
  10.3 5.7 %collective-permute-start.9 = (bf16[32,3072]{1,0:T(8,128)(2,1)S(1)}, bf16[32,3072]{1,0:T(8,128)(2,1)S(1)}, u32[]{:S(2)}, u32[]{:S(2)}) collective-permute-start(bf16[32,3072]{1,0:T(8,128)(2,1)S(1)} %get-tuple-element.33), channel_id=1, source_target_pairs={{0,2},{1,3},{2,0},{3,1},{4,6},{5,7},{6,4},{7,5},{8,10},{9,11},{10,... | collective-permute-start | bytes 589832 | tf_op jit(solution)/shard_map/ppermute | solution.py:327
  12.1 4.8 %collective-permute-start.7 = (bf16[32,1536]{1,0:T(8,128)(2,1)S(1)}, bf16[32,1536]{1,0:T(8,128)(2,1)S(1)}, u32[]{:S(2)}, u32[]{:S(2)}) collective-permute-start(bf16[32,1536]{1,0:T(8,128)(2,1)S(1)} %add_add_fusion), channel_id=1, source_target_pairs={{4,7},{5,6},{6,5},{7,4},{12,15},{13,14},{14,13},{15,12},{20,23},{2... | collective-permute-start | bytes 294920 | tf_op jit(solution)/shard_map/ppermute | solution.py:346
  12.8 4.1 %collective-permute-start.6 = (bf16[32,1536]{1,0:T(8,128)(2,1)S(1)}, bf16[32,1536]{1,0:T(8,128)(2,1)S(1)}, u32[]{:S(2)}, u32[]{:S(2)}) collective-permute-start(bf16[32,1536]{1,0:T(8,128)(2,1)S(1)} %add_add_fusion), channel_id=1, source_target_pairs={{4,6},{5,7},{6,4},{7,5},{12,14},{13,15},{14,12},{15,13},{20,22},{2... | collective-permute-start | bytes 294920 | tf_op jit(solution)/shard_map/ppermute | solution.py:346
  13.4 3.5 %collective-permute-start.5 = (bf16[32,1536]{1,0:T(8,128)(2,1)S(1)}, bf16[32,1536]{1,0:T(8,128)(2,1)S(1)}, u32[]{:S(2)}, u32[]{:S(2)}) collective-permute-start(bf16[32,1536]{1,0:T(8,128)(2,1)S(1)} %add_add_fusion), channel_id=1, source_target_pairs={{4,5},{5,4},{6,7},{7,6},{12,13},{13,12},{14,15},{15,14},{20,21},{2... | collective-permute-start | bytes 294920 | tf_op jit(solution)/shard_map/ppermute | solution.py:346
  15.9 19.3 %copy-start = (bf16[3072,256]{1,0:T(8,128)(2,1)S(1)}, bf16[3072,256]{1,0:T(8,128)(2,1)}, u32[]{:S(2)}) copy-start(bf16[3072,256]{1,0:T(8,128)(2,1)} %constant.22.clone.table_ref) | copy-start | bytes 4718596
  17.0 18.2 %collective-permute-start.10 = (bf16[128,1536]{1,0:T(8,128)(2,1)S(1)}, bf16[128,1536]{1,0:T(8,128)(2,1)S(1)}, u32[]{:S(2)}, u32[]{:S(2)}) collective-permute-start(bf16[128,1536]{1,0:T(8,128)(2,1)S(1)} %constant_dynamic-update-slice_fusion), channel_id=1, source_target_pairs={{4,0},{12,8},{20,16},{28,24},{5,1},{13,9},{21,17},{29,25},{6,2},{1... | collective-permute-start | bytes 1179656 | tf_op jit(solution)/shard_map/ppermute | solution.py:366

commit v10 on v8

--- a/solution.py
+++ b/solution.py
@@ -128,30 +128,28 @@
 
 
 def whiten_kernel(segments, *refs):
-    blocks, (real_ref, imag_ref, valid_ref, high, low) = refs[:segments], refs[segments:]
+    blocks, refs = refs[:segments], refs[segments:]
+    real_ref, imag_ref, both_ref, valid_ref, high, low = refs
     rows = jnp.concatenate([ref[...].astype(jnp.float32) for ref in blocks], axis=0)
     nbins = rows.shape[1] // 2
     real, imag = rows[:, :nbins], rows[:, nbins:]
     for at, re, im in whitening(real, imag, high, low):
-        real_ref[:, at] = re.astype(real_ref.dtype)
-        imag_ref[:, at] = im.astype(imag_ref.dtype)
+        real_ref[:, at] = re
+        imag_ref[:, at] = im
+        both_ref[:, at] = re + im
     valid_ref[...] = usable_rows(real)
 
 
-def total_groups(segments, kind):
-    return -(-segments // 2) if kind == jnp.bfloat16 and segments % 2 == 0 else 1
-
-
 def stack_kernel(
-    segments, slabs_ref, rcv_re, rcv_im, rcv_valid, table_ref, *refs
+    segments, slabs_ref, rcv_re, rcv_im, rcv_both, rcv_valid, table_ref, *refs
 ):
-    *rest, out_ref, src_re, src_im, cross = refs[: 5 if len(refs) == 7 else 4]
+    *rest, out_ref, src_re, src_diff, src_sum, cross = refs[: 6 if len(refs) == 8 else 5]
     half = slabs_ref.shape[0] // (2 * segments)
     nbins = slabs_ref.shape[1]
     keep = rcv_re.shape[0] // segments
     rows = half * keep
     if rest:
-        result, written = refs[5:]
+        result, written = refs[6:]
         part = lax.axis_index("rcv") % 2
         pieces = max(1, half // 4)
         at = pl.multiple_of(part * rows, rows)
@@ -169,49 +167,46 @@
         [slabs[2 * half * t + half : 2 * half * (t + 1)] for t in range(segments)], axis=0
     )
     usable = real < USABLE_BELOW
-    for ref, value in ((src_re, real), (src_im, imag)):
-        value = jnp.where(usable, value, 0.0)
+    real, imag = jnp.where(usable, real, 0.0), jnp.where(usable, imag, 0.0)
+    src_valid = jnp.where(usable[:, :LANES], 1.0, 0.0)
+    for ref, value in ((src_re, real), (src_diff, imag - real), (src_sum, imag + real)):
         for block in range(nbins // LANES):
             ref[block] = value[:, block * LANES : (block + 1) * LANES]
-    src_valid = usable_rows(real)
-    kind = rcv_re.dtype
-    groups = total_groups(segments, kind)
+    tile = min(keep, 16)
 
     def spread(ref, block, row):
-        tile = ref[block, pl.ds(row, 8, stride=0), :]
-        return jnp.concatenate([tile] * (keep // 8), axis=0).astype(kind)
+        return jnp.concatenate([ref[block, pl.ds(row, 8, stride=0), :]] * (tile // 8), axis=0)
 
     def multiply(chunk):
         for sub in range(CHUNK // LANES):
             block = chunk * (CHUNK // LANES) + sub
             at = slice(block * LANES, (block + 1) * LANES)
-            r_re = [rcv_re[t * keep : (t + 1) * keep, at] for t in range(segments)]
-            r_im = [rcv_im[t * keep : (t + 1) * keep, at] for t in range(segments)]
-            for source in range(half):
-                real, imag = [], []
-                for t in range(segments):
-                    row = t * half + source
-                    s_re, s_im = spread(src_re, block, row), spread(src_im, block, row)
-                    real.append(s_re * r_re[t] + s_im * r_im[t])
-                    imag.append(s_im * r_re[t] - s_re * r_im[t])
-                to = slice(source * keep, (source + 1) * keep)
-                share = segments // groups
-                for place, part in enumerate((real, imag)):
-                    for group in range(groups):
-                        value = functools.reduce(jnp.add, part[group * share : (group + 1) * share])
-                        first = (place * groups + group) * CHUNK + sub * LANES
-                        cross[chunk, to, first : first + LANES] = value
+            for first in range(0, keep, tile):
+                rows = [slice(t * keep + first, t * keep + first + tile) for t in range(segments)]
+                r_re = [rcv_re[row, at] for row in rows]
+                r_im = [rcv_im[row, at] for row in rows]
+                r_both = [rcv_both[row, at] for row in rows]
+                for source in range(half):
+                    p, q, w = [], [], []
+                    for t in range(segments):
+                        row = t * half + source
+                        p.append(spread(src_re, block, row) * r_both[t])
+                        q.append(spread(src_diff, block, row) * r_im[t])
+                        w.append(spread(src_sum, block, row) * r_re[t])
+                    p, q, w = (functools.reduce(jnp.add, part) for part in (p, q, w))
+                    to = slice(source * keep + first, source * keep + first + tile)
+                    lanes = slice(sub * LANES, (sub + 1) * LANES)
+                    cross[chunk, 0, to, lanes] = (p + q).astype(cross.dtype)
+                    cross[chunk, 1, to, lanes] = (w - p).astype(cross.dtype)
 
     def project(chunk):
-        value = cross[chunk].astype(jnp.bfloat16)
         parts = []
         for place in range(2):
             first = place * nbins + chunk * CHUNK
-            table = table_ref[first : first + CHUNK]
             parts.append(
                 jnp.dot(
-                    value[:, place * groups * CHUNK : (place + 1) * groups * CHUNK],
-                    jnp.concatenate([table] * groups, axis=0),
+                    cross[chunk, place].astype(jnp.bfloat16),
+                    table_ref[first : first + CHUNK],
                     preferred_element_type=jnp.float32,
                 )
             )
@@ -296,12 +291,12 @@
     segments, (keep, width) = len(blocks), blocks[0].shape
     count, nbins = segments * keep, width // 2
     padded = pltpu.VMEM((count, nbins + 2 * LANES), jnp.bfloat16)
-    part = jax.ShapeDtypeStruct((count, nbins), kind_for(keep))
+    part = jax.ShapeDtypeStruct((count, nbins), jnp.float32)
     return pl.pallas_call(
         functools.partial(whiten_kernel, segments),
-        out_shape=(part, part, jax.ShapeDtypeStruct((count, LANES), jnp.float32)),
+        out_shape=(part, part, part, jax.ShapeDtypeStruct((count, LANES), jnp.float32)),
         in_specs=[VMEM] * segments,
-        out_specs=(VMEM,) * 3,
+        out_specs=(VMEM,) * 4,
         scratch_shapes=[padded, padded],
         compiler_params=pltpu.CompilerParams(vmem_limit_bytes=20 * MEBI),
         cost_estimate=pl.CostEstimate(
@@ -315,17 +310,15 @@
     half, nbins = slabs.shape[0] // (2 * segments), slabs.shape[1]
     keep = receivers[0].shape[0] // segments
     count, rows, lags = segments * half, half * keep, 2 * LAG + 1
-    kind = receivers[0].dtype
-    groups = total_groups(segments, kind)
     part = pltpu.VMEM((nbins // LANES, count, LANES), jnp.float32)
-    cross = pltpu.VMEM((nbins // CHUNK, rows, 2 * groups * CHUNK), kind)
-    scratch = [part, part, cross]
+    cross = pltpu.VMEM((nbins // CHUNK, 2, rows, CHUNK), kind_for(keep))
+    scratch = [part, part, part, cross]
     if rest:
         scratch += [pltpu.VMEM((rows, lags), jnp.float32), pltpu.SemaphoreType.DMA((1 + half,))]
     return pl.pallas_call(
         functools.partial(stack_kernel, segments),
         out_shape=jax.ShapeDtypeStruct((2 * rows if rest else rows, lags), jnp.float32),
-        in_specs=[VMEM] * (5 + len(rest)),
+        in_specs=[VMEM] * (6 + len(rest)),
         out_specs=HBM if rest else VMEM,
         scratch_shapes=scratch,
         compiler_params=pltpu.CompilerParams(vmem_limit_bytes=20 * MEBI),

time: 28 us -> 28.3 us (1.011)
  Pallas kernels: 7.52 us -> 7.96 us
    pallas_call x2, Pallas kernels: 4.58 us -> 4.96 us  [stack_half(): pl.pallas_call(functools.partial(stack_kernel, segments), out_shape=jax.S...]
  transfers between devices with their start and end apart: 11 -> 11, of which waited for: 5 -> 5; matrix products, arithmetic and copies ran while one was open for 0% -> 0% of each run, Pallas kernels for 10% -> 11%
where the time goes in v10:
time: 28.3 us; the launch traced here: 28.2 us
  starting transfers between devices  12.9 us (46%)
  Pallas kernels  7.96 us (28%)
  waiting for transfers between devices  7.19 us (25%)
    ppermute x11, starting transfers between devices, swapped(): return lax.ppermute(value, axis, [(i, i ^ step) for i in range(size)])  12.9 us
    ppermute x11, waiting for transfers between devices, swapped(): return lax.ppermute(value, axis, [(i, i ^ step) for i in range(size)])  7.19 us
    pallas_call x2, Pallas kernels, stack_half(): pl.pallas_call(functools.partial(stack_kernel, segments), out_shape=jax.S...  4.96 us
    pallas_call x1, Pallas kernels, encode(): pl.pallas_call(functools.partial(encode_kernel, segments), out_shape=(sla...  2.02 us
    pallas_call x1, Pallas kernels, whiten_blocks(): pl.pallas_call(functools.partial(whiten_kernel, segments), out_shape=(par...  0.98 us
  transfers between devices with their start and end apart: 11, of which 5 were waited for; matrix products, arithmetic and copies ran while one was open for 0% of the time, Pallas kernels for 11%

profile of v10, /device:TPU:0, one launch (start us, length us, event | category | flops | bytes accessed | tf_op | source)
XLA Modules:
  0.0 28.2 jit_solution(12826037827149807341)
XLA Ops:
  0.0 0.0 copy-start
  0.0 2.0 %encode_and_pick.1 = (bf16[16,1536]{1,0:T(8,128)(2,1)S(1)}, bf16[16,1536]{1,0:T(8,128)(2,1)S(1)}, bf16[32,3072]{1,0:T(8,128)(2,1)S(1)}, bf16[32,3072]{1,0:T(8,12...) custom-call(bf16[128,3072]{1,0:T(8,128)(2,1)} %bitcast.3, s32[1,128]{1,0:T(1,128)} %bitcast.4, ...), custom_call_target="tpu_custom_call" | custom-call | tf_op jit(solution)/shard_map/encode_and_pick/pallas_call | solution.py:271
  2.0 4.0 %collective-permute-start.4 = (bf16[32,3072]{1,0:T(8,128)(2,1)S(1)}, bf16[32,3072]{1,0:T(8,128)(2,1)S(1)}, u32[]{:S(2)}, u32[]{:S(2)}) collective-permute-start(bf16[32,3072]{1,0:T(8,128)(2,1)S(1)} %get-tuple-element.33), channel_id=1, source_target_pairs={{0,3},{1,2},{2,1},{3,0},{4,7},{5,6},{6,5},{7,4},{8,11},{9,10},{10,... | collective-permute-start | bytes 589832 | tf_op jit(solution)/shard_map/ppermute | solution.py:333
  6.0 0.0 collective-permute-start
  6.0 1.2 %collective-permute-done = bf16[16,1536]{1,0:T(8,128)(2,1)S(1)} collective-permute-done((bf16[16,1536]{1,0:T(8,128)(2,1)S(1)}, bf16[16,1536]{1,0:T(8,128)(2,1)S(1)}, u32[]{:S(2)}, u32[]{:S(2)}) %collective-permute-start) | collective-permute-done | bytes 49184 | tf_op jit(solution)/shard_map/ppermute | solution.py:333
  7.2 1.6 %collective-permute-start.1 = (bf16[16,1536]{1,0:T(8,128)(2,1)S(1)}, bf16[16,1536]{1,0:T(8,128)(2,1)S(1)}, u32[]{:S(2)}, u32[]{:S(2)}) collective-permute-start(bf16[16,1536]{1,0:T(8,128)(2,1)S(1)} %add.12), channel_id=1, source_target_pairs={{0,8},{4,12},{8,0},{12,4},{16,24},{20,28},{24,16},{28,20},{1,9},{5... | collective-permute-start | bytes 147464 | tf_op jit(solution)/shard_map/ppermute | solution.py:333
  8.9 2.5 %collective-permute-start.3 = (bf16[16,1536]{1,0:T(8,128)(2,1)S(1)}, bf16[16,1536]{1,0:T(8,128)(2,1)S(1)}, u32[]{:S(2)}, u32[]{:S(2)}) collective-permute-start(bf16[16,1536]{1,0:T(8,128)(2,1)S(1)} %add.12), channel_id=1, source_target_pairs={{0,24},{4,28},{8,16},{12,20},{16,8},{20,12},{24,0},{28,4},{1,25},{... | collective-permute-start | bytes 147464 | tf_op jit(solution)/shard_map/ppermute | solution.py:333
  11.4 0.1 collective-permute-start.2
  11.5 0.0 collective-permute-done.1
  11.5 0.5 %collective-permute-start.8 = (bf16[32,3072]{1,0:T(8,128)(2,1)S(1)}, bf16[32,3072]{1,0:T(8,128)(2,1)S(1)}, u32[]{:S(2)}, u32[]{:S(2)}) collective-permute-start(bf16[32,3072]{1,0:T(8,128)(2,1)S(1)} %get-tuple-element.36), channel_id=1, source_target_pairs={{0,1},{1,0},{2,3},{3,2},{4,5},{5,4},{6,7},{7,6},{8,9},{9,8},{10,11... | collective-permute-start | bytes 589832 | tf_op jit(solution)/shard_map/ppermute | solution.py:333
  12.0 0.5 %collective-permute-start.9 = (bf16[32,3072]{1,0:T(8,128)(2,1)S(1)}, bf16[32,3072]{1,0:T(8,128)(2,1)S(1)}, u32[]{:S(2)}, u32[]{:S(2)}) collective-permute-start(bf16[32,3072]{1,0:T(8,128)(2,1)S(1)} %get-tuple-element.37), channel_id=1, source_target_pairs={{0,2},{1,3},{2,0},{3,1},{4,6},{5,7},{6,4},{7,5},{8,10},{9,11},{10,... | collective-permute-start | bytes 589832 | tf_op jit(solution)/shard_map/ppermute | solution.py:333
  12.5 2.5 %collective-permute-done.3 = bf16[16,1536]{1,0:T(8,128)(2,1)S(1)} collective-permute-done((bf16[16,1536]{1,0:T(8,128)(2,1)S(1)}, bf16[16,1536]{1,0:T(8,128)(2,1)S(1)}, u32[]{:S(2)}, u32[]{:S(2)}) %collective-permute-start.3) | collective-permute-done | bytes 49184 | tf_op jit(solution)/shard_map/ppermute | solution.py:333
  15.0 0.0 collective-permute-done.4.refs_3_
  15.0 1.9 %collective-permute-done.2 = bf16[16,1536]{1,0:T(8,128)(2,1)S(1)} collective-permute-done((bf16[16,1536]{1,0:T(8,128)(2,1)S(1)}, bf16[16,1536]{1,0:T(8,128)(2,1)S(1)}, u32[]{:S(2)}, u32[]{:S(2)}) %collective-permute-start.2) | collective-permute-done | bytes 49184 | tf_op jit(solution)/shard_map/ppermute | solution.py:333
  16.9 0.5 %collective-permute-start.7 = (bf16[16,1536]{1,0:T(8,128)(2,1)S(1)}, bf16[16,1536]{1,0:T(8,128)(2,1)S(1)}, u32[]{:S(2)}, u32[]{:S(2)}) collective-permute-start(bf16[16,1536]{1,0:T(8,128)(2,1)S(1)} %add_add_fusion), channel_id=1, source_target_pairs={{0,3},{1,2},{2,1},{3,0},{4,7},{5,6},{6,5},{7,4},{8,11},{9,10},{10,... | collective-permute-start | bytes 147464 | tf_op jit(solution)/shard_map/ppermute | solution.py:333
  17.4 1.5 %collective-permute-start.6 = (bf16[16,1536]{1,0:T(8,128)(2,1)S(1)}, bf16[16,1536]{1,0:T(8,128)(2,1)S(1)}, u32[]{:S(2)}, u32[]{:S(2)}) collective-permute-start(bf16[16,1536]{1,0:T(8,128)(2,1)S(1)} %add_add_fusion), channel_id=1, source_target_pairs={{0,2},{1,3},{2,0},{3,1},{4,6},{5,7},{6,4},{7,5},{8,10},{9,11},{10,... | collective-permute-start | bytes 147464 | tf_op jit(solution)/shard_map/ppermute | solution.py:333
  19.0 1.5 %collective-permute-start.5 = (bf16[16,1536]{1,0:T(8,128)(2,1)S(1)}, bf16[16,1536]{1,0:T(8,128)(2,1)S(1)}, u32[]{:S(2)}, u32[]{:S(2)}) collective-permute-start(bf16[16,1536]{1,0:T(8,128)(2,1)S(1)} %add_add_fusion), channel_id=1, source_target_pairs={{0,1},{1,0},{2,3},{3,2},{4,5},{5,4},{6,7},{7,6},{8,9},{9,8},{10,11... | collective-permute-start | bytes 147464 | tf_op jit(solution)/shard_map/ppermute | solution.py:333
  20.4 0.0 collective-permute-done.8.refs_1_
  20.4 0.0 collective-permute-done.9.refs_2_
  20.5 1.0 %whiten_receivers.1 = (f32[128,1536]{1,0:T(8,128)S(1)}, f32[128,1536]{1,0:T(8,128)S(1)}, f32[128,1536]{1,0:T(8,128)S(1)}, f32[128,128]{1,0:T(8,128)S(1)}) custom-call(bf16[32,3072]{1,0:T(8,128)(2,1)S(1)} %get-tuple-element.35.refs_0_, bf16[32,3072]{1,0:T(8,128)(2,1)S(1)} %collective-permute-done.8.refs_1_, ...), custom_call_target="tpu_custom_call" | custom-call | flops 402653184 | bytes 1572864 | tf_op jit(solution)/shard_map/whiten_receivers/pallas_call | solution.py:295
  21.4 0.6 %collective-permute-done.7 = bf16[16,1536]{1,0:T(8,128)(2,1)S(1)} collective-permute-done((bf16[16,1536]{1,0:T(8,128)(2,1)S(1)}, bf16[16,1536]{1,0:T(8,128)(2,1)S(1)}, u32[]{:S(2)}, u32[]{:S(2)}) %collective-permute-start.7) | collective-permute-done | bytes 49184 | tf_op jit(solution)/shard_map/ppermute | solution.py:333
  22.1 0.0 collective-permute-done.6
  22.1 1.0 %collective-permute-done.5 = bf16[16,1536]{1,0:T(8,128)(2,1)S(1)} collective-permute-done((bf16[16,1536]{1,0:T(8,128)(2,1)S(1)}, bf16[16,1536]{1,0:T(8,128)(2,1)S(1)}, u32[]{:S(2)}, u32[]{:S(2)}) %collective-permute-start.5) | collective-permute-done | bytes 49184 | tf_op jit(solution)/shard_map/ppermute | solution.py:333
  23.1 0.1 collective-permute-start.10
  23.2 0.0 copy-done
  23.2 2.1 %stack_own_half.1.refs_0_ = f32[256,301]{1,0:T(8,128)S(1)} custom-call(bf16[64,1536]{1,0:T(8,128)(2,1)S(1)} %constant_dynamic-update-slice_fusion.slabs_ref, f32[128,1536]{1,0:T(8,128)S(1)} %get-tuple-element.47.rcv_re, f32[128,1536]{1,0:T(8,128)S(1)} %get-tuple-element.48.rcv_im, f32[128,1536]{1,0:T(8,128)S(1)} %get-tuple-element.49.rcv_both, ...), custom_call_target="tpu_custom_call" | custom-call | flops 471859200 | bytes 3145728 | tf_op jit(solution)/shard_map/stack_own_half/pallas_call | solution.py:318
  25.3 0.0 collective-permute-done.10.slabs_ref
  25.3 2.8 %stack_other_half.1 = f32[512,301]{1,0:T(8,128)} custom-call(bf16[64,1536]{1,0:T(8,128)(2,1)S(1)} %collective-permute-done.10.slabs_ref, f32[128,1536]{1,0:T(8,128)S(1)} %get-tuple-element.47.rcv_re, f32[128,1536]{1,0:T(8,128)S(1)} %get-tuple-element.48.rcv_im, f32[128,1536]{1,0:T(8,128)S(1)} %get-tuple-element.49.rcv_both, ...), custom_call_target="tpu_custom_call" | custom-call | flops 471859200 | bytes 3145728 | tf_op jit(solution)/shard_map/stack_other_half/pallas_call | solution.py:318
  (6 shorter events, 0.0 us)
Async XLA Ops:
  0.0 23.2 %copy-start = (bf16[3072,256]{1,0:T(8,128)(2,1)S(1)}, bf16[3072,256]{1,0:T(8,128)(2,1)}, u32[]{:S(2)}) copy-start(bf16[3072,256]{1,0:T(8,128)(2,1)} %constant.2.clone.table_ref) | copy-start | bytes 4718596
  2.0 12.9 %collective-permute-start.4 = (bf16[32,3072]{1,0:T(8,128)(2,1)S(1)}, bf16[32,3072]{1,0:T(8,128)(2,1)S(1)}, u32[]{:S(2)}, u32[]{:S(2)}) collective-permute-start(bf16[32,3072]{1,0:T(8,128)(2,1)S(1)} %get-tuple-element.33), channel_id=1, source_target_pairs={{0,3},{1,2},{2,1},{3,0},{4,7},{5,6},{6,5},{7,4},{8,11},{9,10},{10,... | collective-permute-start | bytes 589832 | tf_op jit(solution)/shard_map/ppermute | solution.py:333
  6.0 1.2 %collective-permute-start = (bf16[16,1536]{1,0:T(8,128)(2,1)S(1)}, bf16[16,1536]{1,0:T(8,128)(2,1)S(1)}, u32[]{:S(2)}, u32[]{:S(2)}) collective-permute-start(bf16[16,1536]{1,0:T(8,128)(2,1)S(1)} %get-tuple-element.29), channel_id=1, source_target_pairs={{0,4},{4,0},{8,12},{12,8},{16,20},{20,16},{24,28},{28,24},{1,5},{5... | collective-permute-start | bytes 147464 | tf_op jit(solution)/shard_map/ppermute | solution.py:333
  7.2 4.2 %collective-permute-start.1 = (bf16[16,1536]{1,0:T(8,128)(2,1)S(1)}, bf16[16,1536]{1,0:T(8,128)(2,1)S(1)}, u32[]{:S(2)}, u32[]{:S(2)}) collective-permute-start(bf16[16,1536]{1,0:T(8,128)(2,1)S(1)} %add.12), channel_id=1, source_target_pairs={{0,8},{4,12},{8,0},{12,4},{16,24},{20,28},{24,16},{28,20},{1,9},{5... | collective-permute-start | bytes 147464 | tf_op jit(solution)/shard_map/ppermute | solution.py:333
  8.9 6.1 %collective-permute-start.3 = (bf16[16,1536]{1,0:T(8,128)(2,1)S(1)}, bf16[16,1536]{1,0:T(8,128)(2,1)S(1)}, u32[]{:S(2)}, u32[]{:S(2)}) collective-permute-start(bf16[16,1536]{1,0:T(8,128)(2,1)S(1)} %add.12), channel_id=1, source_target_pairs={{0,24},{4,28},{8,16},{12,20},{16,8},{20,12},{24,0},{28,4},{1,25},{... | collective-permute-start | bytes 147464 | tf_op jit(solution)/shard_map/ppermute | solution.py:333
  11.4 5.5 %collective-permute-start.2 = (bf16[16,1536]{1,0:T(8,128)(2,1)S(1)}, bf16[16,1536]{1,0:T(8,128)(2,1)S(1)}, u32[]{:S(2)}, u32[]{:S(2)}) collective-permute-start(bf16[16,1536]{1,0:T(8,128)(2,1)S(1)} %add.12), channel_id=1, source_target_pairs={{0,16},{4,20},{8,24},{12,28},{16,0},{20,4},{24,8},{28,12},{1,17},{... | collective-permute-start | bytes 147464 | tf_op jit(solution)/shard_map/ppermute | solution.py:333
  11.5 9.0 %collective-permute-start.8 = (bf16[32,3072]{1,0:T(8,128)(2,1)S(1)}, bf16[32,3072]{1,0:T(8,128)(2,1)S(1)}, u32[]{:S(2)}, u32[]{:S(2)}) collective-permute-start(bf16[32,3072]{1,0:T(8,128)(2,1)S(1)} %get-tuple-element.36), channel_id=1, source_target_pairs={{0,1},{1,0},{2,3},{3,2},{4,5},{5,4},{6,7},{7,6},{8,9},{9,8},{10,11... | collective-permute-start | bytes 589832 | tf_op jit(solution)/shard_map/ppermute | solution.py:333
  12.0 8.4 %collective-permute-start.9 = (bf16[32,3072]{1,0:T(8,128)(2,1)S(1)}, bf16[32,3072]{1,0:T(8,128)(2,1)S(1)}, u32[]{:S(2)}, u32[]{:S(2)}) collective-permute-start(bf16[32,3072]{1,0:T(8,128)(2,1)S(1)} %get-tuple-element.37), channel_id=1, source_target_pairs={{0,2},{1,3},{2,0},{3,1},{4,6},{5,7},{6,4},{7,5},{8,10},{9,11},{10,... | collective-permute-start | bytes 589832 | tf_op jit(solution)/shard_map/ppermute | solution.py:333
  16.9 5.2 %collective-permute-start.7 = (bf16[16,1536]{1,0:T(8,128)(2,1)S(1)}, bf16[16,1536]{1,0:T(8,128)(2,1)S(1)}, u32[]{:S(2)}, u32[]{:S(2)}) collective-permute-start(bf16[16,1536]{1,0:T(8,128)(2,1)S(1)} %add_add_fusion), channel_id=1, source_target_pairs={{0,3},{1,2},{2,1},{3,0},{4,7},{5,6},{6,5},{7,4},{8,11},{9,10},{10,... | collective-permute-start | bytes 147464 | tf_op jit(solution)/shard_map/ppermute | solution.py:333
  17.4 4.6 %collective-permute-start.6 = (bf16[16,1536]{1,0:T(8,128)(2,1)S(1)}, bf16[16,1536]{1,0:T(8,128)(2,1)S(1)}, u32[]{:S(2)}, u32[]{:S(2)}) collective-permute-start(bf16[16,1536]{1,0:T(8,128)(2,1)S(1)} %add_add_fusion), channel_id=1, source_target_pairs={{0,2},{1,3},{2,0},{3,1},{4,6},{5,7},{6,4},{7,5},{8,10},{9,11},{10,... | collective-permute-start | bytes 147464 | tf_op jit(solution)/shard_map/ppermute | solution.py:333
  19.0 4.1 %collective-permute-start.5 = (bf16[16,1536]{1,0:T(8,128)(2,1)S(1)}, bf16[16,1536]{1,0:T(8,128)(2,1)S(1)}, u32[]{:S(2)}, u32[]{:S(2)}) collective-permute-start(bf16[16,1536]{1,0:T(8,128)(2,1)S(1)} %add_add_fusion), channel_id=1, source_target_pairs={{0,1},{1,0},{2,3},{3,2},{4,5},{5,4},{6,7},{7,6},{8,9},{9,8},{10,11... | collective-permute-start | bytes 147464 | tf_op jit(solution)/shard_map/ppermute | solution.py:333
  23.1 2.2 %collective-permute-start.10 = (bf16[64,1536]{1,0:T(8,128)(2,1)S(1)}, bf16[64,1536]{1,0:T(8,128)(2,1)S(1)}, u32[]{:S(2)}, u32[]{:S(2)}) collective-permute-start(bf16[64,1536]{1,0:T(8,128)(2,1)S(1)} %constant_dynamic-update-slice_fusion.slabs_ref), channel_id=1, source_target_pairs={{0,4},{4,0},{8,12},{12,8},{16,20},{20,16},{24,28},{28,24},{1,5},{5... | collective-permute-start | bytes 589832 | tf_op jit(solution)/shard_map/ppermute | solution.py:333

commit v11 on v10

--- a/solution.py
+++ b/solution.py
@@ -177,49 +177,48 @@
     def spread(ref, block, row):
         return jnp.concatenate([ref[block, pl.ds(row, 8, stride=0), :]] * (tile // 8), axis=0)
 
-    def multiply(chunk):
-        for sub in range(CHUNK // LANES):
-            block = chunk * (CHUNK // LANES) + sub
-            at = slice(block * LANES, (block + 1) * LANES)
-            for first in range(0, keep, tile):
-                rows = [slice(t * keep + first, t * keep + first + tile) for t in range(segments)]
-                r_re = [rcv_re[row, at] for row in rows]
-                r_im = [rcv_im[row, at] for row in rows]
-                r_both = [rcv_both[row, at] for row in rows]
-                for source in range(half):
-                    p, q, w = [], [], []
-                    for t in range(segments):
-                        row = t * half + source
-                        p.append(spread(src_re, block, row) * r_both[t])
-                        q.append(spread(src_diff, block, row) * r_im[t])
-                        w.append(spread(src_sum, block, row) * r_re[t])
-                    p, q, w = (functools.reduce(jnp.add, part) for part in (p, q, w))
-                    to = slice(source * keep + first, source * keep + first + tile)
-                    lanes = slice(sub * LANES, (sub + 1) * LANES)
-                    cross[chunk, 0, to, lanes] = (p + q).astype(cross.dtype)
-                    cross[chunk, 1, to, lanes] = (w - p).astype(cross.dtype)
-
-    def project(chunk):
-        parts = []
-        for place in range(2):
-            first = place * nbins + chunk * CHUNK
-            parts.append(
-                jnp.dot(
-                    cross[chunk, place].astype(jnp.bfloat16),
-                    table_ref[first : first + CHUNK],
-                    preferred_element_type=jnp.float32,
-                )
-            )
-        return parts
-
-    parts = []
-    chunks = nbins // CHUNK
-    for chunk in range(chunks + 1):
-        if chunk < chunks:
-            multiply(chunk)
-        if chunk > 0:
-            parts.append(project(chunk - 1))
-    total_re, total_im = (functools.reduce(jnp.add, part) for part in zip(*parts))
+    def multiply(chunk, sub):
+        block = chunk * (CHUNK // LANES) + sub
+        at = slice(block * LANES, (block + 1) * LANES)
+        lanes = slice(sub * LANES, (sub + 1) * LANES)
+        for first in range(0, keep, tile):
+            rows = [slice(t * keep + first, t * keep + first + tile) for t in range(segments)]
+            r_re = [rcv_re[row, at] for row in rows]
+            r_im = [rcv_im[row, at] for row in rows]
+            r_both = [rcv_both[row, at] for row in rows]
+            for source in range(half):
+                p, q, w = [], [], []
+                for t in range(segments):
+                    row = t * half + source
+                    p.append(spread(src_re, block, row) * r_both[t])
+                    q.append(spread(src_diff, block, row) * r_im[t])
+                    w.append(spread(src_sum, block, row) * r_re[t])
+                p, q, w = (functools.reduce(jnp.add, part) for part in (p, q, w))
+                to = slice(source * keep + first, source * keep + first + tile)
+                cross[chunk, 0, to, lanes] = (p + q).astype(cross.dtype)
+                cross[chunk, 1, to, lanes] = (w - p).astype(cross.dtype)
+
+    def project(chunk, place, part):
+        first = place * nbins + chunk * CHUNK
+        return jnp.dot(
+            cross[chunk, place, part].astype(jnp.bfloat16),
+            table_ref[first : first + CHUNK],
+            preferred_element_type=jnp.float32,
+        )
+
+    chunks, subs = nbins // CHUNK, CHUNK // LANES
+    totals = [[], []]
+    for chunk in range(chunks):
+        for sub in range(subs):
+            multiply(chunk, sub)
+            if chunk > 0 and sub % (subs // 2) == 0:
+                place = sub // (subs // 2)
+                totals[place].append(project(chunk - 1, place, slice(None)))
+    tops = [functools.reduce(jnp.add, part) for part in totals]
+    ends = []
+    for first in (0, half // 2):
+        at = slice(first * keep, (first + half // 2) * keep)
+        ends.append([tops[place][at] + project(chunks - 1, place, at) for place in range(2)])
 
     lags = result.shape[1]
     scale = 2.0 / math.sqrt(nbins)
@@ -231,7 +230,8 @@
             common = common + src_valid[row : row + 1] * rcv_valid[t * keep : (t + 1) * keep, :]
         weight = scale / jnp.maximum(common, 1.0)
         to = slice(source * keep, (source + 1) * keep)
-        even, odd = total_re[to], total_im[to]
+        inside = slice(source % (half // 2) * keep, (source % (half // 2) + 1) * keep)
+        even, odd = (total[inside] for total in ends[source // (half // 2)])
         ahead = even + odd
         behind = even - odd
         low_part = jnp.take_along_axis(
@@ -342,17 +342,17 @@
     )
     receivers[-1] = swapped(receivers[-1], "tm", tm_size, tm_size - 1)
     own = own + swapped(other, "rcv", rcv_size, 1)
+    own, later = lax.optimization_barrier((own, receivers[1:-1]))
+    receivers[1:-1] = [
+        swapped(block, "tm", tm_size, place) for place, block in enumerate(later, 1)
+    ]
     step = 2
     while step < rcv_size:
         wide = min(4, rcv_size // step)
-        parts = [swapped(own, "rcv", rcv_size, place * step) for place in range(wide - 1, 0, -1)]
+        parts = [swapped(own, "rcv", rcv_size, place * step) for place in range(1, wide)]
         if step == 2:
-            parts[-1], later = lax.optimization_barrier((parts[-1], receivers[1:-1]))
-            receivers[1:-1] = [
-                swapped(block, "tm", tm_size, place) for place, block in enumerate(later, 1)
-            ]
-            parts[0], receivers[-1] = lax.optimization_barrier((parts[0], receivers[-1]))
-        own = functools.reduce(jnp.add, parts[::-1], own)
+            parts[-1], receivers[-1] = lax.optimization_barrier((parts[-1], receivers[-1]))
+        own = functools.reduce(jnp.add, parts, own)
         step *= wide
     own = [own] + [swapped(own, "tm", tm_size, place) for place in range(1, tm_size)]
     whitened = whiten_blocks(receivers)

time: 28.3 us -> 27.3 us (0.965)
  waiting for transfers between devices: 7.19 us -> 5.99 us
    ppermute x11, waiting for transfers between devices: 7.19 us -> 5.99 us  [swapped(): return lax.ppermute(value, axis, [(i, i ^ step) for i in range(size)])]
  transfers between devices with their start and end apart: 11 -> 11, of which waited for: 5 -> 6; matrix products, arithmetic and copies ran while one was open for 0% -> 0% of each run, Pallas kernels for 11% -> 11%
where the time goes in v11:
time: 27.3 us; the launch traced here: 27.2 us
  starting transfers between devices  13.1 us (48%)
  Pallas kernels  7.95 us (29%)
  waiting for transfers between devices  5.99 us (22%)
    ppermute x11, starting transfers between devices, swapped(): return lax.ppermute(value, axis, [(i, i ^ step) for i in range(size)])  13.1 us
    ppermute x11, waiting for transfers between devices, swapped(): return lax.ppermute(value, axis, [(i, i ^ step) for i in range(size)])  5.99 us
    pallas_call x2, Pallas kernels, stack_half(): pl.pallas_call(functools.partial(stack_kernel, segments), out_shape=jax.S...  4.95 us
    pallas_call x1, Pallas kernels, encode(): pl.pallas_call(functools.partial(encode_kernel, segments), out_shape=(sla...  2.02 us
    pallas_call x1, Pallas kernels, whiten_blocks(): pl.pallas_call(functools.partial(whiten_kernel, segments), out_shape=(par...  0.98 us
  transfers between devices with their start and end apart: 11, of which 6 were waited for; matrix products, arithmetic and copies ran while one was open for 0% of the time, Pallas kernels for 11%

profile of v11, /device:TPU:0, one launch (start us, length us, event | category | flops | bytes accessed | tf_op | source)
XLA Modules:
  0.0 27.2 jit_solution(8508602063974885232)
XLA Ops:
  0.0 0.0 copy-start
  0.0 2.0 %encode_and_pick.1 = (bf16[16,1536]{1,0:T(8,128)(2,1)S(1)}, bf16[16,1536]{1,0:T(8,128)(2,1)S(1)}, bf16[32,3072]{1,0:T(8,128)(2,1)S(1)}, bf16[32,3072]{1,0:T(8,12...) custom-call(bf16[128,3072]{1,0:T(8,128)(2,1)} %bitcast.3, s32[1,128]{1,0:T(1,128)} %bitcast.4, ...), custom_call_target="tpu_custom_call" | custom-call | tf_op jit(solution)/shard_map/encode_and_pick/pallas_call | solution.py:271
  2.0 4.0 %collective-permute-start.4 = (bf16[32,3072]{1,0:T(8,128)(2,1)S(1)}, bf16[32,3072]{1,0:T(8,128)(2,1)S(1)}, u32[]{:S(2)}, u32[]{:S(2)}) collective-permute-start(bf16[32,3072]{1,0:T(8,128)(2,1)S(1)} %get-tuple-element.33), channel_id=1, source_target_pairs={{0,3},{1,2},{2,1},{3,0},{4,7},{5,6},{6,5},{7,4},{8,11},{9,10},{10,... | collective-permute-start | bytes 589832 | tf_op jit(solution)/shard_map/ppermute | solution.py:333
  6.0 0.0 collective-permute-start
  6.0 1.2 %collective-permute-done = bf16[16,1536]{1,0:T(8,128)(2,1)S(1)} collective-permute-done((bf16[16,1536]{1,0:T(8,128)(2,1)S(1)}, bf16[16,1536]{1,0:T(8,128)(2,1)S(1)}, u32[]{:S(2)}, u32[]{:S(2)}) %collective-permute-start) | collective-permute-done | bytes 49184 | tf_op jit(solution)/shard_map/ppermute | solution.py:333
  7.2 3.7 %collective-permute-start.3 = (bf16[16,1536]{1,0:T(8,128)(2,1)S(1)}, bf16[16,1536]{1,0:T(8,128)(2,1)S(1)}, u32[]{:S(2)}, u32[]{:S(2)}) collective-permute-start(bf16[16,1536]{1,0:T(8,128)(2,1)S(1)} %add.12), channel_id=1, source_target_pairs={{0,24},{4,28},{8,16},{12,20},{16,8},{20,12},{24,0},{28,4},{1,25},{... | collective-permute-start | bytes 147464 | tf_op jit(solution)/shard_map/ppermute | solution.py:333
  10.9 0.0 collective-permute-start.2
  10.9 0.8 %collective-permute-start.1 = (bf16[16,1536]{1,0:T(8,128)(2,1)S(1)}, bf16[16,1536]{1,0:T(8,128)(2,1)S(1)}, u32[]{:S(2)}, u32[]{:S(2)}) collective-permute-start(bf16[16,1536]{1,0:T(8,128)(2,1)S(1)} %add.12), channel_id=1, source_target_pairs={{0,8},{4,12},{8,0},{12,4},{16,24},{20,28},{24,16},{28,20},{1,9},{5... | collective-permute-start | bytes 147464 | tf_op jit(solution)/shard_map/ppermute | solution.py:333
  11.7 0.5 %collective-permute-start.8 = (bf16[32,3072]{1,0:T(8,128)(2,1)S(1)}, bf16[32,3072]{1,0:T(8,128)(2,1)S(1)}, u32[]{:S(2)}, u32[]{:S(2)}) collective-permute-start(bf16[32,3072]{1,0:T(8,128)(2,1)S(1)} %get-tuple-element.36), channel_id=1, source_target_pairs={{0,1},{1,0},{2,3},{3,2},{4,5},{5,4},{6,7},{7,6},{8,9},{9,8},{10,11... | collective-permute-start | bytes 589832 | tf_op jit(solution)/shard_map/ppermute | solution.py:333
  12.2 1.0 %collective-permute-done.3 = bf16[16,1536]{1,0:T(8,128)(2,1)S(1)} collective-permute-done((bf16[16,1536]{1,0:T(8,128)(2,1)S(1)}, bf16[16,1536]{1,0:T(8,128)(2,1)S(1)}, u32[]{:S(2)}, u32[]{:S(2)}) %collective-permute-start.3) | collective-permute-done | bytes 49184 | tf_op jit(solution)/shard_map/ppermute | solution.py:333
  13.3 0.5 %collective-permute-start.9 = (bf16[32,3072]{1,0:T(8,128)(2,1)S(1)}, bf16[32,3072]{1,0:T(8,128)(2,1)S(1)}, u32[]{:S(2)}, u32[]{:S(2)}) collective-permute-start(bf16[32,3072]{1,0:T(8,128)(2,1)S(1)} %get-tuple-element.37), channel_id=1, source_target_pairs={{0,2},{1,3},{2,0},{3,1},{4,6},{5,7},{6,4},{7,5},{8,10},{9,11},{10,... | collective-permute-start | bytes 589832 | tf_op jit(solution)/shard_map/ppermute | solution.py:333
  13.8 0.0 collective-permute-done.4.refs_3_
  13.8 2.1 %collective-permute-done.2 = bf16[16,1536]{1,0:T(8,128)(2,1)S(1)} collective-permute-done((bf16[16,1536]{1,0:T(8,128)(2,1)S(1)}, bf16[16,1536]{1,0:T(8,128)(2,1)S(1)}, u32[]{:S(2)}, u32[]{:S(2)}) %collective-permute-start.2) | collective-permute-done | bytes 49184 | tf_op jit(solution)/shard_map/ppermute | solution.py:333
  15.9 0.0 collective-permute-done.1
  15.9 0.5 %collective-permute-start.7 = (bf16[16,1536]{1,0:T(8,128)(2,1)S(1)}, bf16[16,1536]{1,0:T(8,128)(2,1)S(1)}, u32[]{:S(2)}, u32[]{:S(2)}) collective-permute-start(bf16[16,1536]{1,0:T(8,128)(2,1)S(1)} %add_add_fusion), channel_id=1, source_target_pairs={{0,3},{1,2},{2,1},{3,0},{4,7},{5,6},{6,5},{7,4},{8,11},{9,10},{10,... | collective-permute-start | bytes 147464 | tf_op jit(solution)/shard_map/ppermute | solution.py:333
  16.5 1.5 %collective-permute-start.6 = (bf16[16,1536]{1,0:T(8,128)(2,1)S(1)}, bf16[16,1536]{1,0:T(8,128)(2,1)S(1)}, u32[]{:S(2)}, u32[]{:S(2)}) collective-permute-start(bf16[16,1536]{1,0:T(8,128)(2,1)S(1)} %add_add_fusion), channel_id=1, source_target_pairs={{0,2},{1,3},{2,0},{3,1},{4,6},{5,7},{6,4},{7,5},{8,10},{9,11},{10,... | collective-permute-start | bytes 147464 | tf_op jit(solution)/shard_map/ppermute | solution.py:333
  18.0 1.5 %collective-permute-start.5 = (bf16[16,1536]{1,0:T(8,128)(2,1)S(1)}, bf16[16,1536]{1,0:T(8,128)(2,1)S(1)}, u32[]{:S(2)}, u32[]{:S(2)}) collective-permute-start(bf16[16,1536]{1,0:T(8,128)(2,1)S(1)} %add_add_fusion), channel_id=1, source_target_pairs={{0,1},{1,0},{2,3},{3,2},{4,5},{5,4},{6,7},{7,6},{8,9},{9,8},{10,11... | collective-permute-start | bytes 147464 | tf_op jit(solution)/shard_map/ppermute | solution.py:333
  19.5 0.0 collective-permute-done.8.refs_1_
  19.5 0.8 %collective-permute-done.9.refs_2_ = bf16[32,3072]{1,0:T(8,128)(2,1)S(1)} collective-permute-done((bf16[32,3072]{1,0:T(8,128)(2,1)S(1)}, bf16[32,3072]{1,0:T(8,128)(2,1)S(1)}, u32[]{:S(2)}, u32[]{:S(2)}) %collective-permute-start.9) | collective-permute-done | bytes 196640 | tf_op jit(solution)/shard_map/ppermute | solution.py:333
  20.2 1.0 %whiten_receivers.1 = (f32[128,1536]{1,0:T(8,128)S(1)}, f32[128,1536]{1,0:T(8,128)S(1)}, f32[128,1536]{1,0:T(8,128)S(1)}, f32[128,128]{1,0:T(8,128)S(1)}) custom-call(bf16[32,3072]{1,0:T(8,128)(2,1)S(1)} %get-tuple-element.35.refs_0_, bf16[32,3072]{1,0:T(8,128)(2,1)S(1)} %collective-permute-done.8.refs_1_, ...), custom_call_target="tpu_custom_call" | custom-call | flops 402653184 | bytes 1572864 | tf_op jit(solution)/shard_map/whiten_receivers/pallas_call | solution.py:295
  21.2 0.0 collective-permute-done.7
  21.2 0.1 collective-permute-done.6
  21.3 0.8 %collective-permute-done.5 = bf16[16,1536]{1,0:T(8,128)(2,1)S(1)} collective-permute-done((bf16[16,1536]{1,0:T(8,128)(2,1)S(1)}, bf16[16,1536]{1,0:T(8,128)(2,1)S(1)}, u32[]{:S(2)}, u32[]{:S(2)}) %collective-permute-start.5) | collective-permute-done | bytes 49184 | tf_op jit(solution)/shard_map/ppermute | solution.py:333
  22.1 0.1 collective-permute-start.10
  22.2 0.0 copy-done
  22.2 2.1 %stack_own_half.1.refs_0_ = f32[256,301]{1,0:T(8,128)S(1)} custom-call(bf16[64,1536]{1,0:T(8,128)(2,1)S(1)} %constant_dynamic-update-slice_fusion.slabs_ref, f32[128,1536]{1,0:T(8,128)S(1)} %get-tuple-element.47.rcv_re, f32[128,1536]{1,0:T(8,128)S(1)} %get-tuple-element.48.rcv_im, f32[128,1536]{1,0:T(8,128)S(1)} %get-tuple-element.49.rcv_both, ...), custom_call_target="tpu_custom_call" | custom-call | flops 471859200 | bytes 3145728 | tf_op jit(solution)/shard_map/stack_own_half/pallas_call | solution.py:318
  24.3 0.0 collective-permute-done.10.slabs_ref
  24.3 2.8 %stack_other_half.1 = f32[512,301]{1,0:T(8,128)} custom-call(bf16[64,1536]{1,0:T(8,128)(2,1)S(1)} %collective-permute-done.10.slabs_ref, f32[128,1536]{1,0:T(8,128)S(1)} %get-tuple-element.47.rcv_re, f32[128,1536]{1,0:T(8,128)S(1)} %get-tuple-element.48.rcv_im, f32[128,1536]{1,0:T(8,128)S(1)} %get-tuple-element.49.rcv_both, ...), custom_call_target="tpu_custom_call" | custom-call | flops 471859200 | bytes 3145728 | tf_op jit(solution)/shard_map/stack_other_half/pallas_call | solution.py:318
  (6 shorter events, 0.0 us)
Async XLA Ops:
  0.0 22.2 %copy-start = (bf16[3072,256]{1,0:T(8,128)(2,1)S(1)}, bf16[3072,256]{1,0:T(8,128)(2,1)}, u32[]{:S(2)}) copy-start(bf16[3072,256]{1,0:T(8,128)(2,1)} %constant.2.clone.table_ref) | copy-start | bytes 4718596
  2.0 11.7 %collective-permute-start.4 = (bf16[32,3072]{1,0:T(8,128)(2,1)S(1)}, bf16[32,3072]{1,0:T(8,128)(2,1)S(1)}, u32[]{:S(2)}, u32[]{:S(2)}) collective-permute-start(bf16[32,3072]{1,0:T(8,128)(2,1)S(1)} %get-tuple-element.33), channel_id=1, source_target_pairs={{0,3},{1,2},{2,1},{3,0},{4,7},{5,6},{6,5},{7,4},{8,11},{9,10},{10,... | collective-permute-start | bytes 589832 | tf_op jit(solution)/shard_map/ppermute | solution.py:333
  6.0 1.2 %collective-permute-start = (bf16[16,1536]{1,0:T(8,128)(2,1)S(1)}, bf16[16,1536]{1,0:T(8,128)(2,1)S(1)}, u32[]{:S(2)}, u32[]{:S(2)}) collective-permute-start(bf16[16,1536]{1,0:T(8,128)(2,1)S(1)} %get-tuple-element.29), channel_id=1, source_target_pairs={{0,4},{4,0},{8,12},{12,8},{16,20},{20,16},{24,28},{28,24},{1,5},{5... | collective-permute-start | bytes 147464 | tf_op jit(solution)/shard_map/ppermute | solution.py:333
  7.2 6.0 %collective-permute-start.3 = (bf16[16,1536]{1,0:T(8,128)(2,1)S(1)}, bf16[16,1536]{1,0:T(8,128)(2,1)S(1)}, u32[]{:S(2)}, u32[]{:S(2)}) collective-permute-start(bf16[16,1536]{1,0:T(8,128)(2,1)S(1)} %add.12), channel_id=1, source_target_pairs={{0,24},{4,28},{8,16},{12,20},{16,8},{20,12},{24,0},{28,4},{1,25},{... | collective-permute-start | bytes 147464 | tf_op jit(solution)/shard_map/ppermute | solution.py:333
  10.9 5.0 %collective-permute-start.2 = (bf16[16,1536]{1,0:T(8,128)(2,1)S(1)}, bf16[16,1536]{1,0:T(8,128)(2,1)S(1)}, u32[]{:S(2)}, u32[]{:S(2)}) collective-permute-start(bf16[16,1536]{1,0:T(8,128)(2,1)S(1)} %add.12), channel_id=1, source_target_pairs={{0,16},{4,20},{8,24},{12,28},{16,0},{20,4},{24,8},{28,12},{1,17},{... | collective-permute-start | bytes 147464 | tf_op jit(solution)/shard_map/ppermute | solution.py:333
  10.9 5.0 %collective-permute-start.1 = (bf16[16,1536]{1,0:T(8,128)(2,1)S(1)}, bf16[16,1536]{1,0:T(8,128)(2,1)S(1)}, u32[]{:S(2)}, u32[]{:S(2)}) collective-permute-start(bf16[16,1536]{1,0:T(8,128)(2,1)S(1)} %add.12), channel_id=1, source_target_pairs={{0,8},{4,12},{8,0},{12,4},{16,24},{20,28},{24,16},{28,20},{1,9},{5... | collective-permute-start | bytes 147464 | tf_op jit(solution)/shard_map/ppermute | solution.py:333
  11.7 7.8 %collective-permute-start.8 = (bf16[32,3072]{1,0:T(8,128)(2,1)S(1)}, bf16[32,3072]{1,0:T(8,128)(2,1)S(1)}, u32[]{:S(2)}, u32[]{:S(2)}) collective-permute-start(bf16[32,3072]{1,0:T(8,128)(2,1)S(1)} %get-tuple-element.36), channel_id=1, source_target_pairs={{0,1},{1,0},{2,3},{3,2},{4,5},{5,4},{6,7},{7,6},{8,9},{9,8},{10,11... | collective-permute-start | bytes 589832 | tf_op jit(solution)/shard_map/ppermute | solution.py:333
  13.3 7.0 %collective-permute-start.9 = (bf16[32,3072]{1,0:T(8,128)(2,1)S(1)}, bf16[32,3072]{1,0:T(8,128)(2,1)S(1)}, u32[]{:S(2)}, u32[]{:S(2)}) collective-permute-start(bf16[32,3072]{1,0:T(8,128)(2,1)S(1)} %get-tuple-element.37), channel_id=1, source_target_pairs={{0,2},{1,3},{2,0},{3,1},{4,6},{5,7},{6,4},{7,5},{8,10},{9,11},{10,... | collective-permute-start | bytes 589832 | tf_op jit(solution)/shard_map/ppermute | solution.py:333
  15.9 5.3 %collective-permute-start.7 = (bf16[16,1536]{1,0:T(8,128)(2,1)S(1)}, bf16[16,1536]{1,0:T(8,128)(2,1)S(1)}, u32[]{:S(2)}, u32[]{:S(2)}) collective-permute-start(bf16[16,1536]{1,0:T(8,128)(2,1)S(1)} %add_add_fusion), channel_id=1, source_target_pairs={{0,3},{1,2},{2,1},{3,0},{4,7},{5,6},{6,5},{7,4},{8,11},{9,10},{10,... | collective-permute-start | bytes 147464 | tf_op jit(solution)/shard_map/ppermute | solution.py:333
  16.5 4.8 %collective-permute-start.6 = (bf16[16,1536]{1,0:T(8,128)(2,1)S(1)}, bf16[16,1536]{1,0:T(8,128)(2,1)S(1)}, u32[]{:S(2)}, u32[]{:S(2)}) collective-permute-start(bf16[16,1536]{1,0:T(8,128)(2,1)S(1)} %add_add_fusion), channel_id=1, source_target_pairs={{0,2},{1,3},{2,0},{3,1},{4,6},{5,7},{6,4},{7,5},{8,10},{9,11},{10,... | collective-permute-start | bytes 147464 | tf_op jit(solution)/shard_map/ppermute | solution.py:333
  18.0 4.1 %collective-permute-start.5 = (bf16[16,1536]{1,0:T(8,128)(2,1)S(1)}, bf16[16,1536]{1,0:T(8,128)(2,1)S(1)}, u32[]{:S(2)}, u32[]{:S(2)}) collective-permute-start(bf16[16,1536]{1,0:T(8,128)(2,1)S(1)} %add_add_fusion), channel_id=1, source_target_pairs={{0,1},{1,0},{2,3},{3,2},{4,5},{5,4},{6,7},{7,6},{8,9},{9,8},{10,11... | collective-permute-start | bytes 147464 | tf_op jit(solution)/shard_map/ppermute | solution.py:333
  22.1 2.2 %collective-permute-start.10 = (bf16[64,1536]{1,0:T(8,128)(2,1)S(1)}, bf16[64,1536]{1,0:T(8,128)(2,1)S(1)}, u32[]{:S(2)}, u32[]{:S(2)}) collective-permute-start(bf16[64,1536]{1,0:T(8,128)(2,1)S(1)} %constant_dynamic-update-slice_fusion.slabs_ref), channel_id=1, source_target_pairs={{0,4},{4,0},{8,12},{12,8},{16,20},{20,16},{24,28},{28,24},{1,5},{5... | collective-permute-start | bytes 589832 | tf_op jit(solution)/shard_map/ppermute | solution.py:333

commit v12 on v11

--- a/solution.py
+++ b/solution.py
@@ -21,7 +21,6 @@
 BLOCK = 256
 CHUNK = 512
 MEBI = 1 << 20
-FIRST_LAG = LANES - LAG
 VMEM = pl.BlockSpec(memory_space=pltpu.VMEM)
 HBM = pl.BlockSpec(memory_space=pltpu.HBM)
 
@@ -29,11 +28,15 @@
 def lag_table(nbins):
     winding = np.mod(
         np.arange(1, nbins + 1, dtype=np.int64)[:, None]
-        * np.arange(FIRST_LAG, FIRST_LAG + BLOCK, dtype=np.int64)[None, :],
+        * np.arange(-LAG, LAG + 1, dtype=np.int64)[None, :],
         NT,
     )
     theta = winding * (2.0 * math.pi / NT)
-    return np.concatenate([np.cos(theta), -np.sin(theta)], axis=0).astype(jnp.bfloat16)
+    table = np.stack([np.cos(theta), -np.sin(theta)]).reshape(2, nbins // CHUNK, CHUNK, -1)
+    table = np.swapaxes(table, 0, 1).reshape(2 * nbins, -1)
+    columns = table.shape[1]
+    padded = -(-columns // LANES) * LANES
+    return np.pad(table, ((0, 0), (0, padded - columns))).astype(jnp.bfloat16)
 
 
 def kind_for(rows):
@@ -180,7 +183,6 @@
     def multiply(chunk, sub):
         block = chunk * (CHUNK // LANES) + sub
         at = slice(block * LANES, (block + 1) * LANES)
-        lanes = slice(sub * LANES, (sub + 1) * LANES)
         for first in range(0, keep, tile):
             rows = [slice(t * keep + first, t * keep + first + tile) for t in range(segments)]
             r_re = [rcv_re[row, at] for row in rows]
@@ -195,34 +197,33 @@
                     w.append(spread(src_sum, block, row) * r_re[t])
                 p, q, w = (functools.reduce(jnp.add, part) for part in (p, q, w))
                 to = slice(source * keep + first, source * keep + first + tile)
-                cross[chunk, 0, to, lanes] = (p + q).astype(cross.dtype)
-                cross[chunk, 1, to, lanes] = (w - p).astype(cross.dtype)
-
-    def project(chunk, place, part):
-        first = place * nbins + chunk * CHUNK
+                cross[chunk, to, sub * LANES : (sub + 1) * LANES] = (p + q).astype(cross.dtype)
+                first_im = CHUNK + sub * LANES
+                cross[chunk, to, first_im : first_im + LANES] = (w - p).astype(cross.dtype)
+
+    def project(chunk, part):
+        first = 2 * chunk * CHUNK
         return jnp.dot(
-            cross[chunk, place, part].astype(jnp.bfloat16),
-            table_ref[first : first + CHUNK],
+            cross[chunk, part].astype(jnp.bfloat16),
+            table_ref[first : first + 2 * CHUNK],
             preferred_element_type=jnp.float32,
         )
 
     chunks, subs = nbins // CHUNK, CHUNK // LANES
-    totals = [[], []]
+    totals = []
     for chunk in range(chunks):
         for sub in range(subs):
             multiply(chunk, sub)
-            if chunk > 0 and sub % (subs // 2) == 0:
-                place = sub // (subs // 2)
-                totals[place].append(project(chunk - 1, place, slice(None)))
-    tops = [functools.reduce(jnp.add, part) for part in totals]
+            if chunk > 0 and sub == 0:
+                totals.append(project(chunk - 1, slice(None)))
+    total = functools.reduce(jnp.add, totals)
     ends = []
     for first in (0, half // 2):
         at = slice(first * keep, (first + half // 2) * keep)
-        ends.append([tops[place][at] + project(chunks - 1, place, at) for place in range(2)])
+        ends.append(total[at] + project(chunks - 1, at))
 
     lags = result.shape[1]
     scale = 2.0 / math.sqrt(nbins)
-    mirror = LAG - FIRST_LAG - iota((keep, LANES), 1)
     for source in range(half):
         common = 0.0
         for t in range(segments):
@@ -231,20 +232,10 @@
         weight = scale / jnp.maximum(common, 1.0)
         to = slice(source * keep, (source + 1) * keep)
         inside = slice(source % (half // 2) * keep, (source % (half // 2) + 1) * keep)
-        even, odd = (total[inside] for total in ends[source // (half // 2)])
-        ahead = even + odd
-        behind = even - odd
-        low_part = jnp.take_along_axis(
-            behind[:, :LANES], jnp.clip(mirror, 0, LANES - 1), axis=1
-        )
-        high_part = jnp.take_along_axis(
-            behind[:, LANES:], jnp.clip(mirror - LANES, 0, LANES - 1), axis=1
-        )
-        result[to, :LANES] = jnp.where(mirror < LANES, low_part, high_part) * weight
-        for first in range(0, lags - LANES, LANES):
-            last = min(first + LANES, lags - LANES)
-            value = ahead[:, first : first + LANES] * weight
-            result[to, LANES + first : LANES + last] = value[:, : last - first]
+        value = ends[source // (half // 2)][inside]
+        for first in range(0, lags, LANES):
+            last = min(first + LANES, lags)
+            result[to, first:last] = (value[:, first : first + LANES] * weight)[:, : last - first]
         if rest and (source + 1) % pieces == 0:
             first, count = (source + 1 - pieces) * keep, pieces * keep
             at = pl.multiple_of((1 - part) * rows + first, count)
@@ -311,7 +302,7 @@
     keep = receivers[0].shape[0] // segments
     count, rows, lags = segments * half, half * keep, 2 * LAG + 1
     part = pltpu.VMEM((nbins // LANES, count, LANES), jnp.float32)
-    cross = pltpu.VMEM((nbins // CHUNK, 2, rows, CHUNK), kind_for(keep))
+    cross = pltpu.VMEM((nbins // CHUNK, rows, 2 * CHUNK), kind_for(keep))
     scratch = [part, part, part, cross]
     if rest:
         scratch += [pltpu.VMEM((rows, lags), jnp.float32), pltpu.SemaphoreType.DMA((1 + half,))]

time: 27.3 us -> 27.8 us (1.018)
  Pallas kernels: 7.95 us -> 8.37 us
    pallas_call x2, Pallas kernels: 4.95 us -> 5.33 us  [stack_half(): pl.pallas_call(functools.partial(stack_kernel, segments), out_shape=jax.S...]
  transfers between devices with their start and end apart: 11 -> 11, of which waited for: 6 -> 6; matrix products, arithmetic and copies ran while one was open for 0% -> 0% of each run, Pallas kernels for 11% -> 12%
where the time goes in v12:
time: 27.8 us; the launch traced here: 27.6 us
  starting transfers between devices  13.1 us (47%)
  Pallas kernels  8.37 us (30%)
  waiting for transfers between devices  5.99 us (22%)
    ppermute x11, starting transfers between devices, swapped(): return lax.ppermute(value, axis, [(i, i ^ step) for i in range(size)])  13.1 us
    ppermute x11, waiting for transfers between devices, swapped(): return lax.ppermute(value, axis, [(i, i ^ step) for i in range(size)])  5.99 us
    pallas_call x2, Pallas kernels, stack_half(): pl.pallas_call(functools.partial(stack_kernel, segments), out_shape=jax.S...  5.33 us
    pallas_call x1, Pallas kernels, encode(): pl.pallas_call(functools.partial(encode_kernel, segments), out_shape=(sla...  2.05 us
    pallas_call x1, Pallas kernels, whiten_blocks(): pl.pallas_call(functools.partial(whiten_kernel, segments), out_shape=(par...  0.98 us
  transfers between devices with their start and end apart: 11, of which 6 were waited for; matrix products, arithmetic and copies ran while one was open for 0% of the time, Pallas kernels for 12%

profile of v12, /device:TPU:0, one launch (start us, length us, event | category | flops | bytes accessed | tf_op | source)
XLA Modules:
  0.0 27.6 jit_solution(3039854565624225108)
XLA Ops:
  0.0 0.0 copy-start
  0.0 2.0 %encode_and_pick.1 = (bf16[16,1536]{1,0:T(8,128)(2,1)S(1)}, bf16[16,1536]{1,0:T(8,128)(2,1)S(1)}, bf16[32,3072]{1,0:T(8,128)(2,1)S(1)}, bf16[32,3072]{1,0:T(8,12...) custom-call(bf16[128,3072]{1,0:T(8,128)(2,1)} %bitcast.3, s32[1,128]{1,0:T(1,128)} %bitcast.4, ...), custom_call_target="tpu_custom_call" | custom-call | tf_op jit(solution)/shard_map/encode_and_pick/pallas_call | solution.py:262
  2.1 4.0 %collective-permute-start.4 = (bf16[32,3072]{1,0:T(8,128)(2,1)S(1)}, bf16[32,3072]{1,0:T(8,128)(2,1)S(1)}, u32[]{:S(2)}, u32[]{:S(2)}) collective-permute-start(bf16[32,3072]{1,0:T(8,128)(2,1)S(1)} %get-tuple-element.33), channel_id=1, source_target_pairs={{0,3},{1,2},{2,1},{3,0},{4,7},{5,6},{6,5},{7,4},{8,11},{9,10},{10,... | collective-permute-start | bytes 589832 | tf_op jit(solution)/shard_map/ppermute | solution.py:324
  6.0 0.0 collective-permute-start
  6.0 1.2 %collective-permute-done = bf16[16,1536]{1,0:T(8,128)(2,1)S(1)} collective-permute-done((bf16[16,1536]{1,0:T(8,128)(2,1)S(1)}, bf16[16,1536]{1,0:T(8,128)(2,1)S(1)}, u32[]{:S(2)}, u32[]{:S(2)}) %collective-permute-start) | collective-permute-done | bytes 49184 | tf_op jit(solution)/shard_map/ppermute | solution.py:324
  7.3 3.7 %collective-permute-start.3 = (bf16[16,1536]{1,0:T(8,128)(2,1)S(1)}, bf16[16,1536]{1,0:T(8,128)(2,1)S(1)}, u32[]{:S(2)}, u32[]{:S(2)}) collective-permute-start(bf16[16,1536]{1,0:T(8,128)(2,1)S(1)} %add.12), channel_id=1, source_target_pairs={{0,24},{4,28},{8,16},{12,20},{16,8},{20,12},{24,0},{28,4},{1,25},{... | collective-permute-start | bytes 147464 | tf_op jit(solution)/shard_map/ppermute | solution.py:324
  10.9 0.0 collective-permute-start.2
  10.9 0.8 %collective-permute-start.1 = (bf16[16,1536]{1,0:T(8,128)(2,1)S(1)}, bf16[16,1536]{1,0:T(8,128)(2,1)S(1)}, u32[]{:S(2)}, u32[]{:S(2)}) collective-permute-start(bf16[16,1536]{1,0:T(8,128)(2,1)S(1)} %add.12), channel_id=1, source_target_pairs={{0,8},{4,12},{8,0},{12,4},{16,24},{20,28},{24,16},{28,20},{1,9},{5... | collective-permute-start | bytes 147464 | tf_op jit(solution)/shard_map/ppermute | solution.py:324
  11.7 0.5 %collective-permute-start.8 = (bf16[32,3072]{1,0:T(8,128)(2,1)S(1)}, bf16[32,3072]{1,0:T(8,128)(2,1)S(1)}, u32[]{:S(2)}, u32[]{:S(2)}) collective-permute-start(bf16[32,3072]{1,0:T(8,128)(2,1)S(1)} %get-tuple-element.36), channel_id=1, source_target_pairs={{0,1},{1,0},{2,3},{3,2},{4,5},{5,4},{6,7},{7,6},{8,9},{9,8},{10,11... | collective-permute-start | bytes 589832 | tf_op jit(solution)/shard_map/ppermute | solution.py:324
  12.3 1.0 %collective-permute-done.3 = bf16[16,1536]{1,0:T(8,128)(2,1)S(1)} collective-permute-done((bf16[16,1536]{1,0:T(8,128)(2,1)S(1)}, bf16[16,1536]{1,0:T(8,128)(2,1)S(1)}, u32[]{:S(2)}, u32[]{:S(2)}) %collective-permute-start.3) | collective-permute-done | bytes 49184 | tf_op jit(solution)/shard_map/ppermute | solution.py:324
  13.3 0.5 %collective-permute-start.9 = (bf16[32,3072]{1,0:T(8,128)(2,1)S(1)}, bf16[32,3072]{1,0:T(8,128)(2,1)S(1)}, u32[]{:S(2)}, u32[]{:S(2)}) collective-permute-start(bf16[32,3072]{1,0:T(8,128)(2,1)S(1)} %get-tuple-element.37), channel_id=1, source_target_pairs={{0,2},{1,3},{2,0},{3,1},{4,6},{5,7},{6,4},{7,5},{8,10},{9,11},{10,... | collective-permute-start | bytes 589832 | tf_op jit(solution)/shard_map/ppermute | solution.py:324
  13.8 0.0 collective-permute-done.4.refs_3_
  13.8 2.1 %collective-permute-done.2 = bf16[16,1536]{1,0:T(8,128)(2,1)S(1)} collective-permute-done((bf16[16,1536]{1,0:T(8,128)(2,1)S(1)}, bf16[16,1536]{1,0:T(8,128)(2,1)S(1)}, u32[]{:S(2)}, u32[]{:S(2)}) %collective-permute-start.2) | collective-permute-done | bytes 49184 | tf_op jit(solution)/shard_map/ppermute | solution.py:324
  15.9 0.0 collective-permute-done.1
  15.9 0.5 %collective-permute-start.7 = (bf16[16,1536]{1,0:T(8,128)(2,1)S(1)}, bf16[16,1536]{1,0:T(8,128)(2,1)S(1)}, u32[]{:S(2)}, u32[]{:S(2)}) collective-permute-start(bf16[16,1536]{1,0:T(8,128)(2,1)S(1)} %add_add_fusion), channel_id=1, source_target_pairs={{0,3},{1,2},{2,1},{3,0},{4,7},{5,6},{6,5},{7,4},{8,11},{9,10},{10,... | collective-permute-start | bytes 147464 | tf_op jit(solution)/shard_map/ppermute | solution.py:324
  16.5 1.5 %collective-permute-start.6 = (bf16[16,1536]{1,0:T(8,128)(2,1)S(1)}, bf16[16,1536]{1,0:T(8,128)(2,1)S(1)}, u32[]{:S(2)}, u32[]{:S(2)}) collective-permute-start(bf16[16,1536]{1,0:T(8,128)(2,1)S(1)} %add_add_fusion), channel_id=1, source_target_pairs={{0,2},{1,3},{2,0},{3,1},{4,6},{5,7},{6,4},{7,5},{8,10},{9,11},{10,... | collective-permute-start | bytes 147464 | tf_op jit(solution)/shard_map/ppermute | solution.py:324
  18.0 1.5 %collective-permute-start.5 = (bf16[16,1536]{1,0:T(8,128)(2,1)S(1)}, bf16[16,1536]{1,0:T(8,128)(2,1)S(1)}, u32[]{:S(2)}, u32[]{:S(2)}) collective-permute-start(bf16[16,1536]{1,0:T(8,128)(2,1)S(1)} %add_add_fusion), channel_id=1, source_target_pairs={{0,1},{1,0},{2,3},{3,2},{4,5},{5,4},{6,7},{7,6},{8,9},{9,8},{10,11... | collective-permute-start | bytes 147464 | tf_op jit(solution)/shard_map/ppermute | solution.py:324
  19.5 0.0 collective-permute-done.8.refs_1_
  19.5 0.8 %collective-permute-done.9.refs_2_ = bf16[32,3072]{1,0:T(8,128)(2,1)S(1)} collective-permute-done((bf16[32,3072]{1,0:T(8,128)(2,1)S(1)}, bf16[32,3072]{1,0:T(8,128)(2,1)S(1)}, u32[]{:S(2)}, u32[]{:S(2)}) %collective-permute-start.9) | collective-permute-done | bytes 196640 | tf_op jit(solution)/shard_map/ppermute | solution.py:324
  20.3 1.0 %whiten_receivers.1 = (f32[128,1536]{1,0:T(8,128)S(1)}, f32[128,1536]{1,0:T(8,128)S(1)}, f32[128,1536]{1,0:T(8,128)S(1)}, f32[128,128]{1,0:T(8,128)S(1)}) custom-call(bf16[32,3072]{1,0:T(8,128)(2,1)S(1)} %get-tuple-element.35.refs_0_, bf16[32,3072]{1,0:T(8,128)(2,1)S(1)} %collective-permute-done.8.refs_1_, ...), custom_call_target="tpu_custom_call" | custom-call | flops 402653184 | bytes 1572864 | tf_op jit(solution)/shard_map/whiten_receivers/pallas_call | solution.py:286
  21.3 0.0 collective-permute-done.7
  21.3 0.1 collective-permute-done.6
  21.3 0.8 %collective-permute-done.5 = bf16[16,1536]{1,0:T(8,128)(2,1)S(1)} collective-permute-done((bf16[16,1536]{1,0:T(8,128)(2,1)S(1)}, bf16[16,1536]{1,0:T(8,128)(2,1)S(1)}, u32[]{:S(2)}, u32[]{:S(2)}) %collective-permute-start.5) | collective-permute-done | bytes 49184 | tf_op jit(solution)/shard_map/ppermute | solution.py:324
  22.1 0.1 collective-permute-start.10
  22.2 0.0 copy-done
  22.2 2.3 %stack_own_half.1.refs_0_ = f32[256,301]{1,0:T(8,128)S(1)} custom-call(bf16[64,1536]{1,0:T(8,128)(2,1)S(1)} %constant_dynamic-update-slice_fusion.slabs_ref, f32[128,1536]{1,0:T(8,128)S(1)} %get-tuple-element.47.rcv_re, f32[128,1536]{1,0:T(8,128)S(1)} %get-tuple-element.48.rcv_im, f32[128,1536]{1,0:T(8,128)S(1)} %get-tuple-element.49.rcv_both, ...), custom_call_target="tpu_custom_call" | custom-call | flops 471859200 | bytes 3145728 | tf_op jit(solution)/shard_map/stack_own_half/pallas_call | solution.py:309
  24.5 0.0 collective-permute-done.10.slabs_ref
  24.6 3.0 %stack_other_half.1 = f32[512,301]{1,0:T(8,128)} custom-call(bf16[64,1536]{1,0:T(8,128)(2,1)S(1)} %collective-permute-done.10.slabs_ref, f32[128,1536]{1,0:T(8,128)S(1)} %get-tuple-element.47.rcv_re, f32[128,1536]{1,0:T(8,128)S(1)} %get-tuple-element.48.rcv_im, f32[128,1536]{1,0:T(8,128)S(1)} %get-tuple-element.49.rcv_both, ...), custom_call_target="tpu_custom_call" | custom-call | flops 471859200 | bytes 3145728 | tf_op jit(solution)/shard_map/stack_other_half/pallas_call | solution.py:309
  (6 shorter events, 0.0 us)
Async XLA Ops:
  0.0 22.2 %copy-start = (bf16[3072,384]{1,0:T(8,128)(2,1)S(1)}, bf16[3072,384]{1,0:T(8,128)(2,1)}, u32[]{:S(2)}) copy-start(bf16[3072,384]{1,0:T(8,128)(2,1)} %constant.2.clone.table_ref) | copy-start | bytes 7077892
  2.1 11.7 %collective-permute-start.4 = (bf16[32,3072]{1,0:T(8,128)(2,1)S(1)}, bf16[32,3072]{1,0:T(8,128)(2,1)S(1)}, u32[]{:S(2)}, u32[]{:S(2)}) collective-permute-start(bf16[32,3072]{1,0:T(8,128)(2,1)S(1)} %get-tuple-element.33), channel_id=1, source_target_pairs={{0,3},{1,2},{2,1},{3,0},{4,7},{5,6},{6,5},{7,4},{8,11},{9,10},{10,... | collective-permute-start | bytes 589832 | tf_op jit(solution)/shard_map/ppermute | solution.py:324
  6.0 1.2 %collective-permute-start = (bf16[16,1536]{1,0:T(8,128)(2,1)S(1)}, bf16[16,1536]{1,0:T(8,128)(2,1)S(1)}, u32[]{:S(2)}, u32[]{:S(2)}) collective-permute-start(bf16[16,1536]{1,0:T(8,128)(2,1)S(1)} %get-tuple-element.29), channel_id=1, source_target_pairs={{0,4},{4,0},{8,12},{12,8},{16,20},{20,16},{24,28},{28,24},{1,5},{5... | collective-permute-start | bytes 147464 | tf_op jit(solution)/shard_map/ppermute | solution.py:324
  7.3 6.0 %collective-permute-start.3 = (bf16[16,1536]{1,0:T(8,128)(2,1)S(1)}, bf16[16,1536]{1,0:T(8,128)(2,1)S(1)}, u32[]{:S(2)}, u32[]{:S(2)}) collective-permute-start(bf16[16,1536]{1,0:T(8,128)(2,1)S(1)} %add.12), channel_id=1, source_target_pairs={{0,24},{4,28},{8,16},{12,20},{16,8},{20,12},{24,0},{28,4},{1,25},{... | collective-permute-start | bytes 147464 | tf_op jit(solution)/shard_map/ppermute | solution.py:324
  10.9 5.0 %collective-permute-start.2 = (bf16[16,1536]{1,0:T(8,128)(2,1)S(1)}, bf16[16,1536]{1,0:T(8,128)(2,1)S(1)}, u32[]{:S(2)}, u32[]{:S(2)}) collective-permute-start(bf16[16,1536]{1,0:T(8,128)(2,1)S(1)} %add.12), channel_id=1, source_target_pairs={{0,16},{4,20},{8,24},{12,28},{16,0},{20,4},{24,8},{28,12},{1,17},{... | collective-permute-start | bytes 147464 | tf_op jit(solution)/shard_map/ppermute | solution.py:324
  10.9 5.0 %collective-permute-start.1 = (bf16[16,1536]{1,0:T(8,128)(2,1)S(1)}, bf16[16,1536]{1,0:T(8,128)(2,1)S(1)}, u32[]{:S(2)}, u32[]{:S(2)}) collective-permute-start(bf16[16,1536]{1,0:T(8,128)(2,1)S(1)} %add.12), channel_id=1, source_target_pairs={{0,8},{4,12},{8,0},{12,4},{16,24},{20,28},{24,16},{28,20},{1,9},{5... | collective-permute-start | bytes 147464 | tf_op jit(solution)/shard_map/ppermute | solution.py:324
  11.7 7.8 %collective-permute-start.8 = (bf16[32,3072]{1,0:T(8,128)(2,1)S(1)}, bf16[32,3072]{1,0:T(8,128)(2,1)S(1)}, u32[]{:S(2)}, u32[]{:S(2)}) collective-permute-start(bf16[32,3072]{1,0:T(8,128)(2,1)S(1)} %get-tuple-element.36), channel_id=1, source_target_pairs={{0,1},{1,0},{2,3},{3,2},{4,5},{5,4},{6,7},{7,6},{8,9},{9,8},{10,11... | collective-permute-start | bytes 589832 | tf_op jit(solution)/shard_map/ppermute | solution.py:324
  13.3 7.0 %collective-permute-start.9 = (bf16[32,3072]{1,0:T(8,128)(2,1)S(1)}, bf16[32,3072]{1,0:T(8,128)(2,1)S(1)}, u32[]{:S(2)}, u32[]{:S(2)}) collective-permute-start(bf16[32,3072]{1,0:T(8,128)(2,1)S(1)} %get-tuple-element.37), channel_id=1, source_target_pairs={{0,2},{1,3},{2,0},{3,1},{4,6},{5,7},{6,4},{7,5},{8,10},{9,11},{10,... | collective-permute-start | bytes 589832 | tf_op jit(solution)/shard_map/ppermute | solution.py:324
  15.9 5.3 %collective-permute-start.7 = (bf16[16,1536]{1,0:T(8,128)(2,1)S(1)}, bf16[16,1536]{1,0:T(8,128)(2,1)S(1)}, u32[]{:S(2)}, u32[]{:S(2)}) collective-permute-start(bf16[16,1536]{1,0:T(8,128)(2,1)S(1)} %add_add_fusion), channel_id=1, source_target_pairs={{0,3},{1,2},{2,1},{3,0},{4,7},{5,6},{6,5},{7,4},{8,11},{9,10},{10,... | collective-permute-start | bytes 147464 | tf_op jit(solution)/shard_map/ppermute | solution.py:324
  16.5 4.8 %collective-permute-start.6 = (bf16[16,1536]{1,0:T(8,128)(2,1)S(1)}, bf16[16,1536]{1,0:T(8,128)(2,1)S(1)}, u32[]{:S(2)}, u32[]{:S(2)}) collective-permute-start(bf16[16,1536]{1,0:T(8,128)(2,1)S(1)} %add_add_fusion), channel_id=1, source_target_pairs={{0,2},{1,3},{2,0},{3,1},{4,6},{5,7},{6,4},{7,5},{8,10},{9,11},{10,... | collective-permute-start | bytes 147464 | tf_op jit(solution)/shard_map/ppermute | solution.py:324
  18.0 4.1 %collective-permute-start.5 = (bf16[16,1536]{1,0:T(8,128)(2,1)S(1)}, bf16[16,1536]{1,0:T(8,128)(2,1)S(1)}, u32[]{:S(2)}, u32[]{:S(2)}) collective-permute-start(bf16[16,1536]{1,0:T(8,128)(2,1)S(1)} %add_add_fusion), channel_id=1, source_target_pairs={{0,1},{1,0},{2,3},{3,2},{4,5},{5,4},{6,7},{7,6},{8,9},{9,8},{10,11... | collective-permute-start | bytes 147464 | tf_op jit(solution)/shard_map/ppermute | solution.py:324
  22.1 2.4 %collective-permute-start.10 = (bf16[64,1536]{1,0:T(8,128)(2,1)S(1)}, bf16[64,1536]{1,0:T(8,128)(2,1)S(1)}, u32[]{:S(2)}, u32[]{:S(2)}) collective-permute-start(bf16[64,1536]{1,0:T(8,128)(2,1)S(1)} %constant_dynamic-update-slice_fusion.slabs_ref), channel_id=1, source_target_pairs={{0,4},{4,0},{8,12},{12,8},{16,20},{20,16},{24,28},{28,24},{1,5},{5... | collective-permute-start | bytes 589832 | tf_op jit(solution)/shard_map/ppermute | solution.py:324

commit v13 on v11

--- a/solution.py
+++ b/solution.py
@@ -19,7 +19,6 @@
 
 LANES = 128
 BLOCK = 256
-CHUNK = 512
 MEBI = 1 << 20
 FIRST_LAG = LANES - LAG
 VMEM = pl.BlockSpec(memory_space=pltpu.VMEM)
@@ -177,10 +176,8 @@
     def spread(ref, block, row):
         return jnp.concatenate([ref[block, pl.ds(row, 8, stride=0), :]] * (tile // 8), axis=0)
 
-    def multiply(chunk, sub):
-        block = chunk * (CHUNK // LANES) + sub
-        at = slice(block * LANES, (block + 1) * LANES)
-        lanes = slice(sub * LANES, (sub + 1) * LANES)
+    def multiply(block, carry):
+        at = pl.ds(pl.multiple_of(block * LANES, LANES), LANES)
         for first in range(0, keep, tile):
             rows = [slice(t * keep + first, t * keep + first + tile) for t in range(segments)]
             r_re = [rcv_re[row, at] for row in rows]
@@ -195,30 +192,24 @@
                     w.append(spread(src_sum, block, row) * r_re[t])
                 p, q, w = (functools.reduce(jnp.add, part) for part in (p, q, w))
                 to = slice(source * keep + first, source * keep + first + tile)
-                cross[chunk, 0, to, lanes] = (p + q).astype(cross.dtype)
-                cross[chunk, 1, to, lanes] = (w - p).astype(cross.dtype)
-
-    def project(chunk, place, part):
-        first = place * nbins + chunk * CHUNK
+                cross[0, block, to] = (p + q).astype(cross.dtype)
+                cross[1, block, to] = (w - p).astype(cross.dtype)
+        return carry
+
+    lax.fori_loop(0, nbins // LANES, multiply, 0)
+
+    def project(place, part):
+        value = [cross[place, block, part] for block in range(nbins // LANES)]
         return jnp.dot(
-            cross[chunk, place, part].astype(jnp.bfloat16),
-            table_ref[first : first + CHUNK],
+            jnp.concatenate(value, axis=1).astype(jnp.bfloat16),
+            table_ref[place * nbins : (place + 1) * nbins],
             preferred_element_type=jnp.float32,
         )
 
-    chunks, subs = nbins // CHUNK, CHUNK // LANES
-    totals = [[], []]
-    for chunk in range(chunks):
-        for sub in range(subs):
-            multiply(chunk, sub)
-            if chunk > 0 and sub % (subs // 2) == 0:
-                place = sub // (subs // 2)
-                totals[place].append(project(chunk - 1, place, slice(None)))
-    tops = [functools.reduce(jnp.add, part) for part in totals]
     ends = []
     for first in (0, half // 2):
         at = slice(first * keep, (first + half // 2) * keep)
-        ends.append([tops[place][at] + project(chunks - 1, place, at) for place in range(2)])
+        ends.append([project(place, at) for place in range(2)])
 
     lags = result.shape[1]
     scale = 2.0 / math.sqrt(nbins)
@@ -311,7 +302,7 @@
     keep = receivers[0].shape[0] // segments
     count, rows, lags = segments * half, half * keep, 2 * LAG + 1
     part = pltpu.VMEM((nbins // LANES, count, LANES), jnp.float32)
-    cross = pltpu.VMEM((nbins // CHUNK, 2, rows, CHUNK), kind_for(keep))
+    cross = pltpu.VMEM((2, nbins // LANES, rows, LANES), kind_for(keep))
     scratch = [part, part, part, cross]
     if rest:
         scratch += [pltpu.VMEM((rows, lags), jnp.float32), pltpu.SemaphoreType.DMA((1 + half,))]

time: 27.3 us -> 27.5 us (level)
  transfers between devices with their start and end apart: 11 -> 11, of which waited for: 6 -> 6; matrix products, arithmetic and copies ran while one was open for 0% -> 0% of each run, Pallas kernels for 11% -> 12%
where the time goes in v13:
time: 27.5 us; the launch traced here: 27.3 us
  starting transfers between devices  13.1 us (48%)
  Pallas kernels  8.06 us (29%)
  waiting for transfers between devices  5.99 us (22%)
    ppermute x11, starting transfers between devices, swapped(): return lax.ppermute(value, axis, [(i, i ^ step) for i in range(size)])  13.1 us
    ppermute x11, waiting for transfers between devices, swapped(): return lax.ppermute(value, axis, [(i, i ^ step) for i in range(size)])  5.99 us
    pallas_call x2, Pallas kernels, stack_half(): pl.pallas_call(functools.partial(stack_kernel, segments), out_shape=jax.S...  5.06 us
    pallas_call x1, Pallas kernels, encode(): pl.pallas_call(functools.partial(encode_kernel, segments), out_shape=(sla...  2.02 us
    pallas_call x1, Pallas kernels, whiten_blocks(): pl.pallas_call(functools.partial(whiten_kernel, segments), out_shape=(par...  0.98 us
  transfers between devices with their start and end apart: 11, of which 6 were waited for; matrix products, arithmetic and copies ran while one was open for 0% of the time, Pallas kernels for 12%

profile of v13, /device:TPU:0, one launch (start us, length us, event | category | flops | bytes accessed | tf_op | source)
XLA Modules:
  0.0 27.3 jit_solution(4474950386453175133)
XLA Ops:
  0.0 0.0 copy-start
  0.0 2.0 %encode_and_pick.1 = (bf16[16,1536]{1,0:T(8,128)(2,1)S(1)}, bf16[16,1536]{1,0:T(8,128)(2,1)S(1)}, bf16[32,3072]{1,0:T(8,128)(2,1)S(1)}, bf16[32,3072]{1,0:T(8,12...) custom-call(bf16[128,3072]{1,0:T(8,128)(2,1)} %bitcast.3, s32[1,128]{1,0:T(1,128)} %bitcast.4, ...), custom_call_target="tpu_custom_call" | custom-call | tf_op jit(solution)/shard_map/encode_and_pick/pallas_call | solution.py:262
  2.0 4.0 %collective-permute-start.4 = (bf16[32,3072]{1,0:T(8,128)(2,1)S(1)}, bf16[32,3072]{1,0:T(8,128)(2,1)S(1)}, u32[]{:S(2)}, u32[]{:S(2)}) collective-permute-start(bf16[32,3072]{1,0:T(8,128)(2,1)S(1)} %get-tuple-element.33), channel_id=1, source_target_pairs={{0,3},{1,2},{2,1},{3,0},{4,7},{5,6},{6,5},{7,4},{8,11},{9,10},{10,... | collective-permute-start | bytes 589832 | tf_op jit(solution)/shard_map/ppermute | solution.py:324
  6.0 0.0 collective-permute-start
  6.0 1.2 %collective-permute-done = bf16[16,1536]{1,0:T(8,128)(2,1)S(1)} collective-permute-done((bf16[16,1536]{1,0:T(8,128)(2,1)S(1)}, bf16[16,1536]{1,0:T(8,128)(2,1)S(1)}, u32[]{:S(2)}, u32[]{:S(2)}) %collective-permute-start) | collective-permute-done | bytes 49184 | tf_op jit(solution)/shard_map/ppermute | solution.py:324
  7.2 3.7 %collective-permute-start.3 = (bf16[16,1536]{1,0:T(8,128)(2,1)S(1)}, bf16[16,1536]{1,0:T(8,128)(2,1)S(1)}, u32[]{:S(2)}, u32[]{:S(2)}) collective-permute-start(bf16[16,1536]{1,0:T(8,128)(2,1)S(1)} %add.12), channel_id=1, source_target_pairs={{0,24},{4,28},{8,16},{12,20},{16,8},{20,12},{24,0},{28,4},{1,25},{... | collective-permute-start | bytes 147464 | tf_op jit(solution)/shard_map/ppermute | solution.py:324
  10.9 0.0 collective-permute-start.2
  10.9 0.8 %collective-permute-start.1 = (bf16[16,1536]{1,0:T(8,128)(2,1)S(1)}, bf16[16,1536]{1,0:T(8,128)(2,1)S(1)}, u32[]{:S(2)}, u32[]{:S(2)}) collective-permute-start(bf16[16,1536]{1,0:T(8,128)(2,1)S(1)} %add.12), channel_id=1, source_target_pairs={{0,8},{4,12},{8,0},{12,4},{16,24},{20,28},{24,16},{28,20},{1,9},{5... | collective-permute-start | bytes 147464 | tf_op jit(solution)/shard_map/ppermute | solution.py:324
  11.7 0.5 %collective-permute-start.8 = (bf16[32,3072]{1,0:T(8,128)(2,1)S(1)}, bf16[32,3072]{1,0:T(8,128)(2,1)S(1)}, u32[]{:S(2)}, u32[]{:S(2)}) collective-permute-start(bf16[32,3072]{1,0:T(8,128)(2,1)S(1)} %get-tuple-element.36), channel_id=1, source_target_pairs={{0,1},{1,0},{2,3},{3,2},{4,5},{5,4},{6,7},{7,6},{8,9},{9,8},{10,11... | collective-permute-start | bytes 589832 | tf_op jit(solution)/shard_map/ppermute | solution.py:324
  12.2 1.0 %collective-permute-done.3 = bf16[16,1536]{1,0:T(8,128)(2,1)S(1)} collective-permute-done((bf16[16,1536]{1,0:T(8,128)(2,1)S(1)}, bf16[16,1536]{1,0:T(8,128)(2,1)S(1)}, u32[]{:S(2)}, u32[]{:S(2)}) %collective-permute-start.3) | collective-permute-done | bytes 49184 | tf_op jit(solution)/shard_map/ppermute | solution.py:324
  13.3 0.5 %collective-permute-start.9 = (bf16[32,3072]{1,0:T(8,128)(2,1)S(1)}, bf16[32,3072]{1,0:T(8,128)(2,1)S(1)}, u32[]{:S(2)}, u32[]{:S(2)}) collective-permute-start(bf16[32,3072]{1,0:T(8,128)(2,1)S(1)} %get-tuple-element.37), channel_id=1, source_target_pairs={{0,2},{1,3},{2,0},{3,1},{4,6},{5,7},{6,4},{7,5},{8,10},{9,11},{10,... | collective-permute-start | bytes 589832 | tf_op jit(solution)/shard_map/ppermute | solution.py:324
  13.8 0.0 collective-permute-done.4.refs_3_
  13.8 2.1 %collective-permute-done.2 = bf16[16,1536]{1,0:T(8,128)(2,1)S(1)} collective-permute-done((bf16[16,1536]{1,0:T(8,128)(2,1)S(1)}, bf16[16,1536]{1,0:T(8,128)(2,1)S(1)}, u32[]{:S(2)}, u32[]{:S(2)}) %collective-permute-start.2) | collective-permute-done | bytes 49184 | tf_op jit(solution)/shard_map/ppermute | solution.py:324
  15.9 0.0 collective-permute-done.1
  15.9 0.5 %collective-permute-start.7 = (bf16[16,1536]{1,0:T(8,128)(2,1)S(1)}, bf16[16,1536]{1,0:T(8,128)(2,1)S(1)}, u32[]{:S(2)}, u32[]{:S(2)}) collective-permute-start(bf16[16,1536]{1,0:T(8,128)(2,1)S(1)} %add_add_fusion), channel_id=1, source_target_pairs={{0,3},{1,2},{2,1},{3,0},{4,7},{5,6},{6,5},{7,4},{8,11},{9,10},{10,... | collective-permute-start | bytes 147464 | tf_op jit(solution)/shard_map/ppermute | solution.py:324
  16.5 1.5 %collective-permute-start.6 = (bf16[16,1536]{1,0:T(8,128)(2,1)S(1)}, bf16[16,1536]{1,0:T(8,128)(2,1)S(1)}, u32[]{:S(2)}, u32[]{:S(2)}) collective-permute-start(bf16[16,1536]{1,0:T(8,128)(2,1)S(1)} %add_add_fusion), channel_id=1, source_target_pairs={{0,2},{1,3},{2,0},{3,1},{4,6},{5,7},{6,4},{7,5},{8,10},{9,11},{10,... | collective-permute-start | bytes 147464 | tf_op jit(solution)/shard_map/ppermute | solution.py:324
  18.0 1.5 %collective-permute-start.5 = (bf16[16,1536]{1,0:T(8,128)(2,1)S(1)}, bf16[16,1536]{1,0:T(8,128)(2,1)S(1)}, u32[]{:S(2)}, u32[]{:S(2)}) collective-permute-start(bf16[16,1536]{1,0:T(8,128)(2,1)S(1)} %add_add_fusion), channel_id=1, source_target_pairs={{0,1},{1,0},{2,3},{3,2},{4,5},{5,4},{6,7},{7,6},{8,9},{9,8},{10,11... | collective-permute-start | bytes 147464 | tf_op jit(solution)/shard_map/ppermute | solution.py:324
  19.5 0.0 collective-permute-done.8.refs_1_
  19.5 0.8 %collective-permute-done.9.refs_2_ = bf16[32,3072]{1,0:T(8,128)(2,1)S(1)} collective-permute-done((bf16[32,3072]{1,0:T(8,128)(2,1)S(1)}, bf16[32,3072]{1,0:T(8,128)(2,1)S(1)}, u32[]{:S(2)}, u32[]{:S(2)}) %collective-permute-start.9) | collective-permute-done | bytes 196640 | tf_op jit(solution)/shard_map/ppermute | solution.py:324
  20.2 1.0 %whiten_receivers.1 = (f32[128,1536]{1,0:T(8,128)S(1)}, f32[128,1536]{1,0:T(8,128)S(1)}, f32[128,1536]{1,0:T(8,128)S(1)}, f32[128,128]{1,0:T(8,128)S(1)}) custom-call(bf16[32,3072]{1,0:T(8,128)(2,1)S(1)} %get-tuple-element.35.refs_0_, bf16[32,3072]{1,0:T(8,128)(2,1)S(1)} %collective-permute-done.8.refs_1_, ...), custom_call_target="tpu_custom_call" | custom-call | flops 402653184 | bytes 1572864 | tf_op jit(solution)/shard_map/whiten_receivers/pallas_call | solution.py:286
  21.2 0.0 collective-permute-done.7
  21.2 0.1 collective-permute-done.6
  21.3 0.8 %collective-permute-done.5 = bf16[16,1536]{1,0:T(8,128)(2,1)S(1)} collective-permute-done((bf16[16,1536]{1,0:T(8,128)(2,1)S(1)}, bf16[16,1536]{1,0:T(8,128)(2,1)S(1)}, u32[]{:S(2)}, u32[]{:S(2)}) %collective-permute-start.5) | collective-permute-done | bytes 49184 | tf_op jit(solution)/shard_map/ppermute | solution.py:324
  22.1 0.1 collective-permute-start.10
  22.2 0.0 copy-done
  22.2 2.2 %stack_own_half.1.refs_0_ = f32[256,301]{1,0:T(8,128)S(1)} custom-call(bf16[64,1536]{1,0:T(8,128)(2,1)S(1)} %constant_dynamic-update-slice_fusion.slabs_ref, f32[128,1536]{1,0:T(8,128)S(1)} %get-tuple-element.47.rcv_re, f32[128,1536]{1,0:T(8,128)S(1)} %get-tuple-element.48.rcv_im, f32[128,1536]{1,0:T(8,128)S(1)} %get-tuple-element.49.rcv_both, ...), custom_call_target="tpu_custom_call" | custom-call | flops 471859200 | bytes 3145728 | tf_op jit(solution)/shard_map/stack_own_half/pallas_call | solution.py:309
  24.4 0.0 collective-permute-done.10.slabs_ref
  24.4 2.9 %stack_other_half.1 = f32[512,301]{1,0:T(8,128)} custom-call(bf16[64,1536]{1,0:T(8,128)(2,1)S(1)} %collective-permute-done.10.slabs_ref, f32[128,1536]{1,0:T(8,128)S(1)} %get-tuple-element.47.rcv_re, f32[128,1536]{1,0:T(8,128)S(1)} %get-tuple-element.48.rcv_im, f32[128,1536]{1,0:T(8,128)S(1)} %get-tuple-element.49.rcv_both, ...), custom_call_target="tpu_custom_call" | custom-call | flops 471859200 | bytes 3145728 | tf_op jit(solution)/shard_map/stack_other_half/pallas_call | solution.py:309
  (6 shorter events, 0.0 us)
Async XLA Ops:
  0.0 22.2 %copy-start = (bf16[3072,256]{1,0:T(8,128)(2,1)S(1)}, bf16[3072,256]{1,0:T(8,128)(2,1)}, u32[]{:S(2)}) copy-start(bf16[3072,256]{1,0:T(8,128)(2,1)} %constant.2.clone.table_ref) | copy-start | bytes 4718596
  2.0 11.7 %collective-permute-start.4 = (bf16[32,3072]{1,0:T(8,128)(2,1)S(1)}, bf16[32,3072]{1,0:T(8,128)(2,1)S(1)}, u32[]{:S(2)}, u32[]{:S(2)}) collective-permute-start(bf16[32,3072]{1,0:T(8,128)(2,1)S(1)} %get-tuple-element.33), channel_id=1, source_target_pairs={{0,3},{1,2},{2,1},{3,0},{4,7},{5,6},{6,5},{7,4},{8,11},{9,10},{10,... | collective-permute-start | bytes 589832 | tf_op jit(solution)/shard_map/ppermute | solution.py:324
  6.0 1.2 %collective-permute-start = (bf16[16,1536]{1,0:T(8,128)(2,1)S(1)}, bf16[16,1536]{1,0:T(8,128)(2,1)S(1)}, u32[]{:S(2)}, u32[]{:S(2)}) collective-permute-start(bf16[16,1536]{1,0:T(8,128)(2,1)S(1)} %get-tuple-element.29), channel_id=1, source_target_pairs={{0,4},{4,0},{8,12},{12,8},{16,20},{20,16},{24,28},{28,24},{1,5},{5... | collective-permute-start | bytes 147464 | tf_op jit(solution)/shard_map/ppermute | solution.py:324
  7.2 6.0 %collective-permute-start.3 = (bf16[16,1536]{1,0:T(8,128)(2,1)S(1)}, bf16[16,1536]{1,0:T(8,128)(2,1)S(1)}, u32[]{:S(2)}, u32[]{:S(2)}) collective-permute-start(bf16[16,1536]{1,0:T(8,128)(2,1)S(1)} %add.12), channel_id=1, source_target_pairs={{0,24},{4,28},{8,16},{12,20},{16,8},{20,12},{24,0},{28,4},{1,25},{... | collective-permute-start | bytes 147464 | tf_op jit(solution)/shard_map/ppermute | solution.py:324
  10.9 5.0 %collective-permute-start.2 = (bf16[16,1536]{1,0:T(8,128)(2,1)S(1)}, bf16[16,1536]{1,0:T(8,128)(2,1)S(1)}, u32[]{:S(2)}, u32[]{:S(2)}) collective-permute-start(bf16[16,1536]{1,0:T(8,128)(2,1)S(1)} %add.12), channel_id=1, source_target_pairs={{0,16},{4,20},{8,24},{12,28},{16,0},{20,4},{24,8},{28,12},{1,17},{... | collective-permute-start | bytes 147464 | tf_op jit(solution)/shard_map/ppermute | solution.py:324
  10.9 5.0 %collective-permute-start.1 = (bf16[16,1536]{1,0:T(8,128)(2,1)S(1)}, bf16[16,1536]{1,0:T(8,128)(2,1)S(1)}, u32[]{:S(2)}, u32[]{:S(2)}) collective-permute-start(bf16[16,1536]{1,0:T(8,128)(2,1)S(1)} %add.12), channel_id=1, source_target_pairs={{0,8},{4,12},{8,0},{12,4},{16,24},{20,28},{24,16},{28,20},{1,9},{5... | collective-permute-start | bytes 147464 | tf_op jit(solution)/shard_map/ppermute | solution.py:324
  11.7 7.8 %collective-permute-start.8 = (bf16[32,3072]{1,0:T(8,128)(2,1)S(1)}, bf16[32,3072]{1,0:T(8,128)(2,1)S(1)}, u32[]{:S(2)}, u32[]{:S(2)}) collective-permute-start(bf16[32,3072]{1,0:T(8,128)(2,1)S(1)} %get-tuple-element.36), channel_id=1, source_target_pairs={{0,1},{1,0},{2,3},{3,2},{4,5},{5,4},{6,7},{7,6},{8,9},{9,8},{10,11... | collective-permute-start | bytes 589832 | tf_op jit(solution)/shard_map/ppermute | solution.py:324
  13.3 7.0 %collective-permute-start.9 = (bf16[32,3072]{1,0:T(8,128)(2,1)S(1)}, bf16[32,3072]{1,0:T(8,128)(2,1)S(1)}, u32[]{:S(2)}, u32[]{:S(2)}) collective-permute-start(bf16[32,3072]{1,0:T(8,128)(2,1)S(1)} %get-tuple-element.37), channel_id=1, source_target_pairs={{0,2},{1,3},{2,0},{3,1},{4,6},{5,7},{6,4},{7,5},{8,10},{9,11},{10,... | collective-permute-start | bytes 589832 | tf_op jit(solution)/shard_map/ppermute | solution.py:324
  15.9 5.3 %collective-permute-start.7 = (bf16[16,1536]{1,0:T(8,128)(2,1)S(1)}, bf16[16,1536]{1,0:T(8,128)(2,1)S(1)}, u32[]{:S(2)}, u32[]{:S(2)}) collective-permute-start(bf16[16,1536]{1,0:T(8,128)(2,1)S(1)} %add_add_fusion), channel_id=1, source_target_pairs={{0,3},{1,2},{2,1},{3,0},{4,7},{5,6},{6,5},{7,4},{8,11},{9,10},{10,... | collective-permute-start | bytes 147464 | tf_op jit(solution)/shard_map/ppermute | solution.py:324
  16.5 4.8 %collective-permute-start.6 = (bf16[16,1536]{1,0:T(8,128)(2,1)S(1)}, bf16[16,1536]{1,0:T(8,128)(2,1)S(1)}, u32[]{:S(2)}, u32[]{:S(2)}) collective-permute-start(bf16[16,1536]{1,0:T(8,128)(2,1)S(1)} %add_add_fusion), channel_id=1, source_target_pairs={{0,2},{1,3},{2,0},{3,1},{4,6},{5,7},{6,4},{7,5},{8,10},{9,11},{10,... | collective-permute-start | bytes 147464 | tf_op jit(solution)/shard_map/ppermute | solution.py:324
  18.0 4.1 %collective-permute-start.5 = (bf16[16,1536]{1,0:T(8,128)(2,1)S(1)}, bf16[16,1536]{1,0:T(8,128)(2,1)S(1)}, u32[]{:S(2)}, u32[]{:S(2)}) collective-permute-start(bf16[16,1536]{1,0:T(8,128)(2,1)S(1)} %add_add_fusion), channel_id=1, source_target_pairs={{0,1},{1,0},{2,3},{3,2},{4,5},{5,4},{6,7},{7,6},{8,9},{9,8},{10,11... | collective-permute-start | bytes 147464 | tf_op jit(solution)/shard_map/ppermute | solution.py:324
  22.1 2.3 %collective-permute-start.10 = (bf16[64,1536]{1,0:T(8,128)(2,1)S(1)}, bf16[64,1536]{1,0:T(8,128)(2,1)S(1)}, u32[]{:S(2)}, u32[]{:S(2)}) collective-permute-start(bf16[64,1536]{1,0:T(8,128)(2,1)S(1)} %constant_dynamic-update-slice_fusion.slabs_ref), channel_id=1, source_target_pairs={{0,4},{4,0},{8,12},{12,8},{16,20},{20,16},{24,28},{28,24},{1,5},{5... | collective-permute-start | bytes 589832 | tf_op jit(solution)/shard_map/ppermute | solution.py:324

commit v14 on v13

--- a/solution.py
+++ b/solution.py
@@ -85,7 +85,7 @@
 
 
 def encode_kernel(
-    segments, spectra_ref, valid_ref, sources_ref, own_ref, other_ref, *refs
+    segments, spectra_ref, valid_ref, sources_ref, picked_ref, *refs
 ):
     blocks, refs = refs[:segments], refs[segments:]
     encoded_ref, spectra, valid, sources, high, low, arrived = refs
@@ -99,26 +99,24 @@
     channels, width = spectra_ref.shape
     nbins = width // 2
     rounds, per_round = sources.shape
-    half = rounds * per_round // 2
-    index = lax.axis_index("rcv")
+    count = rounds * per_round
+    first_channel = lax.axis_index("rcv") * channels
     copies[1].wait()
     copies[2].wait()
     diagonal = iota((channels, channels), 0) == iota((channels, channels), 1)
     usable = jnp.sum(jnp.where(diagonal, valid[...], 0), axis=1, keepdims=True) != 0
-    row = iota((2 * half, channels), 0)
-    local = jnp.zeros((2 * half, channels), jnp.int32)
-    for place in range(2 * half):
-        number = (index % 2 if place < half else 1 - index % 2) * half + place % half
-        here = sources[number // per_round, number % per_round] - index * channels
+    row = iota((count, channels), 0)
+    local = jnp.zeros((count, channels), jnp.int32)
+    for place in range(count):
+        here = sources[place // per_round, place % per_round] - first_channel
         local = jnp.where(row == place, here, local)
-    onehot = jnp.where(local == iota((2 * half, channels), 1), 1.0, 0.0).astype(jnp.bfloat16)
+    onehot = jnp.where(local == iota((count, channels), 1), 1.0, 0.0).astype(jnp.bfloat16)
     copies[0].wait()
     encoded = jnp.where(usable, spectra[...].astype(jnp.float32), UNUSABLE).astype(jnp.bfloat16)
     picked = jnp.dot(onehot, encoded, preferred_element_type=jnp.float32)
     for at, re, im in whitening(picked[:, :nbins], picked[:, nbins:], high, low, UNUSABLE):
-        for first, ref in ((0, own_ref), (half, other_ref)):
-            rows = slice(first, first + half)
-            ref[:, at] = jnp.concatenate([re[rows], im[rows]], axis=0).astype(ref.dtype)
+        picked_ref[:count, at] = re.astype(picked_ref.dtype)
+        picked_ref[count:, at] = im.astype(picked_ref.dtype)
     encoded_ref[...] = encoded.astype(encoded_ref.dtype)
     keep = channels // segments
     for step, block in enumerate(blocks):
@@ -139,39 +137,29 @@
     valid_ref[...] = usable_rows(real)
 
 
-def stack_kernel(
-    segments, slabs_ref, rcv_re, rcv_im, rcv_both, rcv_valid, table_ref, *refs
-):
-    *rest, out_ref, src_re, src_diff, src_sum, cross = refs[: 6 if len(refs) == 8 else 5]
-    half = slabs_ref.shape[0] // (2 * segments)
-    nbins = slabs_ref.shape[1]
-    keep = rcv_re.shape[0] // segments
-    rows = half * keep
-    if rest:
-        result, written = refs[6:]
-        part = lax.axis_index("rcv") % 2
-        pieces = max(1, half // 4)
-        at = pl.multiple_of(part * rows, rows)
-        copies = [
-            pltpu.make_async_copy(rest[0], out_ref.at[pl.ds(at, rows)], written.at[0])
-        ]
-        copies[0].start()
-    else:
-        result = out_ref
-    slabs = slabs_ref[...].astype(jnp.float32)
-    real = jnp.concatenate(
-        [slabs[2 * half * t : 2 * half * t + half] for t in range(segments)], axis=0
-    )
-    imag = jnp.concatenate(
-        [slabs[2 * half * t + half : 2 * half * (t + 1)] for t in range(segments)], axis=0
-    )
+def stack_kernel(places, stage, *refs):
+    first_stage, last_stage = stage
+    segments = len(places)
+    slabs, refs = refs[:segments], refs[segments:]
+    rcv_re, rcv_im, rcv_both, rcv_valid, table_ref, *refs = refs
+    before, refs = ([], refs) if first_stage else (refs[:2], refs[2:])
+    after, refs = (refs[:1], refs[1:]) if last_stage else (refs[:2], refs[2:])
+    src_re, src_diff, src_sum, cross, *refs = refs
+    count, nbins = slabs[0].shape[0] // 2, slabs[0].shape[1]
+    rows = cross.shape[2]
+    keep = rows // count
+    core = lax.axis_index("rcv") % 2
+    at_rows = [pl.multiple_of(place(core) * keep, keep) for place in places]
+    values = [slab[...].astype(jnp.float32) for slab in slabs]
+    real = jnp.concatenate([value[:count] for value in values], axis=0)
+    imag = jnp.concatenate([value[count:] for value in values], axis=0)
     usable = real < USABLE_BELOW
     real, imag = jnp.where(usable, real, 0.0), jnp.where(usable, imag, 0.0)
     src_valid = jnp.where(usable[:, :LANES], 1.0, 0.0)
     for ref, value in ((src_re, real), (src_diff, imag - real), (src_sum, imag + real)):
         for block in range(nbins // LANES):
             ref[block] = value[:, block * LANES : (block + 1) * LANES]
-    tile = min(keep, 16)
+    tile = keep if segments <= 2 else min(keep, 16)
 
     def spread(ref, block, row):
         return jnp.concatenate([ref[block, pl.ds(row, 8, stride=0), :]] * (tile // 8), axis=0)
@@ -179,14 +167,14 @@
     def multiply(block, carry):
         at = pl.ds(pl.multiple_of(block * LANES, LANES), LANES)
         for first in range(0, keep, tile):
-            rows = [slice(t * keep + first, t * keep + first + tile) for t in range(segments)]
-            r_re = [rcv_re[row, at] for row in rows]
-            r_im = [rcv_im[row, at] for row in rows]
-            r_both = [rcv_both[row, at] for row in rows]
-            for source in range(half):
+            rcv_rows = [pl.ds(pl.multiple_of(row + first, 8), tile) for row in at_rows]
+            r_re = [rcv_re[row, at] for row in rcv_rows]
+            r_im = [rcv_im[row, at] for row in rcv_rows]
+            r_both = [rcv_both[row, at] for row in rcv_rows]
+            for source in range(count):
                 p, q, w = [], [], []
                 for t in range(segments):
-                    row = t * half + source
+                    row = t * count + source
                     p.append(spread(src_re, block, row) * r_both[t])
                     q.append(spread(src_diff, block, row) * r_im[t])
                     w.append(spread(src_sum, block, row) * r_re[t])
@@ -207,22 +195,36 @@
         )
 
     ends = []
-    for first in (0, half // 2):
-        at = slice(first * keep, (first + half // 2) * keep)
-        ends.append([project(place, at) for place in range(2)])
-
-    lags = result.shape[1]
+    for first in (0, count // 2):
+        at = slice(first * keep, (first + count // 2) * keep)
+        sums = [project(place, at) for place in range(2)]
+        if not first_stage:
+            sums = [before[0][place, at] + sums[place] for place in range(2)]
+        if not last_stage:
+            for place in range(2):
+                after[0][place, at] = sums[place]
+        ends.append(sums)
+
+    lags = 2 * LAG + 1
     scale = 2.0 / math.sqrt(nbins)
     mirror = LAG - FIRST_LAG - iota((keep, LANES), 1)
-    for source in range(half):
-        common = 0.0
-        for t in range(segments):
-            row = t * half + source
-            common = common + src_valid[row : row + 1] * rcv_valid[t * keep : (t + 1) * keep, :]
+    pieces = max(1, count // 8)
+    copies = []
+    for source in range(count):
+        to = slice(source * keep, (source + 1) * keep)
+        common = [
+            src_valid[t * count + source : t * count + source + 1]
+            * rcv_valid[pl.ds(at_rows[t], keep), :]
+            for t in range(segments)
+        ] + ([] if first_stage else [before[1][to]])
+        common = functools.reduce(jnp.add, common)
+        if not last_stage:
+            after[1][to] = common
+            continue
+        result, written = refs
         weight = scale / jnp.maximum(common, 1.0)
-        to = slice(source * keep, (source + 1) * keep)
-        inside = slice(source % (half // 2) * keep, (source % (half // 2) + 1) * keep)
-        even, odd = (total[inside] for total in ends[source // (half // 2)])
+        inside = slice(source % (count // 2) * keep, (source % (count // 2) + 1) * keep)
+        even, odd = (total[inside] for total in ends[source // (count // 2)])
         ahead = even + odd
         behind = even - odd
         low_part = jnp.take_along_axis(
@@ -236,34 +238,30 @@
             last = min(first + LANES, lags - LANES)
             value = ahead[:, first : first + LANES] * weight
             result[to, LANES + first : LANES + last] = value[:, : last - first]
-        if rest and (source + 1) % pieces == 0:
-            first, count = (source + 1 - pieces) * keep, pieces * keep
-            at = pl.multiple_of((1 - part) * rows + first, count)
+        if (source + 1) % pieces == 0:
+            at = pl.ds((source + 1 - pieces) * keep, pieces * keep)
             copies.append(
                 pltpu.make_async_copy(
-                    result.at[pl.ds(first, count)],
-                    out_ref.at[pl.ds(at, count)],
-                    written.at[1 + source // pieces],
+                    result.at[at], after[0].at[at], written.at[source // pieces]
                 )
             )
             copies[-1].start()
-    if rest:
-        for copy in copies:
-            copy.wait()
+    for copy in copies:
+        copy.wait()
 
 
 def encode(segments, spectra, valid, sources):
     channels, width = spectra.shape
     keep = channels // segments
-    slab = jax.ShapeDtypeStruct((sources.size, width // 2), jnp.bfloat16)
+    slab = jax.ShapeDtypeStruct((2 * sources.size, width // 2), jnp.bfloat16)
     block = jax.ShapeDtypeStruct((keep, width), jnp.bfloat16)
     padded = pltpu.VMEM((sources.size, width // 2 + 2 * LANES), jnp.bfloat16)
     pinned = [pltpu.with_memory_space_constraint(x, pltpu.HBM) for x in (spectra, valid, sources)]
     return pl.pallas_call(
         functools.partial(encode_kernel, segments),
-        out_shape=(slab, slab) + (block,) * segments,
+        out_shape=(slab,) + (block,) * segments,
         in_specs=[HBM] * 3,
-        out_specs=(VMEM,) * (2 + segments),
+        out_specs=(VMEM,) * (1 + segments),
         scratch_shapes=[
             pltpu.VMEM((channels, width), kind_for(keep)),
             pltpu.VMEM((channels, width), jnp.bfloat16),
@@ -297,63 +295,87 @@
     )(*blocks)
 
 
-def stack_half(segments, slabs, receivers, table, rest=()):
-    half, nbins = slabs.shape[0] // (2 * segments), slabs.shape[1]
-    keep = receivers[0].shape[0] // segments
-    count, rows, lags = segments * half, half * keep, 2 * LAG + 1
-    part = pltpu.VMEM((nbins // LANES, count, LANES), jnp.float32)
+def stack_stage(keep, slabs, places, receivers, table, before=(), last=True):
+    count, nbins = slabs[0].shape[0] // 2, slabs[0].shape[1]
+    rows, lags = count * keep, 2 * LAG + 1
+    part = pltpu.VMEM((nbins // LANES, len(slabs) * count, LANES), jnp.float32)
     cross = pltpu.VMEM((2, nbins // LANES, rows, LANES), kind_for(keep))
     scratch = [part, part, part, cross]
-    if rest:
-        scratch += [pltpu.VMEM((rows, lags), jnp.float32), pltpu.SemaphoreType.DMA((1 + half,))]
+    sums = (
+        jax.ShapeDtypeStruct((2, rows, BLOCK), jnp.float32),
+        jax.ShapeDtypeStruct((rows, LANES), jnp.float32),
+    )
+    if last:
+        scratch += [pltpu.VMEM((rows, lags), jnp.float32), pltpu.SemaphoreType.DMA((count,))]
     return pl.pallas_call(
-        functools.partial(stack_kernel, segments),
-        out_shape=jax.ShapeDtypeStruct((2 * rows if rest else rows, lags), jnp.float32),
-        in_specs=[VMEM] * (6 + len(rest)),
-        out_specs=HBM if rest else VMEM,
+        functools.partial(stack_kernel, places, (not before, last)),
+        out_shape=jax.ShapeDtypeStruct((rows, lags), jnp.float32) if last else sums,
+        in_specs=[VMEM] * (len(slabs) + len(receivers) + 1 + len(before)),
+        out_specs=HBM if last else (VMEM, VMEM),
         scratch_shapes=scratch,
-        compiler_params=pltpu.CompilerParams(vmem_limit_bytes=20 * MEBI),
+        compiler_params=pltpu.CompilerParams(vmem_limit_bytes=26 * MEBI),
         cost_estimate=pl.CostEstimate(
             flops=4 * rows * nbins * 2 * LAG, bytes_accessed=nbins * 2048, transcendentals=0
         ),
-        name="stack_other_half" if rest else "stack_own_half",
-    )(slabs, *receivers, table, *rest)
+        name="stack_last" if last else "stack_first",
+    )(*slabs, *receivers, table, *before)
 
 
 def swapped(value, axis, size, step):
     return lax.ppermute(value, axis, [(i, i ^ step) for i in range(size)])
+
+
+def gather_shared(picked, receivers, rcv_size, tm_size):
+    core = lax.axis_index("rcv") % 2
+    receivers[3] = swapped(receivers[3], "tm", tm_size, 3)
+    own = picked + swapped(picked, "rcv", rcv_size, 1)
+    own, near = lax.optimization_barrier((own, receivers[1:3]))
+    receivers[1:3] = [swapped(block, "tm", tm_size, place) for place, block in enumerate(near, 1)]
+    far = lax.ppermute(own, "rcv", [(i, i ^ (6 if i % 2 else 4)) for i in range(rcv_size)])
+    near = swapped(own, "rcv", rcv_size, 2)
+    far, receivers[3] = lax.optimization_barrier((far, receivers[3]))
+    partial = far + jnp.where(core == 0, own, jnp.zeros_like(own))
+    own = near + (partial + swapped(partial, "rcv", rcv_size, 1))
+    pairs = [
+        (rcv * tm_size + tm, rcv * tm_size + (tm ^ (2 if rcv % 2 else 1)))
+        for rcv in range(rcv_size)
+        for tm in range(tm_size)
+    ]
+    beside = lax.ppermute(own, ("rcv", "tm"), pairs)
+    late, receivers[1:3] = lax.optimization_barrier((own, receivers[1:3]))
+    across = swapped(late, "tm", tm_size, 3)
+    handed = swapped(beside, "rcv", rcv_size, 1)
+    return own, beside, handed, across
 
 
 def shards(rcv_size, tm_size, spectra, valid, sources):
     channels, _, width = spectra.shape
     keep = channels // tm_size
     rounds, per_round = sources.shape
-    own, other, *receivers = encode(
+    table = jnp.asarray(lag_table(width // 2))
+    picked, *receivers = encode(
         tm_size, spectra[:, 0, :], valid.reshape(1, channels), sources
     )
-    receivers[-1] = swapped(receivers[-1], "tm", tm_size, tm_size - 1)
-    own = own + swapped(other, "rcv", rcv_size, 1)
-    own, later = lax.optimization_barrier((own, receivers[1:-1]))
-    receivers[1:-1] = [
-        swapped(block, "tm", tm_size, place) for place, block in enumerate(later, 1)
-    ]
-    step = 2
-    while step < rcv_size:
-        wide = min(4, rcv_size // step)
-        parts = [swapped(own, "rcv", rcv_size, place * step) for place in range(1, wide)]
-        if step == 2:
-            parts[-1], receivers[-1] = lax.optimization_barrier((parts[-1], receivers[-1]))
-        own = functools.reduce(jnp.add, parts, own)
-        step *= wide
-    own = [own] + [swapped(own, "tm", tm_size, place) for place in range(1, tm_size)]
-    whitened = whiten_blocks(receivers)
-    own, whitened = lax.optimization_barrier((own, whitened))
-    own = jnp.concatenate(own, axis=0)
-    other = swapped(own, "rcv", rcv_size, 1)
-
-    table = jnp.asarray(lag_table(width // 2))
-    first = stack_half(tm_size, own, whitened, table)
-    stack = stack_half(tm_size, other, whitened, table, (first,))
+    if (rcv_size, tm_size) == (8, 4):
+        own, beside, handed, across = gather_shared(picked, receivers, rcv_size, tm_size)
+        whitened = whiten_blocks(receivers)
+        sums = stack_stage(
+            keep, [own, beside], [lambda core: 0, lambda core: 1 + core], whitened, table, last=False
+        )
+        stack = stack_stage(
+            keep, [handed, across], [lambda core: 2 - core, lambda core: 3], whitened, table, sums
+        )
+    else:
+        receivers[1:] = [
+            swapped(receivers[place], "tm", tm_size, place) for place in range(1, tm_size)
+        ]
+        step = 1
+        while step < rcv_size:
+            picked = picked + swapped(picked, "rcv", rcv_size, step)
+            step *= 2
+        slabs = [picked] + [swapped(picked, "tm", tm_size, place) for place in range(1, tm_size)]
+        places = [functools.partial(lambda place, core: place, place) for place in range(tm_size)]
+        stack = stack_stage(keep, slabs, places, whiten_blocks(receivers), table)
     return stack.reshape(rounds, per_round, keep, 2 * LAG + 1)
 
 

time: 27.5 us -> 31.7 us (1.15)
  waiting for transfers between devices: 5.99 us -> 10.3 us
  starting transfers between devices: 13.1 us -> 12.4 us
  Pallas kernels: 8.06 us -> 8.74 us
    ppermute x11 -> x8, starting transfers between devices: 13.1 us -> 8.96 us  [swapped(): return lax.ppermute(value, axis, [(i, i ^ step) for i in range(size)])]
    ppermute x0 -> x2, waiting for transfers between devices: none -> 3.93 us  [the longest x1 3.93 us: gather_shared(): lax.ppermute(own, 'rcv', [(i, i ^ (6 if i % 2 else 4)) for i in range(rcv...]
    ppermute x0 -> x2, starting transfers between devices: none -> 3.48 us  [the longest x1 2.65 us: gather_shared(): lax.ppermute(own, 'rcv', [(i, i ^ (6 if i % 2 else 4)) for i in range(rcv...]
    pallas_call x2, Pallas kernels: 5.06 us -> 5.77 us  [stack_stage(): pl.pallas_call(functools.partial(stack_kernel, places, (not before, last)...]
    ppermute x11 -> x8, waiting for transfers between devices: 5.99 us -> 6.32 us  [swapped(): return lax.ppermute(value, axis, [(i, i ^ step) for i in range(size)])]
  transfers between devices with their start and end apart: 11 -> 10, of which waited for: 6 -> 4; matrix products, arithmetic and copies ran while one was open for 0% -> 0% of each run, Pallas kernels for 12% -> 11%
where the time goes in v14:
time: 31.7 us; the launch traced here: 31.6 us
  starting transfers between devices  12.4 us (39%)
  waiting for transfers between devices  10.3 us (32%)
  Pallas kernels  8.74 us (28%)
    ppermute x8, starting transfers between devices, swapped(): return lax.ppermute(value, axis, [(i, i ^ step) for i in range(size)])  8.96 us
    ppermute x8, waiting for transfers between devices, swapped(): return lax.ppermute(value, axis, [(i, i ^ step) for i in range(size)])  6.32 us
    pallas_call x2, Pallas kernels, stack_stage(): pl.pallas_call(functools.partial(stack_kernel, places, (not before, last)...  5.77 us
    ppermute x1, waiting for transfers between devices, gather_shared(): lax.ppermute(own, 'rcv', [(i, i ^ (6 if i % 2 else 4)) for i in range(rcv...  3.93 us
    ppermute x1, starting transfers between devices, gather_shared(): lax.ppermute(own, 'rcv', [(i, i ^ (6 if i % 2 else 4)) for i in range(rcv...  2.65 us
    pallas_call x1, Pallas kernels, encode(): pl.pallas_call(functools.partial(encode_kernel, segments), out_shape=(sla...  1.99 us
    pallas_call x1, Pallas kernels, whiten_blocks(): pl.pallas_call(functools.partial(whiten_kernel, segments), out_shape=(par...  0.98 us
    ppermute x1, starting transfers between devices, gather_shared(): beside = lax.ppermute(own, ('rcv', 'tm'), pairs)  0.83 us
  transfers between devices with their start and end apart: 10, of which 4 were waited for; matrix products, arithmetic and copies ran while one was open for 0% of the time, Pallas kernels for 11%

profile of v14, /device:TPU:0, one launch (start us, length us, event | category | flops | bytes accessed | tf_op | source)
XLA Modules:
  0.0 31.6 jit_solution(17587987225726056495)
XLA Ops:
  0.0 0.0 copy-start
  0.0 2.0 %encode_and_pick.1 = (bf16[32,1536]{1,0:T(8,128)(2,1)S(1)}, bf16[32,3072]{1,0:T(8,128)(2,1)S(1)}, bf16[32,3072]{1,0:T(8,128)(2,1)S(1)}, bf16[32,3072]{1,0:T(8,128)(2,1)S(1)}, bf16[32,3072]{1,0:T(8,128)(2,1)S(1)}) custom-call(bf16[128,3072]{1,0:T(8,128)(2,1)} %bitcast.3, s32[1,128]{1,0:T(1,128)} %bitcast.4, s32[2,8]{1,0:T(2,128)} %sources_ref.1), custom_call_target="tpu_custom_call" | custom-call | tf_op jit(solution)/shard_map/encode_and_pick/pallas_call | solution.py:260
  2.0 0.5 %collective-permute-start = (bf16[32,1536]{1,0:T(8,128)(2,1)S(1)}, bf16[32,1536]{1,0:T(8,128)(2,1)S(1)}, u32[]{:S(2)}, u32[]{:S(2)}) collective-permute-start(bf16[32,1536]{1,0:T(8,128)(2,1)S(1)} %get-tuple-element.24), channel_id=1, source_target_pairs={{0,4},{4,0},{8,12},{12,8},{16,20},{20,16},{24,28},{28,24},{1,5},{5... | collective-permute-start | bytes 294920 | tf_op jit(solution)/shard_map/ppermute | solution.py:325
  2.5 3.5 %collective-permute-start.3 = (bf16[32,3072]{1,0:T(8,128)(2,1)S(1)}, bf16[32,3072]{1,0:T(8,128)(2,1)S(1)}, u32[]{:S(2)}, u32[]{:S(2)}) collective-permute-start(bf16[32,3072]{1,0:T(8,128)(2,1)S(1)} %get-tuple-element.28), channel_id=1, source_target_pairs={{0,3},{1,2},{2,1},{3,0},{4,7},{5,6},{6,5},{7,4},{8,11},{9,10},{10,... | collective-permute-start | bytes 589832 | tf_op jit(solution)/shard_map/ppermute | solution.py:325
  6.0 0.0 collective-permute-done
  6.1 2.7 %collective-permute-start.2 = (bf16[32,1536]{1,0:T(8,128)(2,1)S(1)}, bf16[32,1536]{1,0:T(8,128)(2,1)S(1)}, u32[]{:S(2)}, u32[]{:S(2)}) collective-permute-start(bf16[32,1536]{1,0:T(8,128)(2,1)S(1)} %add.16), channel_id=1, source_target_pairs={{0,16},{4,28},{8,24},{12,20},{16,0},{20,12},{24,8},{28,4},{1,17},{... | collective-permute-start | bytes 294920 | tf_op jit(solution)/shard_map/ppermute | solution.py:334
  8.7 1.6 %collective-permute-start.1 = (bf16[32,1536]{1,0:T(8,128)(2,1)S(1)}, bf16[32,1536]{1,0:T(8,128)(2,1)S(1)}, u32[]{:S(2)}, u32[]{:S(2)}) collective-permute-start(bf16[32,1536]{1,0:T(8,128)(2,1)S(1)} %add.16), channel_id=1, source_target_pairs={{0,8},{4,12},{8,0},{12,4},{16,24},{20,28},{24,16},{28,20},{1,9},{5... | collective-permute-start | bytes 294920 | tf_op jit(solution)/shard_map/ppermute | solution.py:325
  10.3 3.9 %collective-permute-done.2 = bf16[32,1536]{1,0:T(8,128)(2,1)S(1)} collective-permute-done((bf16[32,1536]{1,0:T(8,128)(2,1)S(1)}, bf16[32,1536]{1,0:T(8,128)(2,1)S(1)}, u32[]{:S(2)}, u32[]{:S(2)}) %collective-permute-start.2) | collective-permute-done | bytes 98336 | tf_op jit(solution)/shard_map/ppermute | solution.py:334
  14.2 0.0 collective-permute-done.3.refs_3_
  14.3 0.1 collective-permute-start.4
  14.3 0.6 %collective-permute-start.7 = (bf16[32,3072]{1,0:T(8,128)(2,1)S(1)}, bf16[32,3072]{1,0:T(8,128)(2,1)S(1)}, u32[]{:S(2)}, u32[]{:S(2)}) collective-permute-start(bf16[32,3072]{1,0:T(8,128)(2,1)S(1)} %get-tuple-element.30), channel_id=1, source_target_pairs={{0,1},{1,0},{2,3},{3,2},{4,5},{5,4},{6,7},{7,6},{8,9},{9,8},{10,11... | collective-permute-start | bytes 589832 | tf_op jit(solution)/shard_map/ppermute | solution.py:325
  14.9 1.2 %collective-permute-start.8 = (bf16[32,3072]{1,0:T(8,128)(2,1)S(1)}, bf16[32,3072]{1,0:T(8,128)(2,1)S(1)}, u32[]{:S(2)}, u32[]{:S(2)}) collective-permute-start(bf16[32,3072]{1,0:T(8,128)(2,1)S(1)} %get-tuple-element.31), channel_id=1, source_target_pairs={{0,2},{1,3},{2,0},{3,1},{4,6},{5,7},{6,4},{7,5},{8,10},{9,11},{10,... | collective-permute-start | bytes 589832 | tf_op jit(solution)/shard_map/ppermute | solution.py:325
  16.2 0.0 collective-permute-done.1
  16.2 0.0 collective-permute-done.4
  16.2 0.8 %collective-permute-start.5 = (bf16[32,1536]{1,0:T(8,128)(2,1)S(1)}, bf16[32,1536]{1,0:T(8,128)(2,1)S(1)}, u32[]{:S(2)}, u32[]{:S(2)}) collective-permute-start(bf16[32,1536]{1,0:T(8,128)(2,1)S(1)} %add_add_fusion.refs_0_), channel_id=1, source_target_pairs={{0,1},{1,0},{2,3},{3,2},{4,6},{5,7},{6,4},{7,5},{8,9},{9,8},{10,11... | collective-permute-start | bytes 294920 | tf_op jit(solution)/shard_map/ppermute | solution.py:344
  17.0 4.6 %collective-permute-done.7.refs_1_ = bf16[32,3072]{1,0:T(8,128)(2,1)S(1)} collective-permute-done((bf16[32,3072]{1,0:T(8,128)(2,1)S(1)}, bf16[32,3072]{1,0:T(8,128)(2,1)S(1)}, u32[]{:S(2)}, u32[]{:S(2)}) %collective-permute-start.7) | collective-permute-done | bytes 196640 | tf_op jit(solution)/shard_map/ppermute | solution.py:325
  21.7 1.0 %collective-permute-done.8.refs_2_ = bf16[32,3072]{1,0:T(8,128)(2,1)S(1)} collective-permute-done((bf16[32,3072]{1,0:T(8,128)(2,1)S(1)}, bf16[32,3072]{1,0:T(8,128)(2,1)S(1)}, u32[]{:S(2)}, u32[]{:S(2)}) %collective-permute-start.8) | collective-permute-done | bytes 196640 | tf_op jit(solution)/shard_map/ppermute | solution.py:325
  22.7 1.4 %collective-permute-start.9 = (bf16[32,1536]{1,0:T(8,128)(2,1)S(1)}, bf16[32,1536]{1,0:T(8,128)(2,1)S(1)}, u32[]{:S(2)}, u32[]{:S(2)}) collective-permute-start(bf16[32,1536]{1,0:T(8,128)(2,1)S(1)} %add_add_fusion.refs_0_), channel_id=1, source_target_pairs={{0,3},{1,2},{2,1},{3,0},{4,7},{5,6},{6,5},{7,4},{8,11},{9,10},{10,... | collective-permute-start | bytes 294920 | tf_op jit(solution)/shard_map/ppermute | solution.py:325
  24.1 0.0 collective-permute-done.5.refs_1_
  24.1 0.0 collective-permute-start.6
  24.1 1.0 %whiten_receivers.1 = (f32[128,1536]{1,0:T(8,128)S(1)}, f32[128,1536]{1,0:T(8,128)S(1)}, f32[128,1536]{1,0:T(8,128)S(1)}, f32[128,128]{1,0:T(8,128)S(1)}) custom-call(bf16[32,3072]{1,0:T(8,128)(2,1)S(1)} %get-tuple-element.33.refs_0_, bf16[32,3072]{1,0:T(8,128)(2,1)S(1)} %collective-permute-done.7.refs_1_, ...), custom_call_target="tpu_custom_call" | custom-call | flops 402653184 | bytes 1572864 | tf_op jit(solution)/shard_map/whiten_receivers/pallas_call | solution.py:284
  25.1 0.0 copy-done
  25.1 2.4 %stack_first.1 = (f32[2,512,256]{2,1,0:T(8,128)S(1)}, f32[512,128]{1,0:T(8,128)S(1)}) custom-call(bf16[32,1536]{1,0:T(8,128)(2,1)S(1)} %add_add_fusion.refs_0_, bf16[32,1536]{1,0:T(8,128)(2,1)S(1)} %collective-permute-done.5.refs_1_, f32[128,1536]{1,0:T(8,128)S(1)} %get-tuple-element.37.refs_2_, f32[128,1536]{1,0:T(8,128)S(1)} %get-tuple-element.38.refs_3_, ...), custom_call_target="tpu_custom_call" | custom-call | flops 943718400 | bytes 3145728 | tf_op jit(solution)/shard_map/stack_first/pallas_call | solution.py:310
  27.5 0.7 %collective-permute-done.9.refs_1_ = bf16[32,1536]{1,0:T(8,128)(2,1)S(1)} collective-permute-done((bf16[32,1536]{1,0:T(8,128)(2,1)S(1)}, bf16[32,1536]{1,0:T(8,128)(2,1)S(1)}, u32[]{:S(2)}, u32[]{:S(2)}) %collective-permute-start.9) | collective-permute-done | bytes 98336 | tf_op jit(solution)/shard_map/ppermute | solution.py:325
  28.2 0.0 collective-permute-done.6.refs_0_
  28.2 3.4 %stack_last.1 = f32[512,301]{1,0:T(8,128)} custom-call(bf16[32,1536]{1,0:T(8,128)(2,1)S(1)} %collective-permute-done.6.refs_0_, bf16[32,1536]{1,0:T(8,128)(2,1)S(1)} %collective-permute-done.9.refs_1_, f32[128,1536]{1,0:T(8,128)S(1)} %get-tuple-element.37.refs_2_, f32[128,1536]{1,0:T(8,128)S(1)} %get-tuple-element.38.refs_3_, ...), custom_call_target="tpu_custom_call" | custom-call | flops 943718400 | bytes 3145728 | tf_op jit(solution)/shard_map/stack_last/pallas_call | solution.py:310
  (3 shorter events, 0.1 us)
Async XLA Ops:
  0.0 25.1 %copy-start = (bf16[3072,256]{1,0:T(8,128)(2,1)S(1)}, bf16[3072,256]{1,0:T(8,128)(2,1)}, u32[]{:S(2)}) copy-start(bf16[3072,256]{1,0:T(8,128)(2,1)} %constant.24.clone.refs_6_) | copy-start | bytes 4718596
  2.0 4.0 %collective-permute-start = (bf16[32,1536]{1,0:T(8,128)(2,1)S(1)}, bf16[32,1536]{1,0:T(8,128)(2,1)S(1)}, u32[]{:S(2)}, u32[]{:S(2)}) collective-permute-start(bf16[32,1536]{1,0:T(8,128)(2,1)S(1)} %get-tuple-element.24), channel_id=1, source_target_pairs={{0,4},{4,0},{8,12},{12,8},{16,20},{20,16},{24,28},{28,24},{1,5},{5... | collective-permute-start | bytes 294920 | tf_op jit(solution)/shard_map/ppermute | solution.py:325
  2.5 11.7 %collective-permute-start.3 = (bf16[32,3072]{1,0:T(8,128)(2,1)S(1)}, bf16[32,3072]{1,0:T(8,128)(2,1)S(1)}, u32[]{:S(2)}, u32[]{:S(2)}) collective-permute-start(bf16[32,3072]{1,0:T(8,128)(2,1)S(1)} %get-tuple-element.28), channel_id=1, source_target_pairs={{0,3},{1,2},{2,1},{3,0},{4,7},{5,6},{6,5},{7,4},{8,11},{9,10},{10,... | collective-permute-start | bytes 589832 | tf_op jit(solution)/shard_map/ppermute | solution.py:325
  6.1 8.2 %collective-permute-start.2 = (bf16[32,1536]{1,0:T(8,128)(2,1)S(1)}, bf16[32,1536]{1,0:T(8,128)(2,1)S(1)}, u32[]{:S(2)}, u32[]{:S(2)}) collective-permute-start(bf16[32,1536]{1,0:T(8,128)(2,1)S(1)} %add.16), channel_id=1, source_target_pairs={{0,16},{4,28},{8,24},{12,20},{16,0},{20,12},{24,8},{28,4},{1,17},{... | collective-permute-start | bytes 294920 | tf_op jit(solution)/shard_map/ppermute | solution.py:334
  8.7 7.4 %collective-permute-start.1 = (bf16[32,1536]{1,0:T(8,128)(2,1)S(1)}, bf16[32,1536]{1,0:T(8,128)(2,1)S(1)}, u32[]{:S(2)}, u32[]{:S(2)}) collective-permute-start(bf16[32,1536]{1,0:T(8,128)(2,1)S(1)} %add.16), channel_id=1, source_target_pairs={{0,8},{4,12},{8,0},{12,4},{16,24},{20,28},{24,16},{28,20},{1,9},{5... | collective-permute-start | bytes 294920 | tf_op jit(solution)/shard_map/ppermute | solution.py:325
  14.3 1.9 %collective-permute-start.4 = (bf16[32,1536]{1,0:T(8,128)(2,1)S(1)}, bf16[32,1536]{1,0:T(8,128)(2,1)S(1)}, u32[]{:S(2)}, u32[]{:S(2)}) collective-permute-start(bf16[32,1536]{1,0:T(8,128)(2,1)S(1)} %select_add_fusion), channel_id=1, source_target_pairs={{0,4},{4,0},{8,12},{12,8},{16,20},{20,16},{24,28},{28,24},{1,5},{5... | collective-permute-start | bytes 294920 | tf_op jit(solution)/shard_map/ppermute | solution.py:325
  14.3 7.3 %collective-permute-start.7 = (bf16[32,3072]{1,0:T(8,128)(2,1)S(1)}, bf16[32,3072]{1,0:T(8,128)(2,1)S(1)}, u32[]{:S(2)}, u32[]{:S(2)}) collective-permute-start(bf16[32,3072]{1,0:T(8,128)(2,1)S(1)} %get-tuple-element.30), channel_id=1, source_target_pairs={{0,1},{1,0},{2,3},{3,2},{4,5},{5,4},{6,7},{7,6},{8,9},{9,8},{10,11... | collective-permute-start | bytes 589832 | tf_op jit(solution)/shard_map/ppermute | solution.py:325
  14.9 7.7 %collective-permute-start.8 = (bf16[32,3072]{1,0:T(8,128)(2,1)S(1)}, bf16[32,3072]{1,0:T(8,128)(2,1)S(1)}, u32[]{:S(2)}, u32[]{:S(2)}) collective-permute-start(bf16[32,3072]{1,0:T(8,128)(2,1)S(1)} %get-tuple-element.31), channel_id=1, source_target_pairs={{0,2},{1,3},{2,0},{3,1},{4,6},{5,7},{6,4},{7,5},{8,10},{9,11},{10,... | collective-permute-start | bytes 589832 | tf_op jit(solution)/shard_map/ppermute | solution.py:325
  16.2 7.9 %collective-permute-start.5 = (bf16[32,1536]{1,0:T(8,128)(2,1)S(1)}, bf16[32,1536]{1,0:T(8,128)(2,1)S(1)}, u32[]{:S(2)}, u32[]{:S(2)}) collective-permute-start(bf16[32,1536]{1,0:T(8,128)(2,1)S(1)} %add_add_fusion.refs_0_), channel_id=1, source_target_pairs={{0,1},{1,0},{2,3},{3,2},{4,6},{5,7},{6,4},{7,5},{8,9},{9,8},{10,11... | collective-permute-start | bytes 294920 | tf_op jit(solution)/shard_map/ppermute | solution.py:344
  22.7 5.5 %collective-permute-start.9 = (bf16[32,1536]{1,0:T(8,128)(2,1)S(1)}, bf16[32,1536]{1,0:T(8,128)(2,1)S(1)}, u32[]{:S(2)}, u32[]{:S(2)}) collective-permute-start(bf16[32,1536]{1,0:T(8,128)(2,1)S(1)} %add_add_fusion.refs_0_), channel_id=1, source_target_pairs={{0,3},{1,2},{2,1},{3,0},{4,7},{5,6},{6,5},{7,4},{8,11},{9,10},{10,... | collective-permute-start | bytes 294920 | tf_op jit(solution)/shard_map/ppermute | solution.py:325
  24.1 4.1 %collective-permute-start.6 = (bf16[32,1536]{1,0:T(8,128)(2,1)S(1)}, bf16[32,1536]{1,0:T(8,128)(2,1)S(1)}, u32[]{:S(2)}, u32[]{:S(2)}) collective-permute-start(bf16[32,1536]{1,0:T(8,128)(2,1)S(1)} %collective-permute-done.5.refs_1_), channel_id=1, source_target_pairs={{0,4},{4,0},{8,12},{12,8},{16,20},{20,16},{24,28},{28,24},{1,5},{5... | collective-permute-start | bytes 294920 | tf_op jit(solution)/shard_map/ppermute | solution.py:325

commit v15 on v14

--- a/solution.py
+++ b/solution.py
@@ -334,6 +334,7 @@
     far = lax.ppermute(own, "rcv", [(i, i ^ (6 if i % 2 else 4)) for i in range(rcv_size)])
     near = swapped(own, "rcv", rcv_size, 2)
     far, receivers[3] = lax.optimization_barrier((far, receivers[3]))
+    near, receivers[1:3] = lax.optimization_barrier((near, receivers[1:3]))
     partial = far + jnp.where(core == 0, own, jnp.zeros_like(own))
     own = near + (partial + swapped(partial, "rcv", rcv_size, 1))
     pairs = [
@@ -342,10 +343,10 @@
         for tm in range(tm_size)
     ]
     beside = lax.ppermute(own, ("rcv", "tm"), pairs)
-    late, receivers[1:3] = lax.optimization_barrier((own, receivers[1:3]))
-    across = swapped(late, "tm", tm_size, 3)
+    across = swapped(own, "tm", tm_size, 3)
+    beside, whitened = lax.optimization_barrier((beside, whiten_blocks(receivers)))
     handed = swapped(beside, "rcv", rcv_size, 1)
-    return own, beside, handed, across
+    return (own, beside), (handed, across), whitened
 
 
 def shards(rcv_size, tm_size, spectra, valid, sources):
@@ -357,14 +358,11 @@
         tm_size, spectra[:, 0, :], valid.reshape(1, channels), sources
     )
     if (rcv_size, tm_size) == (8, 4):
-        own, beside, handed, across = gather_shared(picked, receivers, rcv_size, tm_size)
-        whitened = whiten_blocks(receivers)
-        sums = stack_stage(
-            keep, [own, beside], [lambda core: 0, lambda core: 1 + core], whitened, table, last=False
-        )
-        stack = stack_stage(
-            keep, [handed, across], [lambda core: 2 - core, lambda core: 3], whitened, table, sums
-        )
+        first, rest, whitened = gather_shared(picked, receivers, rcv_size, tm_size)
+        places = [lambda core: 0, lambda core: 1 + core]
+        sums = stack_stage(keep, first, places, whitened, table, last=False)
+        places = [lambda core: 2 - core, lambda core: 3]
+        stack = stack_stage(keep, rest, places, whitened, table, sums)
     else:
         receivers[1:] = [
             swapped(receivers[place], "tm", tm_size, place) for place in range(1, tm_size)

time: 31.7 us -> 27.7 us (0.87)
  waiting for transfers between devices: 10.3 us -> 5.79 us
  starting transfers between devices: 12.4 us -> 12.9 us
    ppermute x8, waiting for transfers between devices: 6.32 us -> 2.37 us  [swapped(): return lax.ppermute(value, axis, [(i, i ^ step) for i in range(size)])]
    ppermute x1, waiting for transfers between devices: 3.93 us -> 2.14 us  [gather_shared(): lax.ppermute(own, 'rcv', [(i, i ^ (6 if i % 2 else 4)) for i in range(rcv...]
    ppermute x1, waiting for transfers between devices: 0.01 us -> 1.27 us  [gather_shared(): beside = lax.ppermute(own, ('rcv', 'tm'), pairs)]
    ppermute x1, starting transfers between devices: 0.83 us -> 1.56 us  [gather_shared(): beside = lax.ppermute(own, ('rcv', 'tm'), pairs)]
  transfers between devices with their start and end apart: 10 -> 10, of which waited for: 4 -> 5; matrix products, arithmetic and copies ran while one was open for 0% -> 0% of each run, Pallas kernels for 11% -> 12%
where the time goes in v15:
time: 27.7 us; the launch traced here: 27.5 us
  starting transfers between devices  12.9 us (47%)
  Pallas kernels  8.74 us (32%)
  waiting for transfers between devices  5.79 us (21%)
    ppermute x8, starting transfers between devices, swapped(): return lax.ppermute(value, axis, [(i, i ^ step) for i in range(size)])  8.68 us
    pallas_call x2, Pallas kernels, stack_stage(): pl.pallas_call(functools.partial(stack_kernel, places, (not before, last)...  5.77 us
    ppermute x1, starting transfers between devices, gather_shared(): lax.ppermute(own, 'rcv', [(i, i ^ (6 if i % 2 else 4)) for i in range(rcv...  2.65 us
    ppermute x8, waiting for transfers between devices, swapped(): return lax.ppermute(value, axis, [(i, i ^ step) for i in range(size)])  2.37 us
    ppermute x1, waiting for transfers between devices, gather_shared(): lax.ppermute(own, 'rcv', [(i, i ^ (6 if i % 2 else 4)) for i in range(rcv...  2.14 us
    pallas_call x1, Pallas kernels, encode(): pl.pallas_call(functools.partial(encode_kernel, segments), out_shape=(sla...  1.99 us
    ppermute x1, starting transfers between devices, gather_shared(): beside = lax.ppermute(own, ('rcv', 'tm'), pairs)  1.56 us
    ppermute x1, waiting for transfers between devices, gather_shared(): beside = lax.ppermute(own, ('rcv', 'tm'), pairs)  1.27 us
  transfers between devices with their start and end apart: 10, of which 5 were waited for; matrix products, arithmetic and copies ran while one was open for 0% of the time, Pallas kernels for 12%

profile of v15, /device:TPU:0, one launch (start us, length us, event | category | flops | bytes accessed | tf_op | source)
XLA Modules:
  0.0 27.5 jit_solution(6680383413381661310)
XLA Ops:
  0.0 0.0 copy-start
  0.0 2.0 %encode_and_pick.1 = (bf16[32,1536]{1,0:T(8,128)(2,1)S(1)}, bf16[32,3072]{1,0:T(8,128)(2,1)S(1)}, bf16[32,3072]{1,0:T(8,128)(2,1)S(1)}, bf16[32,3072]{1,0:T(8,128)(2,1)S(1)}, bf16[32,3072]{1,0:T(8,128)(2,1)S(1)}) custom-call(bf16[128,3072]{1,0:T(8,128)(2,1)} %bitcast.3, s32[1,128]{1,0:T(1,128)} %bitcast.4, s32[2,8]{1,0:T(2,128)} %sources_ref.1), custom_call_target="tpu_custom_call" | custom-call | tf_op jit(solution)/shard_map/encode_and_pick/pallas_call | solution.py:260
  2.0 0.5 %collective-permute-start = (bf16[32,1536]{1,0:T(8,128)(2,1)S(1)}, bf16[32,1536]{1,0:T(8,128)(2,1)S(1)}, u32[]{:S(2)}, u32[]{:S(2)}) collective-permute-start(bf16[32,1536]{1,0:T(8,128)(2,1)S(1)} %get-tuple-element.29), channel_id=1, source_target_pairs={{0,4},{4,0},{8,12},{12,8},{16,20},{20,16},{24,28},{28,24},{1,5},{5... | collective-permute-start | bytes 294920 | tf_op jit(solution)/shard_map/ppermute | solution.py:325
  2.5 3.5 %collective-permute-start.5 = (bf16[32,3072]{1,0:T(8,128)(2,1)S(1)}, bf16[32,3072]{1,0:T(8,128)(2,1)S(1)}, u32[]{:S(2)}, u32[]{:S(2)}) collective-permute-start(bf16[32,3072]{1,0:T(8,128)(2,1)S(1)} %get-tuple-element.36), channel_id=1, source_target_pairs={{0,3},{1,2},{2,1},{3,0},{4,7},{5,6},{6,5},{7,4},{8,11},{9,10},{10,... | collective-permute-start | bytes 589832 | tf_op jit(solution)/shard_map/ppermute | solution.py:325
  6.0 0.0 collective-permute-done
  6.1 2.7 %collective-permute-start.4 = (bf16[32,1536]{1,0:T(8,128)(2,1)S(1)}, bf16[32,1536]{1,0:T(8,128)(2,1)S(1)}, u32[]{:S(2)}, u32[]{:S(2)}) collective-permute-start(bf16[32,1536]{1,0:T(8,128)(2,1)S(1)} %add.16), channel_id=1, source_target_pairs={{0,16},{4,28},{8,24},{12,20},{16,0},{20,12},{24,8},{28,4},{1,17},{... | collective-permute-start | bytes 294920 | tf_op jit(solution)/shard_map/ppermute | solution.py:334
  8.7 1.6 %collective-permute-start.1 = (bf16[32,1536]{1,0:T(8,128)(2,1)S(1)}, bf16[32,1536]{1,0:T(8,128)(2,1)S(1)}, u32[]{:S(2)}, u32[]{:S(2)}) collective-permute-start(bf16[32,1536]{1,0:T(8,128)(2,1)S(1)} %add.16), channel_id=1, source_target_pairs={{0,8},{4,12},{8,0},{12,4},{16,24},{20,28},{24,16},{28,20},{1,9},{5... | collective-permute-start | bytes 294920 | tf_op jit(solution)/shard_map/ppermute | solution.py:325
  10.3 0.5 %collective-permute-start.2 = (bf16[32,3072]{1,0:T(8,128)(2,1)S(1)}, bf16[32,3072]{1,0:T(8,128)(2,1)S(1)}, u32[]{:S(2)}, u32[]{:S(2)}) collective-permute-start(bf16[32,3072]{1,0:T(8,128)(2,1)S(1)} %get-tuple-element.33), channel_id=1, source_target_pairs={{0,1},{1,0},{2,3},{3,2},{4,5},{5,4},{6,7},{7,6},{8,9},{9,8},{10,11... | collective-permute-start | bytes 589832 | tf_op jit(solution)/shard_map/ppermute | solution.py:325
  10.8 1.2 %collective-permute-start.3 = (bf16[32,3072]{1,0:T(8,128)(2,1)S(1)}, bf16[32,3072]{1,0:T(8,128)(2,1)S(1)}, u32[]{:S(2)}, u32[]{:S(2)}) collective-permute-start(bf16[32,3072]{1,0:T(8,128)(2,1)S(1)} %get-tuple-element.34), channel_id=1, source_target_pairs={{0,2},{1,3},{2,0},{3,1},{4,6},{5,7},{6,4},{7,5},{8,10},{9,11},{10,... | collective-permute-start | bytes 589832 | tf_op jit(solution)/shard_map/ppermute | solution.py:325
  12.1 2.1 %collective-permute-done.4 = bf16[32,1536]{1,0:T(8,128)(2,1)S(1)} collective-permute-done((bf16[32,1536]{1,0:T(8,128)(2,1)S(1)}, bf16[32,1536]{1,0:T(8,128)(2,1)S(1)}, u32[]{:S(2)}, u32[]{:S(2)}) %collective-permute-start.4) | collective-permute-done | bytes 98336 | tf_op jit(solution)/shard_map/ppermute | solution.py:334
  14.2 0.0 collective-permute-done.5.refs_3_
  14.3 0.1 collective-permute-start.6
  14.3 0.9 %collective-permute-done.1 = bf16[32,1536]{1,0:T(8,128)(2,1)S(1)} collective-permute-done((bf16[32,1536]{1,0:T(8,128)(2,1)S(1)}, bf16[32,1536]{1,0:T(8,128)(2,1)S(1)}, u32[]{:S(2)}, u32[]{:S(2)}) %collective-permute-start.1) | collective-permute-done | bytes 98336 | tf_op jit(solution)/shard_map/ppermute | solution.py:325
  15.2 1.2 %collective-permute-done.2.refs_1_ = bf16[32,3072]{1,0:T(8,128)(2,1)S(1)} collective-permute-done((bf16[32,3072]{1,0:T(8,128)(2,1)S(1)}, bf16[32,3072]{1,0:T(8,128)(2,1)S(1)}, u32[]{:S(2)}, u32[]{:S(2)}) %collective-permute-start.2) | collective-permute-done | bytes 196640 | tf_op jit(solution)/shard_map/ppermute | solution.py:325
  16.4 0.3 collective-permute-done.3.refs_2_
  16.7 0.0 collective-permute-done.6
  16.7 1.6 %collective-permute-start.7 = (bf16[32,1536]{1,0:T(8,128)(2,1)S(1)}, bf16[32,1536]{1,0:T(8,128)(2,1)S(1)}, u32[]{:S(2)}, u32[]{:S(2)}) collective-permute-start(bf16[32,1536]{1,0:T(8,128)(2,1)S(1)} %add_add_fusion.refs_0_), channel_id=1, source_target_pairs={{0,1},{1,0},{2,3},{3,2},{4,6},{5,7},{6,4},{7,5},{8,9},{9,8},{10,11... | collective-permute-start | bytes 294920 | tf_op jit(solution)/shard_map/ppermute | solution.py:345
  18.3 1.2 %collective-permute-start.9 = (bf16[32,1536]{1,0:T(8,128)(2,1)S(1)}, bf16[32,1536]{1,0:T(8,128)(2,1)S(1)}, u32[]{:S(2)}, u32[]{:S(2)}) collective-permute-start(bf16[32,1536]{1,0:T(8,128)(2,1)S(1)} %add_add_fusion.refs_0_), channel_id=1, source_target_pairs={{0,3},{1,2},{2,1},{3,0},{4,7},{5,6},{6,5},{7,4},{8,11},{9,10},{10,... | collective-permute-start | bytes 294920 | tf_op jit(solution)/shard_map/ppermute | solution.py:325
  19.5 1.0 %whiten_receivers.1 = (f32[128,1536]{1,0:T(8,128)S(1)}, f32[128,1536]{1,0:T(8,128)S(1)}, f32[128,1536]{1,0:T(8,128)S(1)}, f32[128,128]{1,0:T(8,128)S(1)}) custom-call(bf16[32,3072]{1,0:T(8,128)(2,1)S(1)} %get-tuple-element.38.refs_0_, bf16[32,3072]{1,0:T(8,128)(2,1)S(1)} %collective-permute-done.2.refs_1_, ...), custom_call_target="tpu_custom_call" | custom-call | flops 402653184 | bytes 1572864 | tf_op jit(solution)/shard_map/whiten_receivers/pallas_call | solution.py:284
  20.5 1.3 %collective-permute-done.7.refs_1_ = bf16[32,1536]{1,0:T(8,128)(2,1)S(1)} collective-permute-done((bf16[32,1536]{1,0:T(8,128)(2,1)S(1)}, bf16[32,1536]{1,0:T(8,128)(2,1)S(1)}, u32[]{:S(2)}, u32[]{:S(2)}) %collective-permute-start.7) | collective-permute-done | bytes 98336 | tf_op jit(solution)/shard_map/ppermute | solution.py:345
  21.7 0.0 collective-permute-start.8
  21.8 0.0 copy-done
  21.8 2.4 %stack_first.1 = (f32[2,512,256]{2,1,0:T(8,128)S(1)}, f32[512,128]{1,0:T(8,128)S(1)}) custom-call(bf16[32,1536]{1,0:T(8,128)(2,1)S(1)} %add_add_fusion.refs_0_, bf16[32,1536]{1,0:T(8,128)(2,1)S(1)} %collective-permute-done.7.refs_1_, f32[128,1536]{1,0:T(8,128)S(1)} %get-tuple-element.47.refs_2_, f32[128,1536]{1,0:T(8,128)S(1)} %get-tuple-element.48.refs_3_, ...), custom_call_target="tpu_custom_call" | custom-call | flops 943718400 | bytes 3145728 | tf_op jit(solution)/shard_map/stack_first/pallas_call | solution.py:310
  24.2 0.0 collective-permute-done.9.refs_1_
  24.2 0.0 collective-permute-done.8.refs_0_
  24.2 3.4 %stack_last.1 = f32[512,301]{1,0:T(8,128)} custom-call(bf16[32,1536]{1,0:T(8,128)(2,1)S(1)} %collective-permute-done.8.refs_0_, bf16[32,1536]{1,0:T(8,128)(2,1)S(1)} %collective-permute-done.9.refs_1_, f32[128,1536]{1,0:T(8,128)S(1)} %get-tuple-element.47.refs_2_, f32[128,1536]{1,0:T(8,128)S(1)} %get-tuple-element.48.refs_3_, ...), custom_call_target="tpu_custom_call" | custom-call | flops 943718400 | bytes 3145728 | tf_op jit(solution)/shard_map/stack_last/pallas_call | solution.py:310
  (3 shorter events, 0.1 us)
Async XLA Ops:
  0.0 21.8 %copy-start = (bf16[3072,256]{1,0:T(8,128)(2,1)S(1)}, bf16[3072,256]{1,0:T(8,128)(2,1)}, u32[]{:S(2)}) copy-start(bf16[3072,256]{1,0:T(8,128)(2,1)} %constant.24.clone.refs_6_) | copy-start | bytes 4718596
  2.0 4.0 %collective-permute-start = (bf16[32,1536]{1,0:T(8,128)(2,1)S(1)}, bf16[32,1536]{1,0:T(8,128)(2,1)S(1)}, u32[]{:S(2)}, u32[]{:S(2)}) collective-permute-start(bf16[32,1536]{1,0:T(8,128)(2,1)S(1)} %get-tuple-element.29), channel_id=1, source_target_pairs={{0,4},{4,0},{8,12},{12,8},{16,20},{20,16},{24,28},{28,24},{1,5},{5... | collective-permute-start | bytes 294920 | tf_op jit(solution)/shard_map/ppermute | solution.py:325
  2.5 11.7 %collective-permute-start.5 = (bf16[32,3072]{1,0:T(8,128)(2,1)S(1)}, bf16[32,3072]{1,0:T(8,128)(2,1)S(1)}, u32[]{:S(2)}, u32[]{:S(2)}) collective-permute-start(bf16[32,3072]{1,0:T(8,128)(2,1)S(1)} %get-tuple-element.36), channel_id=1, source_target_pairs={{0,3},{1,2},{2,1},{3,0},{4,7},{5,6},{6,5},{7,4},{8,11},{9,10},{10,... | collective-permute-start | bytes 589832 | tf_op jit(solution)/shard_map/ppermute | solution.py:325
  6.1 8.2 %collective-permute-start.4 = (bf16[32,1536]{1,0:T(8,128)(2,1)S(1)}, bf16[32,1536]{1,0:T(8,128)(2,1)S(1)}, u32[]{:S(2)}, u32[]{:S(2)}) collective-permute-start(bf16[32,1536]{1,0:T(8,128)(2,1)S(1)} %add.16), channel_id=1, source_target_pairs={{0,16},{4,28},{8,24},{12,20},{16,0},{20,12},{24,8},{28,4},{1,17},{... | collective-permute-start | bytes 294920 | tf_op jit(solution)/shard_map/ppermute | solution.py:334
  8.7 6.5 %collective-permute-start.1 = (bf16[32,1536]{1,0:T(8,128)(2,1)S(1)}, bf16[32,1536]{1,0:T(8,128)(2,1)S(1)}, u32[]{:S(2)}, u32[]{:S(2)}) collective-permute-start(bf16[32,1536]{1,0:T(8,128)(2,1)S(1)} %add.16), channel_id=1, source_target_pairs={{0,8},{4,12},{8,0},{12,4},{16,24},{20,28},{24,16},{28,20},{1,9},{5... | collective-permute-start | bytes 294920 | tf_op jit(solution)/shard_map/ppermute | solution.py:325
  10.3 6.1 %collective-permute-start.2 = (bf16[32,3072]{1,0:T(8,128)(2,1)S(1)}, bf16[32,3072]{1,0:T(8,128)(2,1)S(1)}, u32[]{:S(2)}, u32[]{:S(2)}) collective-permute-start(bf16[32,3072]{1,0:T(8,128)(2,1)S(1)} %get-tuple-element.33), channel_id=1, source_target_pairs={{0,1},{1,0},{2,3},{3,2},{4,5},{5,4},{6,7},{7,6},{8,9},{9,8},{10,11... | collective-permute-start | bytes 589832 | tf_op jit(solution)/shard_map/ppermute | solution.py:325
  10.8 5.9 %collective-permute-start.3 = (bf16[32,3072]{1,0:T(8,128)(2,1)S(1)}, bf16[32,3072]{1,0:T(8,128)(2,1)S(1)}, u32[]{:S(2)}, u32[]{:S(2)}) collective-permute-start(bf16[32,3072]{1,0:T(8,128)(2,1)S(1)} %get-tuple-element.34), channel_id=1, source_target_pairs={{0,2},{1,3},{2,0},{3,1},{4,6},{5,7},{6,4},{7,5},{8,10},{9,11},{10,... | collective-permute-start | bytes 589832 | tf_op jit(solution)/shard_map/ppermute | solution.py:325
  14.3 2.4 %collective-permute-start.6 = (bf16[32,1536]{1,0:T(8,128)(2,1)S(1)}, bf16[32,1536]{1,0:T(8,128)(2,1)S(1)}, u32[]{:S(2)}, u32[]{:S(2)}) collective-permute-start(bf16[32,1536]{1,0:T(8,128)(2,1)S(1)} %select_add_fusion), channel_id=1, source_target_pairs={{0,4},{4,0},{8,12},{12,8},{16,20},{20,16},{24,28},{28,24},{1,5},{5... | collective-permute-start | bytes 294920 | tf_op jit(solution)/shard_map/ppermute | solution.py:325
  16.7 5.0 %collective-permute-start.7 = (bf16[32,1536]{1,0:T(8,128)(2,1)S(1)}, bf16[32,1536]{1,0:T(8,128)(2,1)S(1)}, u32[]{:S(2)}, u32[]{:S(2)}) collective-permute-start(bf16[32,1536]{1,0:T(8,128)(2,1)S(1)} %add_add_fusion.refs_0_), channel_id=1, source_target_pairs={{0,1},{1,0},{2,3},{3,2},{4,6},{5,7},{6,4},{7,5},{8,9},{9,8},{10,11... | collective-permute-start | bytes 294920 | tf_op jit(solution)/shard_map/ppermute | solution.py:345
  18.3 5.9 %collective-permute-start.9 = (bf16[32,1536]{1,0:T(8,128)(2,1)S(1)}, bf16[32,1536]{1,0:T(8,128)(2,1)S(1)}, u32[]{:S(2)}, u32[]{:S(2)}) collective-permute-start(bf16[32,1536]{1,0:T(8,128)(2,1)S(1)} %add_add_fusion.refs_0_), channel_id=1, source_target_pairs={{0,3},{1,2},{2,1},{3,0},{4,7},{5,6},{6,5},{7,4},{8,11},{9,10},{10,... | collective-permute-start | bytes 294920 | tf_op jit(solution)/shard_map/ppermute | solution.py:325
  21.7 2.4 %collective-permute-start.8 = (bf16[32,1536]{1,0:T(8,128)(2,1)S(1)}, bf16[32,1536]{1,0:T(8,128)(2,1)S(1)}, u32[]{:S(2)}, u32[]{:S(2)}) collective-permute-start(bf16[32,1536]{1,0:T(8,128)(2,1)S(1)} %collective-permute-done.7.refs_1_), channel_id=1, source_target_pairs={{0,4},{4,0},{8,12},{12,8},{16,20},{20,16},{24,28},{28,24},{1,5},{5... | collective-permute-start | bytes 294920 | tf_op jit(solution)/shard_map/ppermute | solution.py:325

commit v16 on v15

--- a/solution.py
+++ b/solution.py
@@ -43,7 +43,13 @@
     return lax.broadcasted_iota(jnp.int32, shape, dim)
 
 
-def whitening(real, imag, high, low, unusable=0.0):
+def band_matrix():
+    shape = (BLOCK + 2 * LANES, BLOCK)
+    near = jnp.abs(iota(shape, 0) - LANES - iota(shape, 1)) <= HALF_WIN
+    return jnp.where(near, 1.0, 0.0).astype(jnp.bfloat16)
+
+
+def whitening(real, imag, high, low, unusable=0.0, band=None):
     count, nbins = real.shape
     blocks = nbins // BLOCK
     span = BLOCK + 2 * LANES
@@ -57,8 +63,7 @@
         part[:, :LANES] = edge
         part[:, LANES : LANES + nbins] = value
         part[:, LANES + nbins :] = edge
-    near = jnp.abs(iota((span, BLOCK), 0) - LANES - iota((span, BLOCK), 1)) <= HALF_WIN
-    band = jnp.where(near, 1.0, 0.0).astype(jnp.bfloat16)
+    band = band_matrix() if band is None else band[...]
     pieces = [
         part[:, block * BLOCK : block * BLOCK + span] for block in range(blocks) for part in (high, low)
     ]
@@ -85,10 +90,10 @@
 
 
 def encode_kernel(
-    segments, spectra_ref, valid_ref, sources_ref, picked_ref, *refs
+    segments, spectra_ref, valid_ref, sources_ref, own_ref, other_ref, *refs
 ):
     blocks, refs = refs[:segments], refs[segments:]
-    encoded_ref, spectra, valid, sources, high, low, arrived = refs
+    encoded_ref, spectra, valid, sources, high, low, band, arrived = refs
     copies = [
         pltpu.make_async_copy(spectra_ref, spectra, arrived.at[0]),
         pltpu.make_async_copy(sources_ref, sources, arrived.at[1]),
@@ -99,24 +104,27 @@
     channels, width = spectra_ref.shape
     nbins = width // 2
     rounds, per_round = sources.shape
-    count = rounds * per_round
-    first_channel = lax.axis_index("rcv") * channels
+    half = rounds * per_round // 2
+    index = lax.axis_index("rcv")
     copies[1].wait()
     copies[2].wait()
     diagonal = iota((channels, channels), 0) == iota((channels, channels), 1)
     usable = jnp.sum(jnp.where(diagonal, valid[...], 0), axis=1, keepdims=True) != 0
-    row = iota((count, channels), 0)
-    local = jnp.zeros((count, channels), jnp.int32)
-    for place in range(count):
-        here = sources[place // per_round, place % per_round] - first_channel
+    row = iota((2 * half, channels), 0)
+    local = jnp.zeros((2 * half, channels), jnp.int32)
+    for place in range(2 * half):
+        number = (index % 2 if place < half else 1 - index % 2) * half + place % half
+        here = sources[number // per_round, number % per_round] - index * channels
         local = jnp.where(row == place, here, local)
-    onehot = jnp.where(local == iota((count, channels), 1), 1.0, 0.0).astype(jnp.bfloat16)
+    onehot = jnp.where(local == iota((2 * half, channels), 1), 1.0, 0.0).astype(jnp.bfloat16)
+    band[...] = band_matrix()
     copies[0].wait()
     encoded = jnp.where(usable, spectra[...].astype(jnp.float32), UNUSABLE).astype(jnp.bfloat16)
     picked = jnp.dot(onehot, encoded, preferred_element_type=jnp.float32)
-    for at, re, im in whitening(picked[:, :nbins], picked[:, nbins:], high, low, UNUSABLE):
-        picked_ref[:count, at] = re.astype(picked_ref.dtype)
-        picked_ref[count:, at] = im.astype(picked_ref.dtype)
+    for at, re, im in whitening(picked[:, :nbins], picked[:, nbins:], high, low, UNUSABLE, band):
+        for first, ref in ((0, own_ref), (half, other_ref)):
+            rows = slice(first, first + half)
+            ref[:, at] = jnp.concatenate([re[rows], im[rows]], axis=0).astype(ref.dtype)
     encoded_ref[...] = encoded.astype(encoded_ref.dtype)
     keep = channels // segments
     for step, block in enumerate(blocks):
@@ -137,22 +145,26 @@
     valid_ref[...] = usable_rows(real)
 
 
-def stack_kernel(places, stage, *refs):
+def stack_kernel(places, halves, stage, *refs):
     first_stage, last_stage = stage
-    segments = len(places)
-    slabs, refs = refs[:segments], refs[segments:]
+    segments, inputs = len(places), 1 + max(slab for pair in halves for slab, _ in pair)
+    slabs, refs = refs[:inputs], refs[inputs:]
     rcv_re, rcv_im, rcv_both, rcv_valid, table_ref, *refs = refs
     before, refs = ([], refs) if first_stage else (refs[:2], refs[2:])
     after, refs = (refs[:1], refs[1:]) if last_stage else (refs[:2], refs[2:])
     src_re, src_diff, src_sum, cross, *refs = refs
-    count, nbins = slabs[0].shape[0] // 2, slabs[0].shape[1]
-    rows = cross.shape[2]
-    keep = rows // count
+    nbins, rows = slabs[0].shape[1], cross.shape[2]
+    count = src_re.shape[1] // segments
+    keep, half = rows // count, count // 2
     core = lax.axis_index("rcv") % 2
     at_rows = [pl.multiple_of(place(core) * keep, keep) for place in places]
-    values = [slab[...].astype(jnp.float32) for slab in slabs]
-    real = jnp.concatenate([value[:count] for value in values], axis=0)
-    imag = jnp.concatenate([value[count:] for value in values], axis=0)
+    values = [
+        slabs[slab][first : first + count].astype(jnp.float32)
+        for pair in halves
+        for slab, first in pair
+    ]
+    real = jnp.concatenate([value[:half] for value in values], axis=0)
+    imag = jnp.concatenate([value[half:] for value in values], axis=0)
     usable = real < USABLE_BELOW
     real, imag = jnp.where(usable, real, 0.0), jnp.where(usable, imag, 0.0)
     src_valid = jnp.where(usable[:, :LANES], 1.0, 0.0)
@@ -239,10 +251,13 @@
             value = ahead[:, first : first + LANES] * weight
             result[to, LANES + first : LANES + last] = value[:, : last - first]
         if (source + 1) % pieces == 0:
-            at = pl.ds((source + 1 - pieces) * keep, pieces * keep)
+            first, size = (source + 1 - pieces) * keep, pieces * keep
+            to = (first + core * half * keep) % rows
             copies.append(
                 pltpu.make_async_copy(
-                    result.at[at], after[0].at[at], written.at[source // pieces]
+                    result.at[pl.ds(first, size)],
+                    after[0].at[pl.ds(pl.multiple_of(to, size), size)],
+                    written.at[source // pieces],
                 )
             )
             copies[-1].start()
@@ -253,15 +268,15 @@
 def encode(segments, spectra, valid, sources):
     channels, width = spectra.shape
     keep = channels // segments
-    slab = jax.ShapeDtypeStruct((2 * sources.size, width // 2), jnp.bfloat16)
+    slab = jax.ShapeDtypeStruct((sources.size, width // 2), jnp.bfloat16)
     block = jax.ShapeDtypeStruct((keep, width), jnp.bfloat16)
     padded = pltpu.VMEM((sources.size, width // 2 + 2 * LANES), jnp.bfloat16)
     pinned = [pltpu.with_memory_space_constraint(x, pltpu.HBM) for x in (spectra, valid, sources)]
     return pl.pallas_call(
         functools.partial(encode_kernel, segments),
-        out_shape=(slab,) + (block,) * segments,
+        out_shape=(slab, slab) + (block,) * segments,
         in_specs=[HBM] * 3,
-        out_specs=(VMEM,) * (1 + segments),
+        out_specs=(VMEM,) * (2 + segments),
         scratch_shapes=[
             pltpu.VMEM((channels, width), kind_for(keep)),
             pltpu.VMEM((channels, width), jnp.bfloat16),
@@ -269,6 +284,7 @@
             pltpu.SMEM(sources.shape, jnp.int32),
             padded,
             padded,
+            pltpu.VMEM((BLOCK + 2 * LANES, BLOCK), jnp.bfloat16),
             pltpu.SemaphoreType.DMA((3,)),
         ],
         compiler_params=pltpu.CompilerParams(vmem_limit_bytes=12 * MEBI),
@@ -295,10 +311,10 @@
     )(*blocks)
 
 
-def stack_stage(keep, slabs, places, receivers, table, before=(), last=True):
-    count, nbins = slabs[0].shape[0] // 2, slabs[0].shape[1]
+def stack_stage(count, keep, slabs, halves, places, receivers, table, before=(), last=True):
+    nbins = slabs[0].shape[1]
     rows, lags = count * keep, 2 * LAG + 1
-    part = pltpu.VMEM((nbins // LANES, len(slabs) * count, LANES), jnp.float32)
+    part = pltpu.VMEM((nbins // LANES, len(places) * count, LANES), jnp.float32)
     cross = pltpu.VMEM((2, nbins // LANES, rows, LANES), kind_for(keep))
     scratch = [part, part, part, cross]
     sums = (
@@ -308,7 +324,7 @@
     if last:
         scratch += [pltpu.VMEM((rows, lags), jnp.float32), pltpu.SemaphoreType.DMA((count,))]
     return pl.pallas_call(
-        functools.partial(stack_kernel, places, (not before, last)),
+        functools.partial(stack_kernel, places, halves, (not before, last)),
         out_shape=jax.ShapeDtypeStruct((rows, lags), jnp.float32) if last else sums,
         in_specs=[VMEM] * (len(slabs) + len(receivers) + 1 + len(before)),
         out_specs=HBM if last else (VMEM, VMEM),
@@ -325,56 +341,71 @@
     return lax.ppermute(value, axis, [(i, i ^ step) for i in range(size)])
 
 
-def gather_shared(picked, receivers, rcv_size, tm_size):
-    core = lax.axis_index("rcv") % 2
+def gather_shared(own, other, receivers, rcv_size, tm_size):
+    def both(one, two):
+        return jnp.concatenate([one, two], axis=0)
+
+    core, count = lax.axis_index("rcv") % 2, own.shape[0]
     receivers[3] = swapped(receivers[3], "tm", tm_size, 3)
-    own = picked + swapped(picked, "rcv", rcv_size, 1)
-    own, near = lax.optimization_barrier((own, receivers[1:3]))
+    rows = both(own, other) + swapped(both(other, own), "rcv", rcv_size, 1)
+    rows, near = lax.optimization_barrier((rows, receivers[1:3]))
     receivers[1:3] = [swapped(block, "tm", tm_size, place) for place, block in enumerate(near, 1)]
-    far = lax.ppermute(own, "rcv", [(i, i ^ (6 if i % 2 else 4)) for i in range(rcv_size)])
-    near = swapped(own, "rcv", rcv_size, 2)
+    far = lax.ppermute(rows, "rcv", [(i, i ^ (6 if i % 2 else 4)) for i in range(rcv_size)])
+    near = swapped(rows, "rcv", rcv_size, 2)
     far, receivers[3] = lax.optimization_barrier((far, receivers[3]))
     near, receivers[1:3] = lax.optimization_barrier((near, receivers[1:3]))
-    partial = far + jnp.where(core == 0, own, jnp.zeros_like(own))
-    own = near + (partial + swapped(partial, "rcv", rcv_size, 1))
+    partial = far + jnp.where(core == 0, rows, jnp.zeros_like(rows))
+    handed = swapped(both(partial[count:], partial[:count]), "rcv", rcv_size, 1)
+    rows = near + (partial + handed)
     pairs = [
         (rcv * tm_size + tm, rcv * tm_size + (tm ^ (2 if rcv % 2 else 1)))
         for rcv in range(rcv_size)
         for tm in range(tm_size)
     ]
-    beside = lax.ppermute(own, ("rcv", "tm"), pairs)
-    across = swapped(own, "tm", tm_size, 3)
-    beside, whitened = lax.optimization_barrier((beside, whiten_blocks(receivers)))
-    handed = swapped(beside, "rcv", rcv_size, 1)
-    return (own, beside), (handed, across), whitened
+    beside = lax.ppermute(rows, ("rcv", "tm"), pairs)
+    across = swapped(rows[:count], "tm", tm_size, 3)
+    beside, across, whitened = lax.optimization_barrier(
+        (beside, across, whiten_blocks(receivers))
+    )
+    handed = swapped(
+        both(both(beside[count:], beside[:count]), across), "rcv", rcv_size, 1
+    )
+    return (rows, beside), (handed, across), whitened
 
 
 def shards(rcv_size, tm_size, spectra, valid, sources):
     channels, _, width = spectra.shape
-    keep = channels // tm_size
-    rounds, per_round = sources.shape
+    keep, count = channels // tm_size, sources.size
     table = jnp.asarray(lag_table(width // 2))
-    picked, *receivers = encode(
+    own, other, *receivers = encode(
         tm_size, spectra[:, 0, :], valid.reshape(1, channels), sources
     )
     if (rcv_size, tm_size) == (8, 4):
-        first, rest, whitened = gather_shared(picked, receivers, rcv_size, tm_size)
+        first, rest, whitened = gather_shared(own, other, receivers, rcv_size, tm_size)
         places = [lambda core: 0, lambda core: 1 + core]
-        sums = stack_stage(keep, first, places, whitened, table, last=False)
+        halves = [((0, 0), (0, count)), ((1, 0), (1, count))]
+        sums = stack_stage(count, keep, first, halves, places, whitened, table, last=False)
         places = [lambda core: 2 - core, lambda core: 3]
-        stack = stack_stage(keep, rest, places, whitened, table, sums)
+        halves = [((0, 0), (0, count)), ((1, 0), (0, 2 * count))]
+        stack = stack_stage(count, keep, rest, halves, places, whitened, table, sums)
     else:
         receivers[1:] = [
             swapped(receivers[place], "tm", tm_size, place) for place in range(1, tm_size)
         ]
-        step = 1
+        both = jnp.concatenate(
+            [own + swapped(other, "rcv", rcv_size, 1), other + swapped(own, "rcv", rcv_size, 1)],
+            axis=0,
+        )
+        step = 2
         while step < rcv_size:
-            picked = picked + swapped(picked, "rcv", rcv_size, step)
+            both = both + swapped(both, "rcv", rcv_size, step)
             step *= 2
-        slabs = [picked] + [swapped(picked, "tm", tm_size, place) for place in range(1, tm_size)]
+        slabs = [both] + [swapped(both, "tm", tm_size, place) for place in range(1, tm_size)]
         places = [functools.partial(lambda place, core: place, place) for place in range(tm_size)]
-        stack = stack_stage(keep, slabs, places, whiten_blocks(receivers), table)
-    return stack.reshape(rounds, per_round, keep, 2 * LAG + 1)
+        halves = [((place, 0), (place, count)) for place in range(tm_size)]
+        whitened = whiten_blocks(receivers)
+        stack = stack_stage(count, keep, slabs, halves, places, whitened, table)
+    return stack.reshape(sources.shape + (keep, 2 * LAG + 1))
 
 
 def solution(mesh):

time: 27.7 us -> 29.4 us (1.061)
  waiting for transfers between devices: 5.79 us -> 7.28 us
    ppermute x8, waiting for transfers between devices: 2.37 us -> 5.13 us  [swapped(): return lax.ppermute(value, axis, [(i, i ^ step) for i in range(size)])]
    ppermute x2, waiting for transfers between devices: 3.42 us -> 2.14 us  [the longest x1 2.14 us: gather_shared(): lax.ppermute(rows, 'rcv', [(i, i ^ (6 if i % 2 else 4)) for i in range(rc...]
where the time goes in v16:
time: 29.4 us; the launch traced here: 29.2 us
  starting transfers between devices  13 us (44%)
  Pallas kernels  8.72 us (30%)
  waiting for transfers between devices  7.28 us (25%)
    ppermute x8, starting transfers between devices, swapped(): return lax.ppermute(value, axis, [(i, i ^ step) for i in range(size)])  8.75 us
    pallas_call x2, Pallas kernels, stack_stage(): pl.pallas_call(functools.partial(stack_kernel, places, halves, (not befor...  5.78 us
    ppermute x8, waiting for transfers between devices, swapped(): return lax.ppermute(value, axis, [(i, i ^ step) for i in range(size)])  5.13 us
    ppermute x1, starting transfers between devices, gather_shared(): lax.ppermute(rows, 'rcv', [(i, i ^ (6 if i % 2 else 4)) for i in range(rc...  2.65 us
    ppermute x1, waiting for transfers between devices, gather_shared(): lax.ppermute(rows, 'rcv', [(i, i ^ (6 if i % 2 else 4)) for i in range(rc...  2.14 us
    pallas_call x1, Pallas kernels, encode(): pl.pallas_call(functools.partial(encode_kernel, segments), out_shape=(sla...  1.96 us
    ppermute x1, starting transfers between devices, gather_shared(): beside = lax.ppermute(rows, ('rcv', 'tm'), pairs)  1.56 us
    pallas_call x1, Pallas kernels, whiten_blocks(): pl.pallas_call(functools.partial(whiten_kernel, segments), out_shape=(par...  0.98 us
  transfers between devices with their start and end apart: 10, of which 5 were waited for; matrix products, arithmetic and copies ran while one was open for 0% of the time, Pallas kernels for 12%

profile of v16, /device:TPU:0, one launch (start us, length us, event | category | flops | bytes accessed | tf_op | source)
XLA Modules:
  0.0 29.2 jit_solution(7005808578226832817)
XLA Ops:
  0.0 2.0 %encode_and_pick.1 = (bf16[16,1536]{1,0:T(8,128)(2,1)S(1)}, bf16[16,1536]{1,0:T(8,128)(2,1)S(1)}, bf16[32,3072]{1,0:T(8,128)(2,1)S(1)}, bf16[32,3072]{1,0:T(8,12...) custom-call(bf16[128,3072]{1,0:T(8,128)(2,1)} %bitcast.3, s32[1,128]{1,0:T(1,128)} %bitcast.4, ...), custom_call_target="tpu_custom_call" | custom-call | tf_op jit(solution)/shard_map/encode_and_pick/pallas_call | solution.py:275
  2.0 0.5 %collective-permute-start = (bf16[32,1536]{1,0:T(8,128)(2,1)S(1)}, bf16[32,1536]{1,0:T(8,128)(2,1)S(1)}, u32[]{:S(2)}, u32[]{:S(2)}) collective-permute-start(bf16[32,1536]{1,0:T(8,128)(2,1)S(1)} %pad_maximum_fusion.1), channel_id=1, source_target_pairs={{0,4},{4,0},{8,12},{12,8},{16,20},{20,16},{24,28},{28,24},{1,5},{5... | collective-permute-start | bytes 294920 | tf_op jit(solution)/shard_map/ppermute | solution.py:341
  2.5 3.5 %collective-permute-start.5 = (bf16[32,3072]{1,0:T(8,128)(2,1)S(1)}, bf16[32,3072]{1,0:T(8,128)(2,1)S(1)}, u32[]{:S(2)}, u32[]{:S(2)}) collective-permute-start(bf16[32,3072]{1,0:T(8,128)(2,1)S(1)} %get-tuple-element.39), channel_id=1, source_target_pairs={{0,3},{1,2},{2,1},{3,0},{4,7},{5,6},{6,5},{7,4},{8,11},{9,10},{10,... | collective-permute-start | bytes 589832 | tf_op jit(solution)/shard_map/ppermute | solution.py:341
  6.0 0.0 collective-permute-done
  6.1 2.7 %collective-permute-start.4 = (bf16[32,1536]{1,0:T(8,128)(2,1)S(1)}, bf16[32,1536]{1,0:T(8,128)(2,1)S(1)}, u32[]{:S(2)}, u32[]{:S(2)}) collective-permute-start(bf16[32,1536]{1,0:T(8,128)(2,1)S(1)} %maximum_add_fusion), channel_id=1, source_target_pairs={{0,16},{4,28},{8,24},{12,20},{16,0},{20,12},{24,8},{28,4},{1,17},{... | collective-permute-start | bytes 294920 | tf_op jit(solution)/shard_map/ppermute | solution.py:353
  8.7 0.0 copy-start
  8.7 1.6 %collective-permute-start.1 = (bf16[32,1536]{1,0:T(8,128)(2,1)S(1)}, bf16[32,1536]{1,0:T(8,128)(2,1)S(1)}, u32[]{:S(2)}, u32[]{:S(2)}) collective-permute-start(bf16[32,1536]{1,0:T(8,128)(2,1)S(1)} %maximum_add_fusion), channel_id=1, source_target_pairs={{0,8},{4,12},{8,0},{12,4},{16,24},{20,28},{24,16},{28,20},{1,9},{5... | collective-permute-start | bytes 294920 | tf_op jit(solution)/shard_map/ppermute | solution.py:341
  10.3 0.5 %collective-permute-start.2 = (bf16[32,3072]{1,0:T(8,128)(2,1)S(1)}, bf16[32,3072]{1,0:T(8,128)(2,1)S(1)}, u32[]{:S(2)}, u32[]{:S(2)}) collective-permute-start(bf16[32,3072]{1,0:T(8,128)(2,1)S(1)} %get-tuple-element.36), channel_id=1, source_target_pairs={{0,1},{1,0},{2,3},{3,2},{4,5},{5,4},{6,7},{7,6},{8,9},{9,8},{10,11... | collective-permute-start | bytes 589832 | tf_op jit(solution)/shard_map/ppermute | solution.py:341
  10.8 1.2 %collective-permute-start.3 = (bf16[32,3072]{1,0:T(8,128)(2,1)S(1)}, bf16[32,3072]{1,0:T(8,128)(2,1)S(1)}, u32[]{:S(2)}, u32[]{:S(2)}) collective-permute-start(bf16[32,3072]{1,0:T(8,128)(2,1)S(1)} %get-tuple-element.37), channel_id=1, source_target_pairs={{0,2},{1,3},{2,0},{3,1},{4,6},{5,7},{6,4},{7,5},{8,10},{9,11},{10,... | collective-permute-start | bytes 589832 | tf_op jit(solution)/shard_map/ppermute | solution.py:341
  12.1 2.1 %collective-permute-done.4 = bf16[32,1536]{1,0:T(8,128)(2,1)S(1)} collective-permute-done((bf16[32,1536]{1,0:T(8,128)(2,1)S(1)}, bf16[32,1536]{1,0:T(8,128)(2,1)S(1)}, u32[]{:S(2)}, u32[]{:S(2)}) %collective-permute-start.4) | collective-permute-done | bytes 98336 | tf_op jit(solution)/shard_map/ppermute | solution.py:353
  14.2 0.0 collective-permute-done.5.refs_3_
  14.3 0.1 collective-permute-start.6
  14.3 0.9 %collective-permute-done.1 = bf16[32,1536]{1,0:T(8,128)(2,1)S(1)} collective-permute-done((bf16[32,1536]{1,0:T(8,128)(2,1)S(1)}, bf16[32,1536]{1,0:T(8,128)(2,1)S(1)}, u32[]{:S(2)}, u32[]{:S(2)}) %collective-permute-start.1) | collective-permute-done | bytes 98336 | tf_op jit(solution)/shard_map/ppermute | solution.py:341
  15.2 1.2 %collective-permute-done.2.refs_1_ = bf16[32,3072]{1,0:T(8,128)(2,1)S(1)} collective-permute-done((bf16[32,3072]{1,0:T(8,128)(2,1)S(1)}, bf16[32,3072]{1,0:T(8,128)(2,1)S(1)}, u32[]{:S(2)}, u32[]{:S(2)}) %collective-permute-start.2) | collective-permute-done | bytes 196640 | tf_op jit(solution)/shard_map/ppermute | solution.py:341
  16.4 0.3 collective-permute-done.3.refs_2_
  16.7 0.0 collective-permute-done.6
  16.7 1.6 %collective-permute-start.7 = (bf16[32,1536]{1,0:T(8,128)(2,1)S(1)}, bf16[32,1536]{1,0:T(8,128)(2,1)S(1)}, u32[]{:S(2)}, u32[]{:S(2)}) collective-permute-start(bf16[32,1536]{1,0:T(8,128)(2,1)S(1)} %add_add_fusion.refs_0_), channel_id=1, source_target_pairs={{0,1},{1,0},{2,3},{3,2},{4,6},{5,7},{6,4},{7,5},{8,9},{9,8},{10,11... | collective-permute-start | bytes 294920 | tf_op jit(solution)/shard_map/ppermute | solution.py:365
  18.3 1.2 %collective-permute-start.8 = (bf16[16,1536]{1,0:T(8,128)(2,1)S(1)}, bf16[16,1536]{1,0:T(8,128)(2,1)S(1)}, u32[]{:S(2)}, u32[]{:S(2)}) collective-permute-start(bf16[16,1536]{1,0:T(8,128)(2,1)S(1)} %slice.22), channel_id=1, source_target_pairs={{0,3},{1,2},{2,1},{3,0},{4,7},{5,6},{6,5},{7,4},{8,11},{9,10},{10,... | collective-permute-start | bytes 147464 | tf_op jit(solution)/shard_map/ppermute | solution.py:341
  19.5 1.0 %whiten_receivers.1 = (f32[128,1536]{1,0:T(8,128)S(1)}, f32[128,1536]{1,0:T(8,128)S(1)}, f32[128,1536]{1,0:T(8,128)S(1)}, f32[128,128]{1,0:T(8,128)S(1)}) custom-call(bf16[32,3072]{1,0:T(8,128)(2,1)S(1)} %get-tuple-element.41.refs_0_, bf16[32,3072]{1,0:T(8,128)(2,1)S(1)} %collective-permute-done.2.refs_1_, ...), custom_call_target="tpu_custom_call" | custom-call | flops 402653184 | bytes 1572864 | tf_op jit(solution)/shard_map/whiten_receivers/pallas_call | solution.py:300
  20.5 2.8 %collective-permute-done.8.refs_1_ = bf16[16,1536]{1,0:T(8,128)(2,1)S(1)} collective-permute-done((bf16[16,1536]{1,0:T(8,128)(2,1)S(1)}, bf16[16,1536]{1,0:T(8,128)(2,1)S(1)}, u32[]{:S(2)}, u32[]{:S(2)}) %collective-permute-start.8) | collective-permute-done | bytes 49184 | tf_op jit(solution)/shard_map/ppermute | solution.py:341
  23.3 0.0 collective-permute-done.7.refs_1_
  23.3 0.1 collective-permute-start.9
  23.4 0.0 copy-done
  23.4 2.4 %stack_first.1 = (f32[2,512,256]{2,1,0:T(8,128)S(1)}, f32[512,128]{1,0:T(8,128)S(1)}) custom-call(bf16[32,1536]{1,0:T(8,128)(2,1)S(1)} %add_add_fusion.refs_0_, bf16[32,1536]{1,0:T(8,128)(2,1)S(1)} %collective-permute-done.7.refs_1_, f32[128,1536]{1,0:T(8,128)S(1)} %get-tuple-element.51.refs_2_, f32[128,1536]{1,0:T(8,128)S(1)} %get-tuple-element.52.refs_3_, ...), custom_call_target="tpu_custom_call" | custom-call | flops 943718400 | bytes 3145728 | tf_op jit(solution)/shard_map/stack_first/pallas_call | solution.py:326
  25.8 0.0 collective-permute-done.9.refs_0_
  25.8 3.4 %stack_last.1 = f32[512,301]{1,0:T(8,128)} custom-call(bf16[48,1536]{1,0:T(8,128)(2,1)S(1)} %collective-permute-done.9.refs_0_, bf16[16,1536]{1,0:T(8,128)(2,1)S(1)} %collective-permute-done.8.refs_1_, f32[128,1536]{1,0:T(8,128)S(1)} %get-tuple-element.51.refs_2_, f32[128,1536]{1,0:T(8,128)S(1)} %get-tuple-element.52.refs_3_, ...), custom_call_target="tpu_custom_call" | custom-call | flops 943718400 | bytes 3145728 | tf_op jit(solution)/shard_map/stack_last/pallas_call | solution.py:326
  (9 shorter events, 0.1 us)
Async XLA Ops:
  2.0 4.0 %collective-permute-start = (bf16[32,1536]{1,0:T(8,128)(2,1)S(1)}, bf16[32,1536]{1,0:T(8,128)(2,1)S(1)}, u32[]{:S(2)}, u32[]{:S(2)}) collective-permute-start(bf16[32,1536]{1,0:T(8,128)(2,1)S(1)} %pad_maximum_fusion.1), channel_id=1, source_target_pairs={{0,4},{4,0},{8,12},{12,8},{16,20},{20,16},{24,28},{28,24},{1,5},{5... | collective-permute-start | bytes 294920 | tf_op jit(solution)/shard_map/ppermute | solution.py:341
  2.5 11.7 %collective-permute-start.5 = (bf16[32,3072]{1,0:T(8,128)(2,1)S(1)}, bf16[32,3072]{1,0:T(8,128)(2,1)S(1)}, u32[]{:S(2)}, u32[]{:S(2)}) collective-permute-start(bf16[32,3072]{1,0:T(8,128)(2,1)S(1)} %get-tuple-element.39), channel_id=1, source_target_pairs={{0,3},{1,2},{2,1},{3,0},{4,7},{5,6},{6,5},{7,4},{8,11},{9,10},{10,... | collective-permute-start | bytes 589832 | tf_op jit(solution)/shard_map/ppermute | solution.py:341
  6.1 8.2 %collective-permute-start.4 = (bf16[32,1536]{1,0:T(8,128)(2,1)S(1)}, bf16[32,1536]{1,0:T(8,128)(2,1)S(1)}, u32[]{:S(2)}, u32[]{:S(2)}) collective-permute-start(bf16[32,1536]{1,0:T(8,128)(2,1)S(1)} %maximum_add_fusion), channel_id=1, source_target_pairs={{0,16},{4,28},{8,24},{12,20},{16,0},{20,12},{24,8},{28,4},{1,17},{... | collective-permute-start | bytes 294920 | tf_op jit(solution)/shard_map/ppermute | solution.py:353
  8.7 14.7 %copy-start = (bf16[3072,256]{1,0:T(8,128)(2,1)S(1)}, bf16[3072,256]{1,0:T(8,128)(2,1)}, u32[]{:S(2)}) copy-start(bf16[3072,256]{1,0:T(8,128)(2,1)} %constant.24.clone.refs_6_) | copy-start | bytes 4718596
  8.7 6.5 %collective-permute-start.1 = (bf16[32,1536]{1,0:T(8,128)(2,1)S(1)}, bf16[32,1536]{1,0:T(8,128)(2,1)S(1)}, u32[]{:S(2)}, u32[]{:S(2)}) collective-permute-start(bf16[32,1536]{1,0:T(8,128)(2,1)S(1)} %maximum_add_fusion), channel_id=1, source_target_pairs={{0,8},{4,12},{8,0},{12,4},{16,24},{20,28},{24,16},{28,20},{1,9},{5... | collective-permute-start | bytes 294920 | tf_op jit(solution)/shard_map/ppermute | solution.py:341
  10.3 6.1 %collective-permute-start.2 = (bf16[32,3072]{1,0:T(8,128)(2,1)S(1)}, bf16[32,3072]{1,0:T(8,128)(2,1)S(1)}, u32[]{:S(2)}, u32[]{:S(2)}) collective-permute-start(bf16[32,3072]{1,0:T(8,128)(2,1)S(1)} %get-tuple-element.36), channel_id=1, source_target_pairs={{0,1},{1,0},{2,3},{3,2},{4,5},{5,4},{6,7},{7,6},{8,9},{9,8},{10,11... | collective-permute-start | bytes 589832 | tf_op jit(solution)/shard_map/ppermute | solution.py:341
  10.8 5.9 %collective-permute-start.3 = (bf16[32,3072]{1,0:T(8,128)(2,1)S(1)}, bf16[32,3072]{1,0:T(8,128)(2,1)S(1)}, u32[]{:S(2)}, u32[]{:S(2)}) collective-permute-start(bf16[32,3072]{1,0:T(8,128)(2,1)S(1)} %get-tuple-element.37), channel_id=1, source_target_pairs={{0,2},{1,3},{2,0},{3,1},{4,6},{5,7},{6,4},{7,5},{8,10},{9,11},{10,... | collective-permute-start | bytes 589832 | tf_op jit(solution)/shard_map/ppermute | solution.py:341
  14.3 2.4 %collective-permute-start.6 = (bf16[32,1536]{1,0:T(8,128)(2,1)S(1)}, bf16[32,1536]{1,0:T(8,128)(2,1)S(1)}, u32[]{:S(2)}, u32[]{:S(2)}) collective-permute-start(bf16[32,1536]{1,0:T(8,128)(2,1)S(1)} %pad_maximum_fusion.2), channel_id=1, source_target_pairs={{0,4},{4,0},{8,12},{12,8},{16,20},{20,16},{24,28},{28,24},{1,5},{5... | collective-permute-start | bytes 294920 | tf_op jit(solution)/shard_map/ppermute | solution.py:341
  16.7 6.6 %collective-permute-start.7 = (bf16[32,1536]{1,0:T(8,128)(2,1)S(1)}, bf16[32,1536]{1,0:T(8,128)(2,1)S(1)}, u32[]{:S(2)}, u32[]{:S(2)}) collective-permute-start(bf16[32,1536]{1,0:T(8,128)(2,1)S(1)} %add_add_fusion.refs_0_), channel_id=1, source_target_pairs={{0,1},{1,0},{2,3},{3,2},{4,6},{5,7},{6,4},{7,5},{8,9},{9,8},{10,11... | collective-permute-start | bytes 294920 | tf_op jit(solution)/shard_map/ppermute | solution.py:365
  18.3 5.0 %collective-permute-start.8 = (bf16[16,1536]{1,0:T(8,128)(2,1)S(1)}, bf16[16,1536]{1,0:T(8,128)(2,1)S(1)}, u32[]{:S(2)}, u32[]{:S(2)}) collective-permute-start(bf16[16,1536]{1,0:T(8,128)(2,1)S(1)} %slice.22), channel_id=1, source_target_pairs={{0,3},{1,2},{2,1},{3,0},{4,7},{5,6},{6,5},{7,4},{8,11},{9,10},{10,... | collective-permute-start | bytes 147464 | tf_op jit(solution)/shard_map/ppermute | solution.py:341
  23.3 2.5 %collective-permute-start.9 = (bf16[48,1536]{1,0:T(8,128)(2,1)S(1)}, bf16[48,1536]{1,0:T(8,128)(2,1)S(1)}, u32[]{:S(2)}, u32[]{:S(2)}) collective-permute-start(bf16[48,1536]{1,0:T(8,128)(2,1)S(1)} %pad_maximum_fusion), channel_id=1, source_target_pairs={{0,4},{4,0},{8,12},{12,8},{16,20},{20,16},{24,28},{28,24},{1,5},{5... | collective-permute-start | bytes 442376 | tf_op jit(solution)/shard_map/ppermute | solution.py:341

commit v17 on v13

--- a/solution.py
+++ b/solution.py
@@ -43,7 +43,13 @@
     return lax.broadcasted_iota(jnp.int32, shape, dim)
 
 
-def whitening(real, imag, high, low, unusable=0.0):
+def band_matrix():
+    shape = (BLOCK + 2 * LANES, BLOCK)
+    near = jnp.abs(iota(shape, 0) - LANES - iota(shape, 1)) <= HALF_WIN
+    return jnp.where(near, 1.0, 0.0).astype(jnp.bfloat16)
+
+
+def whitening(real, imag, high, low, unusable=0.0, band=None):
     count, nbins = real.shape
     blocks = nbins // BLOCK
     span = BLOCK + 2 * LANES
@@ -57,8 +63,7 @@
         part[:, :LANES] = edge
         part[:, LANES : LANES + nbins] = value
         part[:, LANES + nbins :] = edge
-    near = jnp.abs(iota((span, BLOCK), 0) - LANES - iota((span, BLOCK), 1)) <= HALF_WIN
-    band = jnp.where(near, 1.0, 0.0).astype(jnp.bfloat16)
+    band = band_matrix() if band is None else band[...]
     pieces = [
         part[:, block * BLOCK : block * BLOCK + span] for block in range(blocks) for part in (high, low)
     ]
@@ -88,7 +93,7 @@
     segments, spectra_ref, valid_ref, sources_ref, own_ref, other_ref, *refs
 ):
     blocks, refs = refs[:segments], refs[segments:]
-    encoded_ref, spectra, valid, sources, high, low, arrived = refs
+    encoded_ref, spectra, valid, sources, high, low, band, arrived = refs
     copies = [
         pltpu.make_async_copy(spectra_ref, spectra, arrived.at[0]),
         pltpu.make_async_copy(sources_ref, sources, arrived.at[1]),
@@ -112,10 +117,11 @@
         here = sources[number // per_round, number % per_round] - index * channels
         local = jnp.where(row == place, here, local)
     onehot = jnp.where(local == iota((2 * half, channels), 1), 1.0, 0.0).astype(jnp.bfloat16)
+    band[...] = band_matrix()
     copies[0].wait()
     encoded = jnp.where(usable, spectra[...].astype(jnp.float32), UNUSABLE).astype(jnp.bfloat16)
     picked = jnp.dot(onehot, encoded, preferred_element_type=jnp.float32)
-    for at, re, im in whitening(picked[:, :nbins], picked[:, nbins:], high, low, UNUSABLE):
+    for at, re, im in whitening(picked[:, :nbins], picked[:, nbins:], high, low, UNUSABLE, band):
         for first, ref in ((0, own_ref), (half, other_ref)):
             rows = slice(first, first + half)
             ref[:, at] = jnp.concatenate([re[rows], im[rows]], axis=0).astype(ref.dtype)
@@ -139,31 +145,36 @@
     valid_ref[...] = usable_rows(real)
 
 
-def stack_kernel(
-    segments, slabs_ref, rcv_re, rcv_im, rcv_both, rcv_valid, table_ref, *refs
-):
-    *rest, out_ref, src_re, src_diff, src_sum, cross = refs[: 6 if len(refs) == 8 else 5]
-    half = slabs_ref.shape[0] // (2 * segments)
-    nbins = slabs_ref.shape[1]
-    keep = rcv_re.shape[0] // segments
-    rows = half * keep
-    if rest:
-        result, written = refs[6:]
+def stack_kernel(places, stage, *refs):
+    segments, sets = len(places), 1 + max(which for which, _ in places)
+    slabs, refs = refs[0], refs[1:]
+    receivers = [refs[4 * which : 4 * which + 4] for which in range(sets)]
+    table_ref, refs = refs[4 * sets], refs[4 * sets + 1 :]
+    first_stage, stage = stage
+    before, refs = ([], refs) if first_stage else (refs[:2], refs[2:])
+    ready, refs = (refs[0], refs[1:]) if stage == "store" else (None, refs)
+    after, refs = (refs[:2], refs[2:]) if stage == "sums" else (refs[:1], refs[1:])
+    src_re, src_diff, src_sum, cross, *refs = refs
+    nbins, rows = slabs.shape[1], cross.shape[2]
+    count = slabs.shape[0] // (2 * segments)
+    keep = rows // count
+    copies = []
+    if stage == "store":
+        result, written = refs
         part = lax.axis_index("rcv") % 2
-        pieces = max(1, half // 4)
         at = pl.multiple_of(part * rows, rows)
-        copies = [
-            pltpu.make_async_copy(rest[0], out_ref.at[pl.ds(at, rows)], written.at[0])
-        ]
+        copies.append(
+            pltpu.make_async_copy(ready, after[0].at[pl.ds(at, rows)], written.at[count])
+        )
         copies[0].start()
-    else:
-        result = out_ref
-    slabs = slabs_ref[...].astype(jnp.float32)
+    elif stage == "result":
+        result = after[0]
+    values = slabs[...].astype(jnp.float32)
     real = jnp.concatenate(
-        [slabs[2 * half * t : 2 * half * t + half] for t in range(segments)], axis=0
+        [values[2 * count * t : 2 * count * t + count] for t in range(segments)], axis=0
     )
     imag = jnp.concatenate(
-        [slabs[2 * half * t + half : 2 * half * (t + 1)] for t in range(segments)], axis=0
+        [values[2 * count * t + count : 2 * count * (t + 1)] for t in range(segments)], axis=0
     )
     usable = real < USABLE_BELOW
     real, imag = jnp.where(usable, real, 0.0), jnp.where(usable, imag, 0.0)
@@ -171,7 +182,7 @@
     for ref, value in ((src_re, real), (src_diff, imag - real), (src_sum, imag + real)):
         for block in range(nbins // LANES):
             ref[block] = value[:, block * LANES : (block + 1) * LANES]
-    tile = min(keep, 16)
+    tile = keep if segments <= 2 else min(keep, 16)
 
     def spread(ref, block, row):
         return jnp.concatenate([ref[block, pl.ds(row, 8, stride=0), :]] * (tile // 8), axis=0)
@@ -179,14 +190,17 @@
     def multiply(block, carry):
         at = pl.ds(pl.multiple_of(block * LANES, LANES), LANES)
         for first in range(0, keep, tile):
-            rows = [slice(t * keep + first, t * keep + first + tile) for t in range(segments)]
-            r_re = [rcv_re[row, at] for row in rows]
-            r_im = [rcv_im[row, at] for row in rows]
-            r_both = [rcv_both[row, at] for row in rows]
-            for source in range(half):
+            taken = [
+                (receivers[which], slice(place * keep + first, place * keep + first + tile))
+                for which, place in places
+            ]
+            r_re = [block_refs[0][row, at] for block_refs, row in taken]
+            r_im = [block_refs[1][row, at] for block_refs, row in taken]
+            r_both = [block_refs[2][row, at] for block_refs, row in taken]
+            for source in range(count):
                 p, q, w = [], [], []
                 for t in range(segments):
-                    row = t * half + source
+                    row = t * count + source
                     p.append(spread(src_re, block, row) * r_both[t])
                     q.append(spread(src_diff, block, row) * r_im[t])
                     w.append(spread(src_sum, block, row) * r_re[t])
@@ -207,22 +221,34 @@
         )
 
     ends = []
-    for first in (0, half // 2):
-        at = slice(first * keep, (first + half // 2) * keep)
-        ends.append([project(place, at) for place in range(2)])
-
-    lags = result.shape[1]
+    for first in (0, count // 2):
+        at = slice(first * keep, (first + count // 2) * keep)
+        sums = [project(place, at) for place in range(2)]
+        if not first_stage:
+            sums = [before[0][place, at] + sums[place] for place in range(2)]
+        if stage == "sums":
+            for place in range(2):
+                after[0][place, at] = sums[place]
+        ends.append(sums)
+
+    lags = 2 * LAG + 1
     scale = 2.0 / math.sqrt(nbins)
     mirror = LAG - FIRST_LAG - iota((keep, LANES), 1)
-    for source in range(half):
-        common = 0.0
-        for t in range(segments):
-            row = t * half + source
-            common = common + src_valid[row : row + 1] * rcv_valid[t * keep : (t + 1) * keep, :]
+    pieces = max(1, count // 4)
+    for source in range(count):
+        to = slice(source * keep, (source + 1) * keep)
+        common = [
+            src_valid[t * count + source : t * count + source + 1]
+            * receivers[which][3][place * keep : (place + 1) * keep, :]
+            for t, (which, place) in enumerate(places)
+        ] + ([] if first_stage else [before[1][to]])
+        common = functools.reduce(jnp.add, common)
+        if stage == "sums":
+            after[1][to] = common
+            continue
         weight = scale / jnp.maximum(common, 1.0)
-        to = slice(source * keep, (source + 1) * keep)
-        inside = slice(source % (half // 2) * keep, (source % (half // 2) + 1) * keep)
-        even, odd = (total[inside] for total in ends[source // (half // 2)])
+        inside = slice(source % (count // 2) * keep, (source % (count // 2) + 1) * keep)
+        even, odd = (total[inside] for total in ends[source // (count // 2)])
         ahead = even + odd
         behind = even - odd
         low_part = jnp.take_along_axis(
@@ -236,20 +262,19 @@
             last = min(first + LANES, lags - LANES)
             value = ahead[:, first : first + LANES] * weight
             result[to, LANES + first : LANES + last] = value[:, : last - first]
-        if rest and (source + 1) % pieces == 0:
-            first, count = (source + 1 - pieces) * keep, pieces * keep
-            at = pl.multiple_of((1 - part) * rows + first, count)
+        if stage == "store" and (source + 1) % pieces == 0:
+            first, size = (source + 1 - pieces) * keep, pieces * keep
+            at = pl.multiple_of((1 - part) * rows + first, size)
             copies.append(
                 pltpu.make_async_copy(
-                    result.at[pl.ds(first, count)],
-                    out_ref.at[pl.ds(at, count)],
-                    written.at[1 + source // pieces],
+                    result.at[pl.ds(first, size)],
+                    after[0].at[pl.ds(at, size)],
+                    written.at[source // pieces],
                 )
             )
             copies[-1].start()
-    if rest:
-        for copy in copies:
-            copy.wait()
+    for copy in copies:
+        copy.wait()
 
 
 def encode(segments, spectra, valid, sources):
@@ -271,6 +296,7 @@
             pltpu.SMEM(sources.shape, jnp.int32),
             padded,
             padded,
+            pltpu.VMEM((BLOCK + 2 * LANES, BLOCK), jnp.bfloat16),
             pltpu.SemaphoreType.DMA((3,)),
         ],
         compiler_params=pltpu.CompilerParams(vmem_limit_bytes=12 * MEBI),
@@ -297,27 +323,33 @@
     )(*blocks)
 
 
-def stack_half(segments, slabs, receivers, table, rest=()):
-    half, nbins = slabs.shape[0] // (2 * segments), slabs.shape[1]
-    keep = receivers[0].shape[0] // segments
-    count, rows, lags = segments * half, half * keep, 2 * LAG + 1
-    part = pltpu.VMEM((nbins // LANES, count, LANES), jnp.float32)
+def stack_stage(keep, slabs, places, receivers, table, stage, before=(), ready=()):
+    count, nbins = slabs.shape[0] // (2 * len(places)), slabs.shape[1]
+    rows, lags = count * keep, 2 * LAG + 1
+    part = pltpu.VMEM((nbins // LANES, len(places) * count, LANES), jnp.float32)
     cross = pltpu.VMEM((2, nbins // LANES, rows, LANES), kind_for(keep))
     scratch = [part, part, part, cross]
-    if rest:
-        scratch += [pltpu.VMEM((rows, lags), jnp.float32), pltpu.SemaphoreType.DMA((1 + half,))]
+    sums = (
+        jax.ShapeDtypeStruct((2, rows, BLOCK), jnp.float32),
+        jax.ShapeDtypeStruct((rows, LANES), jnp.float32),
+    )
+    if stage == "store":
+        scratch += [pltpu.VMEM((rows, lags), jnp.float32), pltpu.SemaphoreType.DMA((count + 1,))]
+    out_rows = 2 * rows if stage == "store" else rows
+    result = jax.ShapeDtypeStruct((out_rows, lags), jnp.float32)
+    inputs = [slabs, *sum(receivers, ()), table, *before, *ready]
     return pl.pallas_call(
-        functools.partial(stack_kernel, segments),
-        out_shape=jax.ShapeDtypeStruct((2 * rows if rest else rows, lags), jnp.float32),
-        in_specs=[VMEM] * (6 + len(rest)),
-        out_specs=HBM if rest else VMEM,
+        functools.partial(stack_kernel, places, (not before, stage)),
+        out_shape=sums if stage == "sums" else result,
+        in_specs=[VMEM] * len(inputs),
+        out_specs=(VMEM, VMEM) if stage == "sums" else HBM if stage == "store" else VMEM,
         scratch_shapes=scratch,
         compiler_params=pltpu.CompilerParams(vmem_limit_bytes=20 * MEBI),
         cost_estimate=pl.CostEstimate(
             flops=4 * rows * nbins * 2 * LAG, bytes_accessed=nbins * 2048, transcendentals=0
         ),
-        name="stack_other_half" if rest else "stack_own_half",
-    )(slabs, *receivers, table, *rest)
+        name="stack_" + stage,
+    )(*inputs)
 
 
 def swapped(value, axis, size, step):
@@ -346,14 +378,23 @@
         own = functools.reduce(jnp.add, parts, own)
         step *= wide
     own = [own] + [swapped(own, "tm", tm_size, place) for place in range(1, tm_size)]
-    whitened = whiten_blocks(receivers)
-    own, whitened = lax.optimization_barrier((own, whitened))
-    own = jnp.concatenate(own, axis=0)
-    other = swapped(own, "rcv", rcv_size, 1)
-
+    own[-1], receivers[1:-1] = lax.optimization_barrier((own[-1], receivers[1:-1]))
     table = jnp.asarray(lag_table(width // 2))
-    first = stack_half(tm_size, own, whitened, table)
-    stack = stack_half(tm_size, other, whitened, table, (first,))
+    far = tm_size - 1
+    early = tuple(whiten_blocks([receivers[0], receivers[far]]))
+    sums = stack_stage(
+        keep, jnp.concatenate([own[0], own[far]], axis=0), [(0, 0), (0, 1)], [early], table, "sums"
+    )
+    late = tuple(whiten_blocks(receivers[1:far]))
+    rest, sums, late = lax.optimization_barrier((own[1:far], sums, late))
+    slabs = jnp.concatenate([own[0], own[far], *rest], axis=0)
+    other = swapped(slabs, "rcv", rcv_size, 1)
+    places = [(0, place) for place in range(far - 1)]
+    first = stack_stage(
+        keep, slabs[2 * own[0].shape[0] :], places, [late], table, "result", sums
+    )
+    places = [(0, 0), (0, 1)] + [(1, place) for place in range(far - 1)]
+    stack = stack_stage(keep, other, places, [early, late], table, "store", (), (first,))
     return stack.reshape(rounds, per_round, keep, 2 * LAG + 1)
 
 

time: 27.5 us -> 27.7 us (level)
  Pallas kernels: 8.06 us -> 8.81 us
  waiting for transfers between devices: 5.99 us -> 5.48 us
    pallas_call x2 -> x3, Pallas kernels: 5.06 us -> 5.71 us  [stack_stage(): pl.pallas_call(functools.partial(stack_kernel, places, (not before, stage...]
    ppermute x11, waiting for transfers between devices: 5.99 us -> 5.48 us  [swapped(): return lax.ppermute(value, axis, [(i, i ^ step) for i in range(size)])]
    pallas_call x1 -> x2, Pallas kernels: 0.98 us -> 1.02 us  [whiten_blocks(): pl.pallas_call(functools.partial(whiten_kernel, segments), out_shape=(par...]
  transfers between devices with their start and end apart: 11 -> 11, of which waited for: 6 -> 5; matrix products, arithmetic and copies ran while one was open for 0% -> 0% of each run, Pallas kernels for 12% -> 14%
where the time goes in v17:
time: 27.7 us; the launch traced here: 27.6 us
  starting transfers between devices  13.1 us (47%)
  Pallas kernels  8.81 us (32%)
  waiting for transfers between devices  5.48 us (20%)
    ppermute x11, starting transfers between devices, swapped(): return lax.ppermute(value, axis, [(i, i ^ step) for i in range(size)])  13.1 us
    pallas_call x3, Pallas kernels, stack_stage(): pl.pallas_call(functools.partial(stack_kernel, places, (not before, stage...  5.71 us
    ppermute x11, waiting for transfers between devices, swapped(): return lax.ppermute(value, axis, [(i, i ^ step) for i in range(size)])  5.48 us
    pallas_call x1, Pallas kernels, encode(): pl.pallas_call(functools.partial(encode_kernel, segments), out_shape=(sla...  2.08 us
    pallas_call x2, Pallas kernels, whiten_blocks(): pl.pallas_call(functools.partial(whiten_kernel, segments), out_shape=(par...  1.02 us
  transfers between devices with their start and end apart: 11, of which 5 were waited for; matrix products, arithmetic and copies ran while one was open for 0% of the time, Pallas kernels for 14%

profile of v17, /device:TPU:0, one launch (start us, length us, event | category | flops | bytes accessed | tf_op | source)
XLA Modules:
  0.0 27.6 jit_solution(5437969842737873536)
XLA Ops:
  0.0 0.0 copy-start
  0.0 2.1 %encode_and_pick.1 = (bf16[16,1536]{1,0:T(8,128)(2,1)S(1)}, bf16[16,1536]{1,0:T(8,128)(2,1)S(1)}, bf16[32,3072]{1,0:T(8,128)(2,1)S(1)}, bf16[32,3072]{1,0:T(8,12...) custom-call(bf16[128,3072]{1,0:T(8,128)(2,1)} %bitcast.3, s32[1,128]{1,0:T(1,128)} %bitcast.4, ...), custom_call_target="tpu_custom_call" | custom-call | tf_op jit(solution)/shard_map/encode_and_pick/pallas_call | solution.py:287
  2.1 4.0 %collective-permute-start.4 = (bf16[32,3072]{1,0:T(8,128)(2,1)S(1)}, bf16[32,3072]{1,0:T(8,128)(2,1)S(1)}, u32[]{:S(2)}, u32[]{:S(2)}) collective-permute-start(bf16[32,3072]{1,0:T(8,128)(2,1)S(1)} %get-tuple-element.42), channel_id=1, source_target_pairs={{0,3},{1,2},{2,1},{3,0},{4,7},{5,6},{6,5},{7,4},{8,11},{9,10},{10,... | collective-permute-start | bytes 589832 | tf_op jit(solution)/shard_map/ppermute | solution.py:356
  6.0 0.0 collective-permute-start
  6.1 1.2 %collective-permute-done = bf16[16,1536]{1,0:T(8,128)(2,1)S(1)} collective-permute-done((bf16[16,1536]{1,0:T(8,128)(2,1)S(1)}, bf16[16,1536]{1,0:T(8,128)(2,1)S(1)}, u32[]{:S(2)}, u32[]{:S(2)}) %collective-permute-start) | collective-permute-done | bytes 49184 | tf_op jit(solution)/shard_map/ppermute | solution.py:356
  7.3 3.7 %collective-permute-start.3 = (bf16[16,1536]{1,0:T(8,128)(2,1)S(1)}, bf16[16,1536]{1,0:T(8,128)(2,1)S(1)}, u32[]{:S(2)}, u32[]{:S(2)}) collective-permute-start(bf16[16,1536]{1,0:T(8,128)(2,1)S(1)} %add.12), channel_id=1, source_target_pairs={{0,24},{4,28},{8,16},{12,20},{16,8},{20,12},{24,0},{28,4},{1,25},{... | collective-permute-start | bytes 147464 | tf_op jit(solution)/shard_map/ppermute | solution.py:356
  11.0 0.0 collective-permute-start.2
  11.0 0.8 %collective-permute-start.1 = (bf16[16,1536]{1,0:T(8,128)(2,1)S(1)}, bf16[16,1536]{1,0:T(8,128)(2,1)S(1)}, u32[]{:S(2)}, u32[]{:S(2)}) collective-permute-start(bf16[16,1536]{1,0:T(8,128)(2,1)S(1)} %add.12), channel_id=1, source_target_pairs={{0,8},{4,12},{8,0},{12,4},{16,24},{20,28},{24,16},{28,20},{1,9},{5... | collective-permute-start | bytes 147464 | tf_op jit(solution)/shard_map/ppermute | solution.py:356
  11.8 0.5 %collective-permute-start.6 = (bf16[32,3072]{1,0:T(8,128)(2,1)S(1)}, bf16[32,3072]{1,0:T(8,128)(2,1)S(1)}, u32[]{:S(2)}, u32[]{:S(2)}) collective-permute-start(bf16[32,3072]{1,0:T(8,128)(2,1)S(1)} %get-tuple-element.44), channel_id=1, source_target_pairs={{0,1},{1,0},{2,3},{3,2},{4,5},{5,4},{6,7},{7,6},{8,9},{9,8},{10,11... | collective-permute-start | bytes 589832 | tf_op jit(solution)/shard_map/ppermute | solution.py:356
  12.3 1.0 %collective-permute-done.3 = bf16[16,1536]{1,0:T(8,128)(2,1)S(1)} collective-permute-done((bf16[16,1536]{1,0:T(8,128)(2,1)S(1)}, bf16[16,1536]{1,0:T(8,128)(2,1)S(1)}, u32[]{:S(2)}, u32[]{:S(2)}) %collective-permute-start.3) | collective-permute-done | bytes 49184 | tf_op jit(solution)/shard_map/ppermute | solution.py:356
  13.3 0.5 %collective-permute-start.7 = (bf16[32,3072]{1,0:T(8,128)(2,1)S(1)}, bf16[32,3072]{1,0:T(8,128)(2,1)S(1)}, u32[]{:S(2)}, u32[]{:S(2)}) collective-permute-start(bf16[32,3072]{1,0:T(8,128)(2,1)S(1)} %get-tuple-element.45), channel_id=1, source_target_pairs={{0,2},{1,3},{2,0},{3,1},{4,6},{5,7},{6,4},{7,5},{8,10},{9,11},{10,... | collective-permute-start | bytes 589832 | tf_op jit(solution)/shard_map/ppermute | solution.py:356
  13.8 0.0 collective-permute-done.4.refs_1_
  13.8 2.1 %collective-permute-done.2 = bf16[16,1536]{1,0:T(8,128)(2,1)S(1)} collective-permute-done((bf16[16,1536]{1,0:T(8,128)(2,1)S(1)}, bf16[16,1536]{1,0:T(8,128)(2,1)S(1)}, u32[]{:S(2)}, u32[]{:S(2)}) %collective-permute-start.2) | collective-permute-done | bytes 49184 | tf_op jit(solution)/shard_map/ppermute | solution.py:356
  16.0 0.0 collective-permute-done.1
  16.0 0.5 %collective-permute-start.5 = (bf16[16,1536]{1,0:T(8,128)(2,1)S(1)}, bf16[16,1536]{1,0:T(8,128)(2,1)S(1)}, u32[]{:S(2)}, u32[]{:S(2)}) collective-permute-start(bf16[16,1536]{1,0:T(8,128)(2,1)S(1)} %add_add_fusion), channel_id=1, source_target_pairs={{0,3},{1,2},{2,1},{3,0},{4,7},{5,6},{6,5},{7,4},{8,11},{9,10},{10,... | collective-permute-start | bytes 147464 | tf_op jit(solution)/shard_map/ppermute | solution.py:356
  16.5 1.5 %collective-permute-start.9 = (bf16[16,1536]{1,0:T(8,128)(2,1)S(1)}, bf16[16,1536]{1,0:T(8,128)(2,1)S(1)}, u32[]{:S(2)}, u32[]{:S(2)}) collective-permute-start(bf16[16,1536]{1,0:T(8,128)(2,1)S(1)} %add_add_fusion), channel_id=1, source_target_pairs={{0,2},{1,3},{2,0},{3,1},{4,6},{5,7},{6,4},{7,5},{8,10},{9,11},{10,... | collective-permute-start | bytes 147464 | tf_op jit(solution)/shard_map/ppermute | solution.py:356
  18.0 1.5 %collective-permute-start.8 = (bf16[16,1536]{1,0:T(8,128)(2,1)S(1)}, bf16[16,1536]{1,0:T(8,128)(2,1)S(1)}, u32[]{:S(2)}, u32[]{:S(2)}) collective-permute-start(bf16[16,1536]{1,0:T(8,128)(2,1)S(1)} %add_add_fusion), channel_id=1, source_target_pairs={{0,1},{1,0},{2,3},{3,2},{4,5},{5,4},{6,7},{7,6},{8,9},{9,8},{10,11... | collective-permute-start | bytes 147464 | tf_op jit(solution)/shard_map/ppermute | solution.py:356
  19.5 0.5 %whiten_receivers.2 = (f32[64,1536]{1,0:T(8,128)S(1)}, f32[64,1536]{1,0:T(8,128)S(1)}, f32[64,1536]{1,0:T(8,128)S(1)}, f32[64,128]{1,0:T(8,128)S(1)}) custom-call(bf16[32,3072]{1,0:T(8,128)(2,1)S(1)} %get-tuple-element.47.refs_0_, bf16[32,3072]{1,0:T(8,128)(2,1)S(1)} %collective-permute-done.4.refs_1_), custom_call_target="tpu_custom_call" | custom-call | flops 201326592 | bytes 786432 | tf_op jit(solution)/shard_map/whiten_receivers/pallas_call | solution.py:312
  20.0 0.0 collective-permute-done.6.refs_0_
  20.1 0.2 collective-permute-done.7.refs_1_
  20.3 0.8 %collective-permute-done.5 = bf16[16,1536]{1,0:T(8,128)(2,1)S(1)} collective-permute-done((bf16[16,1536]{1,0:T(8,128)(2,1)S(1)}, bf16[16,1536]{1,0:T(8,128)(2,1)S(1)}, u32[]{:S(2)}, u32[]{:S(2)}) %collective-permute-start.5) | collective-permute-done | bytes 49184 | tf_op jit(solution)/shard_map/ppermute | solution.py:356
  21.1 0.5 %whiten_receivers.3 = (f32[64,1536]{1,0:T(8,128)S(1)}, f32[64,1536]{1,0:T(8,128)S(1)}, f32[64,1536]{1,0:T(8,128)S(1)}, f32[64,128]{1,0:T(8,128)S(1)}) custom-call(bf16[32,3072]{1,0:T(8,128)(2,1)S(1)} %collective-permute-done.6.refs_0_, bf16[32,3072]{1,0:T(8,128)(2,1)S(1)} %collective-permute-done.7.refs_1_), custom_call_target="tpu_custom_call" | custom-call | flops 201326592 | bytes 786432 | tf_op jit(solution)/shard_map/whiten_receivers/pallas_call | solution.py:312
  21.7 0.0 copy-done
  21.7 1.4 %stack_sums.1 = (f32[2,256,256]{2,1,0:T(8,128)S(1)}, f32[256,128]{1,0:T(8,128)S(1)}) custom-call(bf16[32,1536]{1,0:T(8,128)(2,1)S(1)} %pad_maximum_fusion.1.refs_0_, f32[64,1536]{1,0:T(8,128)S(1)} %get-tuple-element.49.refs_1_, f32[64,1536]{1,0:T(8,128)S(1)} %get-tuple-element.50.refs_2_, f32[64,1536]{1,0:T(8,128)S(1)} %get-tuple-element.51.refs_3_, ...), custom_call_target="tpu_custom_call" | custom-call | flops 471859200 | bytes 3145728 | tf_op jit(solution)/shard_map/stack_sums/pallas_call | solution.py:341
  23.0 0.0 collective-permute-done.9
  23.0 0.0 collective-permute-done.8
  23.1 0.1 collective-permute-start.10
  23.2 1.5 %stack_result.1.refs_10_ = f32[256,301]{1,0:T(8,128)S(1)} custom-call(bf16[32,1536]{1,0:T(8,128)(2,1)S(1)} %pad_maximum_fusion.2.refs_0_, f32[64,1536]{1,0:T(8,128)S(1)} %get-tuple-element.63.refs_1_.refs_5_, f32[64,1536]{1,0:T(8,128)S(1)} %get-tuple-element.64.refs_2_.refs_6_, f32[64,1536]{1,0:T(8,128)S(1)} %get-tuple-element.65.refs_3_.refs_7_, ...), custom_call_target="tpu_custom_call" | custom-call | flops 471859200 | bytes 3145728 | tf_op jit(solution)/shard_map/stack_result/pallas_call | solution.py:341
  24.6 0.0 collective-permute-done.10.refs_0_
  24.7 2.9 %stack_store.1 = f32[512,301]{1,0:T(8,128)} custom-call(bf16[64,1536]{1,0:T(8,128)(2,1)S(1)} %collective-permute-done.10.refs_0_, f32[64,1536]{1,0:T(8,128)S(1)} %get-tuple-element.49.refs_1_, f32[64,1536]{1,0:T(8,128)S(1)} %get-tuple-element.50.refs_2_, f32[64,1536]{1,0:T(8,128)S(1)} %get-tuple-element.51.refs_3_, f32[64,128]{1,0:T(8,128)S(1)} %get-tuple-element.52.refs_4_, ...), custom_call_target="tpu_custom_call" | custom-call | flops 471859200 | bytes 3145728 | tf_op jit(solution)/shard_map/stack_store/pallas_call | solution.py:341
  (5 shorter events, 0.1 us)
Async XLA Ops:
  0.0 21.7 %copy-start = (bf16[3072,256]{1,0:T(8,128)(2,1)S(1)}, bf16[3072,256]{1,0:T(8,128)(2,1)}, u32[]{:S(2)}) copy-start(bf16[3072,256]{1,0:T(8,128)(2,1)} %constant.2.clone.refs_5_.refs_9_) | copy-start | bytes 4718596
  2.1 11.7 %collective-permute-start.4 = (bf16[32,3072]{1,0:T(8,128)(2,1)S(1)}, bf16[32,3072]{1,0:T(8,128)(2,1)S(1)}, u32[]{:S(2)}, u32[]{:S(2)}) collective-permute-start(bf16[32,3072]{1,0:T(8,128)(2,1)S(1)} %get-tuple-element.42), channel_id=1, source_target_pairs={{0,3},{1,2},{2,1},{3,0},{4,7},{5,6},{6,5},{7,4},{8,11},{9,10},{10,... | collective-permute-start | bytes 589832 | tf_op jit(solution)/shard_map/ppermute | solution.py:356
  6.0 1.2 %collective-permute-start = (bf16[16,1536]{1,0:T(8,128)(2,1)S(1)}, bf16[16,1536]{1,0:T(8,128)(2,1)S(1)}, u32[]{:S(2)}, u32[]{:S(2)}) collective-permute-start(bf16[16,1536]{1,0:T(8,128)(2,1)S(1)} %get-tuple-element.38), channel_id=1, source_target_pairs={{0,4},{4,0},{8,12},{12,8},{16,20},{20,16},{24,28},{28,24},{1,5},{5... | collective-permute-start | bytes 147464 | tf_op jit(solution)/shard_map/ppermute | solution.py:356
  7.3 6.0 %collective-permute-start.3 = (bf16[16,1536]{1,0:T(8,128)(2,1)S(1)}, bf16[16,1536]{1,0:T(8,128)(2,1)S(1)}, u32[]{:S(2)}, u32[]{:S(2)}) collective-permute-start(bf16[16,1536]{1,0:T(8,128)(2,1)S(1)} %add.12), channel_id=1, source_target_pairs={{0,24},{4,28},{8,16},{12,20},{16,8},{20,12},{24,0},{28,4},{1,25},{... | collective-permute-start | bytes 147464 | tf_op jit(solution)/shard_map/ppermute | solution.py:356
  11.0 5.0 %collective-permute-start.2 = (bf16[16,1536]{1,0:T(8,128)(2,1)S(1)}, bf16[16,1536]{1,0:T(8,128)(2,1)S(1)}, u32[]{:S(2)}, u32[]{:S(2)}) collective-permute-start(bf16[16,1536]{1,0:T(8,128)(2,1)S(1)} %add.12), channel_id=1, source_target_pairs={{0,16},{4,20},{8,24},{12,28},{16,0},{20,4},{24,8},{28,12},{1,17},{... | collective-permute-start | bytes 147464 | tf_op jit(solution)/shard_map/ppermute | solution.py:356
  11.0 5.0 %collective-permute-start.1 = (bf16[16,1536]{1,0:T(8,128)(2,1)S(1)}, bf16[16,1536]{1,0:T(8,128)(2,1)S(1)}, u32[]{:S(2)}, u32[]{:S(2)}) collective-permute-start(bf16[16,1536]{1,0:T(8,128)(2,1)S(1)} %add.12), channel_id=1, source_target_pairs={{0,8},{4,12},{8,0},{12,4},{16,24},{20,28},{24,16},{28,20},{1,9},{5... | collective-permute-start | bytes 147464 | tf_op jit(solution)/shard_map/ppermute | solution.py:356
  11.8 8.3 %collective-permute-start.6 = (bf16[32,3072]{1,0:T(8,128)(2,1)S(1)}, bf16[32,3072]{1,0:T(8,128)(2,1)S(1)}, u32[]{:S(2)}, u32[]{:S(2)}) collective-permute-start(bf16[32,3072]{1,0:T(8,128)(2,1)S(1)} %get-tuple-element.44), channel_id=1, source_target_pairs={{0,1},{1,0},{2,3},{3,2},{4,5},{5,4},{6,7},{7,6},{8,9},{9,8},{10,11... | collective-permute-start | bytes 589832 | tf_op jit(solution)/shard_map/ppermute | solution.py:356
  13.3 7.0 %collective-permute-start.7 = (bf16[32,3072]{1,0:T(8,128)(2,1)S(1)}, bf16[32,3072]{1,0:T(8,128)(2,1)S(1)}, u32[]{:S(2)}, u32[]{:S(2)}) collective-permute-start(bf16[32,3072]{1,0:T(8,128)(2,1)S(1)} %get-tuple-element.45), channel_id=1, source_target_pairs={{0,2},{1,3},{2,0},{3,1},{4,6},{5,7},{6,4},{7,5},{8,10},{9,11},{10,... | collective-permute-start | bytes 589832 | tf_op jit(solution)/shard_map/ppermute | solution.py:356
  16.0 5.2 %collective-permute-start.5 = (bf16[16,1536]{1,0:T(8,128)(2,1)S(1)}, bf16[16,1536]{1,0:T(8,128)(2,1)S(1)}, u32[]{:S(2)}, u32[]{:S(2)}) collective-permute-start(bf16[16,1536]{1,0:T(8,128)(2,1)S(1)} %add_add_fusion), channel_id=1, source_target_pairs={{0,3},{1,2},{2,1},{3,0},{4,7},{5,6},{6,5},{7,4},{8,11},{9,10},{10,... | collective-permute-start | bytes 147464 | tf_op jit(solution)/shard_map/ppermute | solution.py:356
  16.5 6.5 %collective-permute-start.9 = (bf16[16,1536]{1,0:T(8,128)(2,1)S(1)}, bf16[16,1536]{1,0:T(8,128)(2,1)S(1)}, u32[]{:S(2)}, u32[]{:S(2)}) collective-permute-start(bf16[16,1536]{1,0:T(8,128)(2,1)S(1)} %add_add_fusion), channel_id=1, source_target_pairs={{0,2},{1,3},{2,0},{3,1},{4,6},{5,7},{6,4},{7,5},{8,10},{9,11},{10,... | collective-permute-start | bytes 147464 | tf_op jit(solution)/shard_map/ppermute | solution.py:356
  18.0 5.0 %collective-permute-start.8 = (bf16[16,1536]{1,0:T(8,128)(2,1)S(1)}, bf16[16,1536]{1,0:T(8,128)(2,1)S(1)}, u32[]{:S(2)}, u32[]{:S(2)}) collective-permute-start(bf16[16,1536]{1,0:T(8,128)(2,1)S(1)} %add_add_fusion), channel_id=1, source_target_pairs={{0,1},{1,0},{2,3},{3,2},{4,5},{5,4},{6,7},{7,6},{8,9},{9,8},{10,11... | collective-permute-start | bytes 147464 | tf_op jit(solution)/shard_map/ppermute | solution.py:356
  23.1 1.6 %collective-permute-start.10 = (bf16[64,1536]{1,0:T(8,128)(2,1)S(1)}, bf16[64,1536]{1,0:T(8,128)(2,1)S(1)}, u32[]{:S(2)}, u32[]{:S(2)}) collective-permute-start(bf16[64,1536]{1,0:T(8,128)(2,1)S(1)} %pad_maximum_fusion), channel_id=1, source_target_pairs={{0,4},{4,0},{8,12},{12,8},{16,20},{20,16},{24,28},{28,24},{1,5},{5... | collective-permute-start | bytes 589832 | tf_op jit(solution)/shard_map/ppermute | solution.py:356

commit v18 on v17

--- a/solution.py
+++ b/solution.py
@@ -378,14 +378,14 @@
         own = functools.reduce(jnp.add, parts, own)
         step *= wide
     own = [own] + [swapped(own, "tm", tm_size, place) for place in range(1, tm_size)]
-    own[-1], receivers[1:-1] = lax.optimization_barrier((own[-1], receivers[1:-1]))
     table = jnp.asarray(lag_table(width // 2))
     far = tm_size - 1
     early = tuple(whiten_blocks([receivers[0], receivers[far]]))
+    late = tuple(whiten_blocks(receivers[1:far]))
+    own[far], early, late = lax.optimization_barrier((own[far], early, late))
     sums = stack_stage(
         keep, jnp.concatenate([own[0], own[far]], axis=0), [(0, 0), (0, 1)], [early], table, "sums"
     )
-    late = tuple(whiten_blocks(receivers[1:far]))
     rest, sums, late = lax.optimization_barrier((own[1:far], sums, late))
     slabs = jnp.concatenate([own[0], own[far], *rest], axis=0)
     other = swapped(slabs, "rcv", rcv_size, 1)

time: 27.7 us -> 27.2 us (0.982)
  waiting for transfers between devices: 5.48 us -> 4.96 us
    ppermute x11, waiting for transfers between devices: 5.48 us -> 4.96 us  [swapped(): return lax.ppermute(value, axis, [(i, i ^ step) for i in range(size)])]
where the time goes in v18:
time: 27.2 us; the launch traced here: 27 us
  starting transfers between devices  13.1 us (48%)
  Pallas kernels  8.81 us (32%)
  waiting for transfers between devices  4.96 us (18%)
    ppermute x11, starting transfers between devices, swapped(): return lax.ppermute(value, axis, [(i, i ^ step) for i in range(size)])  13.1 us
    pallas_call x3, Pallas kernels, stack_stage(): pl.pallas_call(functools.partial(stack_kernel, places, (not before, stage...  5.72 us
    ppermute x11, waiting for transfers between devices, swapped(): return lax.ppermute(value, axis, [(i, i ^ step) for i in range(size)])  4.96 us
    pallas_call x1, Pallas kernels, encode(): pl.pallas_call(functools.partial(encode_kernel, segments), out_shape=(sla...  2.08 us
    pallas_call x2, Pallas kernels, whiten_blocks(): pl.pallas_call(functools.partial(whiten_kernel, segments), out_shape=(par...  1.02 us
  transfers between devices with their start and end apart: 11, of which 5 were waited for; matrix products, arithmetic and copies ran while one was open for 0% of the time, Pallas kernels for 14%

profile of v18, /device:TPU:0, one launch (start us, length us, event | category | flops | bytes accessed | tf_op | source)
XLA Modules:
  0.0 27.0 jit_solution(12054583290332533578)
XLA Ops:
  0.0 0.0 copy-start
  0.0 2.1 %encode_and_pick.1 = (bf16[16,1536]{1,0:T(8,128)(2,1)S(1)}, bf16[16,1536]{1,0:T(8,128)(2,1)S(1)}, bf16[32,3072]{1,0:T(8,128)(2,1)S(1)}, bf16[32,3072]{1,0:T(8,12...) custom-call(bf16[128,3072]{1,0:T(8,128)(2,1)} %bitcast.3, s32[1,128]{1,0:T(1,128)} %bitcast.4, ...), custom_call_target="tpu_custom_call" | custom-call | tf_op jit(solution)/shard_map/encode_and_pick/pallas_call | solution.py:287
  2.1 4.0 %collective-permute-start.4 = (bf16[32,3072]{1,0:T(8,128)(2,1)S(1)}, bf16[32,3072]{1,0:T(8,128)(2,1)S(1)}, u32[]{:S(2)}, u32[]{:S(2)}) collective-permute-start(bf16[32,3072]{1,0:T(8,128)(2,1)S(1)} %get-tuple-element.48), channel_id=1, source_target_pairs={{0,3},{1,2},{2,1},{3,0},{4,7},{5,6},{6,5},{7,4},{8,11},{9,10},{10,... | collective-permute-start | bytes 589832 | tf_op jit(solution)/shard_map/ppermute | solution.py:356
  6.0 0.0 collective-permute-start
  6.1 1.2 %collective-permute-done = bf16[16,1536]{1,0:T(8,128)(2,1)S(1)} collective-permute-done((bf16[16,1536]{1,0:T(8,128)(2,1)S(1)}, bf16[16,1536]{1,0:T(8,128)(2,1)S(1)}, u32[]{:S(2)}, u32[]{:S(2)}) %collective-permute-start) | collective-permute-done | bytes 49184 | tf_op jit(solution)/shard_map/ppermute | solution.py:356
  7.3 3.7 %collective-permute-start.3 = (bf16[16,1536]{1,0:T(8,128)(2,1)S(1)}, bf16[16,1536]{1,0:T(8,128)(2,1)S(1)}, u32[]{:S(2)}, u32[]{:S(2)}) collective-permute-start(bf16[16,1536]{1,0:T(8,128)(2,1)S(1)} %add.12), channel_id=1, source_target_pairs={{0,24},{4,28},{8,16},{12,20},{16,8},{20,12},{24,0},{28,4},{1,25},{... | collective-permute-start | bytes 147464 | tf_op jit(solution)/shard_map/ppermute | solution.py:356
  11.0 0.0 collective-permute-start.2
  11.0 0.8 %collective-permute-start.1 = (bf16[16,1536]{1,0:T(8,128)(2,1)S(1)}, bf16[16,1536]{1,0:T(8,128)(2,1)S(1)}, u32[]{:S(2)}, u32[]{:S(2)}) collective-permute-start(bf16[16,1536]{1,0:T(8,128)(2,1)S(1)} %add.12), channel_id=1, source_target_pairs={{0,8},{4,12},{8,0},{12,4},{16,24},{20,28},{24,16},{28,20},{1,9},{5... | collective-permute-start | bytes 147464 | tf_op jit(solution)/shard_map/ppermute | solution.py:356
  11.8 0.5 %collective-permute-start.6 = (bf16[32,3072]{1,0:T(8,128)(2,1)S(1)}, bf16[32,3072]{1,0:T(8,128)(2,1)S(1)}, u32[]{:S(2)}, u32[]{:S(2)}) collective-permute-start(bf16[32,3072]{1,0:T(8,128)(2,1)S(1)} %get-tuple-element.56), channel_id=1, source_target_pairs={{0,1},{1,0},{2,3},{3,2},{4,5},{5,4},{6,7},{7,6},{8,9},{9,8},{10,11... | collective-permute-start | bytes 589832 | tf_op jit(solution)/shard_map/ppermute | solution.py:356
  12.3 1.0 %collective-permute-done.3 = bf16[16,1536]{1,0:T(8,128)(2,1)S(1)} collective-permute-done((bf16[16,1536]{1,0:T(8,128)(2,1)S(1)}, bf16[16,1536]{1,0:T(8,128)(2,1)S(1)}, u32[]{:S(2)}, u32[]{:S(2)}) %collective-permute-start.3) | collective-permute-done | bytes 49184 | tf_op jit(solution)/shard_map/ppermute | solution.py:356
  13.3 0.5 %collective-permute-start.7 = (bf16[32,3072]{1,0:T(8,128)(2,1)S(1)}, bf16[32,3072]{1,0:T(8,128)(2,1)S(1)}, u32[]{:S(2)}, u32[]{:S(2)}) collective-permute-start(bf16[32,3072]{1,0:T(8,128)(2,1)S(1)} %get-tuple-element.57), channel_id=1, source_target_pairs={{0,2},{1,3},{2,0},{3,1},{4,6},{5,7},{6,4},{7,5},{8,10},{9,11},{10,... | collective-permute-start | bytes 589832 | tf_op jit(solution)/shard_map/ppermute | solution.py:356
  13.8 0.0 collective-permute-done.4.refs_1_
  13.8 2.1 %collective-permute-done.2 = bf16[16,1536]{1,0:T(8,128)(2,1)S(1)} collective-permute-done((bf16[16,1536]{1,0:T(8,128)(2,1)S(1)}, bf16[16,1536]{1,0:T(8,128)(2,1)S(1)}, u32[]{:S(2)}, u32[]{:S(2)}) %collective-permute-start.2) | collective-permute-done | bytes 49184 | tf_op jit(solution)/shard_map/ppermute | solution.py:356
  16.0 0.0 collective-permute-done.1
  16.0 0.5 %collective-permute-start.5 = (bf16[16,1536]{1,0:T(8,128)(2,1)S(1)}, bf16[16,1536]{1,0:T(8,128)(2,1)S(1)}, u32[]{:S(2)}, u32[]{:S(2)}) collective-permute-start(bf16[16,1536]{1,0:T(8,128)(2,1)S(1)} %add_add_fusion), channel_id=1, source_target_pairs={{0,3},{1,2},{2,1},{3,0},{4,7},{5,6},{6,5},{7,4},{8,11},{9,10},{10,... | collective-permute-start | bytes 147464 | tf_op jit(solution)/shard_map/ppermute | solution.py:356
  16.5 1.5 %collective-permute-start.9 = (bf16[16,1536]{1,0:T(8,128)(2,1)S(1)}, bf16[16,1536]{1,0:T(8,128)(2,1)S(1)}, u32[]{:S(2)}, u32[]{:S(2)}) collective-permute-start(bf16[16,1536]{1,0:T(8,128)(2,1)S(1)} %add_add_fusion), channel_id=1, source_target_pairs={{0,2},{1,3},{2,0},{3,1},{4,6},{5,7},{6,4},{7,5},{8,10},{9,11},{10,... | collective-permute-start | bytes 147464 | tf_op jit(solution)/shard_map/ppermute | solution.py:356
  18.0 1.5 %collective-permute-start.8 = (bf16[16,1536]{1,0:T(8,128)(2,1)S(1)}, bf16[16,1536]{1,0:T(8,128)(2,1)S(1)}, u32[]{:S(2)}, u32[]{:S(2)}) collective-permute-start(bf16[16,1536]{1,0:T(8,128)(2,1)S(1)} %add_add_fusion), channel_id=1, source_target_pairs={{0,1},{1,0},{2,3},{3,2},{4,5},{5,4},{6,7},{7,6},{8,9},{9,8},{10,11... | collective-permute-start | bytes 147464 | tf_op jit(solution)/shard_map/ppermute | solution.py:356
  19.5 0.5 %whiten_receivers.2 = (f32[64,1536]{1,0:T(8,128)S(1)}, f32[64,1536]{1,0:T(8,128)S(1)}, f32[64,1536]{1,0:T(8,128)S(1)}, f32[64,128]{1,0:T(8,128)S(1)}) custom-call(bf16[32,3072]{1,0:T(8,128)(2,1)S(1)} %get-tuple-element.50.refs_0_, bf16[32,3072]{1,0:T(8,128)(2,1)S(1)} %collective-permute-done.4.refs_1_), custom_call_target="tpu_custom_call" | custom-call | flops 201326592 | bytes 786432 | tf_op jit(solution)/shard_map/whiten_receivers/pallas_call | solution.py:312
  20.0 0.0 collective-permute-done.6.refs_0_
  20.1 0.2 collective-permute-done.7.refs_1_
  20.3 0.5 %whiten_receivers.3 = (f32[64,1536]{1,0:T(8,128)S(1)}, f32[64,1536]{1,0:T(8,128)S(1)}, f32[64,1536]{1,0:T(8,128)S(1)}, f32[64,128]{1,0:T(8,128)S(1)}) custom-call(bf16[32,3072]{1,0:T(8,128)(2,1)S(1)} %collective-permute-done.6.refs_0_, bf16[32,3072]{1,0:T(8,128)(2,1)S(1)} %collective-permute-done.7.refs_1_), custom_call_target="tpu_custom_call" | custom-call | flops 201326592 | bytes 786432 | tf_op jit(solution)/shard_map/whiten_receivers/pallas_call | solution.py:312
  20.8 0.3 %collective-permute-done.5 = bf16[16,1536]{1,0:T(8,128)(2,1)S(1)} collective-permute-done((bf16[16,1536]{1,0:T(8,128)(2,1)S(1)}, bf16[16,1536]{1,0:T(8,128)(2,1)S(1)}, u32[]{:S(2)}, u32[]{:S(2)}) %collective-permute-start.5) | collective-permute-done | bytes 49184 | tf_op jit(solution)/shard_map/ppermute | solution.py:356
  21.1 0.0 copy-done
  21.2 1.4 %stack_sums.1 = (f32[2,256,256]{2,1,0:T(8,128)S(1)}, f32[256,128]{1,0:T(8,128)S(1)}) custom-call(bf16[32,1536]{1,0:T(8,128)(2,1)S(1)} %pad_maximum_fusion.1.refs_0_, f32[64,1536]{1,0:T(8,128)S(1)} %get-tuple-element.63.refs_1_, f32[64,1536]{1,0:T(8,128)S(1)} %get-tuple-element.64.refs_2_, f32[64,1536]{1,0:T(8,128)S(1)} %get-tuple-element.65.refs_3_, ...), custom_call_target="tpu_custom_call" | custom-call | flops 471859200 | bytes 3145728 | tf_op jit(solution)/shard_map/stack_sums/pallas_call | solution.py:341
  22.5 0.0 collective-permute-done.9
  22.5 0.0 collective-permute-done.8
  22.6 0.1 collective-permute-start.10
  22.7 1.5 %stack_result.1.refs_10_ = f32[256,301]{1,0:T(8,128)S(1)} custom-call(bf16[32,1536]{1,0:T(8,128)(2,1)S(1)} %pad_maximum_fusion.2.refs_0_, f32[64,1536]{1,0:T(8,128)S(1)} %get-tuple-element.75.refs_1_.refs_5_, f32[64,1536]{1,0:T(8,128)S(1)} %get-tuple-element.76.refs_2_.refs_6_, f32[64,1536]{1,0:T(8,128)S(1)} %get-tuple-element.77.refs_3_.refs_7_, ...), custom_call_target="tpu_custom_call" | custom-call | flops 471859200 | bytes 3145728 | tf_op jit(solution)/shard_map/stack_result/pallas_call | solution.py:341
  24.1 0.0 collective-permute-done.10.refs_0_
  24.1 2.9 %stack_store.1 = f32[512,301]{1,0:T(8,128)} custom-call(bf16[64,1536]{1,0:T(8,128)(2,1)S(1)} %collective-permute-done.10.refs_0_, f32[64,1536]{1,0:T(8,128)S(1)} %get-tuple-element.63.refs_1_, f32[64,1536]{1,0:T(8,128)S(1)} %get-tuple-element.64.refs_2_, f32[64,1536]{1,0:T(8,128)S(1)} %get-tuple-element.65.refs_3_, f32[64,128]{1,0:T(8,128)S(1)} %get-tuple-element.66.refs_4_, ...), custom_call_target="tpu_custom_call" | custom-call | flops 471859200 | bytes 3145728 | tf_op jit(solution)/shard_map/stack_store/pallas_call | solution.py:341
  (5 shorter events, 0.1 us)
Async XLA Ops:
  0.0 21.1 %copy-start = (bf16[3072,256]{1,0:T(8,128)(2,1)S(1)}, bf16[3072,256]{1,0:T(8,128)(2,1)}, u32[]{:S(2)}) copy-start(bf16[3072,256]{1,0:T(8,128)(2,1)} %constant.2.clone.refs_5_.refs_9_) | copy-start | bytes 4718596
  2.1 11.7 %collective-permute-start.4 = (bf16[32,3072]{1,0:T(8,128)(2,1)S(1)}, bf16[32,3072]{1,0:T(8,128)(2,1)S(1)}, u32[]{:S(2)}, u32[]{:S(2)}) collective-permute-start(bf16[32,3072]{1,0:T(8,128)(2,1)S(1)} %get-tuple-element.48), channel_id=1, source_target_pairs={{0,3},{1,2},{2,1},{3,0},{4,7},{5,6},{6,5},{7,4},{8,11},{9,10},{10,... | collective-permute-start | bytes 589832 | tf_op jit(solution)/shard_map/ppermute | solution.py:356
  6.0 1.2 %collective-permute-start = (bf16[16,1536]{1,0:T(8,128)(2,1)S(1)}, bf16[16,1536]{1,0:T(8,128)(2,1)S(1)}, u32[]{:S(2)}, u32[]{:S(2)}) collective-permute-start(bf16[16,1536]{1,0:T(8,128)(2,1)S(1)} %get-tuple-element.44), channel_id=1, source_target_pairs={{0,4},{4,0},{8,12},{12,8},{16,20},{20,16},{24,28},{28,24},{1,5},{5... | collective-permute-start | bytes 147464 | tf_op jit(solution)/shard_map/ppermute | solution.py:356
  7.3 6.0 %collective-permute-start.3 = (bf16[16,1536]{1,0:T(8,128)(2,1)S(1)}, bf16[16,1536]{1,0:T(8,128)(2,1)S(1)}, u32[]{:S(2)}, u32[]{:S(2)}) collective-permute-start(bf16[16,1536]{1,0:T(8,128)(2,1)S(1)} %add.12), channel_id=1, source_target_pairs={{0,24},{4,28},{8,16},{12,20},{16,8},{20,12},{24,0},{28,4},{1,25},{... | collective-permute-start | bytes 147464 | tf_op jit(solution)/shard_map/ppermute | solution.py:356
  11.0 5.0 %collective-permute-start.2 = (bf16[16,1536]{1,0:T(8,128)(2,1)S(1)}, bf16[16,1536]{1,0:T(8,128)(2,1)S(1)}, u32[]{:S(2)}, u32[]{:S(2)}) collective-permute-start(bf16[16,1536]{1,0:T(8,128)(2,1)S(1)} %add.12), channel_id=1, source_target_pairs={{0,16},{4,20},{8,24},{12,28},{16,0},{20,4},{24,8},{28,12},{1,17},{... | collective-permute-start | bytes 147464 | tf_op jit(solution)/shard_map/ppermute | solution.py:356
  11.0 5.0 %collective-permute-start.1 = (bf16[16,1536]{1,0:T(8,128)(2,1)S(1)}, bf16[16,1536]{1,0:T(8,128)(2,1)S(1)}, u32[]{:S(2)}, u32[]{:S(2)}) collective-permute-start(bf16[16,1536]{1,0:T(8,128)(2,1)S(1)} %add.12), channel_id=1, source_target_pairs={{0,8},{4,12},{8,0},{12,4},{16,24},{20,28},{24,16},{28,20},{1,9},{5... | collective-permute-start | bytes 147464 | tf_op jit(solution)/shard_map/ppermute | solution.py:356
  11.8 8.3 %collective-permute-start.6 = (bf16[32,3072]{1,0:T(8,128)(2,1)S(1)}, bf16[32,3072]{1,0:T(8,128)(2,1)S(1)}, u32[]{:S(2)}, u32[]{:S(2)}) collective-permute-start(bf16[32,3072]{1,0:T(8,128)(2,1)S(1)} %get-tuple-element.56), channel_id=1, source_target_pairs={{0,1},{1,0},{2,3},{3,2},{4,5},{5,4},{6,7},{7,6},{8,9},{9,8},{10,11... | collective-permute-start | bytes 589832 | tf_op jit(solution)/shard_map/ppermute | solution.py:356
  13.3 7.0 %collective-permute-start.7 = (bf16[32,3072]{1,0:T(8,128)(2,1)S(1)}, bf16[32,3072]{1,0:T(8,128)(2,1)S(1)}, u32[]{:S(2)}, u32[]{:S(2)}) collective-permute-start(bf16[32,3072]{1,0:T(8,128)(2,1)S(1)} %get-tuple-element.57), channel_id=1, source_target_pairs={{0,2},{1,3},{2,0},{3,1},{4,6},{5,7},{6,4},{7,5},{8,10},{9,11},{10,... | collective-permute-start | bytes 589832 | tf_op jit(solution)/shard_map/ppermute | solution.py:356
  16.0 5.2 %collective-permute-start.5 = (bf16[16,1536]{1,0:T(8,128)(2,1)S(1)}, bf16[16,1536]{1,0:T(8,128)(2,1)S(1)}, u32[]{:S(2)}, u32[]{:S(2)}) collective-permute-start(bf16[16,1536]{1,0:T(8,128)(2,1)S(1)} %add_add_fusion), channel_id=1, source_target_pairs={{0,3},{1,2},{2,1},{3,0},{4,7},{5,6},{6,5},{7,4},{8,11},{9,10},{10,... | collective-permute-start | bytes 147464 | tf_op jit(solution)/shard_map/ppermute | solution.py:356
  16.5 6.0 %collective-permute-start.9 = (bf16[16,1536]{1,0:T(8,128)(2,1)S(1)}, bf16[16,1536]{1,0:T(8,128)(2,1)S(1)}, u32[]{:S(2)}, u32[]{:S(2)}) collective-permute-start(bf16[16,1536]{1,0:T(8,128)(2,1)S(1)} %add_add_fusion), channel_id=1, source_target_pairs={{0,2},{1,3},{2,0},{3,1},{4,6},{5,7},{6,4},{7,5},{8,10},{9,11},{10,... | collective-permute-start | bytes 147464 | tf_op jit(solution)/shard_map/ppermute | solution.py:356
  18.0 4.5 %collective-permute-start.8 = (bf16[16,1536]{1,0:T(8,128)(2,1)S(1)}, bf16[16,1536]{1,0:T(8,128)(2,1)S(1)}, u32[]{:S(2)}, u32[]{:S(2)}) collective-permute-start(bf16[16,1536]{1,0:T(8,128)(2,1)S(1)} %add_add_fusion), channel_id=1, source_target_pairs={{0,1},{1,0},{2,3},{3,2},{4,5},{5,4},{6,7},{7,6},{8,9},{9,8},{10,11... | collective-permute-start | bytes 147464 | tf_op jit(solution)/shard_map/ppermute | solution.py:356
  22.6 1.6 %collective-permute-start.10 = (bf16[64,1536]{1,0:T(8,128)(2,1)S(1)}, bf16[64,1536]{1,0:T(8,128)(2,1)S(1)}, u32[]{:S(2)}, u32[]{:S(2)}) collective-permute-start(bf16[64,1536]{1,0:T(8,128)(2,1)S(1)} %pad_maximum_fusion), channel_id=1, source_target_pairs={{0,4},{4,0},{8,12},{12,8},{16,20},{20,16},{24,28},{28,24},{1,5},{5... | collective-permute-start | bytes 589832 | tf_op jit(solution)/shard_map/ppermute | solution.py:356

commit v19 on v18

--- a/solution.py
+++ b/solution.py
@@ -375,14 +375,15 @@
         parts = [swapped(own, "rcv", rcv_size, place * step) for place in range(1, wide)]
         if step == 2:
             parts[-1], receivers[-1] = lax.optimization_barrier((parts[-1], receivers[-1]))
+            early = tuple(whiten_blocks([receivers[0], receivers[-1]]))
+            parts[-2:-1], early = lax.optimization_barrier((parts[-2:-1], early))
         own = functools.reduce(jnp.add, parts, own)
         step *= wide
     own = [own] + [swapped(own, "tm", tm_size, place) for place in range(1, tm_size)]
     table = jnp.asarray(lag_table(width // 2))
     far = tm_size - 1
-    early = tuple(whiten_blocks([receivers[0], receivers[far]]))
     late = tuple(whiten_blocks(receivers[1:far]))
-    own[far], early, late = lax.optimization_barrier((own[far], early, late))
+    own[far], late = lax.optimization_barrier((own[far], late))
     sums = stack_stage(
         keep, jnp.concatenate([own[0], own[far]], axis=0), [(0, 0), (0, 1)], [early], table, "sums"
     )

time: 27.2 us -> 27.2 us (level)
  no operation moved by 1% of the time
where the time goes in v19:
time: 27.2 us; the launch traced here: 27 us
  starting transfers between devices  13.1 us (48%)
  Pallas kernels  8.81 us (32%)
  waiting for transfers between devices  4.97 us (18%)
    ppermute x11, starting transfers between devices, swapped(): return lax.ppermute(value, axis, [(i, i ^ step) for i in range(size)])  13.1 us
    pallas_call x3, Pallas kernels, stack_stage(): pl.pallas_call(functools.partial(stack_kernel, places, (not before, stage...  5.72 us
    ppermute x11, waiting for transfers between devices, swapped(): return lax.ppermute(value, axis, [(i, i ^ step) for i in range(size)])  4.97 us
    pallas_call x1, Pallas kernels, encode(): pl.pallas_call(functools.partial(encode_kernel, segments), out_shape=(sla...  2.08 us
    pallas_call x2, Pallas kernels, whiten_blocks(): pl.pallas_call(functools.partial(whiten_kernel, segments), out_shape=(par...  1.02 us
  transfers between devices with their start and end apart: 11, of which 5 were waited for; matrix products, arithmetic and copies ran while one was open for 0% of the time, Pallas kernels for 14%

profile of v19, /device:TPU:0, one launch (start us, length us, event | category | flops | bytes accessed | tf_op | source)
XLA Modules:
  0.0 27.0 jit_solution(13492712487494217944)
XLA Ops:
  0.0 0.0 copy-start
  0.0 2.1 %encode_and_pick.1 = (bf16[16,1536]{1,0:T(8,128)(2,1)S(1)}, bf16[16,1536]{1,0:T(8,128)(2,1)S(1)}, bf16[32,3072]{1,0:T(8,128)(2,1)S(1)}, bf16[32,3072]{1,0:T(8,12...) custom-call(bf16[128,3072]{1,0:T(8,128)(2,1)} %bitcast.3, s32[1,128]{1,0:T(1,128)} %bitcast.4, ...), custom_call_target="tpu_custom_call" | custom-call | tf_op jit(solution)/shard_map/encode_and_pick/pallas_call | solution.py:287
  2.1 4.0 %collective-permute-start.4 = (bf16[32,3072]{1,0:T(8,128)(2,1)S(1)}, bf16[32,3072]{1,0:T(8,128)(2,1)S(1)}, u32[]{:S(2)}, u32[]{:S(2)}) collective-permute-start(bf16[32,3072]{1,0:T(8,128)(2,1)S(1)} %get-tuple-element.50), channel_id=1, source_target_pairs={{0,3},{1,2},{2,1},{3,0},{4,7},{5,6},{6,5},{7,4},{8,11},{9,10},{10,... | collective-permute-start | bytes 589832 | tf_op jit(solution)/shard_map/ppermute | solution.py:356
  6.0 0.0 collective-permute-start
  6.1 1.2 %collective-permute-done = bf16[16,1536]{1,0:T(8,128)(2,1)S(1)} collective-permute-done((bf16[16,1536]{1,0:T(8,128)(2,1)S(1)}, bf16[16,1536]{1,0:T(8,128)(2,1)S(1)}, u32[]{:S(2)}, u32[]{:S(2)}) %collective-permute-start) | collective-permute-done | bytes 49184 | tf_op jit(solution)/shard_map/ppermute | solution.py:356
  7.3 3.7 %collective-permute-start.3 = (bf16[16,1536]{1,0:T(8,128)(2,1)S(1)}, bf16[16,1536]{1,0:T(8,128)(2,1)S(1)}, u32[]{:S(2)}, u32[]{:S(2)}) collective-permute-start(bf16[16,1536]{1,0:T(8,128)(2,1)S(1)} %add.12), channel_id=1, source_target_pairs={{0,24},{4,28},{8,16},{12,20},{16,8},{20,12},{24,0},{28,4},{1,25},{... | collective-permute-start | bytes 147464 | tf_op jit(solution)/shard_map/ppermute | solution.py:356
  11.0 0.0 collective-permute-start.2
  11.0 0.8 %collective-permute-start.1 = (bf16[16,1536]{1,0:T(8,128)(2,1)S(1)}, bf16[16,1536]{1,0:T(8,128)(2,1)S(1)}, u32[]{:S(2)}, u32[]{:S(2)}) collective-permute-start(bf16[16,1536]{1,0:T(8,128)(2,1)S(1)} %add.12), channel_id=1, source_target_pairs={{0,8},{4,12},{8,0},{12,4},{16,24},{20,28},{24,16},{28,20},{1,9},{5... | collective-permute-start | bytes 147464 | tf_op jit(solution)/shard_map/ppermute | solution.py:356
  11.8 0.5 %collective-permute-start.6 = (bf16[32,3072]{1,0:T(8,128)(2,1)S(1)}, bf16[32,3072]{1,0:T(8,128)(2,1)S(1)}, u32[]{:S(2)}, u32[]{:S(2)}) collective-permute-start(bf16[32,3072]{1,0:T(8,128)(2,1)S(1)} %get-tuple-element.58), channel_id=1, source_target_pairs={{0,1},{1,0},{2,3},{3,2},{4,5},{5,4},{6,7},{7,6},{8,9},{9,8},{10,11... | collective-permute-start | bytes 589832 | tf_op jit(solution)/shard_map/ppermute | solution.py:356
  12.3 1.0 %collective-permute-done.3 = bf16[16,1536]{1,0:T(8,128)(2,1)S(1)} collective-permute-done((bf16[16,1536]{1,0:T(8,128)(2,1)S(1)}, bf16[16,1536]{1,0:T(8,128)(2,1)S(1)}, u32[]{:S(2)}, u32[]{:S(2)}) %collective-permute-start.3) | collective-permute-done | bytes 49184 | tf_op jit(solution)/shard_map/ppermute | solution.py:356
  13.3 0.5 %collective-permute-start.7 = (bf16[32,3072]{1,0:T(8,128)(2,1)S(1)}, bf16[32,3072]{1,0:T(8,128)(2,1)S(1)}, u32[]{:S(2)}, u32[]{:S(2)}) collective-permute-start(bf16[32,3072]{1,0:T(8,128)(2,1)S(1)} %get-tuple-element.59), channel_id=1, source_target_pairs={{0,2},{1,3},{2,0},{3,1},{4,6},{5,7},{6,4},{7,5},{8,10},{9,11},{10,... | collective-permute-start | bytes 589832 | tf_op jit(solution)/shard_map/ppermute | solution.py:356
  13.8 0.0 collective-permute-done.4.refs_1_
  13.8 0.5 %whiten_receivers.2 = (f32[64,1536]{1,0:T(8,128)S(1)}, f32[64,1536]{1,0:T(8,128)S(1)}, f32[64,1536]{1,0:T(8,128)S(1)}, f32[64,128]{1,0:T(8,128)S(1)}) custom-call(bf16[32,3072]{1,0:T(8,128)(2,1)S(1)} %get-tuple-element.49.refs_0_, bf16[32,3072]{1,0:T(8,128)(2,1)S(1)} %collective-permute-done.4.refs_1_), custom_call_target="tpu_custom_call" | custom-call | flops 201326592 | bytes 786432 | tf_op jit(solution)/shard_map/whiten_receivers/pallas_call | solution.py:312
  14.3 1.6 %collective-permute-done.2 = bf16[16,1536]{1,0:T(8,128)(2,1)S(1)} collective-permute-done((bf16[16,1536]{1,0:T(8,128)(2,1)S(1)}, bf16[16,1536]{1,0:T(8,128)(2,1)S(1)}, u32[]{:S(2)}, u32[]{:S(2)}) %collective-permute-start.2) | collective-permute-done | bytes 49184 | tf_op jit(solution)/shard_map/ppermute | solution.py:356
  16.0 0.0 collective-permute-done.1
  16.0 0.5 %collective-permute-start.5 = (bf16[16,1536]{1,0:T(8,128)(2,1)S(1)}, bf16[16,1536]{1,0:T(8,128)(2,1)S(1)}, u32[]{:S(2)}, u32[]{:S(2)}) collective-permute-start(bf16[16,1536]{1,0:T(8,128)(2,1)S(1)} %add_add_fusion), channel_id=1, source_target_pairs={{0,3},{1,2},{2,1},{3,0},{4,7},{5,6},{6,5},{7,4},{8,11},{9,10},{10,... | collective-permute-start | bytes 147464 | tf_op jit(solution)/shard_map/ppermute | solution.py:356
  16.5 1.5 %collective-permute-start.9 = (bf16[16,1536]{1,0:T(8,128)(2,1)S(1)}, bf16[16,1536]{1,0:T(8,128)(2,1)S(1)}, u32[]{:S(2)}, u32[]{:S(2)}) collective-permute-start(bf16[16,1536]{1,0:T(8,128)(2,1)S(1)} %add_add_fusion), channel_id=1, source_target_pairs={{0,2},{1,3},{2,0},{3,1},{4,6},{5,7},{6,4},{7,5},{8,10},{9,11},{10,... | collective-permute-start | bytes 147464 | tf_op jit(solution)/shard_map/ppermute | solution.py:356
  18.0 1.5 %collective-permute-start.8 = (bf16[16,1536]{1,0:T(8,128)(2,1)S(1)}, bf16[16,1536]{1,0:T(8,128)(2,1)S(1)}, u32[]{:S(2)}, u32[]{:S(2)}) collective-permute-start(bf16[16,1536]{1,0:T(8,128)(2,1)S(1)} %add_add_fusion), channel_id=1, source_target_pairs={{0,1},{1,0},{2,3},{3,2},{4,5},{5,4},{6,7},{7,6},{8,9},{9,8},{10,11... | collective-permute-start | bytes 147464 | tf_op jit(solution)/shard_map/ppermute | solution.py:356
  19.5 0.0 collective-permute-done.6.refs_0_
  19.5 0.8 %collective-permute-done.7.refs_1_ = bf16[32,3072]{1,0:T(8,128)(2,1)S(1)} collective-permute-done((bf16[32,3072]{1,0:T(8,128)(2,1)S(1)}, bf16[32,3072]{1,0:T(8,128)(2,1)S(1)}, u32[]{:S(2)}, u32[]{:S(2)}) %collective-permute-start.7) | collective-permute-done | bytes 196640 | tf_op jit(solution)/shard_map/ppermute | solution.py:356
  20.3 0.5 %whiten_receivers.3 = (f32[64,1536]{1,0:T(8,128)S(1)}, f32[64,1536]{1,0:T(8,128)S(1)}, f32[64,1536]{1,0:T(8,128)S(1)}, f32[64,128]{1,0:T(8,128)S(1)}) custom-call(bf16[32,3072]{1,0:T(8,128)(2,1)S(1)} %collective-permute-done.6.refs_0_, bf16[32,3072]{1,0:T(8,128)(2,1)S(1)} %collective-permute-done.7.refs_1_), custom_call_target="tpu_custom_call" | custom-call | flops 201326592 | bytes 786432 | tf_op jit(solution)/shard_map/whiten_receivers/pallas_call | solution.py:312
  20.8 0.3 %collective-permute-done.5 = bf16[16,1536]{1,0:T(8,128)(2,1)S(1)} collective-permute-done((bf16[16,1536]{1,0:T(8,128)(2,1)S(1)}, bf16[16,1536]{1,0:T(8,128)(2,1)S(1)}, u32[]{:S(2)}, u32[]{:S(2)}) %collective-permute-start.5) | collective-permute-done | bytes 49184 | tf_op jit(solution)/shard_map/ppermute | solution.py:356
  21.1 0.0 copy-done
  21.2 1.4 %stack_sums.1 = (f32[2,256,256]{2,1,0:T(8,128)S(1)}, f32[256,128]{1,0:T(8,128)S(1)}) custom-call(bf16[32,1536]{1,0:T(8,128)(2,1)S(1)} %pad_maximum_fusion.1.refs_0_, f32[64,1536]{1,0:T(8,128)S(1)} %get-tuple-element.65.refs_1_, f32[64,1536]{1,0:T(8,128)S(1)} %get-tuple-element.66.refs_2_, f32[64,1536]{1,0:T(8,128)S(1)} %get-tuple-element.67.refs_3_, ...), custom_call_target="tpu_custom_call" | custom-call | flops 471859200 | bytes 3145728 | tf_op jit(solution)/shard_map/stack_sums/pallas_call | solution.py:341
  22.5 0.0 collective-permute-done.9
  22.5 0.0 collective-permute-done.8
  22.6 0.1 collective-permute-start.10
  22.7 1.5 %stack_result.1.refs_10_ = f32[256,301]{1,0:T(8,128)S(1)} custom-call(bf16[32,1536]{1,0:T(8,128)(2,1)S(1)} %pad_maximum_fusion.2.refs_0_, f32[64,1536]{1,0:T(8,128)S(1)} %get-tuple-element.77.refs_1_.refs_5_, f32[64,1536]{1,0:T(8,128)S(1)} %get-tuple-element.78.refs_2_.refs_6_, f32[64,1536]{1,0:T(8,128)S(1)} %get-tuple-element.79.refs_3_.refs_7_, ...), custom_call_target="tpu_custom_call" | custom-call | flops 471859200 | bytes 3145728 | tf_op jit(solution)/shard_map/stack_result/pallas_call | solution.py:341
  24.1 0.0 collective-permute-done.10.refs_0_
  24.1 2.9 %stack_store.1 = f32[512,301]{1,0:T(8,128)} custom-call(bf16[64,1536]{1,0:T(8,128)(2,1)S(1)} %collective-permute-done.10.refs_0_, f32[64,1536]{1,0:T(8,128)S(1)} %get-tuple-element.65.refs_1_, f32[64,1536]{1,0:T(8,128)S(1)} %get-tuple-element.66.refs_2_, f32[64,1536]{1,0:T(8,128)S(1)} %get-tuple-element.67.refs_3_, f32[64,128]{1,0:T(8,128)S(1)} %get-tuple-element.68.refs_4_, ...), custom_call_target="tpu_custom_call" | custom-call | flops 471859200 | bytes 3145728 | tf_op jit(solution)/shard_map/stack_store/pallas_call | solution.py:341
  (5 shorter events, 0.1 us)
Async XLA Ops:
  0.0 21.1 %copy-start = (bf16[3072,256]{1,0:T(8,128)(2,1)S(1)}, bf16[3072,256]{1,0:T(8,128)(2,1)}, u32[]{:S(2)}) copy-start(bf16[3072,256]{1,0:T(8,128)(2,1)} %constant.2.clone.refs_5_.refs_9_) | copy-start | bytes 4718596
  2.1 11.7 %collective-permute-start.4 = (bf16[32,3072]{1,0:T(8,128)(2,1)S(1)}, bf16[32,3072]{1,0:T(8,128)(2,1)S(1)}, u32[]{:S(2)}, u32[]{:S(2)}) collective-permute-start(bf16[32,3072]{1,0:T(8,128)(2,1)S(1)} %get-tuple-element.50), channel_id=1, source_target_pairs={{0,3},{1,2},{2,1},{3,0},{4,7},{5,6},{6,5},{7,4},{8,11},{9,10},{10,... | collective-permute-start | bytes 589832 | tf_op jit(solution)/shard_map/ppermute | solution.py:356
  6.0 1.2 %collective-permute-start = (bf16[16,1536]{1,0:T(8,128)(2,1)S(1)}, bf16[16,1536]{1,0:T(8,128)(2,1)S(1)}, u32[]{:S(2)}, u32[]{:S(2)}) collective-permute-start(bf16[16,1536]{1,0:T(8,128)(2,1)S(1)} %get-tuple-element.45), channel_id=1, source_target_pairs={{0,4},{4,0},{8,12},{12,8},{16,20},{20,16},{24,28},{28,24},{1,5},{5... | collective-permute-start | bytes 147464 | tf_op jit(solution)/shard_map/ppermute | solution.py:356
  7.3 6.0 %collective-permute-start.3 = (bf16[16,1536]{1,0:T(8,128)(2,1)S(1)}, bf16[16,1536]{1,0:T(8,128)(2,1)S(1)}, u32[]{:S(2)}, u32[]{:S(2)}) collective-permute-start(bf16[16,1536]{1,0:T(8,128)(2,1)S(1)} %add.12), channel_id=1, source_target_pairs={{0,24},{4,28},{8,16},{12,20},{16,8},{20,12},{24,0},{28,4},{1,25},{... | collective-permute-start | bytes 147464 | tf_op jit(solution)/shard_map/ppermute | solution.py:356
  11.0 5.0 %collective-permute-start.2 = (bf16[16,1536]{1,0:T(8,128)(2,1)S(1)}, bf16[16,1536]{1,0:T(8,128)(2,1)S(1)}, u32[]{:S(2)}, u32[]{:S(2)}) collective-permute-start(bf16[16,1536]{1,0:T(8,128)(2,1)S(1)} %add.12), channel_id=1, source_target_pairs={{0,16},{4,20},{8,24},{12,28},{16,0},{20,4},{24,8},{28,12},{1,17},{... | collective-permute-start | bytes 147464 | tf_op jit(solution)/shard_map/ppermute | solution.py:356
  11.0 5.0 %collective-permute-start.1 = (bf16[16,1536]{1,0:T(8,128)(2,1)S(1)}, bf16[16,1536]{1,0:T(8,128)(2,1)S(1)}, u32[]{:S(2)}, u32[]{:S(2)}) collective-permute-start(bf16[16,1536]{1,0:T(8,128)(2,1)S(1)} %add.12), channel_id=1, source_target_pairs={{0,8},{4,12},{8,0},{12,4},{16,24},{20,28},{24,16},{28,20},{1,9},{5... | collective-permute-start | bytes 147464 | tf_op jit(solution)/shard_map/ppermute | solution.py:356
  11.8 7.8 %collective-permute-start.6 = (bf16[32,3072]{1,0:T(8,128)(2,1)S(1)}, bf16[32,3072]{1,0:T(8,128)(2,1)S(1)}, u32[]{:S(2)}, u32[]{:S(2)}) collective-permute-start(bf16[32,3072]{1,0:T(8,128)(2,1)S(1)} %get-tuple-element.58), channel_id=1, source_target_pairs={{0,1},{1,0},{2,3},{3,2},{4,5},{5,4},{6,7},{7,6},{8,9},{9,8},{10,11... | collective-permute-start | bytes 589832 | tf_op jit(solution)/shard_map/ppermute | solution.py:356
  13.3 7.0 %collective-permute-start.7 = (bf16[32,3072]{1,0:T(8,128)(2,1)S(1)}, bf16[32,3072]{1,0:T(8,128)(2,1)S(1)}, u32[]{:S(2)}, u32[]{:S(2)}) collective-permute-start(bf16[32,3072]{1,0:T(8,128)(2,1)S(1)} %get-tuple-element.59), channel_id=1, source_target_pairs={{0,2},{1,3},{2,0},{3,1},{4,6},{5,7},{6,4},{7,5},{8,10},{9,11},{10,... | collective-permute-start | bytes 589832 | tf_op jit(solution)/shard_map/ppermute | solution.py:356
  16.0 5.2 %collective-permute-start.5 = (bf16[16,1536]{1,0:T(8,128)(2,1)S(1)}, bf16[16,1536]{1,0:T(8,128)(2,1)S(1)}, u32[]{:S(2)}, u32[]{:S(2)}) collective-permute-start(bf16[16,1536]{1,0:T(8,128)(2,1)S(1)} %add_add_fusion), channel_id=1, source_target_pairs={{0,3},{1,2},{2,1},{3,0},{4,7},{5,6},{6,5},{7,4},{8,11},{9,10},{10,... | collective-permute-start | bytes 147464 | tf_op jit(solution)/shard_map/ppermute | solution.py:356
  16.5 6.0 %collective-permute-start.9 = (bf16[16,1536]{1,0:T(8,128)(2,1)S(1)}, bf16[16,1536]{1,0:T(8,128)(2,1)S(1)}, u32[]{:S(2)}, u32[]{:S(2)}) collective-permute-start(bf16[16,1536]{1,0:T(8,128)(2,1)S(1)} %add_add_fusion), channel_id=1, source_target_pairs={{0,2},{1,3},{2,0},{3,1},{4,6},{5,7},{6,4},{7,5},{8,10},{9,11},{10,... | collective-permute-start | bytes 147464 | tf_op jit(solution)/shard_map/ppermute | solution.py:356
  18.0 4.5 %collective-permute-start.8 = (bf16[16,1536]{1,0:T(8,128)(2,1)S(1)}, bf16[16,1536]{1,0:T(8,128)(2,1)S(1)}, u32[]{:S(2)}, u32[]{:S(2)}) collective-permute-start(bf16[16,1536]{1,0:T(8,128)(2,1)S(1)} %add_add_fusion), channel_id=1, source_target_pairs={{0,1},{1,0},{2,3},{3,2},{4,5},{5,4},{6,7},{7,6},{8,9},{9,8},{10,11... | collective-permute-start | bytes 147464 | tf_op jit(solution)/shard_map/ppermute | solution.py:356
  22.6 1.6 %collective-permute-start.10 = (bf16[64,1536]{1,0:T(8,128)(2,1)S(1)}, bf16[64,1536]{1,0:T(8,128)(2,1)S(1)}, u32[]{:S(2)}, u32[]{:S(2)}) collective-permute-start(bf16[64,1536]{1,0:T(8,128)(2,1)S(1)} %pad_maximum_fusion), channel_id=1, source_target_pairs={{0,4},{4,0},{8,12},{12,8},{16,20},{20,16},{24,28},{28,24},{1,5},{5... | collective-permute-start | bytes 589832 | tf_op jit(solution)/shard_map/ppermute | solution.py:356

commit v20 on v19

--- a/solution.py
+++ b/solution.py
@@ -364,9 +364,10 @@
         tm_size, spectra[:, 0, :], valid.reshape(1, channels), sources
     )
     receivers[-1] = swapped(receivers[-1], "tm", tm_size, tm_size - 1)
+    receivers[-2] = swapped(receivers[-2], "tm", tm_size, tm_size - 2)
     own = own + swapped(other, "rcv", rcv_size, 1)
-    own, later = lax.optimization_barrier((own, receivers[1:-1]))
-    receivers[1:-1] = [
+    own, later = lax.optimization_barrier((own, receivers[1:-2]))
+    receivers[1:-2] = [
         swapped(block, "tm", tm_size, place) for place, block in enumerate(later, 1)
     ]
     step = 2
@@ -374,15 +375,15 @@
         wide = min(4, rcv_size // step)
         parts = [swapped(own, "rcv", rcv_size, place * step) for place in range(1, wide)]
         if step == 2:
-            parts[-1], receivers[-1] = lax.optimization_barrier((parts[-1], receivers[-1]))
-            early = tuple(whiten_blocks([receivers[0], receivers[-1]]))
+            parts[-1], receivers[-2:] = lax.optimization_barrier((parts[-1], receivers[-2:]))
+            early = tuple(whiten_blocks([receivers[0], receivers[-1], receivers[-2]]))
             parts[-2:-1], early = lax.optimization_barrier((parts[-2:-1], early))
         own = functools.reduce(jnp.add, parts, own)
         step *= wide
     own = [own] + [swapped(own, "tm", tm_size, place) for place in range(1, tm_size)]
     table = jnp.asarray(lag_table(width // 2))
     far = tm_size - 1
-    late = tuple(whiten_blocks(receivers[1:far]))
+    late = tuple(whiten_blocks(receivers[1:-2]))
     own[far], late = lax.optimization_barrier((own[far], late))
     sums = stack_stage(
         keep, jnp.concatenate([own[0], own[far]], axis=0), [(0, 0), (0, 1)], [early], table, "sums"
@@ -390,11 +391,11 @@
     rest, sums, late = lax.optimization_barrier((own[1:far], sums, late))
     slabs = jnp.concatenate([own[0], own[far], *rest], axis=0)
     other = swapped(slabs, "rcv", rcv_size, 1)
-    places = [(0, place) for place in range(far - 1)]
+    between = [(1, place) for place in range(far - 2)] + [(0, 2)]
     first = stack_stage(
-        keep, slabs[2 * own[0].shape[0] :], places, [late], table, "result", sums
-    )
-    places = [(0, 0), (0, 1)] + [(1, place) for place in range(far - 1)]
+        keep, slabs[2 * own[0].shape[0] :], between, [early, late], table, "result", sums
+    )
+    places = [(0, 0), (0, 1)] + between
     stack = stack_stage(keep, other, places, [early, late], table, "store", (), (first,))
     return stack.reshape(rounds, per_round, keep, 2 * LAG + 1)
 

time: 27.2 us -> 28.5 us (1.048)
  waiting for transfers between devices: 4.97 us -> 6.31 us
    ppermute x11, waiting for transfers between devices: 4.97 us -> 6.31 us  [swapped(): return lax.ppermute(value, axis, [(i, i ^ step) for i in range(size)])]
where the time goes in v20:
time: 28.5 us; the launch traced here: 28.3 us
  starting transfers between devices  12.9 us (45%)
  Pallas kernels  8.89 us (31%)
  waiting for transfers between devices  6.31 us (22%)
    ppermute x11, starting transfers between devices, swapped(): return lax.ppermute(value, axis, [(i, i ^ step) for i in range(size)])  12.9 us
    ppermute x11, waiting for transfers between devices, swapped(): return lax.ppermute(value, axis, [(i, i ^ step) for i in range(size)])  6.31 us
    pallas_call x3, Pallas kernels, stack_stage(): pl.pallas_call(functools.partial(stack_kernel, places, (not before, stage...  5.72 us
    pallas_call x1, Pallas kernels, encode(): pl.pallas_call(functools.partial(encode_kernel, segments), out_shape=(sla...  2.08 us
    pallas_call x2, Pallas kernels, whiten_blocks(): pl.pallas_call(functools.partial(whiten_kernel, segments), out_shape=(par...  1.1 us
  transfers between devices with their start and end apart: 11, of which 5 were waited for; matrix products, arithmetic and copies ran while one was open for 0% of the time, Pallas kernels for 14%

profile of v20, /device:TPU:0, one launch (start us, length us, event | category | flops | bytes accessed | tf_op | source)
XLA Modules:
  0.0 28.3 jit_solution(1291843588119658658)
XLA Ops:
  0.0 0.0 copy-start
  0.0 2.1 %encode_and_pick.1 = (bf16[16,1536]{1,0:T(8,128)(2,1)S(1)}, bf16[16,1536]{1,0:T(8,128)(2,1)S(1)}, bf16[32,3072]{1,0:T(8,128)(2,1)S(1)}, bf16[32,3072]{1,0:T(8,12...) custom-call(bf16[128,3072]{1,0:T(8,128)(2,1)} %bitcast.3, s32[1,128]{1,0:T(1,128)} %bitcast.4, ...), custom_call_target="tpu_custom_call" | custom-call | tf_op jit(solution)/shard_map/encode_and_pick/pallas_call | solution.py:287
  2.1 3.0 %collective-permute-start.4 = (bf16[32,3072]{1,0:T(8,128)(2,1)S(1)}, bf16[32,3072]{1,0:T(8,128)(2,1)S(1)}, u32[]{:S(2)}, u32[]{:S(2)}) collective-permute-start(bf16[32,3072]{1,0:T(8,128)(2,1)S(1)} %get-tuple-element.49), channel_id=1, source_target_pairs={{0,2},{1,3},{2,0},{3,1},{4,6},{5,7},{6,4},{7,5},{8,10},{9,11},{10,... | collective-permute-start | bytes 589832 | tf_op jit(solution)/shard_map/ppermute | solution.py:356
  5.1 1.4 %collective-permute-start.5 = (bf16[32,3072]{1,0:T(8,128)(2,1)S(1)}, bf16[32,3072]{1,0:T(8,128)(2,1)S(1)}, u32[]{:S(2)}, u32[]{:S(2)}) collective-permute-start(bf16[32,3072]{1,0:T(8,128)(2,1)S(1)} %get-tuple-element.50), channel_id=1, source_target_pairs={{0,3},{1,2},{2,1},{3,0},{4,7},{5,6},{6,5},{7,4},{8,11},{9,10},{10,... | collective-permute-start | bytes 589832 | tf_op jit(solution)/shard_map/ppermute | solution.py:356
  6.6 0.0 collective-permute-start
  6.6 1.2 %collective-permute-done = bf16[16,1536]{1,0:T(8,128)(2,1)S(1)} collective-permute-done((bf16[16,1536]{1,0:T(8,128)(2,1)S(1)}, bf16[16,1536]{1,0:T(8,128)(2,1)S(1)}, u32[]{:S(2)}, u32[]{:S(2)}) %collective-permute-start) | collective-permute-done | bytes 49184 | tf_op jit(solution)/shard_map/ppermute | solution.py:356
  7.8 3.7 %collective-permute-start.3 = (bf16[16,1536]{1,0:T(8,128)(2,1)S(1)}, bf16[16,1536]{1,0:T(8,128)(2,1)S(1)}, u32[]{:S(2)}, u32[]{:S(2)}) collective-permute-start(bf16[16,1536]{1,0:T(8,128)(2,1)S(1)} %add.12), channel_id=1, source_target_pairs={{0,24},{4,28},{8,16},{12,20},{16,8},{20,12},{24,0},{28,4},{1,25},{... | collective-permute-start | bytes 147464 | tf_op jit(solution)/shard_map/ppermute | solution.py:356
  11.5 0.0 collective-permute-start.2
  11.5 0.8 %collective-permute-start.1 = (bf16[16,1536]{1,0:T(8,128)(2,1)S(1)}, bf16[16,1536]{1,0:T(8,128)(2,1)S(1)}, u32[]{:S(2)}, u32[]{:S(2)}) collective-permute-start(bf16[16,1536]{1,0:T(8,128)(2,1)S(1)} %add.12), channel_id=1, source_target_pairs={{0,8},{4,12},{8,0},{12,4},{16,24},{20,28},{24,16},{28,20},{1,9},{5... | collective-permute-start | bytes 147464 | tf_op jit(solution)/shard_map/ppermute | solution.py:356
  12.3 1.6 %collective-permute-done.3 = bf16[16,1536]{1,0:T(8,128)(2,1)S(1)} collective-permute-done((bf16[16,1536]{1,0:T(8,128)(2,1)S(1)}, bf16[16,1536]{1,0:T(8,128)(2,1)S(1)}, u32[]{:S(2)}, u32[]{:S(2)}) %collective-permute-start.3) | collective-permute-done | bytes 49184 | tf_op jit(solution)/shard_map/ppermute | solution.py:356
  13.8 0.4 %collective-permute-start.7 = (bf16[32,3072]{1,0:T(8,128)(2,1)S(1)}, bf16[32,3072]{1,0:T(8,128)(2,1)S(1)}, u32[]{:S(2)}, u32[]{:S(2)}) collective-permute-start(bf16[32,3072]{1,0:T(8,128)(2,1)S(1)} %get-tuple-element.59), channel_id=1, source_target_pairs={{0,1},{1,0},{2,3},{3,2},{4,5},{5,4},{6,7},{7,6},{8,9},{9,8},{10,11... | collective-permute-start | bytes 589832 | tf_op jit(solution)/shard_map/ppermute | solution.py:356
  14.2 0.1 collective-permute-done.4.refs_2_
  14.2 0.0 collective-permute-done.5.refs_1_
  14.2 0.7 %whiten_receivers.2 = (f32[96,1536]{1,0:T(8,128)S(1)}, f32[96,1536]{1,0:T(8,128)S(1)}, f32[96,1536]{1,0:T(8,128)S(1)}, f32[96,128]{1,0:T(8,128)S(1)}) custom-call(bf16[32,3072]{1,0:T(8,128)(2,1)S(1)} %get-tuple-element.48.refs_0_, bf16[32,3072]{1,0:T(8,128)(2,1)S(1)} %collective-permute-done.5.refs_1_, bf16[32,3072]{1,0:T(8,128)(2,1)S(1)} %collective-permute-done.4.refs_2_), custom_call_target="tpu_custom_call" | custom-call | flops 301989888 | bytes 1179648 | tf_op jit(solution)/shard_map/whiten_receivers/pallas_call | solution.py:312
  15.0 1.5 %collective-permute-done.2 = bf16[16,1536]{1,0:T(8,128)(2,1)S(1)} collective-permute-done((bf16[16,1536]{1,0:T(8,128)(2,1)S(1)}, bf16[16,1536]{1,0:T(8,128)(2,1)S(1)}, u32[]{:S(2)}, u32[]{:S(2)}) %collective-permute-start.2) | collective-permute-done | bytes 49184 | tf_op jit(solution)/shard_map/ppermute | solution.py:356
  16.5 0.0 collective-permute-done.1
  16.5 1.6 %collective-permute-start.6 = (bf16[16,1536]{1,0:T(8,128)(2,1)S(1)}, bf16[16,1536]{1,0:T(8,128)(2,1)S(1)}, u32[]{:S(2)}, u32[]{:S(2)}) collective-permute-start(bf16[16,1536]{1,0:T(8,128)(2,1)S(1)} %add_add_fusion), channel_id=1, source_target_pairs={{0,3},{1,2},{2,1},{3,0},{4,7},{5,6},{6,5},{7,4},{8,11},{9,10},{10,... | collective-permute-start | bytes 147464 | tf_op jit(solution)/shard_map/ppermute | solution.py:356
  18.0 0.5 %collective-permute-start.9 = (bf16[16,1536]{1,0:T(8,128)(2,1)S(1)}, bf16[16,1536]{1,0:T(8,128)(2,1)S(1)}, u32[]{:S(2)}, u32[]{:S(2)}) collective-permute-start(bf16[16,1536]{1,0:T(8,128)(2,1)S(1)} %add_add_fusion), channel_id=1, source_target_pairs={{0,2},{1,3},{2,0},{3,1},{4,6},{5,7},{6,4},{7,5},{8,10},{9,11},{10,... | collective-permute-start | bytes 147464 | tf_op jit(solution)/shard_map/ppermute | solution.py:356
  18.5 1.5 %collective-permute-start.8 = (bf16[16,1536]{1,0:T(8,128)(2,1)S(1)}, bf16[16,1536]{1,0:T(8,128)(2,1)S(1)}, u32[]{:S(2)}, u32[]{:S(2)}) collective-permute-start(bf16[16,1536]{1,0:T(8,128)(2,1)S(1)} %add_add_fusion), channel_id=1, source_target_pairs={{0,1},{1,0},{2,3},{3,2},{4,5},{5,4},{6,7},{7,6},{8,9},{9,8},{10,11... | collective-permute-start | bytes 147464 | tf_op jit(solution)/shard_map/ppermute | solution.py:356
  20.0 0.0 collective-permute-done.7.refs_0_
  20.1 0.4 %whiten_receivers.3 = (f32[32,1536]{1,0:T(8,128)S(1)}, f32[32,1536]{1,0:T(8,128)S(1)}, f32[32,1536]{1,0:T(8,128)S(1)}, f32[32,128]{1,0:T(8,128)S(1)}) custom-call(bf16[32,3072]{1,0:T(8,128)(2,1)S(1)} %collective-permute-done.7.refs_0_), custom_call_target="tpu_custom_call" | custom-call | flops 100663296 | bytes 393216 | tf_op jit(solution)/shard_map/whiten_receivers/pallas_call | solution.py:312
  20.4 2.0 %collective-permute-done.6 = bf16[16,1536]{1,0:T(8,128)(2,1)S(1)} collective-permute-done((bf16[16,1536]{1,0:T(8,128)(2,1)S(1)}, bf16[16,1536]{1,0:T(8,128)(2,1)S(1)}, u32[]{:S(2)}, u32[]{:S(2)}) %collective-permute-start.6) | collective-permute-done | bytes 49184 | tf_op jit(solution)/shard_map/ppermute | solution.py:356
  22.4 0.0 copy-done
  22.4 1.4 %stack_sums.1 = (f32[2,256,256]{2,1,0:T(8,128)S(1)}, f32[256,128]{1,0:T(8,128)S(1)}) custom-call(bf16[32,1536]{1,0:T(8,128)(2,1)S(1)} %pad_maximum_fusion.1.refs_0_, f32[96,1536]{1,0:T(8,128)S(1)} %get-tuple-element.65.refs_1_, f32[96,1536]{1,0:T(8,128)S(1)} %get-tuple-element.66.refs_2_, f32[96,1536]{1,0:T(8,128)S(1)} %get-tuple-element.67.refs_3_, ...), custom_call_target="tpu_custom_call" | custom-call | flops 471859200 | bytes 3145728 | tf_op jit(solution)/shard_map/stack_sums/pallas_call | solution.py:341
  23.8 0.0 collective-permute-done.9
  23.8 0.0 collective-permute-done.8
  23.8 0.1 collective-permute-start.10
  23.9 1.5 %stack_result.1.refs_10_ = f32[256,301]{1,0:T(8,128)S(1)} custom-call(bf16[32,1536]{1,0:T(8,128)(2,1)S(1)} %pad_maximum_fusion.2.refs_0_, f32[96,1536]{1,0:T(8,128)S(1)} %get-tuple-element.65.refs_1_, f32[96,1536]{1,0:T(8,128)S(1)} %get-tuple-element.66.refs_2_, f32[96,1536]{1,0:T(8,128)S(1)} %get-tuple-element.67.refs_3_, ...), custom_call_target="tpu_custom_call" | custom-call | flops 471859200 | bytes 3145728 | tf_op jit(solution)/shard_map/stack_result/pallas_call | solution.py:341
  25.4 0.0 collective-permute-done.10.refs_0_
  25.4 2.9 %stack_store.1 = f32[512,301]{1,0:T(8,128)} custom-call(bf16[64,1536]{1,0:T(8,128)(2,1)S(1)} %collective-permute-done.10.refs_0_, f32[96,1536]{1,0:T(8,128)S(1)} %get-tuple-element.65.refs_1_, f32[96,1536]{1,0:T(8,128)S(1)} %get-tuple-element.66.refs_2_, f32[96,1536]{1,0:T(8,128)S(1)} %get-tuple-element.67.refs_3_, f32[96,128]{1,0:T(8,128)S(1)} %get-tuple-element.68.refs_4_, ...), custom_call_target="tpu_custom_call" | custom-call | flops 471859200 | bytes 3145728 | tf_op jit(solution)/shard_map/stack_store/pallas_call | solution.py:341
  (5 shorter events, 0.1 us)
Async XLA Ops:
  0.0 22.4 %copy-start = (bf16[3072,256]{1,0:T(8,128)(2,1)S(1)}, bf16[3072,256]{1,0:T(8,128)(2,1)}, u32[]{:S(2)}) copy-start(bf16[3072,256]{1,0:T(8,128)(2,1)} %constant.2.clone.refs_5_.refs_9_) | copy-start | bytes 4718596
  2.1 12.1 %collective-permute-start.4 = (bf16[32,3072]{1,0:T(8,128)(2,1)S(1)}, bf16[32,3072]{1,0:T(8,128)(2,1)S(1)}, u32[]{:S(2)}, u32[]{:S(2)}) collective-permute-start(bf16[32,3072]{1,0:T(8,128)(2,1)S(1)} %get-tuple-element.49), channel_id=1, source_target_pairs={{0,2},{1,3},{2,0},{3,1},{4,6},{5,7},{6,4},{7,5},{8,10},{9,11},{10,... | collective-permute-start | bytes 589832 | tf_op jit(solution)/shard_map/ppermute | solution.py:356
  5.1 9.1 %collective-permute-start.5 = (bf16[32,3072]{1,0:T(8,128)(2,1)S(1)}, bf16[32,3072]{1,0:T(8,128)(2,1)S(1)}, u32[]{:S(2)}, u32[]{:S(2)}) collective-permute-start(bf16[32,3072]{1,0:T(8,128)(2,1)S(1)} %get-tuple-element.50), channel_id=1, source_target_pairs={{0,3},{1,2},{2,1},{3,0},{4,7},{5,6},{6,5},{7,4},{8,11},{9,10},{10,... | collective-permute-start | bytes 589832 | tf_op jit(solution)/shard_map/ppermute | solution.py:356
  6.6 1.2 %collective-permute-start = (bf16[16,1536]{1,0:T(8,128)(2,1)S(1)}, bf16[16,1536]{1,0:T(8,128)(2,1)S(1)}, u32[]{:S(2)}, u32[]{:S(2)}) collective-permute-start(bf16[16,1536]{1,0:T(8,128)(2,1)S(1)} %get-tuple-element.45), channel_id=1, source_target_pairs={{0,4},{4,0},{8,12},{12,8},{16,20},{20,16},{24,28},{28,24},{1,5},{5... | collective-permute-start | bytes 147464 | tf_op jit(solution)/shard_map/ppermute | solution.py:356
  7.8 6.0 %collective-permute-start.3 = (bf16[16,1536]{1,0:T(8,128)(2,1)S(1)}, bf16[16,1536]{1,0:T(8,128)(2,1)S(1)}, u32[]{:S(2)}, u32[]{:S(2)}) collective-permute-start(bf16[16,1536]{1,0:T(8,128)(2,1)S(1)} %add.12), channel_id=1, source_target_pairs={{0,24},{4,28},{8,16},{12,20},{16,8},{20,12},{24,0},{28,4},{1,25},{... | collective-permute-start | bytes 147464 | tf_op jit(solution)/shard_map/ppermute | solution.py:356
  11.5 5.0 %collective-permute-start.2 = (bf16[16,1536]{1,0:T(8,128)(2,1)S(1)}, bf16[16,1536]{1,0:T(8,128)(2,1)S(1)}, u32[]{:S(2)}, u32[]{:S(2)}) collective-permute-start(bf16[16,1536]{1,0:T(8,128)(2,1)S(1)} %add.12), channel_id=1, source_target_pairs={{0,16},{4,20},{8,24},{12,28},{16,0},{20,4},{24,8},{28,12},{1,17},{... | collective-permute-start | bytes 147464 | tf_op jit(solution)/shard_map/ppermute | solution.py:356
  11.5 5.0 %collective-permute-start.1 = (bf16[16,1536]{1,0:T(8,128)(2,1)S(1)}, bf16[16,1536]{1,0:T(8,128)(2,1)S(1)}, u32[]{:S(2)}, u32[]{:S(2)}) collective-permute-start(bf16[16,1536]{1,0:T(8,128)(2,1)S(1)} %add.12), channel_id=1, source_target_pairs={{0,8},{4,12},{8,0},{12,4},{16,24},{20,28},{24,16},{28,20},{1,9},{5... | collective-permute-start | bytes 147464 | tf_op jit(solution)/shard_map/ppermute | solution.py:356
  13.8 6.2 %collective-permute-start.7 = (bf16[32,3072]{1,0:T(8,128)(2,1)S(1)}, bf16[32,3072]{1,0:T(8,128)(2,1)S(1)}, u32[]{:S(2)}, u32[]{:S(2)}) collective-permute-start(bf16[32,3072]{1,0:T(8,128)(2,1)S(1)} %get-tuple-element.59), channel_id=1, source_target_pairs={{0,1},{1,0},{2,3},{3,2},{4,5},{5,4},{6,7},{7,6},{8,9},{9,8},{10,11... | collective-permute-start | bytes 589832 | tf_op jit(solution)/shard_map/ppermute | solution.py:356
  16.5 5.9 %collective-permute-start.6 = (bf16[16,1536]{1,0:T(8,128)(2,1)S(1)}, bf16[16,1536]{1,0:T(8,128)(2,1)S(1)}, u32[]{:S(2)}, u32[]{:S(2)}) collective-permute-start(bf16[16,1536]{1,0:T(8,128)(2,1)S(1)} %add_add_fusion), channel_id=1, source_target_pairs={{0,3},{1,2},{2,1},{3,0},{4,7},{5,6},{6,5},{7,4},{8,11},{9,10},{10,... | collective-permute-start | bytes 147464 | tf_op jit(solution)/shard_map/ppermute | solution.py:356
  18.0 5.7 %collective-permute-start.9 = (bf16[16,1536]{1,0:T(8,128)(2,1)S(1)}, bf16[16,1536]{1,0:T(8,128)(2,1)S(1)}, u32[]{:S(2)}, u32[]{:S(2)}) collective-permute-start(bf16[16,1536]{1,0:T(8,128)(2,1)S(1)} %add_add_fusion), channel_id=1, source_target_pairs={{0,2},{1,3},{2,0},{3,1},{4,6},{5,7},{6,4},{7,5},{8,10},{9,11},{10,... | collective-permute-start | bytes 147464 | tf_op jit(solution)/shard_map/ppermute | solution.py:356
  18.5 5.2 %collective-permute-start.8 = (bf16[16,1536]{1,0:T(8,128)(2,1)S(1)}, bf16[16,1536]{1,0:T(8,128)(2,1)S(1)}, u32[]{:S(2)}, u32[]{:S(2)}) collective-permute-start(bf16[16,1536]{1,0:T(8,128)(2,1)S(1)} %add_add_fusion), channel_id=1, source_target_pairs={{0,1},{1,0},{2,3},{3,2},{4,5},{5,4},{6,7},{7,6},{8,9},{9,8},{10,11... | collective-permute-start | bytes 147464 | tf_op jit(solution)/shard_map/ppermute | solution.py:356
  23.8 1.6 %collective-permute-start.10 = (bf16[64,1536]{1,0:T(8,128)(2,1)S(1)}, bf16[64,1536]{1,0:T(8,128)(2,1)S(1)}, u32[]{:S(2)}, u32[]{:S(2)}) collective-permute-start(bf16[64,1536]{1,0:T(8,128)(2,1)S(1)} %pad_maximum_fusion), channel_id=1, source_target_pairs={{0,4},{4,0},{8,12},{12,8},{16,20},{20,16},{24,28},{28,24},{1,5},{5... | collective-permute-start | bytes 589832 | tf_op jit(solution)/shard_map/ppermute | solution.py:356

commit v21 on v19

--- a/solution.py
+++ b/solution.py
@@ -366,15 +366,15 @@
     receivers[-1] = swapped(receivers[-1], "tm", tm_size, tm_size - 1)
     own = own + swapped(other, "rcv", rcv_size, 1)
     own, later = lax.optimization_barrier((own, receivers[1:-1]))
+    last, receivers[-1] = lax.optimization_barrier((later[-1], receivers[-1]))
     receivers[1:-1] = [
-        swapped(block, "tm", tm_size, place) for place, block in enumerate(later, 1)
+        swapped(block, "tm", tm_size, place) for place, block in enumerate(later[:-1] + [last], 1)
     ]
     step = 2
     while step < rcv_size:
         wide = min(4, rcv_size // step)
         parts = [swapped(own, "rcv", rcv_size, place * step) for place in range(1, wide)]
         if step == 2:
-            parts[-1], receivers[-1] = lax.optimization_barrier((parts[-1], receivers[-1]))
             early = tuple(whiten_blocks([receivers[0], receivers[-1]]))
             parts[-2:-1], early = lax.optimization_barrier((parts[-2:-1], early))
         own = functools.reduce(jnp.add, parts, own)

time: 27.2 us -> 27.2 us (level)
  transfers between devices with their start and end apart: 11 -> 11, of which waited for: 5 -> 4; matrix products, arithmetic and copies ran while one was open for 0% -> 0% of each run, Pallas kernels for 14% -> 14%
where the time goes in v21:
time: 27.2 us; the launch traced here: 27 us
  starting transfers between devices  12.9 us (47%)
  Pallas kernels  8.81 us (32%)
  waiting for transfers between devices  5.07 us (19%)
    ppermute x11, starting transfers between devices, swapped(): return lax.ppermute(value, axis, [(i, i ^ step) for i in range(size)])  12.9 us
    pallas_call x3, Pallas kernels, stack_stage(): pl.pallas_call(functools.partial(stack_kernel, places, (not before, stage...  5.71 us
    ppermute x11, waiting for transfers between devices, swapped(): return lax.ppermute(value, axis, [(i, i ^ step) for i in range(size)])  5.07 us
    pallas_call x1, Pallas kernels, encode(): pl.pallas_call(functools.partial(encode_kernel, segments), out_shape=(sla...  2.08 us
    pallas_call x2, Pallas kernels, whiten_blocks(): pl.pallas_call(functools.partial(whiten_kernel, segments), out_shape=(par...  1.02 us
  transfers between devices with their start and end apart: 11, of which 4 were waited for; matrix products, arithmetic and copies ran while one was open for 0% of the time, Pallas kernels for 14%

profile of v21, /device:TPU:0, one launch (start us, length us, event | category | flops | bytes accessed | tf_op | source)
XLA Modules:
  0.0 27.0 jit_solution(15576625298030059392)
XLA Ops:
  0.0 0.0 copy-start
  0.0 2.1 %encode_and_pick.1 = (bf16[16,1536]{1,0:T(8,128)(2,1)S(1)}, bf16[16,1536]{1,0:T(8,128)(2,1)S(1)}, bf16[32,3072]{1,0:T(8,128)(2,1)S(1)}, bf16[32,3072]{1,0:T(8,12...) custom-call(bf16[128,3072]{1,0:T(8,128)(2,1)} %bitcast.3, s32[1,128]{1,0:T(1,128)} %bitcast.4, ...), custom_call_target="tpu_custom_call" | custom-call | tf_op jit(solution)/shard_map/encode_and_pick/pallas_call | solution.py:287
  2.1 4.0 %collective-permute-start.3 = (bf16[32,3072]{1,0:T(8,128)(2,1)S(1)}, bf16[32,3072]{1,0:T(8,128)(2,1)S(1)}, u32[]{:S(2)}, u32[]{:S(2)}) collective-permute-start(bf16[32,3072]{1,0:T(8,128)(2,1)S(1)} %get-tuple-element.51), channel_id=1, source_target_pairs={{0,3},{1,2},{2,1},{3,0},{4,7},{5,6},{6,5},{7,4},{8,11},{9,10},{10,... | collective-permute-start | bytes 589832 | tf_op jit(solution)/shard_map/ppermute | solution.py:356
  6.0 0.0 collective-permute-start
  6.1 1.2 %collective-permute-done = bf16[16,1536]{1,0:T(8,128)(2,1)S(1)} collective-permute-done((bf16[16,1536]{1,0:T(8,128)(2,1)S(1)}, bf16[16,1536]{1,0:T(8,128)(2,1)S(1)}, u32[]{:S(2)}, u32[]{:S(2)}) %collective-permute-start) | collective-permute-done | bytes 49184 | tf_op jit(solution)/shard_map/ppermute | solution.py:356
  7.3 2.7 %collective-permute-start.2 = (bf16[16,1536]{1,0:T(8,128)(2,1)S(1)}, bf16[16,1536]{1,0:T(8,128)(2,1)S(1)}, u32[]{:S(2)}, u32[]{:S(2)}) collective-permute-start(bf16[16,1536]{1,0:T(8,128)(2,1)S(1)} %add.12), channel_id=1, source_target_pairs={{0,16},{4,20},{8,24},{12,28},{16,0},{20,4},{24,8},{28,12},{1,17},{... | collective-permute-start | bytes 147464 | tf_op jit(solution)/shard_map/ppermute | solution.py:356
  10.0 1.3 %collective-permute-start.4 = (bf16[16,1536]{1,0:T(8,128)(2,1)S(1)}, bf16[16,1536]{1,0:T(8,128)(2,1)S(1)}, u32[]{:S(2)}, u32[]{:S(2)}) collective-permute-start(bf16[16,1536]{1,0:T(8,128)(2,1)S(1)} %add.12), channel_id=1, source_target_pairs={{0,24},{4,28},{8,16},{12,20},{16,8},{20,12},{24,0},{28,4},{1,25},{... | collective-permute-start | bytes 147464 | tf_op jit(solution)/shard_map/ppermute | solution.py:356
  11.3 0.2 collective-permute-start.1
  11.5 0.5 %collective-permute-start.6 = (bf16[32,3072]{1,0:T(8,128)(2,1)S(1)}, bf16[32,3072]{1,0:T(8,128)(2,1)S(1)}, u32[]{:S(2)}, u32[]{:S(2)}) collective-permute-start(bf16[32,3072]{1,0:T(8,128)(2,1)S(1)} %get-tuple-element.58), channel_id=1, source_target_pairs={{0,1},{1,0},{2,3},{3,2},{4,5},{5,4},{6,7},{7,6},{8,9},{9,8},{10,11... | collective-permute-start | bytes 589832 | tf_op jit(solution)/shard_map/ppermute | solution.py:356
  12.1 0.0 collective-permute-done.3.refs_1_
  12.1 0.6 %collective-permute-start.7 = (bf16[32,3072]{1,0:T(8,128)(2,1)S(1)}, bf16[32,3072]{1,0:T(8,128)(2,1)S(1)}, u32[]{:S(2)}, u32[]{:S(2)}) collective-permute-start(bf16[32,3072]{1,0:T(8,128)(2,1)S(1)} %get-tuple-element.59), channel_id=1, source_target_pairs={{0,2},{1,3},{2,0},{3,1},{4,6},{5,7},{6,4},{7,5},{8,10},{9,11},{10,... | collective-permute-start | bytes 589832 | tf_op jit(solution)/shard_map/ppermute | solution.py:356
  12.7 0.5 %whiten_receivers.2 = (f32[64,1536]{1,0:T(8,128)S(1)}, f32[64,1536]{1,0:T(8,128)S(1)}, f32[64,1536]{1,0:T(8,128)S(1)}, f32[64,128]{1,0:T(8,128)S(1)}) custom-call(bf16[32,3072]{1,0:T(8,128)(2,1)S(1)} %get-tuple-element.49.refs_0_, bf16[32,3072]{1,0:T(8,128)(2,1)S(1)} %collective-permute-done.3.refs_1_), custom_call_target="tpu_custom_call" | custom-call | flops 201326592 | bytes 786432 | tf_op jit(solution)/shard_map/whiten_receivers/pallas_call | solution.py:312
  13.2 0.2 collective-permute-done.2
  13.4 2.5 %collective-permute-done.4 = bf16[16,1536]{1,0:T(8,128)(2,1)S(1)} collective-permute-done((bf16[16,1536]{1,0:T(8,128)(2,1)S(1)}, bf16[16,1536]{1,0:T(8,128)(2,1)S(1)}, u32[]{:S(2)}, u32[]{:S(2)}) %collective-permute-start.4) | collective-permute-done | bytes 49184 | tf_op jit(solution)/shard_map/ppermute | solution.py:356
  15.9 0.0 collective-permute-done.1
  15.9 0.5 %collective-permute-start.5 = (bf16[16,1536]{1,0:T(8,128)(2,1)S(1)}, bf16[16,1536]{1,0:T(8,128)(2,1)S(1)}, u32[]{:S(2)}, u32[]{:S(2)}) collective-permute-start(bf16[16,1536]{1,0:T(8,128)(2,1)S(1)} %add_add_fusion), channel_id=1, source_target_pairs={{0,3},{1,2},{2,1},{3,0},{4,7},{5,6},{6,5},{7,4},{8,11},{9,10},{10,... | collective-permute-start | bytes 147464 | tf_op jit(solution)/shard_map/ppermute | solution.py:356
  16.5 1.5 %collective-permute-start.9 = (bf16[16,1536]{1,0:T(8,128)(2,1)S(1)}, bf16[16,1536]{1,0:T(8,128)(2,1)S(1)}, u32[]{:S(2)}, u32[]{:S(2)}) collective-permute-start(bf16[16,1536]{1,0:T(8,128)(2,1)S(1)} %add_add_fusion), channel_id=1, source_target_pairs={{0,2},{1,3},{2,0},{3,1},{4,6},{5,7},{6,4},{7,5},{8,10},{9,11},{10,... | collective-permute-start | bytes 147464 | tf_op jit(solution)/shard_map/ppermute | solution.py:356
  18.0 1.5 %collective-permute-start.8 = (bf16[16,1536]{1,0:T(8,128)(2,1)S(1)}, bf16[16,1536]{1,0:T(8,128)(2,1)S(1)}, u32[]{:S(2)}, u32[]{:S(2)}) collective-permute-start(bf16[16,1536]{1,0:T(8,128)(2,1)S(1)} %add_add_fusion), channel_id=1, source_target_pairs={{0,1},{1,0},{2,3},{3,2},{4,5},{5,4},{6,7},{7,6},{8,9},{9,8},{10,11... | collective-permute-start | bytes 147464 | tf_op jit(solution)/shard_map/ppermute | solution.py:356
  19.5 0.0 collective-permute-done.6.refs_0_
  19.5 0.0 collective-permute-done.7.refs_1_
  19.5 0.5 %whiten_receivers.3 = (f32[64,1536]{1,0:T(8,128)S(1)}, f32[64,1536]{1,0:T(8,128)S(1)}, f32[64,1536]{1,0:T(8,128)S(1)}, f32[64,128]{1,0:T(8,128)S(1)}) custom-call(bf16[32,3072]{1,0:T(8,128)(2,1)S(1)} %collective-permute-done.6.refs_0_, bf16[32,3072]{1,0:T(8,128)(2,1)S(1)} %collective-permute-done.7.refs_1_), custom_call_target="tpu_custom_call" | custom-call | flops 201326592 | bytes 786432 | tf_op jit(solution)/shard_map/whiten_receivers/pallas_call | solution.py:312
  20.0 1.1 %collective-permute-done.5 = bf16[16,1536]{1,0:T(8,128)(2,1)S(1)} collective-permute-done((bf16[16,1536]{1,0:T(8,128)(2,1)S(1)}, bf16[16,1536]{1,0:T(8,128)(2,1)S(1)}, u32[]{:S(2)}, u32[]{:S(2)}) %collective-permute-start.5) | collective-permute-done | bytes 49184 | tf_op jit(solution)/shard_map/ppermute | solution.py:356
  21.1 0.0 copy-done
  21.1 1.4 %stack_sums.1 = (f32[2,256,256]{2,1,0:T(8,128)S(1)}, f32[256,128]{1,0:T(8,128)S(1)}) custom-call(bf16[32,1536]{1,0:T(8,128)(2,1)S(1)} %pad_maximum_fusion.1.refs_0_, f32[64,1536]{1,0:T(8,128)S(1)} %get-tuple-element.65.refs_1_, f32[64,1536]{1,0:T(8,128)S(1)} %get-tuple-element.66.refs_2_, f32[64,1536]{1,0:T(8,128)S(1)} %get-tuple-element.67.refs_3_, ...), custom_call_target="tpu_custom_call" | custom-call | flops 471859200 | bytes 3145728 | tf_op jit(solution)/shard_map/stack_sums/pallas_call | solution.py:341
  22.5 0.0 collective-permute-done.9
  22.5 0.0 collective-permute-done.8
  22.5 0.1 collective-permute-start.10
  22.6 1.5 %stack_result.1.refs_10_ = f32[256,301]{1,0:T(8,128)S(1)} custom-call(bf16[32,1536]{1,0:T(8,128)(2,1)S(1)} %pad_maximum_fusion.2.refs_0_, f32[64,1536]{1,0:T(8,128)S(1)} %get-tuple-element.77.refs_1_.refs_5_, f32[64,1536]{1,0:T(8,128)S(1)} %get-tuple-element.78.refs_2_.refs_6_, f32[64,1536]{1,0:T(8,128)S(1)} %get-tuple-element.79.refs_3_.refs_7_, ...), custom_call_target="tpu_custom_call" | custom-call | flops 471859200 | bytes 3145728 | tf_op jit(solution)/shard_map/stack_result/pallas_call | solution.py:341
  24.1 0.0 collective-permute-done.10.refs_0_
  24.1 2.9 %stack_store.1 = f32[512,301]{1,0:T(8,128)} custom-call(bf16[64,1536]{1,0:T(8,128)(2,1)S(1)} %collective-permute-done.10.refs_0_, f32[64,1536]{1,0:T(8,128)S(1)} %get-tuple-element.65.refs_1_, f32[64,1536]{1,0:T(8,128)S(1)} %get-tuple-element.66.refs_2_, f32[64,1536]{1,0:T(8,128)S(1)} %get-tuple-element.67.refs_3_, f32[64,128]{1,0:T(8,128)S(1)} %get-tuple-element.68.refs_4_, ...), custom_call_target="tpu_custom_call" | custom-call | flops 471859200 | bytes 3145728 | tf_op jit(solution)/shard_map/stack_store/pallas_call | solution.py:341
  (5 shorter events, 0.1 us)
Async XLA Ops:
  0.0 21.1 %copy-start = (bf16[3072,256]{1,0:T(8,128)(2,1)S(1)}, bf16[3072,256]{1,0:T(8,128)(2,1)}, u32[]{:S(2)}) copy-start(bf16[3072,256]{1,0:T(8,128)(2,1)} %constant.2.clone.refs_5_.refs_9_) | copy-start | bytes 4718596
  2.1 10.0 %collective-permute-start.3 = (bf16[32,3072]{1,0:T(8,128)(2,1)S(1)}, bf16[32,3072]{1,0:T(8,128)(2,1)S(1)}, u32[]{:S(2)}, u32[]{:S(2)}) collective-permute-start(bf16[32,3072]{1,0:T(8,128)(2,1)S(1)} %get-tuple-element.51), channel_id=1, source_target_pairs={{0,3},{1,2},{2,1},{3,0},{4,7},{5,6},{6,5},{7,4},{8,11},{9,10},{10,... | collective-permute-start | bytes 589832 | tf_op jit(solution)/shard_map/ppermute | solution.py:356
  6.0 1.2 %collective-permute-start = (bf16[16,1536]{1,0:T(8,128)(2,1)S(1)}, bf16[16,1536]{1,0:T(8,128)(2,1)S(1)}, u32[]{:S(2)}, u32[]{:S(2)}) collective-permute-start(bf16[16,1536]{1,0:T(8,128)(2,1)S(1)} %get-tuple-element.45), channel_id=1, source_target_pairs={{0,4},{4,0},{8,12},{12,8},{16,20},{20,16},{24,28},{28,24},{1,5},{5... | collective-permute-start | bytes 147464 | tf_op jit(solution)/shard_map/ppermute | solution.py:356
  7.3 6.1 %collective-permute-start.2 = (bf16[16,1536]{1,0:T(8,128)(2,1)S(1)}, bf16[16,1536]{1,0:T(8,128)(2,1)S(1)}, u32[]{:S(2)}, u32[]{:S(2)}) collective-permute-start(bf16[16,1536]{1,0:T(8,128)(2,1)S(1)} %add.12), channel_id=1, source_target_pairs={{0,16},{4,20},{8,24},{12,28},{16,0},{20,4},{24,8},{28,12},{1,17},{... | collective-permute-start | bytes 147464 | tf_op jit(solution)/shard_map/ppermute | solution.py:356
  10.0 6.0 %collective-permute-start.4 = (bf16[16,1536]{1,0:T(8,128)(2,1)S(1)}, bf16[16,1536]{1,0:T(8,128)(2,1)S(1)}, u32[]{:S(2)}, u32[]{:S(2)}) collective-permute-start(bf16[16,1536]{1,0:T(8,128)(2,1)S(1)} %add.12), channel_id=1, source_target_pairs={{0,24},{4,28},{8,16},{12,20},{16,8},{20,12},{24,0},{28,4},{1,25},{... | collective-permute-start | bytes 147464 | tf_op jit(solution)/shard_map/ppermute | solution.py:356
  11.3 4.6 %collective-permute-start.1 = (bf16[16,1536]{1,0:T(8,128)(2,1)S(1)}, bf16[16,1536]{1,0:T(8,128)(2,1)S(1)}, u32[]{:S(2)}, u32[]{:S(2)}) collective-permute-start(bf16[16,1536]{1,0:T(8,128)(2,1)S(1)} %add.12), channel_id=1, source_target_pairs={{0,8},{4,12},{8,0},{12,4},{16,24},{20,28},{24,16},{28,20},{1,9},{5... | collective-permute-start | bytes 147464 | tf_op jit(solution)/shard_map/ppermute | solution.py:356
  11.5 8.0 %collective-permute-start.6 = (bf16[32,3072]{1,0:T(8,128)(2,1)S(1)}, bf16[32,3072]{1,0:T(8,128)(2,1)S(1)}, u32[]{:S(2)}, u32[]{:S(2)}) collective-permute-start(bf16[32,3072]{1,0:T(8,128)(2,1)S(1)} %get-tuple-element.58), channel_id=1, source_target_pairs={{0,1},{1,0},{2,3},{3,2},{4,5},{5,4},{6,7},{7,6},{8,9},{9,8},{10,11... | collective-permute-start | bytes 589832 | tf_op jit(solution)/shard_map/ppermute | solution.py:356
  12.1 7.4 %collective-permute-start.7 = (bf16[32,3072]{1,0:T(8,128)(2,1)S(1)}, bf16[32,3072]{1,0:T(8,128)(2,1)S(1)}, u32[]{:S(2)}, u32[]{:S(2)}) collective-permute-start(bf16[32,3072]{1,0:T(8,128)(2,1)S(1)} %get-tuple-element.59), channel_id=1, source_target_pairs={{0,2},{1,3},{2,0},{3,1},{4,6},{5,7},{6,4},{7,5},{8,10},{9,11},{10,... | collective-permute-start | bytes 589832 | tf_op jit(solution)/shard_map/ppermute | solution.py:356
  15.9 5.2 %collective-permute-start.5 = (bf16[16,1536]{1,0:T(8,128)(2,1)S(1)}, bf16[16,1536]{1,0:T(8,128)(2,1)S(1)}, u32[]{:S(2)}, u32[]{:S(2)}) collective-permute-start(bf16[16,1536]{1,0:T(8,128)(2,1)S(1)} %add_add_fusion), channel_id=1, source_target_pairs={{0,3},{1,2},{2,1},{3,0},{4,7},{5,6},{6,5},{7,4},{8,11},{9,10},{10,... | collective-permute-start | bytes 147464 | tf_op jit(solution)/shard_map/ppermute | solution.py:356
  16.5 6.0 %collective-permute-start.9 = (bf16[16,1536]{1,0:T(8,128)(2,1)S(1)}, bf16[16,1536]{1,0:T(8,128)(2,1)S(1)}, u32[]{:S(2)}, u32[]{:S(2)}) collective-permute-start(bf16[16,1536]{1,0:T(8,128)(2,1)S(1)} %add_add_fusion), channel_id=1, source_target_pairs={{0,2},{1,3},{2,0},{3,1},{4,6},{5,7},{6,4},{7,5},{8,10},{9,11},{10,... | collective-permute-start | bytes 147464 | tf_op jit(solution)/shard_map/ppermute | solution.py:356
  18.0 4.5 %collective-permute-start.8 = (bf16[16,1536]{1,0:T(8,128)(2,1)S(1)}, bf16[16,1536]{1,0:T(8,128)(2,1)S(1)}, u32[]{:S(2)}, u32[]{:S(2)}) collective-permute-start(bf16[16,1536]{1,0:T(8,128)(2,1)S(1)} %add_add_fusion), channel_id=1, source_target_pairs={{0,1},{1,0},{2,3},{3,2},{4,5},{5,4},{6,7},{7,6},{8,9},{9,8},{10,11... | collective-permute-start | bytes 147464 | tf_op jit(solution)/shard_map/ppermute | solution.py:356
  22.5 1.6 %collective-permute-start.10 = (bf16[64,1536]{1,0:T(8,128)(2,1)S(1)}, bf16[64,1536]{1,0:T(8,128)(2,1)S(1)}, u32[]{:S(2)}, u32[]{:S(2)}) collective-permute-start(bf16[64,1536]{1,0:T(8,128)(2,1)S(1)} %pad_maximum_fusion), channel_id=1, source_target_pairs={{0,4},{4,0},{8,12},{12,8},{16,20},{20,16},{24,28},{28,24},{1,5},{5... | collective-permute-start | bytes 589832 | tf_op jit(solution)/shard_map/ppermute | solution.py:356

commit v22 on v21

--- a/solution.py
+++ b/solution.py
@@ -122,9 +122,13 @@
     encoded = jnp.where(usable, spectra[...].astype(jnp.float32), UNUSABLE).astype(jnp.bfloat16)
     picked = jnp.dot(onehot, encoded, preferred_element_type=jnp.float32)
     for at, re, im in whitening(picked[:, :nbins], picked[:, nbins:], high, low, UNUSABLE, band):
-        for first, ref in ((0, own_ref), (half, other_ref)):
-            rows = slice(first, first + half)
-            ref[:, at] = jnp.concatenate([re[rows], im[rows]], axis=0).astype(ref.dtype)
+        own_rows, other_rows = (
+            jnp.concatenate([re[first : first + half], im[first : first + half]], axis=0)
+            for first in (0, half)
+        )
+        own_ref[:, at] = own_rows.astype(own_ref.dtype)
+        other_ref[: 2 * half, at] = other_rows.astype(other_ref.dtype)
+        other_ref[2 * half :, at] = own_rows.astype(other_ref.dtype)
     encoded_ref[...] = encoded.astype(encoded_ref.dtype)
     keep = channels // segments
     for step, block in enumerate(blocks):
@@ -281,12 +285,13 @@
     channels, width = spectra.shape
     keep = channels // segments
     slab = jax.ShapeDtypeStruct((sources.size, width // 2), jnp.bfloat16)
+    slabs = jax.ShapeDtypeStruct((2 * sources.size, width // 2), jnp.bfloat16)
     block = jax.ShapeDtypeStruct((keep, width), jnp.bfloat16)
     padded = pltpu.VMEM((sources.size, width // 2 + 2 * LANES), jnp.bfloat16)
     pinned = [pltpu.with_memory_space_constraint(x, pltpu.HBM) for x in (spectra, valid, sources)]
     return pl.pallas_call(
         functools.partial(encode_kernel, segments),
-        out_shape=(slab, slab) + (block,) * segments,
+        out_shape=(slab, slabs) + (block,) * segments,
         in_specs=[HBM] * 3,
         out_specs=(VMEM,) * (2 + segments),
         scratch_shapes=[
@@ -364,7 +369,7 @@
         tm_size, spectra[:, 0, :], valid.reshape(1, channels), sources
     )
     receivers[-1] = swapped(receivers[-1], "tm", tm_size, tm_size - 1)
-    own = own + swapped(other, "rcv", rcv_size, 1)
+    own = own + swapped(other, "rcv", rcv_size, 1)[: own.shape[0]]
     own, later = lax.optimization_barrier((own, receivers[1:-1]))
     last, receivers[-1] = lax.optimization_barrier((later[-1], receivers[-1]))
     receivers[1:-1] = [

time: 27.2 us -> 26 us (0.956)
  waiting for transfers between devices: 5.07 us -> 2.64 us
  starting transfers between devices: 12.9 us -> 14.2 us
    ppermute x11, waiting for transfers between devices: 5.07 us -> 2.64 us  [swapped(): return lax.ppermute(value, axis, [(i, i ^ step) for i in range(size)])]
    ppermute x11, starting transfers between devices: 12.9 us -> 14.2 us  [swapped(): return lax.ppermute(value, axis, [(i, i ^ step) for i in range(size)])]
  transfers between devices with their start and end apart: 11 -> 11, of which waited for: 4 -> 3; matrix products, arithmetic and copies ran while one was open for 0% -> 0% of each run, Pallas kernels for 14% -> 15%
where the time goes in v22:
time: 26 us; the launch traced here: 25.8 us
  starting transfers between devices  14.2 us (55%)
  Pallas kernels  8.81 us (34%)
  waiting for transfers between devices  2.64 us (10%)
    ppermute x11, starting transfers between devices, swapped(): return lax.ppermute(value, axis, [(i, i ^ step) for i in range(size)])  14.2 us
    pallas_call x3, Pallas kernels, stack_stage(): pl.pallas_call(functools.partial(stack_kernel, places, (not before, stage...  5.72 us
    ppermute x11, waiting for transfers between devices, swapped(): return lax.ppermute(value, axis, [(i, i ^ step) for i in range(size)])  2.64 us
    pallas_call x1, Pallas kernels, encode(): pl.pallas_call(functools.partial(encode_kernel, segments), out_shape=(sla...  2.08 us
    pallas_call x2, Pallas kernels, whiten_blocks(): pl.pallas_call(functools.partial(whiten_kernel, segments), out_shape=(par...  1.02 us
  transfers between devices with their start and end apart: 11, of which 3 were waited for; matrix products, arithmetic and copies ran while one was open for 0% of the time, Pallas kernels for 15%

profile of v22, /device:TPU:0, one launch (start us, length us, event | category | flops | bytes accessed | tf_op | source)
XLA Modules:
  0.0 25.8 jit_solution(6333924331490922389)
XLA Ops:
  0.0 0.0 copy-start
  0.0 2.1 %encode_and_pick.1 = (bf16[16,1536]{1,0:T(8,128)(2,1)S(1)}, bf16[32,1536]{1,0:T(8,128)(2,1)S(1)}, bf16[32,3072]{1,0:T(8,128)(2,1)S(1)}, bf16[32,3072]{1,0:T(8,12...) custom-call(bf16[128,3072]{1,0:T(8,128)(2,1)} %bitcast.3, s32[1,128]{1,0:T(1,128)} %bitcast.4, ...), custom_call_target="tpu_custom_call" | custom-call | tf_op jit(solution)/shard_map/encode_and_pick/pallas_call | solution.py:292
  2.1 0.5 %collective-permute-start = (bf16[32,1536]{1,0:T(8,128)(2,1)S(1)}, bf16[32,1536]{1,0:T(8,128)(2,1)S(1)}, u32[]{:S(2)}, u32[]{:S(2)}) collective-permute-start(bf16[32,1536]{1,0:T(8,128)(2,1)S(1)} %get-tuple-element.45), channel_id=1, source_target_pairs={{0,4},{4,0},{8,12},{12,8},{16,20},{20,16},{24,28},{28,24},{1,5},{5... | collective-permute-start | bytes 294920 | tf_op jit(solution)/shard_map/ppermute | solution.py:361
  2.6 3.5 %collective-permute-start.3 = (bf16[32,3072]{1,0:T(8,128)(2,1)S(1)}, bf16[32,3072]{1,0:T(8,128)(2,1)S(1)}, u32[]{:S(2)}, u32[]{:S(2)}) collective-permute-start(bf16[32,3072]{1,0:T(8,128)(2,1)S(1)} %get-tuple-element.51), channel_id=1, source_target_pairs={{0,3},{1,2},{2,1},{3,0},{4,7},{5,6},{6,5},{7,4},{8,11},{9,10},{10,... | collective-permute-start | bytes 589832 | tf_op jit(solution)/shard_map/ppermute | solution.py:361
  6.1 0.0 collective-permute-done
  6.1 2.7 %collective-permute-start.2 = (bf16[16,1536]{1,0:T(8,128)(2,1)S(1)}, bf16[16,1536]{1,0:T(8,128)(2,1)S(1)}, u32[]{:S(2)}, u32[]{:S(2)}) collective-permute-start(bf16[16,1536]{1,0:T(8,128)(2,1)S(1)} %slice_add_fusion), channel_id=1, source_target_pairs={{0,16},{4,20},{8,24},{12,28},{16,0},{20,4},{24,8},{28,12},{1,17},{... | collective-permute-start | bytes 147464 | tf_op jit(solution)/shard_map/ppermute | solution.py:361
  8.8 1.3 %collective-permute-start.4 = (bf16[16,1536]{1,0:T(8,128)(2,1)S(1)}, bf16[16,1536]{1,0:T(8,128)(2,1)S(1)}, u32[]{:S(2)}, u32[]{:S(2)}) collective-permute-start(bf16[16,1536]{1,0:T(8,128)(2,1)S(1)} %slice_add_fusion), channel_id=1, source_target_pairs={{0,24},{4,28},{8,16},{12,20},{16,8},{20,12},{24,0},{28,4},{1,25},{... | collective-permute-start | bytes 147464 | tf_op jit(solution)/shard_map/ppermute | solution.py:361
  10.1 0.2 collective-permute-start.1
  10.4 0.5 %collective-permute-start.6 = (bf16[32,3072]{1,0:T(8,128)(2,1)S(1)}, bf16[32,3072]{1,0:T(8,128)(2,1)S(1)}, u32[]{:S(2)}, u32[]{:S(2)}) collective-permute-start(bf16[32,3072]{1,0:T(8,128)(2,1)S(1)} %get-tuple-element.58), channel_id=1, source_target_pairs={{0,1},{1,0},{2,3},{3,2},{4,5},{5,4},{6,7},{7,6},{8,9},{9,8},{10,11... | collective-permute-start | bytes 589832 | tf_op jit(solution)/shard_map/ppermute | solution.py:361
  10.9 0.7 %collective-permute-done.3.refs_1_ = bf16[32,3072]{1,0:T(8,128)(2,1)S(1)} collective-permute-done((bf16[32,3072]{1,0:T(8,128)(2,1)S(1)}, bf16[32,3072]{1,0:T(8,128)(2,1)S(1)}, u32[]{:S(2)}, u32[]{:S(2)}) %collective-permute-start.3) | collective-permute-done | bytes 196640 | tf_op jit(solution)/shard_map/ppermute | solution.py:361
  11.6 1.7 %collective-permute-start.7 = (bf16[32,3072]{1,0:T(8,128)(2,1)S(1)}, bf16[32,3072]{1,0:T(8,128)(2,1)S(1)}, u32[]{:S(2)}, u32[]{:S(2)}) collective-permute-start(bf16[32,3072]{1,0:T(8,128)(2,1)S(1)} %get-tuple-element.59), channel_id=1, source_target_pairs={{0,2},{1,3},{2,0},{3,1},{4,6},{5,7},{6,4},{7,5},{8,10},{9,11},{10,... | collective-permute-start | bytes 589832 | tf_op jit(solution)/shard_map/ppermute | solution.py:361
  13.4 0.5 %whiten_receivers.2 = (f32[64,1536]{1,0:T(8,128)S(1)}, f32[64,1536]{1,0:T(8,128)S(1)}, f32[64,1536]{1,0:T(8,128)S(1)}, f32[64,128]{1,0:T(8,128)S(1)}) custom-call(bf16[32,3072]{1,0:T(8,128)(2,1)S(1)} %get-tuple-element.49.refs_0_, bf16[32,3072]{1,0:T(8,128)(2,1)S(1)} %collective-permute-done.3.refs_1_), custom_call_target="tpu_custom_call" | custom-call | flops 201326592 | bytes 786432 | tf_op jit(solution)/shard_map/whiten_receivers/pallas_call | solution.py:317
  13.9 0.0 collective-permute-done.2
  13.9 0.9 %collective-permute-done.4 = bf16[16,1536]{1,0:T(8,128)(2,1)S(1)} collective-permute-done((bf16[16,1536]{1,0:T(8,128)(2,1)S(1)}, bf16[16,1536]{1,0:T(8,128)(2,1)S(1)}, u32[]{:S(2)}, u32[]{:S(2)}) %collective-permute-start.4) | collective-permute-done | bytes 49184 | tf_op jit(solution)/shard_map/ppermute | solution.py:361
  14.8 0.0 collective-permute-done.1
  14.8 1.3 %collective-permute-start.5 = (bf16[16,1536]{1,0:T(8,128)(2,1)S(1)}, bf16[16,1536]{1,0:T(8,128)(2,1)S(1)}, u32[]{:S(2)}, u32[]{:S(2)}) collective-permute-start(bf16[16,1536]{1,0:T(8,128)(2,1)S(1)} %add_add_fusion), channel_id=1, source_target_pairs={{0,3},{1,2},{2,1},{3,0},{4,7},{5,6},{6,5},{7,4},{8,11},{9,10},{10,... | collective-permute-start | bytes 147464 | tf_op jit(solution)/shard_map/ppermute | solution.py:361
  16.1 1.1 %collective-permute-start.9 = (bf16[16,1536]{1,0:T(8,128)(2,1)S(1)}, bf16[16,1536]{1,0:T(8,128)(2,1)S(1)}, u32[]{:S(2)}, u32[]{:S(2)}) collective-permute-start(bf16[16,1536]{1,0:T(8,128)(2,1)S(1)} %add_add_fusion), channel_id=1, source_target_pairs={{0,2},{1,3},{2,0},{3,1},{4,6},{5,7},{6,4},{7,5},{8,10},{9,11},{10,... | collective-permute-start | bytes 147464 | tf_op jit(solution)/shard_map/ppermute | solution.py:361
  17.1 1.2 %collective-permute-start.8 = (bf16[16,1536]{1,0:T(8,128)(2,1)S(1)}, bf16[16,1536]{1,0:T(8,128)(2,1)S(1)}, u32[]{:S(2)}, u32[]{:S(2)}) collective-permute-start(bf16[16,1536]{1,0:T(8,128)(2,1)S(1)} %add_add_fusion), channel_id=1, source_target_pairs={{0,1},{1,0},{2,3},{3,2},{4,5},{5,4},{6,7},{7,6},{8,9},{9,8},{10,11... | collective-permute-start | bytes 147464 | tf_op jit(solution)/shard_map/ppermute | solution.py:361
  18.3 0.0 collective-permute-done.6.refs_0_
  18.3 1.0 %collective-permute-done.7.refs_1_ = bf16[32,3072]{1,0:T(8,128)(2,1)S(1)} collective-permute-done((bf16[32,3072]{1,0:T(8,128)(2,1)S(1)}, bf16[32,3072]{1,0:T(8,128)(2,1)S(1)}, u32[]{:S(2)}, u32[]{:S(2)}) %collective-permute-start.7) | collective-permute-done | bytes 196640 | tf_op jit(solution)/shard_map/ppermute | solution.py:361
  19.3 0.5 %whiten_receivers.3 = (f32[64,1536]{1,0:T(8,128)S(1)}, f32[64,1536]{1,0:T(8,128)S(1)}, f32[64,1536]{1,0:T(8,128)S(1)}, f32[64,128]{1,0:T(8,128)S(1)}) custom-call(bf16[32,3072]{1,0:T(8,128)(2,1)S(1)} %collective-permute-done.6.refs_0_, bf16[32,3072]{1,0:T(8,128)(2,1)S(1)} %collective-permute-done.7.refs_1_), custom_call_target="tpu_custom_call" | custom-call | flops 201326592 | bytes 786432 | tf_op jit(solution)/shard_map/whiten_receivers/pallas_call | solution.py:317
  19.9 0.0 collective-permute-done.5
  19.9 0.0 copy-done
  19.9 1.4 %stack_sums.1 = (f32[2,256,256]{2,1,0:T(8,128)S(1)}, f32[256,128]{1,0:T(8,128)S(1)}) custom-call(bf16[32,1536]{1,0:T(8,128)(2,1)S(1)} %pad_maximum_fusion.1.refs_0_, f32[64,1536]{1,0:T(8,128)S(1)} %get-tuple-element.65.refs_1_, f32[64,1536]{1,0:T(8,128)S(1)} %get-tuple-element.66.refs_2_, f32[64,1536]{1,0:T(8,128)S(1)} %get-tuple-element.67.refs_3_, ...), custom_call_target="tpu_custom_call" | custom-call | flops 471859200 | bytes 3145728 | tf_op jit(solution)/shard_map/stack_sums/pallas_call | solution.py:346
  21.3 0.0 collective-permute-done.9
  21.3 0.0 collective-permute-done.8
  21.3 0.1 collective-permute-start.10
  21.4 1.5 %stack_result.1.refs_10_ = f32[256,301]{1,0:T(8,128)S(1)} custom-call(bf16[32,1536]{1,0:T(8,128)(2,1)S(1)} %pad_maximum_fusion.2.refs_0_, f32[64,1536]{1,0:T(8,128)S(1)} %get-tuple-element.77.refs_1_.refs_5_, f32[64,1536]{1,0:T(8,128)S(1)} %get-tuple-element.78.refs_2_.refs_6_, f32[64,1536]{1,0:T(8,128)S(1)} %get-tuple-element.79.refs_3_.refs_7_, ...), custom_call_target="tpu_custom_call" | custom-call | flops 471859200 | bytes 3145728 | tf_op jit(solution)/shard_map/stack_result/pallas_call | solution.py:346
  22.9 0.0 collective-permute-done.10.refs_0_
  22.9 2.9 %stack_store.1 = f32[512,301]{1,0:T(8,128)} custom-call(bf16[64,1536]{1,0:T(8,128)(2,1)S(1)} %collective-permute-done.10.refs_0_, f32[64,1536]{1,0:T(8,128)S(1)} %get-tuple-element.65.refs_1_, f32[64,1536]{1,0:T(8,128)S(1)} %get-tuple-element.66.refs_2_, f32[64,1536]{1,0:T(8,128)S(1)} %get-tuple-element.67.refs_3_, f32[64,128]{1,0:T(8,128)S(1)} %get-tuple-element.68.refs_4_, ...), custom_call_target="tpu_custom_call" | custom-call | flops 471859200 | bytes 3145728 | tf_op jit(solution)/shard_map/stack_store/pallas_call | solution.py:346
  (5 shorter events, 0.1 us)
Async XLA Ops:
  0.0 19.9 %copy-start = (bf16[3072,256]{1,0:T(8,128)(2,1)S(1)}, bf16[3072,256]{1,0:T(8,128)(2,1)}, u32[]{:S(2)}) copy-start(bf16[3072,256]{1,0:T(8,128)(2,1)} %constant.2.clone.refs_5_.refs_9_) | copy-start | bytes 4718596
  2.1 4.0 %collective-permute-start = (bf16[32,1536]{1,0:T(8,128)(2,1)S(1)}, bf16[32,1536]{1,0:T(8,128)(2,1)S(1)}, u32[]{:S(2)}, u32[]{:S(2)}) collective-permute-start(bf16[32,1536]{1,0:T(8,128)(2,1)S(1)} %get-tuple-element.45), channel_id=1, source_target_pairs={{0,4},{4,0},{8,12},{12,8},{16,20},{20,16},{24,28},{28,24},{1,5},{5... | collective-permute-start | bytes 294920 | tf_op jit(solution)/shard_map/ppermute | solution.py:361
  2.6 9.0 %collective-permute-start.3 = (bf16[32,3072]{1,0:T(8,128)(2,1)S(1)}, bf16[32,3072]{1,0:T(8,128)(2,1)S(1)}, u32[]{:S(2)}, u32[]{:S(2)}) collective-permute-start(bf16[32,3072]{1,0:T(8,128)(2,1)S(1)} %get-tuple-element.51), channel_id=1, source_target_pairs={{0,3},{1,2},{2,1},{3,0},{4,7},{5,6},{6,5},{7,4},{8,11},{9,10},{10,... | collective-permute-start | bytes 589832 | tf_op jit(solution)/shard_map/ppermute | solution.py:361
  6.1 7.7 %collective-permute-start.2 = (bf16[16,1536]{1,0:T(8,128)(2,1)S(1)}, bf16[16,1536]{1,0:T(8,128)(2,1)S(1)}, u32[]{:S(2)}, u32[]{:S(2)}) collective-permute-start(bf16[16,1536]{1,0:T(8,128)(2,1)S(1)} %slice_add_fusion), channel_id=1, source_target_pairs={{0,16},{4,20},{8,24},{12,28},{16,0},{20,4},{24,8},{28,12},{1,17},{... | collective-permute-start | bytes 147464 | tf_op jit(solution)/shard_map/ppermute | solution.py:361
  8.8 6.0 %collective-permute-start.4 = (bf16[16,1536]{1,0:T(8,128)(2,1)S(1)}, bf16[16,1536]{1,0:T(8,128)(2,1)S(1)}, u32[]{:S(2)}, u32[]{:S(2)}) collective-permute-start(bf16[16,1536]{1,0:T(8,128)(2,1)S(1)} %slice_add_fusion), channel_id=1, source_target_pairs={{0,24},{4,28},{8,16},{12,20},{16,8},{20,12},{24,0},{28,4},{1,25},{... | collective-permute-start | bytes 147464 | tf_op jit(solution)/shard_map/ppermute | solution.py:361
  10.1 4.6 %collective-permute-start.1 = (bf16[16,1536]{1,0:T(8,128)(2,1)S(1)}, bf16[16,1536]{1,0:T(8,128)(2,1)S(1)}, u32[]{:S(2)}, u32[]{:S(2)}) collective-permute-start(bf16[16,1536]{1,0:T(8,128)(2,1)S(1)} %slice_add_fusion), channel_id=1, source_target_pairs={{0,8},{4,12},{8,0},{12,4},{16,24},{20,28},{24,16},{28,20},{1,9},{5... | collective-permute-start | bytes 147464 | tf_op jit(solution)/shard_map/ppermute | solution.py:361
  10.4 8.0 %collective-permute-start.6 = (bf16[32,3072]{1,0:T(8,128)(2,1)S(1)}, bf16[32,3072]{1,0:T(8,128)(2,1)S(1)}, u32[]{:S(2)}, u32[]{:S(2)}) collective-permute-start(bf16[32,3072]{1,0:T(8,128)(2,1)S(1)} %get-tuple-element.58), channel_id=1, source_target_pairs={{0,1},{1,0},{2,3},{3,2},{4,5},{5,4},{6,7},{7,6},{8,9},{9,8},{10,11... | collective-permute-start | bytes 589832 | tf_op jit(solution)/shard_map/ppermute | solution.py:361
  11.6 7.7 %collective-permute-start.7 = (bf16[32,3072]{1,0:T(8,128)(2,1)S(1)}, bf16[32,3072]{1,0:T(8,128)(2,1)S(1)}, u32[]{:S(2)}, u32[]{:S(2)}) collective-permute-start(bf16[32,3072]{1,0:T(8,128)(2,1)S(1)} %get-tuple-element.59), channel_id=1, source_target_pairs={{0,2},{1,3},{2,0},{3,1},{4,6},{5,7},{6,4},{7,5},{8,10},{9,11},{10,... | collective-permute-start | bytes 589832 | tf_op jit(solution)/shard_map/ppermute | solution.py:361
  14.8 5.1 %collective-permute-start.5 = (bf16[16,1536]{1,0:T(8,128)(2,1)S(1)}, bf16[16,1536]{1,0:T(8,128)(2,1)S(1)}, u32[]{:S(2)}, u32[]{:S(2)}) collective-permute-start(bf16[16,1536]{1,0:T(8,128)(2,1)S(1)} %add_add_fusion), channel_id=1, source_target_pairs={{0,3},{1,2},{2,1},{3,0},{4,7},{5,6},{6,5},{7,4},{8,11},{9,10},{10,... | collective-permute-start | bytes 147464 | tf_op jit(solution)/shard_map/ppermute | solution.py:361
  16.1 5.2 %collective-permute-start.9 = (bf16[16,1536]{1,0:T(8,128)(2,1)S(1)}, bf16[16,1536]{1,0:T(8,128)(2,1)S(1)}, u32[]{:S(2)}, u32[]{:S(2)}) collective-permute-start(bf16[16,1536]{1,0:T(8,128)(2,1)S(1)} %add_add_fusion), channel_id=1, source_target_pairs={{0,2},{1,3},{2,0},{3,1},{4,6},{5,7},{6,4},{7,5},{8,10},{9,11},{10,... | collective-permute-start | bytes 147464 | tf_op jit(solution)/shard_map/ppermute | solution.py:361
  17.1 4.1 %collective-permute-start.8 = (bf16[16,1536]{1,0:T(8,128)(2,1)S(1)}, bf16[16,1536]{1,0:T(8,128)(2,1)S(1)}, u32[]{:S(2)}, u32[]{:S(2)}) collective-permute-start(bf16[16,1536]{1,0:T(8,128)(2,1)S(1)} %add_add_fusion), channel_id=1, source_target_pairs={{0,1},{1,0},{2,3},{3,2},{4,5},{5,4},{6,7},{7,6},{8,9},{9,8},{10,11... | collective-permute-start | bytes 147464 | tf_op jit(solution)/shard_map/ppermute | solution.py:361
  21.3 1.6 %collective-permute-start.10 = (bf16[64,1536]{1,0:T(8,128)(2,1)S(1)}, bf16[64,1536]{1,0:T(8,128)(2,1)S(1)}, u32[]{:S(2)}, u32[]{:S(2)}) collective-permute-start(bf16[64,1536]{1,0:T(8,128)(2,1)S(1)} %pad_maximum_fusion), channel_id=1, source_target_pairs={{0,4},{4,0},{8,12},{12,8},{16,20},{20,16},{24,28},{28,24},{1,5},{5... | collective-permute-start | bytes 589832 | tf_op jit(solution)/shard_map/ppermute | solution.py:361

commit v23 on v22

--- a/solution.py
+++ b/solution.py
@@ -371,15 +371,16 @@
     receivers[-1] = swapped(receivers[-1], "tm", tm_size, tm_size - 1)
     own = own + swapped(other, "rcv", rcv_size, 1)[: own.shape[0]]
     own, later = lax.optimization_barrier((own, receivers[1:-1]))
-    last, receivers[-1] = lax.optimization_barrier((later[-1], receivers[-1]))
-    receivers[1:-1] = [
-        swapped(block, "tm", tm_size, place) for place, block in enumerate(later[:-1] + [last], 1)
+    receivers[1:-2] = [
+        swapped(block, "tm", tm_size, place) for place, block in enumerate(later[:-1], 1)
     ]
     step = 2
     while step < rcv_size:
         wide = min(4, rcv_size // step)
         parts = [swapped(own, "rcv", rcv_size, place * step) for place in range(1, wide)]
         if step == 2:
+            parts[0], last = lax.optimization_barrier((parts[0], later[-1]))
+            receivers[-2] = swapped(last, "tm", tm_size, tm_size - 2)
             early = tuple(whiten_blocks([receivers[0], receivers[-1]]))
             parts[-2:-1], early = lax.optimization_barrier((parts[-2:-1], early))
         own = functools.reduce(jnp.add, parts, own)

time: 26 us -> 27.4 us (1.054)
  waiting for transfers between devices: 2.64 us -> 4.38 us
  starting transfers between devices: 14.2 us -> 13.9 us
    ppermute x11, waiting for transfers between devices: 2.64 us -> 4.38 us  [swapped(): return lax.ppermute(value, axis, [(i, i ^ step) for i in range(size)])]
  transfers between devices with their start and end apart: 11 -> 11, of which waited for: 3 -> 3; matrix products, arithmetic and copies ran while one was open for 0% -> 0% of each run, Pallas kernels for 15% -> 14%
where the time goes in v23:
time: 27.4 us; the launch traced here: 27.3 us
  starting transfers between devices  13.9 us (51%)
  Pallas kernels  8.81 us (32%)
  waiting for transfers between devices  4.38 us (16%)
    ppermute x11, starting transfers between devices, swapped(): return lax.ppermute(value, axis, [(i, i ^ step) for i in range(size)])  13.9 us
    pallas_call x3, Pallas kernels, stack_stage(): pl.pallas_call(functools.partial(stack_kernel, places, (not before, stage...  5.71 us
    ppermute x11, waiting for transfers between devices, swapped(): return lax.ppermute(value, axis, [(i, i ^ step) for i in range(size)])  4.38 us
    pallas_call x1, Pallas kernels, encode(): pl.pallas_call(functools.partial(encode_kernel, segments), out_shape=(sla...  2.08 us
    pallas_call x2, Pallas kernels, whiten_blocks(): pl.pallas_call(functools.partial(whiten_kernel, segments), out_shape=(par...  1.02 us
  transfers between devices with their start and end apart: 11, of which 3 were waited for; matrix products, arithmetic and copies ran while one was open for 0% of the time, Pallas kernels for 14%

profile of v23, /device:TPU:0, one launch (start us, length us, event | category | flops | bytes accessed | tf_op | source)
XLA Modules:
  0.0 27.3 jit_solution(15349722129823686285)
XLA Ops:
  0.0 0.0 copy-start
  0.0 2.1 %encode_and_pick.1 = (bf16[16,1536]{1,0:T(8,128)(2,1)S(1)}, bf16[32,1536]{1,0:T(8,128)(2,1)S(1)}, bf16[32,3072]{1,0:T(8,128)(2,1)S(1)}, bf16[32,3072]{1,0:T(8,12...) custom-call(bf16[128,3072]{1,0:T(8,128)(2,1)} %bitcast.3, s32[1,128]{1,0:T(1,128)} %bitcast.4, ...), custom_call_target="tpu_custom_call" | custom-call | tf_op jit(solution)/shard_map/encode_and_pick/pallas_call | solution.py:292
  2.1 0.5 %collective-permute-start = (bf16[32,1536]{1,0:T(8,128)(2,1)S(1)}, bf16[32,1536]{1,0:T(8,128)(2,1)S(1)}, u32[]{:S(2)}, u32[]{:S(2)}) collective-permute-start(bf16[32,1536]{1,0:T(8,128)(2,1)S(1)} %get-tuple-element.45), channel_id=1, source_target_pairs={{0,4},{4,0},{8,12},{12,8},{16,20},{20,16},{24,28},{28,24},{1,5},{5... | collective-permute-start | bytes 294920 | tf_op jit(solution)/shard_map/ppermute | solution.py:361
  2.6 3.5 %collective-permute-start.3 = (bf16[32,3072]{1,0:T(8,128)(2,1)S(1)}, bf16[32,3072]{1,0:T(8,128)(2,1)S(1)}, u32[]{:S(2)}, u32[]{:S(2)}) collective-permute-start(bf16[32,3072]{1,0:T(8,128)(2,1)S(1)} %get-tuple-element.52), channel_id=1, source_target_pairs={{0,3},{1,2},{2,1},{3,0},{4,7},{5,6},{6,5},{7,4},{8,11},{9,10},{10,... | collective-permute-start | bytes 589832 | tf_op jit(solution)/shard_map/ppermute | solution.py:361
  6.1 0.0 collective-permute-done
  6.1 1.6 %collective-permute-start.1 = (bf16[16,1536]{1,0:T(8,128)(2,1)S(1)}, bf16[16,1536]{1,0:T(8,128)(2,1)S(1)}, u32[]{:S(2)}, u32[]{:S(2)}) collective-permute-start(bf16[16,1536]{1,0:T(8,128)(2,1)S(1)} %slice_add_fusion), channel_id=1, source_target_pairs={{0,8},{4,12},{8,0},{12,4},{16,24},{20,28},{24,16},{28,20},{1,9},{5... | collective-permute-start | bytes 147464 | tf_op jit(solution)/shard_map/ppermute | solution.py:361
  7.8 2.6 %collective-permute-start.2 = (bf16[16,1536]{1,0:T(8,128)(2,1)S(1)}, bf16[16,1536]{1,0:T(8,128)(2,1)S(1)}, u32[]{:S(2)}, u32[]{:S(2)}) collective-permute-start(bf16[16,1536]{1,0:T(8,128)(2,1)S(1)} %slice_add_fusion), channel_id=1, source_target_pairs={{0,16},{4,20},{8,24},{12,28},{16,0},{20,4},{24,8},{28,12},{1,17},{... | collective-permute-start | bytes 147464 | tf_op jit(solution)/shard_map/ppermute | solution.py:361
  10.4 0.2 collective-permute-start.4
  10.6 0.5 %collective-permute-start.6 = (bf16[32,3072]{1,0:T(8,128)(2,1)S(1)}, bf16[32,3072]{1,0:T(8,128)(2,1)S(1)}, u32[]{:S(2)}, u32[]{:S(2)}) collective-permute-start(bf16[32,3072]{1,0:T(8,128)(2,1)S(1)} %get-tuple-element.58), channel_id=1, source_target_pairs={{0,1},{1,0},{2,3},{3,2},{4,5},{5,4},{6,7},{7,6},{8,9},{9,8},{10,11... | collective-permute-start | bytes 589832 | tf_op jit(solution)/shard_map/ppermute | solution.py:361
  11.1 0.0 collective-permute-done.1
  11.1 1.2 %collective-permute-start.7 = (bf16[32,3072]{1,0:T(8,128)(2,1)S(1)}, bf16[32,3072]{1,0:T(8,128)(2,1)S(1)}, u32[]{:S(2)}, u32[]{:S(2)}) collective-permute-start(bf16[32,3072]{1,0:T(8,128)(2,1)S(1)} %get-tuple-element.59), channel_id=1, source_target_pairs={{0,2},{1,3},{2,0},{3,1},{4,6},{5,7},{6,4},{7,5},{8,10},{9,11},{10,... | collective-permute-start | bytes 589832 | tf_op jit(solution)/shard_map/ppermute | solution.py:361
  12.4 0.0 collective-permute-done.3.refs_1_
  12.4 0.5 %whiten_receivers.2 = (f32[64,1536]{1,0:T(8,128)S(1)}, f32[64,1536]{1,0:T(8,128)S(1)}, f32[64,1536]{1,0:T(8,128)S(1)}, f32[64,128]{1,0:T(8,128)S(1)}) custom-call(bf16[32,3072]{1,0:T(8,128)(2,1)S(1)} %get-tuple-element.51.refs_0_, bf16[32,3072]{1,0:T(8,128)(2,1)S(1)} %collective-permute-done.3.refs_1_), custom_call_target="tpu_custom_call" | custom-call | flops 201326592 | bytes 786432 | tf_op jit(solution)/shard_map/whiten_receivers/pallas_call | solution.py:317
  12.9 0.8 %collective-permute-done.2 = bf16[16,1536]{1,0:T(8,128)(2,1)S(1)} collective-permute-done((bf16[16,1536]{1,0:T(8,128)(2,1)S(1)}, bf16[16,1536]{1,0:T(8,128)(2,1)S(1)}, u32[]{:S(2)}, u32[]{:S(2)}) %collective-permute-start.2) | collective-permute-done | bytes 49184 | tf_op jit(solution)/shard_map/ppermute | solution.py:361
  13.7 2.6 %collective-permute-done.4 = bf16[16,1536]{1,0:T(8,128)(2,1)S(1)} collective-permute-done((bf16[16,1536]{1,0:T(8,128)(2,1)S(1)}, bf16[16,1536]{1,0:T(8,128)(2,1)S(1)}, u32[]{:S(2)}, u32[]{:S(2)}) %collective-permute-start.4) | collective-permute-done | bytes 49184 | tf_op jit(solution)/shard_map/ppermute | solution.py:361
  16.3 1.3 %collective-permute-start.5 = (bf16[16,1536]{1,0:T(8,128)(2,1)S(1)}, bf16[16,1536]{1,0:T(8,128)(2,1)S(1)}, u32[]{:S(2)}, u32[]{:S(2)}) collective-permute-start(bf16[16,1536]{1,0:T(8,128)(2,1)S(1)} %add_add_fusion), channel_id=1, source_target_pairs={{0,3},{1,2},{2,1},{3,0},{4,7},{5,6},{6,5},{7,4},{8,11},{9,10},{10,... | collective-permute-start | bytes 147464 | tf_op jit(solution)/shard_map/ppermute | solution.py:361
  17.6 0.8 %collective-permute-start.9 = (bf16[16,1536]{1,0:T(8,128)(2,1)S(1)}, bf16[16,1536]{1,0:T(8,128)(2,1)S(1)}, u32[]{:S(2)}, u32[]{:S(2)}) collective-permute-start(bf16[16,1536]{1,0:T(8,128)(2,1)S(1)} %add_add_fusion), channel_id=1, source_target_pairs={{0,2},{1,3},{2,0},{3,1},{4,6},{5,7},{6,4},{7,5},{8,10},{9,11},{10,... | collective-permute-start | bytes 147464 | tf_op jit(solution)/shard_map/ppermute | solution.py:361
  18.3 1.5 %collective-permute-start.8 = (bf16[16,1536]{1,0:T(8,128)(2,1)S(1)}, bf16[16,1536]{1,0:T(8,128)(2,1)S(1)}, u32[]{:S(2)}, u32[]{:S(2)}) collective-permute-start(bf16[16,1536]{1,0:T(8,128)(2,1)S(1)} %add_add_fusion), channel_id=1, source_target_pairs={{0,1},{1,0},{2,3},{3,2},{4,5},{5,4},{6,7},{7,6},{8,9},{9,8},{10,11... | collective-permute-start | bytes 147464 | tf_op jit(solution)/shard_map/ppermute | solution.py:361
  19.8 0.0 collective-permute-done.6.refs_0_
  19.8 0.0 collective-permute-done.7.refs_1_
  19.8 0.5 %whiten_receivers.3 = (f32[64,1536]{1,0:T(8,128)S(1)}, f32[64,1536]{1,0:T(8,128)S(1)}, f32[64,1536]{1,0:T(8,128)S(1)}, f32[64,128]{1,0:T(8,128)S(1)}) custom-call(bf16[32,3072]{1,0:T(8,128)(2,1)S(1)} %collective-permute-done.6.refs_0_, bf16[32,3072]{1,0:T(8,128)(2,1)S(1)} %collective-permute-done.7.refs_1_), custom_call_target="tpu_custom_call" | custom-call | flops 201326592 | bytes 786432 | tf_op jit(solution)/shard_map/whiten_receivers/pallas_call | solution.py:317
  20.4 1.0 %collective-permute-done.5 = bf16[16,1536]{1,0:T(8,128)(2,1)S(1)} collective-permute-done((bf16[16,1536]{1,0:T(8,128)(2,1)S(1)}, bf16[16,1536]{1,0:T(8,128)(2,1)S(1)}, u32[]{:S(2)}, u32[]{:S(2)}) %collective-permute-start.5) | collective-permute-done | bytes 49184 | tf_op jit(solution)/shard_map/ppermute | solution.py:361
  21.4 0.0 copy-done
  21.4 1.4 %stack_sums.1 = (f32[2,256,256]{2,1,0:T(8,128)S(1)}, f32[256,128]{1,0:T(8,128)S(1)}) custom-call(bf16[32,1536]{1,0:T(8,128)(2,1)S(1)} %pad_maximum_fusion.1.refs_0_, f32[64,1536]{1,0:T(8,128)S(1)} %get-tuple-element.65.refs_1_, f32[64,1536]{1,0:T(8,128)S(1)} %get-tuple-element.66.refs_2_, f32[64,1536]{1,0:T(8,128)S(1)} %get-tuple-element.67.refs_3_, ...), custom_call_target="tpu_custom_call" | custom-call | flops 471859200 | bytes 3145728 | tf_op jit(solution)/shard_map/stack_sums/pallas_call | solution.py:346
  22.7 0.0 collective-permute-done.9
  22.7 0.0 collective-permute-done.8
  22.8 0.1 collective-permute-start.10
  22.9 1.5 %stack_result.1.refs_10_ = f32[256,301]{1,0:T(8,128)S(1)} custom-call(bf16[32,1536]{1,0:T(8,128)(2,1)S(1)} %pad_maximum_fusion.2.refs_0_, f32[64,1536]{1,0:T(8,128)S(1)} %get-tuple-element.77.refs_1_.refs_5_, f32[64,1536]{1,0:T(8,128)S(1)} %get-tuple-element.78.refs_2_.refs_6_, f32[64,1536]{1,0:T(8,128)S(1)} %get-tuple-element.79.refs_3_.refs_7_, ...), custom_call_target="tpu_custom_call" | custom-call | flops 471859200 | bytes 3145728 | tf_op jit(solution)/shard_map/stack_result/pallas_call | solution.py:346
  24.3 0.0 collective-permute-done.10.refs_0_
  24.4 2.9 %stack_store.1 = f32[512,301]{1,0:T(8,128)} custom-call(bf16[64,1536]{1,0:T(8,128)(2,1)S(1)} %collective-permute-done.10.refs_0_, f32[64,1536]{1,0:T(8,128)S(1)} %get-tuple-element.65.refs_1_, f32[64,1536]{1,0:T(8,128)S(1)} %get-tuple-element.66.refs_2_, f32[64,1536]{1,0:T(8,128)S(1)} %get-tuple-element.67.refs_3_, f32[64,128]{1,0:T(8,128)S(1)} %get-tuple-element.68.refs_4_, ...), custom_call_target="tpu_custom_call" | custom-call | flops 471859200 | bytes 3145728 | tf_op jit(solution)/shard_map/stack_store/pallas_call | solution.py:346
  (5 shorter events, 0.1 us)
Async XLA Ops:
  0.0 21.4 %copy-start = (bf16[3072,256]{1,0:T(8,128)(2,1)S(1)}, bf16[3072,256]{1,0:T(8,128)(2,1)}, u32[]{:S(2)}) copy-start(bf16[3072,256]{1,0:T(8,128)(2,1)} %constant.2.clone.refs_5_.refs_9_) | copy-start | bytes 4718596
  2.1 4.0 %collective-permute-start = (bf16[32,1536]{1,0:T(8,128)(2,1)S(1)}, bf16[32,1536]{1,0:T(8,128)(2,1)S(1)}, u32[]{:S(2)}, u32[]{:S(2)}) collective-permute-start(bf16[32,1536]{1,0:T(8,128)(2,1)S(1)} %get-tuple-element.45), channel_id=1, source_target_pairs={{0,4},{4,0},{8,12},{12,8},{16,20},{20,16},{24,28},{28,24},{1,5},{5... | collective-permute-start | bytes 294920 | tf_op jit(solution)/shard_map/ppermute | solution.py:361
  2.6 9.8 %collective-permute-start.3 = (bf16[32,3072]{1,0:T(8,128)(2,1)S(1)}, bf16[32,3072]{1,0:T(8,128)(2,1)S(1)}, u32[]{:S(2)}, u32[]{:S(2)}) collective-permute-start(bf16[32,3072]{1,0:T(8,128)(2,1)S(1)} %get-tuple-element.52), channel_id=1, source_target_pairs={{0,3},{1,2},{2,1},{3,0},{4,7},{5,6},{6,5},{7,4},{8,11},{9,10},{10,... | collective-permute-start | bytes 589832 | tf_op jit(solution)/shard_map/ppermute | solution.py:361
  6.1 5.0 %collective-permute-start.1 = (bf16[16,1536]{1,0:T(8,128)(2,1)S(1)}, bf16[16,1536]{1,0:T(8,128)(2,1)S(1)}, u32[]{:S(2)}, u32[]{:S(2)}) collective-permute-start(bf16[16,1536]{1,0:T(8,128)(2,1)S(1)} %slice_add_fusion), channel_id=1, source_target_pairs={{0,8},{4,12},{8,0},{12,4},{16,24},{20,28},{24,16},{28,20},{1,9},{5... | collective-permute-start | bytes 147464 | tf_op jit(solution)/shard_map/ppermute | solution.py:361
  7.8 5.9 %collective-permute-start.2 = (bf16[16,1536]{1,0:T(8,128)(2,1)S(1)}, bf16[16,1536]{1,0:T(8,128)(2,1)S(1)}, u32[]{:S(2)}, u32[]{:S(2)}) collective-permute-start(bf16[16,1536]{1,0:T(8,128)(2,1)S(1)} %slice_add_fusion), channel_id=1, source_target_pairs={{0,16},{4,20},{8,24},{12,28},{16,0},{20,4},{24,8},{28,12},{1,17},{... | collective-permute-start | bytes 147464 | tf_op jit(solution)/shard_map/ppermute | solution.py:361
  10.4 5.9 %collective-permute-start.4 = (bf16[16,1536]{1,0:T(8,128)(2,1)S(1)}, bf16[16,1536]{1,0:T(8,128)(2,1)S(1)}, u32[]{:S(2)}, u32[]{:S(2)}) collective-permute-start(bf16[16,1536]{1,0:T(8,128)(2,1)S(1)} %slice_add_fusion), channel_id=1, source_target_pairs={{0,24},{4,28},{8,16},{12,20},{16,8},{20,12},{24,0},{28,4},{1,25},{... | collective-permute-start | bytes 147464 | tf_op jit(solution)/shard_map/ppermute | solution.py:361
  10.6 9.2 %collective-permute-start.6 = (bf16[32,3072]{1,0:T(8,128)(2,1)S(1)}, bf16[32,3072]{1,0:T(8,128)(2,1)S(1)}, u32[]{:S(2)}, u32[]{:S(2)}) collective-permute-start(bf16[32,3072]{1,0:T(8,128)(2,1)S(1)} %get-tuple-element.58), channel_id=1, source_target_pairs={{0,1},{1,0},{2,3},{3,2},{4,5},{5,4},{6,7},{7,6},{8,9},{9,8},{10,11... | collective-permute-start | bytes 589832 | tf_op jit(solution)/shard_map/ppermute | solution.py:361
  11.1 8.7 %collective-permute-start.7 = (bf16[32,3072]{1,0:T(8,128)(2,1)S(1)}, bf16[32,3072]{1,0:T(8,128)(2,1)S(1)}, u32[]{:S(2)}, u32[]{:S(2)}) collective-permute-start(bf16[32,3072]{1,0:T(8,128)(2,1)S(1)} %get-tuple-element.59), channel_id=1, source_target_pairs={{0,2},{1,3},{2,0},{3,1},{4,6},{5,7},{6,4},{7,5},{8,10},{9,11},{10,... | collective-permute-start | bytes 589832 | tf_op jit(solution)/shard_map/ppermute | solution.py:361
  16.3 5.1 %collective-permute-start.5 = (bf16[16,1536]{1,0:T(8,128)(2,1)S(1)}, bf16[16,1536]{1,0:T(8,128)(2,1)S(1)}, u32[]{:S(2)}, u32[]{:S(2)}) collective-permute-start(bf16[16,1536]{1,0:T(8,128)(2,1)S(1)} %add_add_fusion), channel_id=1, source_target_pairs={{0,3},{1,2},{2,1},{3,0},{4,7},{5,6},{6,5},{7,4},{8,11},{9,10},{10,... | collective-permute-start | bytes 147464 | tf_op jit(solution)/shard_map/ppermute | solution.py:361
  17.6 5.2 %collective-permute-start.9 = (bf16[16,1536]{1,0:T(8,128)(2,1)S(1)}, bf16[16,1536]{1,0:T(8,128)(2,1)S(1)}, u32[]{:S(2)}, u32[]{:S(2)}) collective-permute-start(bf16[16,1536]{1,0:T(8,128)(2,1)S(1)} %add_add_fusion), channel_id=1, source_target_pairs={{0,2},{1,3},{2,0},{3,1},{4,6},{5,7},{6,4},{7,5},{8,10},{9,11},{10,... | collective-permute-start | bytes 147464 | tf_op jit(solution)/shard_map/ppermute | solution.py:361
  18.3 4.4 %collective-permute-start.8 = (bf16[16,1536]{1,0:T(8,128)(2,1)S(1)}, bf16[16,1536]{1,0:T(8,128)(2,1)S(1)}, u32[]{:S(2)}, u32[]{:S(2)}) collective-permute-start(bf16[16,1536]{1,0:T(8,128)(2,1)S(1)} %add_add_fusion), channel_id=1, source_target_pairs={{0,1},{1,0},{2,3},{3,2},{4,5},{5,4},{6,7},{7,6},{8,9},{9,8},{10,11... | collective-permute-start | bytes 147464 | tf_op jit(solution)/shard_map/ppermute | solution.py:361
  22.8 1.6 %collective-permute-start.10 = (bf16[64,1536]{1,0:T(8,128)(2,1)S(1)}, bf16[64,1536]{1,0:T(8,128)(2,1)S(1)}, u32[]{:S(2)}, u32[]{:S(2)}) collective-permute-start(bf16[64,1536]{1,0:T(8,128)(2,1)S(1)} %pad_maximum_fusion), channel_id=1, source_target_pairs={{0,4},{4,0},{8,12},{12,8},{16,20},{20,16},{24,28},{28,24},{1,5},{5... | collective-permute-start | bytes 589832 | tf_op jit(solution)/shard_map/ppermute | solution.py:361

commit v24 on v22

--- a/solution.py
+++ b/solution.py
@@ -185,7 +185,7 @@
     src_valid = jnp.where(usable[:, :LANES], 1.0, 0.0)
     for ref, value in ((src_re, real), (src_diff, imag - real), (src_sum, imag + real)):
         for block in range(nbins // LANES):
-            ref[block] = value[:, block * LANES : (block + 1) * LANES]
+            ref[block, : segments * count] = value[:, block * LANES : (block + 1) * LANES]
     tile = keep if segments <= 2 else min(keep, 16)
 
     def spread(ref, block, row):
@@ -331,7 +331,7 @@
 def stack_stage(keep, slabs, places, receivers, table, stage, before=(), ready=()):
     count, nbins = slabs.shape[0] // (2 * len(places)), slabs.shape[1]
     rows, lags = count * keep, 2 * LAG + 1
-    part = pltpu.VMEM((nbins // LANES, len(places) * count, LANES), jnp.float32)
+    part = pltpu.VMEM((nbins // LANES, len(places) * count + 8, LANES), jnp.float32)
     cross = pltpu.VMEM((2, nbins // LANES, rows, LANES), kind_for(keep))
     scratch = [part, part, part, cross]
     sums = (

time: 26 us -> 25.9 us (level)
  no operation moved by 1% of the time
where the time goes in v24:
time: 25.9 us; the launch traced here: 25.8 us
  starting transfers between devices  14.2 us (55%)
  Pallas kernels  8.8 us (34%)
  waiting for transfers between devices  2.64 us (10%)
    ppermute x11, starting transfers between devices, swapped(): return lax.ppermute(value, axis, [(i, i ^ step) for i in range(size)])  14.2 us
    pallas_call x3, Pallas kernels, stack_stage(): pl.pallas_call(functools.partial(stack_kernel, places, (not before, stage...  5.7 us
    ppermute x11, waiting for transfers between devices, swapped(): return lax.ppermute(value, axis, [(i, i ^ step) for i in range(size)])  2.64 us
    pallas_call x1, Pallas kernels, encode(): pl.pallas_call(functools.partial(encode_kernel, segments), out_shape=(sla...  2.08 us
    pallas_call x2, Pallas kernels, whiten_blocks(): pl.pallas_call(functools.partial(whiten_kernel, segments), out_shape=(par...  1.02 us
  transfers between devices with their start and end apart: 11, of which 3 were waited for; matrix products, arithmetic and copies ran while one was open for 0% of the time, Pallas kernels for 15%

profile of v24, /device:TPU:0, one launch (start us, length us, event | category | flops | bytes accessed | tf_op | source)
XLA Modules:
  0.0 25.8 jit_solution(11233310034992084001)
XLA Ops:
  0.0 0.0 copy-start
  0.0 2.1 %encode_and_pick.1 = (bf16[16,1536]{1,0:T(8,128)(2,1)S(1)}, bf16[32,1536]{1,0:T(8,128)(2,1)S(1)}, bf16[32,3072]{1,0:T(8,128)(2,1)S(1)}, bf16[32,3072]{1,0:T(8,12...) custom-call(bf16[128,3072]{1,0:T(8,128)(2,1)} %bitcast.3, s32[1,128]{1,0:T(1,128)} %bitcast.4, ...), custom_call_target="tpu_custom_call" | custom-call | tf_op jit(solution)/shard_map/encode_and_pick/pallas_call | solution.py:292
  2.1 0.5 %collective-permute-start = (bf16[32,1536]{1,0:T(8,128)(2,1)S(1)}, bf16[32,1536]{1,0:T(8,128)(2,1)S(1)}, u32[]{:S(2)}, u32[]{:S(2)}) collective-permute-start(bf16[32,1536]{1,0:T(8,128)(2,1)S(1)} %get-tuple-element.45), channel_id=1, source_target_pairs={{0,4},{4,0},{8,12},{12,8},{16,20},{20,16},{24,28},{28,24},{1,5},{5... | collective-permute-start | bytes 294920 | tf_op jit(solution)/shard_map/ppermute | solution.py:361
  2.6 3.5 %collective-permute-start.3 = (bf16[32,3072]{1,0:T(8,128)(2,1)S(1)}, bf16[32,3072]{1,0:T(8,128)(2,1)S(1)}, u32[]{:S(2)}, u32[]{:S(2)}) collective-permute-start(bf16[32,3072]{1,0:T(8,128)(2,1)S(1)} %get-tuple-element.51), channel_id=1, source_target_pairs={{0,3},{1,2},{2,1},{3,0},{4,7},{5,6},{6,5},{7,4},{8,11},{9,10},{10,... | collective-permute-start | bytes 589832 | tf_op jit(solution)/shard_map/ppermute | solution.py:361
  6.1 0.0 collective-permute-done
  6.1 2.7 %collective-permute-start.2 = (bf16[16,1536]{1,0:T(8,128)(2,1)S(1)}, bf16[16,1536]{1,0:T(8,128)(2,1)S(1)}, u32[]{:S(2)}, u32[]{:S(2)}) collective-permute-start(bf16[16,1536]{1,0:T(8,128)(2,1)S(1)} %slice_add_fusion), channel_id=1, source_target_pairs={{0,16},{4,20},{8,24},{12,28},{16,0},{20,4},{24,8},{28,12},{1,17},{... | collective-permute-start | bytes 147464 | tf_op jit(solution)/shard_map/ppermute | solution.py:361
  8.8 1.3 %collective-permute-start.4 = (bf16[16,1536]{1,0:T(8,128)(2,1)S(1)}, bf16[16,1536]{1,0:T(8,128)(2,1)S(1)}, u32[]{:S(2)}, u32[]{:S(2)}) collective-permute-start(bf16[16,1536]{1,0:T(8,128)(2,1)S(1)} %slice_add_fusion), channel_id=1, source_target_pairs={{0,24},{4,28},{8,16},{12,20},{16,8},{20,12},{24,0},{28,4},{1,25},{... | collective-permute-start | bytes 147464 | tf_op jit(solution)/shard_map/ppermute | solution.py:361
  10.1 0.2 collective-permute-start.1
  10.4 0.5 %collective-permute-start.6 = (bf16[32,3072]{1,0:T(8,128)(2,1)S(1)}, bf16[32,3072]{1,0:T(8,128)(2,1)S(1)}, u32[]{:S(2)}, u32[]{:S(2)}) collective-permute-start(bf16[32,3072]{1,0:T(8,128)(2,1)S(1)} %get-tuple-element.58), channel_id=1, source_target_pairs={{0,1},{1,0},{2,3},{3,2},{4,5},{5,4},{6,7},{7,6},{8,9},{9,8},{10,11... | collective-permute-start | bytes 589832 | tf_op jit(solution)/shard_map/ppermute | solution.py:361
  10.9 0.7 %collective-permute-done.3.refs_1_ = bf16[32,3072]{1,0:T(8,128)(2,1)S(1)} collective-permute-done((bf16[32,3072]{1,0:T(8,128)(2,1)S(1)}, bf16[32,3072]{1,0:T(8,128)(2,1)S(1)}, u32[]{:S(2)}, u32[]{:S(2)}) %collective-permute-start.3) | collective-permute-done | bytes 196640 | tf_op jit(solution)/shard_map/ppermute | solution.py:361
  11.6 1.7 %collective-permute-start.7 = (bf16[32,3072]{1,0:T(8,128)(2,1)S(1)}, bf16[32,3072]{1,0:T(8,128)(2,1)S(1)}, u32[]{:S(2)}, u32[]{:S(2)}) collective-permute-start(bf16[32,3072]{1,0:T(8,128)(2,1)S(1)} %get-tuple-element.59), channel_id=1, source_target_pairs={{0,2},{1,3},{2,0},{3,1},{4,6},{5,7},{6,4},{7,5},{8,10},{9,11},{10,... | collective-permute-start | bytes 589832 | tf_op jit(solution)/shard_map/ppermute | solution.py:361
  13.4 0.5 %whiten_receivers.2 = (f32[64,1536]{1,0:T(8,128)S(1)}, f32[64,1536]{1,0:T(8,128)S(1)}, f32[64,1536]{1,0:T(8,128)S(1)}, f32[64,128]{1,0:T(8,128)S(1)}) custom-call(bf16[32,3072]{1,0:T(8,128)(2,1)S(1)} %get-tuple-element.49.refs_0_, bf16[32,3072]{1,0:T(8,128)(2,1)S(1)} %collective-permute-done.3.refs_1_), custom_call_target="tpu_custom_call" | custom-call | flops 201326592 | bytes 786432 | tf_op jit(solution)/shard_map/whiten_receivers/pallas_call | solution.py:317
  13.9 0.0 collective-permute-done.2
  13.9 0.9 %collective-permute-done.4 = bf16[16,1536]{1,0:T(8,128)(2,1)S(1)} collective-permute-done((bf16[16,1536]{1,0:T(8,128)(2,1)S(1)}, bf16[16,1536]{1,0:T(8,128)(2,1)S(1)}, u32[]{:S(2)}, u32[]{:S(2)}) %collective-permute-start.4) | collective-permute-done | bytes 49184 | tf_op jit(solution)/shard_map/ppermute | solution.py:361
  14.8 0.0 collective-permute-done.1
  14.8 1.3 %collective-permute-start.5 = (bf16[16,1536]{1,0:T(8,128)(2,1)S(1)}, bf16[16,1536]{1,0:T(8,128)(2,1)S(1)}, u32[]{:S(2)}, u32[]{:S(2)}) collective-permute-start(bf16[16,1536]{1,0:T(8,128)(2,1)S(1)} %add_add_fusion), channel_id=1, source_target_pairs={{0,3},{1,2},{2,1},{3,0},{4,7},{5,6},{6,5},{7,4},{8,11},{9,10},{10,... | collective-permute-start | bytes 147464 | tf_op jit(solution)/shard_map/ppermute | solution.py:361
  16.1 1.1 %collective-permute-start.9 = (bf16[16,1536]{1,0:T(8,128)(2,1)S(1)}, bf16[16,1536]{1,0:T(8,128)(2,1)S(1)}, u32[]{:S(2)}, u32[]{:S(2)}) collective-permute-start(bf16[16,1536]{1,0:T(8,128)(2,1)S(1)} %add_add_fusion), channel_id=1, source_target_pairs={{0,2},{1,3},{2,0},{3,1},{4,6},{5,7},{6,4},{7,5},{8,10},{9,11},{10,... | collective-permute-start | bytes 147464 | tf_op jit(solution)/shard_map/ppermute | solution.py:361
  17.1 1.2 %collective-permute-start.8 = (bf16[16,1536]{1,0:T(8,128)(2,1)S(1)}, bf16[16,1536]{1,0:T(8,128)(2,1)S(1)}, u32[]{:S(2)}, u32[]{:S(2)}) collective-permute-start(bf16[16,1536]{1,0:T(8,128)(2,1)S(1)} %add_add_fusion), channel_id=1, source_target_pairs={{0,1},{1,0},{2,3},{3,2},{4,5},{5,4},{6,7},{7,6},{8,9},{9,8},{10,11... | collective-permute-start | bytes 147464 | tf_op jit(solution)/shard_map/ppermute | solution.py:361
  18.3 0.0 collective-permute-done.6.refs_0_
  18.3 1.0 %collective-permute-done.7.refs_1_ = bf16[32,3072]{1,0:T(8,128)(2,1)S(1)} collective-permute-done((bf16[32,3072]{1,0:T(8,128)(2,1)S(1)}, bf16[32,3072]{1,0:T(8,128)(2,1)S(1)}, u32[]{:S(2)}, u32[]{:S(2)}) %collective-permute-start.7) | collective-permute-done | bytes 196640 | tf_op jit(solution)/shard_map/ppermute | solution.py:361
  19.3 0.5 %whiten_receivers.3 = (f32[64,1536]{1,0:T(8,128)S(1)}, f32[64,1536]{1,0:T(8,128)S(1)}, f32[64,1536]{1,0:T(8,128)S(1)}, f32[64,128]{1,0:T(8,128)S(1)}) custom-call(bf16[32,3072]{1,0:T(8,128)(2,1)S(1)} %collective-permute-done.6.refs_0_, bf16[32,3072]{1,0:T(8,128)(2,1)S(1)} %collective-permute-done.7.refs_1_), custom_call_target="tpu_custom_call" | custom-call | flops 201326592 | bytes 786432 | tf_op jit(solution)/shard_map/whiten_receivers/pallas_call | solution.py:317
  19.9 0.0 collective-permute-done.5
  19.9 0.0 copy-done
  19.9 1.4 %stack_sums.1 = (f32[2,256,256]{2,1,0:T(8,128)S(1)}, f32[256,128]{1,0:T(8,128)S(1)}) custom-call(bf16[32,1536]{1,0:T(8,128)(2,1)S(1)} %pad_maximum_fusion.1.refs_0_, f32[64,1536]{1,0:T(8,128)S(1)} %get-tuple-element.65.refs_1_, f32[64,1536]{1,0:T(8,128)S(1)} %get-tuple-element.66.refs_2_, f32[64,1536]{1,0:T(8,128)S(1)} %get-tuple-element.67.refs_3_, ...), custom_call_target="tpu_custom_call" | custom-call | flops 471859200 | bytes 3145728 | tf_op jit(solution)/shard_map/stack_sums/pallas_call | solution.py:346
  21.3 0.0 collective-permute-done.9
  21.3 0.0 collective-permute-done.8
  21.3 0.1 collective-permute-start.10
  21.4 1.5 %stack_result.1.refs_10_ = f32[256,301]{1,0:T(8,128)S(1)} custom-call(bf16[32,1536]{1,0:T(8,128)(2,1)S(1)} %pad_maximum_fusion.2.refs_0_, f32[64,1536]{1,0:T(8,128)S(1)} %get-tuple-element.77.refs_1_.refs_5_, f32[64,1536]{1,0:T(8,128)S(1)} %get-tuple-element.78.refs_2_.refs_6_, f32[64,1536]{1,0:T(8,128)S(1)} %get-tuple-element.79.refs_3_.refs_7_, ...), custom_call_target="tpu_custom_call" | custom-call | flops 471859200 | bytes 3145728 | tf_op jit(solution)/shard_map/stack_result/pallas_call | solution.py:346
  22.9 0.0 collective-permute-done.10.refs_0_
  22.9 2.9 %stack_store.1 = f32[512,301]{1,0:T(8,128)} custom-call(bf16[64,1536]{1,0:T(8,128)(2,1)S(1)} %collective-permute-done.10.refs_0_, f32[64,1536]{1,0:T(8,128)S(1)} %get-tuple-element.65.refs_1_, f32[64,1536]{1,0:T(8,128)S(1)} %get-tuple-element.66.refs_2_, f32[64,1536]{1,0:T(8,128)S(1)} %get-tuple-element.67.refs_3_, f32[64,128]{1,0:T(8,128)S(1)} %get-tuple-element.68.refs_4_, ...), custom_call_target="tpu_custom_call" | custom-call | flops 471859200 | bytes 3145728 | tf_op jit(solution)/shard_map/stack_store/pallas_call | solution.py:346
  (5 shorter events, 0.1 us)
Async XLA Ops:
  0.0 19.9 %copy-start = (bf16[3072,256]{1,0:T(8,128)(2,1)S(1)}, bf16[3072,256]{1,0:T(8,128)(2,1)}, u32[]{:S(2)}) copy-start(bf16[3072,256]{1,0:T(8,128)(2,1)} %constant.2.clone.refs_5_.refs_9_) | copy-start | bytes 4718596
  2.1 4.0 %collective-permute-start = (bf16[32,1536]{1,0:T(8,128)(2,1)S(1)}, bf16[32,1536]{1,0:T(8,128)(2,1)S(1)}, u32[]{:S(2)}, u32[]{:S(2)}) collective-permute-start(bf16[32,1536]{1,0:T(8,128)(2,1)S(1)} %get-tuple-element.45), channel_id=1, source_target_pairs={{0,4},{4,0},{8,12},{12,8},{16,20},{20,16},{24,28},{28,24},{1,5},{5... | collective-permute-start | bytes 294920 | tf_op jit(solution)/shard_map/ppermute | solution.py:361
  2.6 9.0 %collective-permute-start.3 = (bf16[32,3072]{1,0:T(8,128)(2,1)S(1)}, bf16[32,3072]{1,0:T(8,128)(2,1)S(1)}, u32[]{:S(2)}, u32[]{:S(2)}) collective-permute-start(bf16[32,3072]{1,0:T(8,128)(2,1)S(1)} %get-tuple-element.51), channel_id=1, source_target_pairs={{0,3},{1,2},{2,1},{3,0},{4,7},{5,6},{6,5},{7,4},{8,11},{9,10},{10,... | collective-permute-start | bytes 589832 | tf_op jit(solution)/shard_map/ppermute | solution.py:361
  6.1 7.7 %collective-permute-start.2 = (bf16[16,1536]{1,0:T(8,128)(2,1)S(1)}, bf16[16,1536]{1,0:T(8,128)(2,1)S(1)}, u32[]{:S(2)}, u32[]{:S(2)}) collective-permute-start(bf16[16,1536]{1,0:T(8,128)(2,1)S(1)} %slice_add_fusion), channel_id=1, source_target_pairs={{0,16},{4,20},{8,24},{12,28},{16,0},{20,4},{24,8},{28,12},{1,17},{... | collective-permute-start | bytes 147464 | tf_op jit(solution)/shard_map/ppermute | solution.py:361
  8.8 6.0 %collective-permute-start.4 = (bf16[16,1536]{1,0:T(8,128)(2,1)S(1)}, bf16[16,1536]{1,0:T(8,128)(2,1)S(1)}, u32[]{:S(2)}, u32[]{:S(2)}) collective-permute-start(bf16[16,1536]{1,0:T(8,128)(2,1)S(1)} %slice_add_fusion), channel_id=1, source_target_pairs={{0,24},{4,28},{8,16},{12,20},{16,8},{20,12},{24,0},{28,4},{1,25},{... | collective-permute-start | bytes 147464 | tf_op jit(solution)/shard_map/ppermute | solution.py:361
  10.1 4.6 %collective-permute-start.1 = (bf16[16,1536]{1,0:T(8,128)(2,1)S(1)}, bf16[16,1536]{1,0:T(8,128)(2,1)S(1)}, u32[]{:S(2)}, u32[]{:S(2)}) collective-permute-start(bf16[16,1536]{1,0:T(8,128)(2,1)S(1)} %slice_add_fusion), channel_id=1, source_target_pairs={{0,8},{4,12},{8,0},{12,4},{16,24},{20,28},{24,16},{28,20},{1,9},{5... | collective-permute-start | bytes 147464 | tf_op jit(solution)/shard_map/ppermute | solution.py:361
  10.4 8.0 %collective-permute-start.6 = (bf16[32,3072]{1,0:T(8,128)(2,1)S(1)}, bf16[32,3072]{1,0:T(8,128)(2,1)S(1)}, u32[]{:S(2)}, u32[]{:S(2)}) collective-permute-start(bf16[32,3072]{1,0:T(8,128)(2,1)S(1)} %get-tuple-element.58), channel_id=1, source_target_pairs={{0,1},{1,0},{2,3},{3,2},{4,5},{5,4},{6,7},{7,6},{8,9},{9,8},{10,11... | collective-permute-start | bytes 589832 | tf_op jit(solution)/shard_map/ppermute | solution.py:361
  11.6 7.7 %collective-permute-start.7 = (bf16[32,3072]{1,0:T(8,128)(2,1)S(1)}, bf16[32,3072]{1,0:T(8,128)(2,1)S(1)}, u32[]{:S(2)}, u32[]{:S(2)}) collective-permute-start(bf16[32,3072]{1,0:T(8,128)(2,1)S(1)} %get-tuple-element.59), channel_id=1, source_target_pairs={{0,2},{1,3},{2,0},{3,1},{4,6},{5,7},{6,4},{7,5},{8,10},{9,11},{10,... | collective-permute-start | bytes 589832 | tf_op jit(solution)/shard_map/ppermute | solution.py:361
  14.8 5.1 %collective-permute-start.5 = (bf16[16,1536]{1,0:T(8,128)(2,1)S(1)}, bf16[16,1536]{1,0:T(8,128)(2,1)S(1)}, u32[]{:S(2)}, u32[]{:S(2)}) collective-permute-start(bf16[16,1536]{1,0:T(8,128)(2,1)S(1)} %add_add_fusion), channel_id=1, source_target_pairs={{0,3},{1,2},{2,1},{3,0},{4,7},{5,6},{6,5},{7,4},{8,11},{9,10},{10,... | collective-permute-start | bytes 147464 | tf_op jit(solution)/shard_map/ppermute | solution.py:361
  16.1 5.2 %collective-permute-start.9 = (bf16[16,1536]{1,0:T(8,128)(2,1)S(1)}, bf16[16,1536]{1,0:T(8,128)(2,1)S(1)}, u32[]{:S(2)}, u32[]{:S(2)}) collective-permute-start(bf16[16,1536]{1,0:T(8,128)(2,1)S(1)} %add_add_fusion), channel_id=1, source_target_pairs={{0,2},{1,3},{2,0},{3,1},{4,6},{5,7},{6,4},{7,5},{8,10},{9,11},{10,... | collective-permute-start | bytes 147464 | tf_op jit(solution)/shard_map/ppermute | solution.py:361
  17.1 4.1 %collective-permute-start.8 = (bf16[16,1536]{1,0:T(8,128)(2,1)S(1)}, bf16[16,1536]{1,0:T(8,128)(2,1)S(1)}, u32[]{:S(2)}, u32[]{:S(2)}) collective-permute-start(bf16[16,1536]{1,0:T(8,128)(2,1)S(1)} %add_add_fusion), channel_id=1, source_target_pairs={{0,1},{1,0},{2,3},{3,2},{4,5},{5,4},{6,7},{7,6},{8,9},{9,8},{10,11... | collective-permute-start | bytes 147464 | tf_op jit(solution)/shard_map/ppermute | solution.py:361
  21.3 1.6 %collective-permute-start.10 = (bf16[64,1536]{1,0:T(8,128)(2,1)S(1)}, bf16[64,1536]{1,0:T(8,128)(2,1)S(1)}, u32[]{:S(2)}, u32[]{:S(2)}) collective-permute-start(bf16[64,1536]{1,0:T(8,128)(2,1)S(1)} %pad_maximum_fusion), channel_id=1, source_target_pairs={{0,4},{4,0},{8,12},{12,8},{16,20},{20,16},{24,28},{28,24},{1,5},{5... | collective-permute-start | bytes 589832 | tf_op jit(solution)/shard_map/ppermute | solution.py:361

commit v25 on v24

--- a/solution.py
+++ b/solution.py
@@ -371,9 +371,9 @@
     receivers[-1] = swapped(receivers[-1], "tm", tm_size, tm_size - 1)
     own = own + swapped(other, "rcv", rcv_size, 1)[: own.shape[0]]
     own, later = lax.optimization_barrier((own, receivers[1:-1]))
-    last, receivers[-1] = lax.optimization_barrier((later[-1], receivers[-1]))
+    last, receivers[-1] = lax.optimization_barrier((later[0], receivers[-1]))
     receivers[1:-1] = [
-        swapped(block, "tm", tm_size, place) for place, block in enumerate(later[:-1] + [last], 1)
+        swapped(block, "tm", tm_size, place) for place, block in enumerate([last] + later[1:], 1)
     ]
     step = 2
     while step < rcv_size:

time: 25.9 us -> 26.9 us (1.039)
  waiting for transfers between devices: 2.64 us -> 3.63 us
    ppermute x11, waiting for transfers between devices: 2.64 us -> 3.63 us  [swapped(): return lax.ppermute(value, axis, [(i, i ^ step) for i in range(size)])]
  transfers between devices with their start and end apart: 11 -> 11, of which waited for: 3 -> 4; matrix products, arithmetic and copies ran while one was open for 0% -> 0% of each run, Pallas kernels for 15% -> 14%
where the time goes in v25:
time: 26.9 us; the launch traced here: 26.7 us
  starting transfers between devices  14.1 us (52%)
  Pallas kernels  8.79 us (33%)
  waiting for transfers between devices  3.63 us (13%)
    ppermute x11, starting transfers between devices, swapped(): return lax.ppermute(value, axis, [(i, i ^ step) for i in range(size)])  14.1 us
    pallas_call x3, Pallas kernels, stack_stage(): pl.pallas_call(functools.partial(stack_kernel, places, (not before, stage...  5.7 us
    ppermute x11, waiting for transfers between devices, swapped(): return lax.ppermute(value, axis, [(i, i ^ step) for i in range(size)])  3.63 us
    pallas_call x1, Pallas kernels, encode(): pl.pallas_call(functools.partial(encode_kernel, segments), out_shape=(sla...  2.08 us
    pallas_call x2, Pallas kernels, whiten_blocks(): pl.pallas_call(functools.partial(whiten_kernel, segments), out_shape=(par...  1.02 us
  transfers between devices with their start and end apart: 11, of which 4 were waited for; matrix products, arithmetic and copies ran while one was open for 0% of the time, Pallas kernels for 14%

profile of v25, /device:TPU:0, one launch (start us, length us, event | category | flops | bytes accessed | tf_op | source)
XLA Modules:
  0.0 26.7 jit_solution(12695401464050390756)
XLA Ops:
  0.0 0.0 copy-start
  0.0 2.1 %encode_and_pick.1 = (bf16[16,1536]{1,0:T(8,128)(2,1)S(1)}, bf16[32,1536]{1,0:T(8,128)(2,1)S(1)}, bf16[32,3072]{1,0:T(8,128)(2,1)S(1)}, bf16[32,3072]{1,0:T(8,12...) custom-call(bf16[128,3072]{1,0:T(8,128)(2,1)} %bitcast.3, s32[1,128]{1,0:T(1,128)} %bitcast.4, ...), custom_call_target="tpu_custom_call" | custom-call | tf_op jit(solution)/shard_map/encode_and_pick/pallas_call | solution.py:292
  2.1 0.5 %collective-permute-start = (bf16[32,1536]{1,0:T(8,128)(2,1)S(1)}, bf16[32,1536]{1,0:T(8,128)(2,1)S(1)}, u32[]{:S(2)}, u32[]{:S(2)}) collective-permute-start(bf16[32,1536]{1,0:T(8,128)(2,1)S(1)} %get-tuple-element.45), channel_id=1, source_target_pairs={{0,4},{4,0},{8,12},{12,8},{16,20},{20,16},{24,28},{28,24},{1,5},{5... | collective-permute-start | bytes 294920 | tf_op jit(solution)/shard_map/ppermute | solution.py:361
  2.6 3.5 %collective-permute-start.3 = (bf16[32,3072]{1,0:T(8,128)(2,1)S(1)}, bf16[32,3072]{1,0:T(8,128)(2,1)S(1)}, u32[]{:S(2)}, u32[]{:S(2)}) collective-permute-start(bf16[32,3072]{1,0:T(8,128)(2,1)S(1)} %get-tuple-element.51), channel_id=1, source_target_pairs={{0,3},{1,2},{2,1},{3,0},{4,7},{5,6},{6,5},{7,4},{8,11},{9,10},{10,... | collective-permute-start | bytes 589832 | tf_op jit(solution)/shard_map/ppermute | solution.py:361
  6.1 0.0 collective-permute-done
  6.1 2.7 %collective-permute-start.2 = (bf16[16,1536]{1,0:T(8,128)(2,1)S(1)}, bf16[16,1536]{1,0:T(8,128)(2,1)S(1)}, u32[]{:S(2)}, u32[]{:S(2)}) collective-permute-start(bf16[16,1536]{1,0:T(8,128)(2,1)S(1)} %slice_add_fusion), channel_id=1, source_target_pairs={{0,16},{4,20},{8,24},{12,28},{16,0},{20,4},{24,8},{28,12},{1,17},{... | collective-permute-start | bytes 147464 | tf_op jit(solution)/shard_map/ppermute | solution.py:361
  8.8 1.3 %collective-permute-start.4 = (bf16[16,1536]{1,0:T(8,128)(2,1)S(1)}, bf16[16,1536]{1,0:T(8,128)(2,1)S(1)}, u32[]{:S(2)}, u32[]{:S(2)}) collective-permute-start(bf16[16,1536]{1,0:T(8,128)(2,1)S(1)} %slice_add_fusion), channel_id=1, source_target_pairs={{0,24},{4,28},{8,16},{12,20},{16,8},{20,12},{24,0},{28,4},{1,25},{... | collective-permute-start | bytes 147464 | tf_op jit(solution)/shard_map/ppermute | solution.py:361
  10.1 0.2 collective-permute-start.1
  10.4 0.5 %collective-permute-start.7 = (bf16[32,3072]{1,0:T(8,128)(2,1)S(1)}, bf16[32,3072]{1,0:T(8,128)(2,1)S(1)}, u32[]{:S(2)}, u32[]{:S(2)}) collective-permute-start(bf16[32,3072]{1,0:T(8,128)(2,1)S(1)} %get-tuple-element.59), channel_id=1, source_target_pairs={{0,2},{1,3},{2,0},{3,1},{4,6},{5,7},{6,4},{7,5},{8,10},{9,11},{10,... | collective-permute-start | bytes 589832 | tf_op jit(solution)/shard_map/ppermute | solution.py:361
  10.9 0.7 %collective-permute-done.3.refs_1_ = bf16[32,3072]{1,0:T(8,128)(2,1)S(1)} collective-permute-done((bf16[32,3072]{1,0:T(8,128)(2,1)S(1)}, bf16[32,3072]{1,0:T(8,128)(2,1)S(1)}, u32[]{:S(2)}, u32[]{:S(2)}) %collective-permute-start.3) | collective-permute-done | bytes 196640 | tf_op jit(solution)/shard_map/ppermute | solution.py:361
  11.6 1.7 %collective-permute-start.6 = (bf16[32,3072]{1,0:T(8,128)(2,1)S(1)}, bf16[32,3072]{1,0:T(8,128)(2,1)S(1)}, u32[]{:S(2)}, u32[]{:S(2)}) collective-permute-start(bf16[32,3072]{1,0:T(8,128)(2,1)S(1)} %get-tuple-element.58), channel_id=1, source_target_pairs={{0,1},{1,0},{2,3},{3,2},{4,5},{5,4},{6,7},{7,6},{8,9},{9,8},{10,11... | collective-permute-start | bytes 589832 | tf_op jit(solution)/shard_map/ppermute | solution.py:361
  13.3 0.5 %whiten_receivers.2 = (f32[64,1536]{1,0:T(8,128)S(1)}, f32[64,1536]{1,0:T(8,128)S(1)}, f32[64,1536]{1,0:T(8,128)S(1)}, f32[64,128]{1,0:T(8,128)S(1)}) custom-call(bf16[32,3072]{1,0:T(8,128)(2,1)S(1)} %get-tuple-element.49.refs_0_, bf16[32,3072]{1,0:T(8,128)(2,1)S(1)} %collective-permute-done.3.refs_1_), custom_call_target="tpu_custom_call" | custom-call | flops 201326592 | bytes 786432 | tf_op jit(solution)/shard_map/whiten_receivers/pallas_call | solution.py:317
  13.9 0.0 collective-permute-done.2
  13.9 0.9 %collective-permute-done.4 = bf16[16,1536]{1,0:T(8,128)(2,1)S(1)} collective-permute-done((bf16[16,1536]{1,0:T(8,128)(2,1)S(1)}, bf16[16,1536]{1,0:T(8,128)(2,1)S(1)}, u32[]{:S(2)}, u32[]{:S(2)}) %collective-permute-start.4) | collective-permute-done | bytes 49184 | tf_op jit(solution)/shard_map/ppermute | solution.py:361
  14.8 0.0 collective-permute-done.1
  14.8 1.3 %collective-permute-start.5 = (bf16[16,1536]{1,0:T(8,128)(2,1)S(1)}, bf16[16,1536]{1,0:T(8,128)(2,1)S(1)}, u32[]{:S(2)}, u32[]{:S(2)}) collective-permute-start(bf16[16,1536]{1,0:T(8,128)(2,1)S(1)} %add_add_fusion), channel_id=1, source_target_pairs={{0,3},{1,2},{2,1},{3,0},{4,7},{5,6},{6,5},{7,4},{8,11},{9,10},{10,... | collective-permute-start | bytes 147464 | tf_op jit(solution)/shard_map/ppermute | solution.py:361
  16.1 0.8 %collective-permute-start.9 = (bf16[16,1536]{1,0:T(8,128)(2,1)S(1)}, bf16[16,1536]{1,0:T(8,128)(2,1)S(1)}, u32[]{:S(2)}, u32[]{:S(2)}) collective-permute-start(bf16[16,1536]{1,0:T(8,128)(2,1)S(1)} %add_add_fusion), channel_id=1, source_target_pairs={{0,2},{1,3},{2,0},{3,1},{4,6},{5,7},{6,4},{7,5},{8,10},{9,11},{10,... | collective-permute-start | bytes 147464 | tf_op jit(solution)/shard_map/ppermute | solution.py:361
  16.8 1.5 %collective-permute-start.8 = (bf16[16,1536]{1,0:T(8,128)(2,1)S(1)}, bf16[16,1536]{1,0:T(8,128)(2,1)S(1)}, u32[]{:S(2)}, u32[]{:S(2)}) collective-permute-start(bf16[16,1536]{1,0:T(8,128)(2,1)S(1)} %add_add_fusion), channel_id=1, source_target_pairs={{0,1},{1,0},{2,3},{3,2},{4,5},{5,4},{6,7},{7,6},{8,9},{9,8},{10,11... | collective-permute-start | bytes 147464 | tf_op jit(solution)/shard_map/ppermute | solution.py:361
  18.3 0.0 collective-permute-done.7.refs_1_
  18.3 1.0 %collective-permute-done.6.refs_0_ = bf16[32,3072]{1,0:T(8,128)(2,1)S(1)} collective-permute-done((bf16[32,3072]{1,0:T(8,128)(2,1)S(1)}, bf16[32,3072]{1,0:T(8,128)(2,1)S(1)}, u32[]{:S(2)}, u32[]{:S(2)}) %collective-permute-start.6) | collective-permute-done | bytes 196640 | tf_op jit(solution)/shard_map/ppermute | solution.py:361
  19.3 0.5 %whiten_receivers.3 = (f32[64,1536]{1,0:T(8,128)S(1)}, f32[64,1536]{1,0:T(8,128)S(1)}, f32[64,1536]{1,0:T(8,128)S(1)}, f32[64,128]{1,0:T(8,128)S(1)}) custom-call(bf16[32,3072]{1,0:T(8,128)(2,1)S(1)} %collective-permute-done.6.refs_0_, bf16[32,3072]{1,0:T(8,128)(2,1)S(1)} %collective-permute-done.7.refs_1_), custom_call_target="tpu_custom_call" | custom-call | flops 201326592 | bytes 786432 | tf_op jit(solution)/shard_map/whiten_receivers/pallas_call | solution.py:317
  19.9 1.0 %collective-permute-done.5 = bf16[16,1536]{1,0:T(8,128)(2,1)S(1)} collective-permute-done((bf16[16,1536]{1,0:T(8,128)(2,1)S(1)}, bf16[16,1536]{1,0:T(8,128)(2,1)S(1)}, u32[]{:S(2)}, u32[]{:S(2)}) %collective-permute-start.5) | collective-permute-done | bytes 49184 | tf_op jit(solution)/shard_map/ppermute | solution.py:361
  20.8 0.0 copy-done
  20.9 1.4 %stack_sums.1 = (f32[2,256,256]{2,1,0:T(8,128)S(1)}, f32[256,128]{1,0:T(8,128)S(1)}) custom-call(bf16[32,1536]{1,0:T(8,128)(2,1)S(1)} %pad_maximum_fusion.1.refs_0_, f32[64,1536]{1,0:T(8,128)S(1)} %get-tuple-element.65.refs_1_, f32[64,1536]{1,0:T(8,128)S(1)} %get-tuple-element.66.refs_2_, f32[64,1536]{1,0:T(8,128)S(1)} %get-tuple-element.67.refs_3_, ...), custom_call_target="tpu_custom_call" | custom-call | flops 471859200 | bytes 3145728 | tf_op jit(solution)/shard_map/stack_sums/pallas_call | solution.py:346
  22.2 0.0 collective-permute-done.9
  22.2 0.0 collective-permute-done.8
  22.3 0.1 collective-permute-start.10
  22.4 1.5 %stack_result.1.refs_10_ = f32[256,301]{1,0:T(8,128)S(1)} custom-call(bf16[32,1536]{1,0:T(8,128)(2,1)S(1)} %pad_maximum_fusion.2.refs_0_, f32[64,1536]{1,0:T(8,128)S(1)} %get-tuple-element.77.refs_1_.refs_5_, f32[64,1536]{1,0:T(8,128)S(1)} %get-tuple-element.78.refs_2_.refs_6_, f32[64,1536]{1,0:T(8,128)S(1)} %get-tuple-element.79.refs_3_.refs_7_, ...), custom_call_target="tpu_custom_call" | custom-call | flops 471859200 | bytes 3145728 | tf_op jit(solution)/shard_map/stack_result/pallas_call | solution.py:346
  23.8 0.0 collective-permute-done.10.refs_0_
  23.9 2.9 %stack_store.1 = f32[512,301]{1,0:T(8,128)} custom-call(bf16[64,1536]{1,0:T(8,128)(2,1)S(1)} %collective-permute-done.10.refs_0_, f32[64,1536]{1,0:T(8,128)S(1)} %get-tuple-element.65.refs_1_, f32[64,1536]{1,0:T(8,128)S(1)} %get-tuple-element.66.refs_2_, f32[64,1536]{1,0:T(8,128)S(1)} %get-tuple-element.67.refs_3_, f32[64,128]{1,0:T(8,128)S(1)} %get-tuple-element.68.refs_4_, ...), custom_call_target="tpu_custom_call" | custom-call | flops 471859200 | bytes 3145728 | tf_op jit(solution)/shard_map/stack_store/pallas_call | solution.py:346
  (5 shorter events, 0.1 us)
Async XLA Ops:
  0.0 20.8 %copy-start = (bf16[3072,256]{1,0:T(8,128)(2,1)S(1)}, bf16[3072,256]{1,0:T(8,128)(2,1)}, u32[]{:S(2)}) copy-start(bf16[3072,256]{1,0:T(8,128)(2,1)} %constant.2.clone.refs_5_.refs_9_) | copy-start | bytes 4718596
  2.1 4.0 %collective-permute-start = (bf16[32,1536]{1,0:T(8,128)(2,1)S(1)}, bf16[32,1536]{1,0:T(8,128)(2,1)S(1)}, u32[]{:S(2)}, u32[]{:S(2)}) collective-permute-start(bf16[32,1536]{1,0:T(8,128)(2,1)S(1)} %get-tuple-element.45), channel_id=1, source_target_pairs={{0,4},{4,0},{8,12},{12,8},{16,20},{20,16},{24,28},{28,24},{1,5},{5... | collective-permute-start | bytes 294920 | tf_op jit(solution)/shard_map/ppermute | solution.py:361
  2.6 9.0 %collective-permute-start.3 = (bf16[32,3072]{1,0:T(8,128)(2,1)S(1)}, bf16[32,3072]{1,0:T(8,128)(2,1)S(1)}, u32[]{:S(2)}, u32[]{:S(2)}) collective-permute-start(bf16[32,3072]{1,0:T(8,128)(2,1)S(1)} %get-tuple-element.51), channel_id=1, source_target_pairs={{0,3},{1,2},{2,1},{3,0},{4,7},{5,6},{6,5},{7,4},{8,11},{9,10},{10,... | collective-permute-start | bytes 589832 | tf_op jit(solution)/shard_map/ppermute | solution.py:361
  6.1 7.7 %collective-permute-start.2 = (bf16[16,1536]{1,0:T(8,128)(2,1)S(1)}, bf16[16,1536]{1,0:T(8,128)(2,1)S(1)}, u32[]{:S(2)}, u32[]{:S(2)}) collective-permute-start(bf16[16,1536]{1,0:T(8,128)(2,1)S(1)} %slice_add_fusion), channel_id=1, source_target_pairs={{0,16},{4,20},{8,24},{12,28},{16,0},{20,4},{24,8},{28,12},{1,17},{... | collective-permute-start | bytes 147464 | tf_op jit(solution)/shard_map/ppermute | solution.py:361
  8.8 6.0 %collective-permute-start.4 = (bf16[16,1536]{1,0:T(8,128)(2,1)S(1)}, bf16[16,1536]{1,0:T(8,128)(2,1)S(1)}, u32[]{:S(2)}, u32[]{:S(2)}) collective-permute-start(bf16[16,1536]{1,0:T(8,128)(2,1)S(1)} %slice_add_fusion), channel_id=1, source_target_pairs={{0,24},{4,28},{8,16},{12,20},{16,8},{20,12},{24,0},{28,4},{1,25},{... | collective-permute-start | bytes 147464 | tf_op jit(solution)/shard_map/ppermute | solution.py:361
  10.1 4.6 %collective-permute-start.1 = (bf16[16,1536]{1,0:T(8,128)(2,1)S(1)}, bf16[16,1536]{1,0:T(8,128)(2,1)S(1)}, u32[]{:S(2)}, u32[]{:S(2)}) collective-permute-start(bf16[16,1536]{1,0:T(8,128)(2,1)S(1)} %slice_add_fusion), channel_id=1, source_target_pairs={{0,8},{4,12},{8,0},{12,4},{16,24},{20,28},{24,16},{28,20},{1,9},{5... | collective-permute-start | bytes 147464 | tf_op jit(solution)/shard_map/ppermute | solution.py:361
  10.4 8.0 %collective-permute-start.7 = (bf16[32,3072]{1,0:T(8,128)(2,1)S(1)}, bf16[32,3072]{1,0:T(8,128)(2,1)S(1)}, u32[]{:S(2)}, u32[]{:S(2)}) collective-permute-start(bf16[32,3072]{1,0:T(8,128)(2,1)S(1)} %get-tuple-element.59), channel_id=1, source_target_pairs={{0,2},{1,3},{2,0},{3,1},{4,6},{5,7},{6,4},{7,5},{8,10},{9,11},{10,... | collective-permute-start | bytes 589832 | tf_op jit(solution)/shard_map/ppermute | solution.py:361
  11.6 7.7 %collective-permute-start.6 = (bf16[32,3072]{1,0:T(8,128)(2,1)S(1)}, bf16[32,3072]{1,0:T(8,128)(2,1)S(1)}, u32[]{:S(2)}, u32[]{:S(2)}) collective-permute-start(bf16[32,3072]{1,0:T(8,128)(2,1)S(1)} %get-tuple-element.58), channel_id=1, source_target_pairs={{0,1},{1,0},{2,3},{3,2},{4,5},{5,4},{6,7},{7,6},{8,9},{9,8},{10,11... | collective-permute-start | bytes 589832 | tf_op jit(solution)/shard_map/ppermute | solution.py:361
  14.8 6.1 %collective-permute-start.5 = (bf16[16,1536]{1,0:T(8,128)(2,1)S(1)}, bf16[16,1536]{1,0:T(8,128)(2,1)S(1)}, u32[]{:S(2)}, u32[]{:S(2)}) collective-permute-start(bf16[16,1536]{1,0:T(8,128)(2,1)S(1)} %add_add_fusion), channel_id=1, source_target_pairs={{0,3},{1,2},{2,1},{3,0},{4,7},{5,6},{6,5},{7,4},{8,11},{9,10},{10,... | collective-permute-start | bytes 147464 | tf_op jit(solution)/shard_map/ppermute | solution.py:361
  16.1 6.2 %collective-permute-start.9 = (bf16[16,1536]{1,0:T(8,128)(2,1)S(1)}, bf16[16,1536]{1,0:T(8,128)(2,1)S(1)}, u32[]{:S(2)}, u32[]{:S(2)}) collective-permute-start(bf16[16,1536]{1,0:T(8,128)(2,1)S(1)} %add_add_fusion), channel_id=1, source_target_pairs={{0,2},{1,3},{2,0},{3,1},{4,6},{5,7},{6,4},{7,5},{8,10},{9,11},{10,... | collective-permute-start | bytes 147464 | tf_op jit(solution)/shard_map/ppermute | solution.py:361
  16.8 5.4 %collective-permute-start.8 = (bf16[16,1536]{1,0:T(8,128)(2,1)S(1)}, bf16[16,1536]{1,0:T(8,128)(2,1)S(1)}, u32[]{:S(2)}, u32[]{:S(2)}) collective-permute-start(bf16[16,1536]{1,0:T(8,128)(2,1)S(1)} %add_add_fusion), channel_id=1, source_target_pairs={{0,1},{1,0},{2,3},{3,2},{4,5},{5,4},{6,7},{7,6},{8,9},{9,8},{10,11... | collective-permute-start | bytes 147464 | tf_op jit(solution)/shard_map/ppermute | solution.py:361
  22.3 1.6 %collective-permute-start.10 = (bf16[64,1536]{1,0:T(8,128)(2,1)S(1)}, bf16[64,1536]{1,0:T(8,128)(2,1)S(1)}, u32[]{:S(2)}, u32[]{:S(2)}) collective-permute-start(bf16[64,1536]{1,0:T(8,128)(2,1)S(1)} %pad_maximum_fusion), channel_id=1, source_target_pairs={{0,4},{4,0},{8,12},{12,8},{16,20},{20,16},{24,28},{28,24},{1,5},{5... | collective-permute-start | bytes 589832 | tf_op jit(solution)/shard_map/ppermute | solution.py:361

commit v26 on v24

--- a/solution.py
+++ b/solution.py
@@ -191,7 +191,7 @@
     def spread(ref, block, row):
         return jnp.concatenate([ref[block, pl.ds(row, 8, stride=0), :]] * (tile // 8), axis=0)
 
-    def multiply(block, carry):
+    def multiply(sources, block, carry):
         at = pl.ds(pl.multiple_of(block * LANES, LANES), LANES)
         for first in range(0, keep, tile):
             taken = [
@@ -201,7 +201,7 @@
             r_re = [block_refs[0][row, at] for block_refs, row in taken]
             r_im = [block_refs[1][row, at] for block_refs, row in taken]
             r_both = [block_refs[2][row, at] for block_refs, row in taken]
-            for source in range(count):
+            for source in sources:
                 p, q, w = [], [], []
                 for t in range(segments):
                     row = t * count + source
@@ -214,8 +214,6 @@
                 cross[1, block, to] = (w - p).astype(cross.dtype)
         return carry
 
-    lax.fori_loop(0, nbins // LANES, multiply, 0)
-
     def project(place, part):
         value = [cross[place, block, part] for block in range(nbins // LANES)]
         return jnp.dot(
@@ -224,8 +222,14 @@
             preferred_element_type=jnp.float32,
         )
 
+    lags = 2 * LAG + 1
+    scale = 2.0 / math.sqrt(nbins)
+    mirror = LAG - FIRST_LAG - iota((keep, LANES), 1)
+    pieces = max(1, count // 4)
     ends = []
     for first in (0, count // 2):
+        sources = range(first, first + count // 2)
+        lax.fori_loop(0, nbins // LANES, functools.partial(multiply, sources), 0)
         at = slice(first * keep, (first + count // 2) * keep)
         sums = [project(place, at) for place in range(2)]
         if not first_stage:
@@ -234,49 +238,44 @@
             for place in range(2):
                 after[0][place, at] = sums[place]
         ends.append(sums)
-
-    lags = 2 * LAG + 1
-    scale = 2.0 / math.sqrt(nbins)
-    mirror = LAG - FIRST_LAG - iota((keep, LANES), 1)
-    pieces = max(1, count // 4)
-    for source in range(count):
-        to = slice(source * keep, (source + 1) * keep)
-        common = [
-            src_valid[t * count + source : t * count + source + 1]
-            * receivers[which][3][place * keep : (place + 1) * keep, :]
-            for t, (which, place) in enumerate(places)
-        ] + ([] if first_stage else [before[1][to]])
-        common = functools.reduce(jnp.add, common)
-        if stage == "sums":
-            after[1][to] = common
-            continue
-        weight = scale / jnp.maximum(common, 1.0)
-        inside = slice(source % (count // 2) * keep, (source % (count // 2) + 1) * keep)
-        even, odd = (total[inside] for total in ends[source // (count // 2)])
-        ahead = even + odd
-        behind = even - odd
-        low_part = jnp.take_along_axis(
-            behind[:, :LANES], jnp.clip(mirror, 0, LANES - 1), axis=1
-        )
-        high_part = jnp.take_along_axis(
-            behind[:, LANES:], jnp.clip(mirror - LANES, 0, LANES - 1), axis=1
-        )
-        result[to, :LANES] = jnp.where(mirror < LANES, low_part, high_part) * weight
-        for first in range(0, lags - LANES, LANES):
-            last = min(first + LANES, lags - LANES)
-            value = ahead[:, first : first + LANES] * weight
-            result[to, LANES + first : LANES + last] = value[:, : last - first]
-        if stage == "store" and (source + 1) % pieces == 0:
-            first, size = (source + 1 - pieces) * keep, pieces * keep
-            at = pl.multiple_of((1 - part) * rows + first, size)
-            copies.append(
-                pltpu.make_async_copy(
-                    result.at[pl.ds(first, size)],
-                    after[0].at[pl.ds(at, size)],
-                    written.at[source // pieces],
+        for source in sources:
+            to = slice(source * keep, (source + 1) * keep)
+            common = [
+                src_valid[t * count + source : t * count + source + 1]
+                * receivers[which][3][place * keep : (place + 1) * keep, :]
+                for t, (which, place) in enumerate(places)
+            ] + ([] if first_stage else [before[1][to]])
+            common = functools.reduce(jnp.add, common)
+            if stage == "sums":
+                after[1][to] = common
+                continue
+            weight = scale / jnp.maximum(common, 1.0)
+            inside = slice(source % (count // 2) * keep, (source % (count // 2) + 1) * keep)
+            even, odd = (total[inside] for total in ends[source // (count // 2)])
+            ahead = even + odd
+            behind = even - odd
+            low_part = jnp.take_along_axis(
+                behind[:, :LANES], jnp.clip(mirror, 0, LANES - 1), axis=1
+            )
+            high_part = jnp.take_along_axis(
+                behind[:, LANES:], jnp.clip(mirror - LANES, 0, LANES - 1), axis=1
+            )
+            result[to, :LANES] = jnp.where(mirror < LANES, low_part, high_part) * weight
+            for first in range(0, lags - LANES, LANES):
+                last = min(first + LANES, lags - LANES)
+                value = ahead[:, first : first + LANES] * weight
+                result[to, LANES + first : LANES + last] = value[:, : last - first]
+            if stage == "store" and (source + 1) % pieces == 0:
+                first, size = (source + 1 - pieces) * keep, pieces * keep
+                at = pl.multiple_of((1 - part) * rows + first, size)
+                copies.append(
+                    pltpu.make_async_copy(
+                        result.at[pl.ds(first, size)],
+                        after[0].at[pl.ds(at, size)],
+                        written.at[source // pieces],
+                    )
                 )
-            )
-            copies[-1].start()
+                copies[-1].start()
     for copy in copies:
         copy.wait()
 

time: 25.9 us -> 27.2 us (1.050)
  Pallas kernels: 8.8 us -> 10 us
    pallas_call x3, Pallas kernels: 5.7 us -> 6.95 us  [stack_stage(): pl.pallas_call(functools.partial(stack_kernel, places, (not before, stage...]
  transfers between devices with their start and end apart: 11 -> 11, of which waited for: 3 -> 3; matrix products, arithmetic and copies ran while one was open for 0% -> 0% of each run, Pallas kernels for 15% -> 17%
where the time goes in v26:
time: 27.2 us; the launch traced here: 27 us
  starting transfers between devices  14.2 us (52%)
  Pallas kernels  10 us (37%)
  waiting for transfers between devices  2.64 us (10%)
    ppermute x11, starting transfers between devices, swapped(): return lax.ppermute(value, axis, [(i, i ^ step) for i in range(size)])  14.2 us
    pallas_call x3, Pallas kernels, stack_stage(): pl.pallas_call(functools.partial(stack_kernel, places, (not before, stage...  6.95 us
    ppermute x11, waiting for transfers between devices, swapped(): return lax.ppermute(value, axis, [(i, i ^ step) for i in range(size)])  2.64 us
    pallas_call x1, Pallas kernels, encode(): pl.pallas_call(functools.partial(encode_kernel, segments), out_shape=(sla...  2.08 us
    pallas_call x2, Pallas kernels, whiten_blocks(): pl.pallas_call(functools.partial(whiten_kernel, segments), out_shape=(par...  1.02 us
  transfers between devices with their start and end apart: 11, of which 3 were waited for; matrix products, arithmetic and copies ran while one was open for 0% of the time, Pallas kernels for 17%

profile of v26, /device:TPU:0, one launch (start us, length us, event | category | flops | bytes accessed | tf_op | source)
XLA Modules:
  0.0 27.0 jit_solution(1289703865037326578)
XLA Ops:
  0.0 0.0 copy-start
  0.0 2.1 %encode_and_pick.1 = (bf16[16,1536]{1,0:T(8,128)(2,1)S(1)}, bf16[32,1536]{1,0:T(8,128)(2,1)S(1)}, bf16[32,3072]{1,0:T(8,128)(2,1)S(1)}, bf16[32,3072]{1,0:T(8,12...) custom-call(bf16[128,3072]{1,0:T(8,128)(2,1)} %bitcast.3, s32[1,128]{1,0:T(1,128)} %bitcast.4, ...), custom_call_target="tpu_custom_call" | custom-call | tf_op jit(solution)/shard_map/encode_and_pick/pallas_call | solution.py:291
  2.1 0.5 %collective-permute-start = (bf16[32,1536]{1,0:T(8,128)(2,1)S(1)}, bf16[32,1536]{1,0:T(8,128)(2,1)S(1)}, u32[]{:S(2)}, u32[]{:S(2)}) collective-permute-start(bf16[32,1536]{1,0:T(8,128)(2,1)S(1)} %get-tuple-element.45), channel_id=1, source_target_pairs={{0,4},{4,0},{8,12},{12,8},{16,20},{20,16},{24,28},{28,24},{1,5},{5... | collective-permute-start | bytes 294920 | tf_op jit(solution)/shard_map/ppermute | solution.py:360
  2.6 3.5 %collective-permute-start.3 = (bf16[32,3072]{1,0:T(8,128)(2,1)S(1)}, bf16[32,3072]{1,0:T(8,128)(2,1)S(1)}, u32[]{:S(2)}, u32[]{:S(2)}) collective-permute-start(bf16[32,3072]{1,0:T(8,128)(2,1)S(1)} %get-tuple-element.51), channel_id=1, source_target_pairs={{0,3},{1,2},{2,1},{3,0},{4,7},{5,6},{6,5},{7,4},{8,11},{9,10},{10,... | collective-permute-start | bytes 589832 | tf_op jit(solution)/shard_map/ppermute | solution.py:360
  6.1 0.0 collective-permute-done
  6.1 2.7 %collective-permute-start.2 = (bf16[16,1536]{1,0:T(8,128)(2,1)S(1)}, bf16[16,1536]{1,0:T(8,128)(2,1)S(1)}, u32[]{:S(2)}, u32[]{:S(2)}) collective-permute-start(bf16[16,1536]{1,0:T(8,128)(2,1)S(1)} %slice_add_fusion), channel_id=1, source_target_pairs={{0,16},{4,20},{8,24},{12,28},{16,0},{20,4},{24,8},{28,12},{1,17},{... | collective-permute-start | bytes 147464 | tf_op jit(solution)/shard_map/ppermute | solution.py:360
  8.8 1.3 %collective-permute-start.4 = (bf16[16,1536]{1,0:T(8,128)(2,1)S(1)}, bf16[16,1536]{1,0:T(8,128)(2,1)S(1)}, u32[]{:S(2)}, u32[]{:S(2)}) collective-permute-start(bf16[16,1536]{1,0:T(8,128)(2,1)S(1)} %slice_add_fusion), channel_id=1, source_target_pairs={{0,24},{4,28},{8,16},{12,20},{16,8},{20,12},{24,0},{28,4},{1,25},{... | collective-permute-start | bytes 147464 | tf_op jit(solution)/shard_map/ppermute | solution.py:360
  10.1 0.2 collective-permute-start.1
  10.4 0.5 %collective-permute-start.6 = (bf16[32,3072]{1,0:T(8,128)(2,1)S(1)}, bf16[32,3072]{1,0:T(8,128)(2,1)S(1)}, u32[]{:S(2)}, u32[]{:S(2)}) collective-permute-start(bf16[32,3072]{1,0:T(8,128)(2,1)S(1)} %get-tuple-element.58), channel_id=1, source_target_pairs={{0,1},{1,0},{2,3},{3,2},{4,5},{5,4},{6,7},{7,6},{8,9},{9,8},{10,11... | collective-permute-start | bytes 589832 | tf_op jit(solution)/shard_map/ppermute | solution.py:360
  10.9 0.7 %collective-permute-done.3.refs_1_ = bf16[32,3072]{1,0:T(8,128)(2,1)S(1)} collective-permute-done((bf16[32,3072]{1,0:T(8,128)(2,1)S(1)}, bf16[32,3072]{1,0:T(8,128)(2,1)S(1)}, u32[]{:S(2)}, u32[]{:S(2)}) %collective-permute-start.3) | collective-permute-done | bytes 196640 | tf_op jit(solution)/shard_map/ppermute | solution.py:360
  11.6 1.7 %collective-permute-start.7 = (bf16[32,3072]{1,0:T(8,128)(2,1)S(1)}, bf16[32,3072]{1,0:T(8,128)(2,1)S(1)}, u32[]{:S(2)}, u32[]{:S(2)}) collective-permute-start(bf16[32,3072]{1,0:T(8,128)(2,1)S(1)} %get-tuple-element.59), channel_id=1, source_target_pairs={{0,2},{1,3},{2,0},{3,1},{4,6},{5,7},{6,4},{7,5},{8,10},{9,11},{10,... | collective-permute-start | bytes 589832 | tf_op jit(solution)/shard_map/ppermute | solution.py:360
  13.4 0.5 %whiten_receivers.2 = (f32[64,1536]{1,0:T(8,128)S(1)}, f32[64,1536]{1,0:T(8,128)S(1)}, f32[64,1536]{1,0:T(8,128)S(1)}, f32[64,128]{1,0:T(8,128)S(1)}) custom-call(bf16[32,3072]{1,0:T(8,128)(2,1)S(1)} %get-tuple-element.49.refs_0_, bf16[32,3072]{1,0:T(8,128)(2,1)S(1)} %collective-permute-done.3.refs_1_), custom_call_target="tpu_custom_call" | custom-call | flops 201326592 | bytes 786432 | tf_op jit(solution)/shard_map/whiten_receivers/pallas_call | solution.py:316
  13.9 0.0 collective-permute-done.2
  13.9 0.9 %collective-permute-done.4 = bf16[16,1536]{1,0:T(8,128)(2,1)S(1)} collective-permute-done((bf16[16,1536]{1,0:T(8,128)(2,1)S(1)}, bf16[16,1536]{1,0:T(8,128)(2,1)S(1)}, u32[]{:S(2)}, u32[]{:S(2)}) %collective-permute-start.4) | collective-permute-done | bytes 49184 | tf_op jit(solution)/shard_map/ppermute | solution.py:360
  14.8 0.0 collective-permute-done.1
  14.8 1.3 %collective-permute-start.5 = (bf16[16,1536]{1,0:T(8,128)(2,1)S(1)}, bf16[16,1536]{1,0:T(8,128)(2,1)S(1)}, u32[]{:S(2)}, u32[]{:S(2)}) collective-permute-start(bf16[16,1536]{1,0:T(8,128)(2,1)S(1)} %add_add_fusion), channel_id=1, source_target_pairs={{0,3},{1,2},{2,1},{3,0},{4,7},{5,6},{6,5},{7,4},{8,11},{9,10},{10,... | collective-permute-start | bytes 147464 | tf_op jit(solution)/shard_map/ppermute | solution.py:360
  16.1 1.1 %collective-permute-start.9 = (bf16[16,1536]{1,0:T(8,128)(2,1)S(1)}, bf16[16,1536]{1,0:T(8,128)(2,1)S(1)}, u32[]{:S(2)}, u32[]{:S(2)}) collective-permute-start(bf16[16,1536]{1,0:T(8,128)(2,1)S(1)} %add_add_fusion), channel_id=1, source_target_pairs={{0,2},{1,3},{2,0},{3,1},{4,6},{5,7},{6,4},{7,5},{8,10},{9,11},{10,... | collective-permute-start | bytes 147464 | tf_op jit(solution)/shard_map/ppermute | solution.py:360
  17.1 1.2 %collective-permute-start.8 = (bf16[16,1536]{1,0:T(8,128)(2,1)S(1)}, bf16[16,1536]{1,0:T(8,128)(2,1)S(1)}, u32[]{:S(2)}, u32[]{:S(2)}) collective-permute-start(bf16[16,1536]{1,0:T(8,128)(2,1)S(1)} %add_add_fusion), channel_id=1, source_target_pairs={{0,1},{1,0},{2,3},{3,2},{4,5},{5,4},{6,7},{7,6},{8,9},{9,8},{10,11... | collective-permute-start | bytes 147464 | tf_op jit(solution)/shard_map/ppermute | solution.py:360
  18.3 0.0 collective-permute-done.6.refs_0_
  18.3 1.0 %collective-permute-done.7.refs_1_ = bf16[32,3072]{1,0:T(8,128)(2,1)S(1)} collective-permute-done((bf16[32,3072]{1,0:T(8,128)(2,1)S(1)}, bf16[32,3072]{1,0:T(8,128)(2,1)S(1)}, u32[]{:S(2)}, u32[]{:S(2)}) %collective-permute-start.7) | collective-permute-done | bytes 196640 | tf_op jit(solution)/shard_map/ppermute | solution.py:360
  19.3 0.5 %whiten_receivers.3 = (f32[64,1536]{1,0:T(8,128)S(1)}, f32[64,1536]{1,0:T(8,128)S(1)}, f32[64,1536]{1,0:T(8,128)S(1)}, f32[64,128]{1,0:T(8,128)S(1)}) custom-call(bf16[32,3072]{1,0:T(8,128)(2,1)S(1)} %collective-permute-done.6.refs_0_, bf16[32,3072]{1,0:T(8,128)(2,1)S(1)} %collective-permute-done.7.refs_1_), custom_call_target="tpu_custom_call" | custom-call | flops 201326592 | bytes 786432 | tf_op jit(solution)/shard_map/whiten_receivers/pallas_call | solution.py:316
  19.9 0.0 collective-permute-done.5
  19.9 0.0 copy-done
  19.9 1.7 %stack_sums.1 = (f32[2,256,256]{2,1,0:T(8,128)S(1)}, f32[256,128]{1,0:T(8,128)S(1)}) custom-call(bf16[32,1536]{1,0:T(8,128)(2,1)S(1)} %pad_maximum_fusion.1.refs_0_, f32[64,1536]{1,0:T(8,128)S(1)} %get-tuple-element.65.refs_1_, f32[64,1536]{1,0:T(8,128)S(1)} %get-tuple-element.66.refs_2_, f32[64,1536]{1,0:T(8,128)S(1)} %get-tuple-element.67.refs_3_, ...), custom_call_target="tpu_custom_call" | custom-call | flops 471859200 | bytes 3145728 | tf_op jit(solution)/shard_map/stack_sums/pallas_call | solution.py:345
  21.6 0.0 collective-permute-done.9
  21.6 0.0 collective-permute-done.8
  21.6 0.1 collective-permute-start.10
  21.7 1.9 %stack_result.1.refs_10_ = f32[256,301]{1,0:T(8,128)S(1)} custom-call(bf16[32,1536]{1,0:T(8,128)(2,1)S(1)} %pad_maximum_fusion.2.refs_0_, f32[64,1536]{1,0:T(8,128)S(1)} %get-tuple-element.77.refs_1_.refs_5_, f32[64,1536]{1,0:T(8,128)S(1)} %get-tuple-element.78.refs_2_.refs_6_, f32[64,1536]{1,0:T(8,128)S(1)} %get-tuple-element.79.refs_3_.refs_7_, ...), custom_call_target="tpu_custom_call" | custom-call | flops 471859200 | bytes 3145728 | tf_op jit(solution)/shard_map/stack_result/pallas_call | solution.py:345
  23.6 0.0 collective-permute-done.10.refs_0_
  23.6 3.4 %stack_store.1 = f32[512,301]{1,0:T(8,128)} custom-call(bf16[64,1536]{1,0:T(8,128)(2,1)S(1)} %collective-permute-done.10.refs_0_, f32[64,1536]{1,0:T(8,128)S(1)} %get-tuple-element.65.refs_1_, f32[64,1536]{1,0:T(8,128)S(1)} %get-tuple-element.66.refs_2_, f32[64,1536]{1,0:T(8,128)S(1)} %get-tuple-element.67.refs_3_, f32[64,128]{1,0:T(8,128)S(1)} %get-tuple-element.68.refs_4_, ...), custom_call_target="tpu_custom_call" | custom-call | flops 471859200 | bytes 3145728 | tf_op jit(solution)/shard_map/stack_store/pallas_call | solution.py:345
  (5 shorter events, 0.1 us)
Async XLA Ops:
  0.0 19.9 %copy-start = (bf16[3072,256]{1,0:T(8,128)(2,1)S(1)}, bf16[3072,256]{1,0:T(8,128)(2,1)}, u32[]{:S(2)}) copy-start(bf16[3072,256]{1,0:T(8,128)(2,1)} %constant.2.clone.refs_5_.refs_9_) | copy-start | bytes 4718596
  2.1 4.0 %collective-permute-start = (bf16[32,1536]{1,0:T(8,128)(2,1)S(1)}, bf16[32,1536]{1,0:T(8,128)(2,1)S(1)}, u32[]{:S(2)}, u32[]{:S(2)}) collective-permute-start(bf16[32,1536]{1,0:T(8,128)(2,1)S(1)} %get-tuple-element.45), channel_id=1, source_target_pairs={{0,4},{4,0},{8,12},{12,8},{16,20},{20,16},{24,28},{28,24},{1,5},{5... | collective-permute-start | bytes 294920 | tf_op jit(solution)/shard_map/ppermute | solution.py:360
  2.6 9.0 %collective-permute-start.3 = (bf16[32,3072]{1,0:T(8,128)(2,1)S(1)}, bf16[32,3072]{1,0:T(8,128)(2,1)S(1)}, u32[]{:S(2)}, u32[]{:S(2)}) collective-permute-start(bf16[32,3072]{1,0:T(8,128)(2,1)S(1)} %get-tuple-element.51), channel_id=1, source_target_pairs={{0,3},{1,2},{2,1},{3,0},{4,7},{5,6},{6,5},{7,4},{8,11},{9,10},{10,... | collective-permute-start | bytes 589832 | tf_op jit(solution)/shard_map/ppermute | solution.py:360
  6.1 7.7 %collective-permute-start.2 = (bf16[16,1536]{1,0:T(8,128)(2,1)S(1)}, bf16[16,1536]{1,0:T(8,128)(2,1)S(1)}, u32[]{:S(2)}, u32[]{:S(2)}) collective-permute-start(bf16[16,1536]{1,0:T(8,128)(2,1)S(1)} %slice_add_fusion), channel_id=1, source_target_pairs={{0,16},{4,20},{8,24},{12,28},{16,0},{20,4},{24,8},{28,12},{1,17},{... | collective-permute-start | bytes 147464 | tf_op jit(solution)/shard_map/ppermute | solution.py:360
  8.8 6.0 %collective-permute-start.4 = (bf16[16,1536]{1,0:T(8,128)(2,1)S(1)}, bf16[16,1536]{1,0:T(8,128)(2,1)S(1)}, u32[]{:S(2)}, u32[]{:S(2)}) collective-permute-start(bf16[16,1536]{1,0:T(8,128)(2,1)S(1)} %slice_add_fusion), channel_id=1, source_target_pairs={{0,24},{4,28},{8,16},{12,20},{16,8},{20,12},{24,0},{28,4},{1,25},{... | collective-permute-start | bytes 147464 | tf_op jit(solution)/shard_map/ppermute | solution.py:360
  10.1 4.6 %collective-permute-start.1 = (bf16[16,1536]{1,0:T(8,128)(2,1)S(1)}, bf16[16,1536]{1,0:T(8,128)(2,1)S(1)}, u32[]{:S(2)}, u32[]{:S(2)}) collective-permute-start(bf16[16,1536]{1,0:T(8,128)(2,1)S(1)} %slice_add_fusion), channel_id=1, source_target_pairs={{0,8},{4,12},{8,0},{12,4},{16,24},{20,28},{24,16},{28,20},{1,9},{5... | collective-permute-start | bytes 147464 | tf_op jit(solution)/shard_map/ppermute | solution.py:360
  10.4 8.0 %collective-permute-start.6 = (bf16[32,3072]{1,0:T(8,128)(2,1)S(1)}, bf16[32,3072]{1,0:T(8,128)(2,1)S(1)}, u32[]{:S(2)}, u32[]{:S(2)}) collective-permute-start(bf16[32,3072]{1,0:T(8,128)(2,1)S(1)} %get-tuple-element.58), channel_id=1, source_target_pairs={{0,1},{1,0},{2,3},{3,2},{4,5},{5,4},{6,7},{7,6},{8,9},{9,8},{10,11... | collective-permute-start | bytes 589832 | tf_op jit(solution)/shard_map/ppermute | solution.py:360
  11.6 7.7 %collective-permute-start.7 = (bf16[32,3072]{1,0:T(8,128)(2,1)S(1)}, bf16[32,3072]{1,0:T(8,128)(2,1)S(1)}, u32[]{:S(2)}, u32[]{:S(2)}) collective-permute-start(bf16[32,3072]{1,0:T(8,128)(2,1)S(1)} %get-tuple-element.59), channel_id=1, source_target_pairs={{0,2},{1,3},{2,0},{3,1},{4,6},{5,7},{6,4},{7,5},{8,10},{9,11},{10,... | collective-permute-start | bytes 589832 | tf_op jit(solution)/shard_map/ppermute | solution.py:360
  14.8 5.1 %collective-permute-start.5 = (bf16[16,1536]{1,0:T(8,128)(2,1)S(1)}, bf16[16,1536]{1,0:T(8,128)(2,1)S(1)}, u32[]{:S(2)}, u32[]{:S(2)}) collective-permute-start(bf16[16,1536]{1,0:T(8,128)(2,1)S(1)} %add_add_fusion), channel_id=1, source_target_pairs={{0,3},{1,2},{2,1},{3,0},{4,7},{5,6},{6,5},{7,4},{8,11},{9,10},{10,... | collective-permute-start | bytes 147464 | tf_op jit(solution)/shard_map/ppermute | solution.py:360
  16.1 5.5 %collective-permute-start.9 = (bf16[16,1536]{1,0:T(8,128)(2,1)S(1)}, bf16[16,1536]{1,0:T(8,128)(2,1)S(1)}, u32[]{:S(2)}, u32[]{:S(2)}) collective-permute-start(bf16[16,1536]{1,0:T(8,128)(2,1)S(1)} %add_add_fusion), channel_id=1, source_target_pairs={{0,2},{1,3},{2,0},{3,1},{4,6},{5,7},{6,4},{7,5},{8,10},{9,11},{10,... | collective-permute-start | bytes 147464 | tf_op jit(solution)/shard_map/ppermute | solution.py:360
  17.1 4.5 %collective-permute-start.8 = (bf16[16,1536]{1,0:T(8,128)(2,1)S(1)}, bf16[16,1536]{1,0:T(8,128)(2,1)S(1)}, u32[]{:S(2)}, u32[]{:S(2)}) collective-permute-start(bf16[16,1536]{1,0:T(8,128)(2,1)S(1)} %add_add_fusion), channel_id=1, source_target_pairs={{0,1},{1,0},{2,3},{3,2},{4,5},{5,4},{6,7},{7,6},{8,9},{9,8},{10,11... | collective-permute-start | bytes 147464 | tf_op jit(solution)/shard_map/ppermute | solution.py:360
  21.6 2.0 %collective-permute-start.10 = (bf16[64,1536]{1,0:T(8,128)(2,1)S(1)}, bf16[64,1536]{1,0:T(8,128)(2,1)S(1)}, u32[]{:S(2)}, u32[]{:S(2)}) collective-permute-start(bf16[64,1536]{1,0:T(8,128)(2,1)S(1)} %pad_maximum_fusion), channel_id=1, source_target_pairs={{0,4},{4,0},{8,12},{12,8},{16,20},{20,16},{24,28},{28,24},{1,5},{5... | collective-permute-start | bytes 589832 | tf_op jit(solution)/shard_map/ppermute | solution.py:360
